TPU v7x, 512 devices: a whole 4x8x8 slice. The times are simulated.
512 devices in a mesh: slab: 32 (over z, x), head: 8 (over y_lo, core), cfg: 2 (over y_hi).
Axes of the slice: x: 4, y: 8 (y_hi: 2, y_lo: 4; y = y_hi * 4 + y_lo), z: 8, core: 2. Of those that a mesh axis runs over, the one named last changes fastest.
Arguments:
- tokens: bfloat16 [8192, 3072], P(('cfg', 'slab'), 'head'), parts along dimension 0, may hold values from -20 to 20
- q_weight: bfloat16 [3072, 3072], P('slab', 'head'), may hold values from -0.109375 to 0.109375
- k_weight: bfloat16 [3072, 3072], P('slab', 'head'), may hold values from -0.109375 to 0.109375
- v_weight: bfloat16 [3072, 3072], P('slab', 'head'), may hold values from -0.109375 to 0.109375
- out_weight: bfloat16 [3072, 3072], P('head', 'slab'), may hold values from -0.109375 to 0.109375
- q_gain: float32 [128], replicated, may hold values from 1 to 2.5
- k_gain: float32 [128], replicated, may hold values from 1 to 2.5
- key_tiles: int32 [24, 64, 6], P('head', 'slab'), may hold values from -1 to 63, as said below
Outputs:
- mixed: bfloat16 [8192, 3072], P(('cfg', 'slab'), 'head'), parts along dimension 0
There are 2 independent parts, one for each index of `cfg`. A program takes and returns all parts, laid end to end along the dimension named above; an argument that names none is the same for every part. Nothing has to cross between parts.
Inputs may be any that keep to these rules, and one draw needn't show every extreme that they name: `key_tiles`: for head h and query tile t of frame f, the row lists in increasing order the tiles of frames f - 1, f and f + 1 whose tile row and tile column lie within that head's reach of t's (a reach of its own for each head, for rows and for columns), then -1 in the remaining slots. Tiles are numbered by frame, then tile row, then tile column; every list holds t itself.
All inputs are finite; a program needn't handle non-finite values.
Results may differ from a plain program's by a relative error of at most 0.018.
Values may be sent and summed in bfloat16 or wider, within the bound.
No kernel may reach another device: no remote copies, remote signals or barrier semaphores. Data moves between devices by JAX's collectives and lax.ppermute only.
A program may use at most 64 MiB of HBM per device.

v0:
```python
import jax
import jax.numpy as jnp
from jax import lax
from jax.sharding import PartitionSpec as P

HDIM = 128
TILE = 64


def extended_2(block, sides, width):
    for axis, dim in sides:
        count = lax.axis_size(axis)
        forward = [(i, i + 1) for i in range(count - 1)]
        backward = [(target, source) for source, target in forward]
        low = lax.ppermute(
            lax.slice_in_dim(block, block.shape[dim] - width, None, axis=dim), axis, forward
        )
        high = lax.ppermute(lax.slice_in_dim(block, 0, width, axis=dim), axis, backward)
        block = jnp.concatenate([low, block, high], axis=dim)
    return block


def head_norm(matrix, gain):
    shaped = matrix.reshape(matrix.shape[0], -1, HDIM)
    scaled = shaped * lax.rsqrt(jnp.mean(shaped * shaped, axis=-1, keepdims=True) + 1e-06) * gain
    return scaled.reshape(matrix.shape[0], -1).astype(jnp.bfloat16)


def split_heads(matrix, local_heads):
    return matrix.reshape(matrix.shape[0], local_heads, HDIM).transpose(1, 0, 2)


def head_terms(q_heads, keys_all, values_all, allowed, local_heads):
    scale = 1.0 / HDIM**0.5
    k_heads = split_heads(keys_all, local_heads)
    v_heads = split_heads(values_all, local_heads)

    def one_head(operands):
        q_one, k_one, v_one, mask_one = operands
        score = jnp.dot(q_one, k_one.T, preferred_element_type=jnp.float32) * scale
        weight = jnp.where(mask_one, jnp.exp(score), jnp.zeros_like(score))
        summed = jnp.dot(weight.astype(jnp.bfloat16), v_one, preferred_element_type=jnp.float32)
        return (summed, jnp.sum(weight, axis=1))

    return lax.map(one_head, (q_heads, k_heads, v_heads, allowed))


def on_device(tokens, q_weight, k_weight, v_weight, out_weight, q_gain, k_gain, key_tiles):
    whole = lax.all_gather(tokens, "head", axis=1, tiled=True)
    rows = whole.shape[0]
    width = q_weight.shape[1]
    local_heads = width // HDIM

    def add_rows(piece):
        return jnp.dot(whole, piece, preferred_element_type=jnp.float32)

    query = add_rows(lax.all_gather(q_weight, "slab", axis=0, tiled=True))
    key = add_rows(lax.all_gather(k_weight, "slab", axis=0, tiled=True))
    value = add_rows(lax.all_gather(v_weight, "slab", axis=0, tiled=True))
    q_norm = head_norm(query, q_gain)
    k_norm = head_norm(key, k_gain)
    v_cast = value.astype(jnp.bfloat16)
    q_heads = split_heads(q_norm, local_heads)
    tiles_here = rows // TILE
    slab_pos = lax.axis_index("slab")
    near_ids = (slab_pos - 1) * tiles_here + jnp.arange(3 * tiles_here, dtype=jnp.int32)
    live = jnp.any(key_tiles[:, :, :, None] == near_ids[None, None, None, :], axis=2)
    allowed = jnp.repeat(jnp.repeat(live, TILE, axis=1), TILE, axis=2)
    packed = jnp.stack([k_norm, v_cast], axis=1)
    extended = extended_2(packed, (("slab", 0),), rows)
    summed, total = head_terms(q_heads, extended[:, 0], extended[:, 1], allowed, local_heads)
    attended = (summed / total[:, :, None]).astype(jnp.bfloat16)
    attended = attended.transpose(1, 0, 2).reshape(rows, width)
    terms = jnp.dot(
        attended,
        lax.all_gather(out_weight, "slab", axis=1, tiled=True),
        preferred_element_type=jnp.float32,
    )
    return lax.psum_scatter(terms.astype(jnp.bfloat16), "head", scatter_dimension=1, tiled=True)


def solution(mesh):
    placed = (
        P(("cfg", "slab"), "head"),
        P("slab", "head"),
        P("slab", "head"),
        P("slab", "head"),
        P("head", "slab"),
        P(),
        P(),
        P("head", "slab", None),
    )
    return jax.shard_map(
        on_device, mesh=mesh, in_specs=placed, out_specs=P(("cfg", "slab"), "head"), check_vma=False
    )
```

profile of v0, /device:TPU:1, one launch (start us, length us, event | category | flops | bytes accessed | tf_op | source)
XLA Modules:
  0.0 399.6 jit_solution(6859922489210414610)
XLA Ops:
  6.5 0.7 all-gather.7.cloned.1.call-update
  7.3 0.7 all-gather.9.cloned.1.call-update
  8.1 0.7 all-gather.5.cloned.1.call-update
  8.8 0.5 all-gather.11.cloned.1.call-update
  9.4 0.8 compare_reduce_fusion
  10.5 0.7 broadcast_bitcast_fusion
  11.2 22.6 %all_gather.15 = bf16[128,3072]{1,0:T(8,128)(2,1)S(1)} all-gather(bf16[128,384]{1,0:T(8,128)(2,1)} %param.10), channel_id=1, replica_groups=mesh['slab'=32,'head'=8,'cfg'=2] {'head'}, dimensions={1}, use_global_device_ids=true | all-gather | bytes 884736 | tf_op jit(solution)/shard_map/all_gather | solution.py:49
  33.8 63.1 %all-gather.7.cloned.1.call-done = bf16[3072,384]{1,0:T(8,128)(2,1)} async-done(((bf16[96,384]{1,0:T(8,128)(2,1)}), bf16[3072,384]{1,0:T(8,128)(2,1)}) %all-gather.7.cloned.1.call-update) | async-done | bytes 2359312 | tf_op jit(solution)/shard_map/all_gather | solution.py:58
  96.9 2.3 fusion.17
  99.5 81.8 %all-gather.9.cloned.1.call-done = bf16[3072,384]{1,0:T(8,128)(2,1)} async-done(((bf16[96,384]{1,0:T(8,128)(2,1)}), bf16[3072,384]{1,0:T(8,128)(2,1)}) %all-gather.9.cloned.1.call-update) | async-done | bytes 2359312 | tf_op jit(solution)/shard_map/all_gather | solution.py:59
  181.3 2.3 fusion.12
  183.6 1.3 collective-permute-start.1
  184.9 4.0 %collective-permute-start = (bf16[128,2,384]{2,0,1:T(8,128)(2,1)S(1)}, bf16[128,2,384]{2,0,1:T(8,128)(2,1)S(1)}, u32[]{:S(2)}, u32[]{:S(2)}) collective-permute-start(bf16[128,2,384]{2,0,1:T(8,128)(2,1)S(1)} %pad_maximum_fusion.1), channel_id=1, source_target_pairs={{0,16},{16,32},{32,48},{48,64},{64,80},{80,96},{96,112},{112,128},... | collective-permute-start | bytes 589832 | tf_op jit(solution)/shard_map/ppermute | solution.py:15
  189.0 76.8 %all-gather.5.cloned.1.call-done = bf16[3072,384]{1,0:T(8,128)(2,1)} async-done(((bf16[96,384]{1,0:T(8,128)(2,1)}), bf16[3072,384]{1,0:T(8,128)(2,1)}) %all-gather.5.cloned.1.call-update) | async-done | bytes 2359312 | tf_op jit(solution)/shard_map/all_gather | solution.py:57
  265.8 2.3 fusion.16
  269.2 2.1 while.12
  269.4 0.3 fusion.33
  270.1 0.3 fusion.33
  270.8 0.3 fusion.33
  271.4 78.7 %all-gather.11.cloned.1.call-done = bf16[384,3072]{0,1:T(8,128)(2,1)} async-done(((bf16[384,96]{0,1:T(8,128)(2,1)}), bf16[384,3072]{0,1:T(8,128)(2,1)}) %all-gather.11.cloned.1.call-update) | async-done | bytes 2359312 | tf_op jit(solution)/shard_map/all_gather | solution.py:76
  350.1 2.6 convolution_convert_fusion
  352.6 1.2 copy.61
  353.8 37.6 %reduce-scatter.4.cloned.1.call-done = bf16[384,128]{1,0:T(8,128)(2,1)} async-done(((bf16[3072,128]{1,0:T(8,128)(2,1)}), bf16[384,128]{1,0:T(8,128)(2,1)}) %reduce-scatter.4.cloned.1.call-update) | async-done | bytes 98320
  391.5 1.6 copy.62
  (49 shorter events, 3.1 us)
Async XLA Ops:
  6.5 2.9 copy-start
  6.5 90.4 %all-gather.7.cloned.1.call-start = ((), (), s32[]{:S(2)}) async-start(), calls=%async_computation.2 | async-start | bytes 2433024 | tf_op jit(solution)/shard_map/all_gather | solution.py:58
  7.3 174.1 %all-gather.9.cloned.1.call-start = ((), (), s32[]{:S(2)}) async-start(), calls=%async_computation.3 | async-start | bytes 2433024 | tf_op jit(solution)/shard_map/all_gather | solution.py:59
  8.0 257.8 %all-gather.5.cloned.1.call-start = ((), (), s32[]{:S(2)}) async-start(), calls=%async_computation.1 | async-start | bytes 2433024 | tf_op jit(solution)/shard_map/all_gather | solution.py:57
  8.7 341.3 %all-gather.11.cloned.1.call-start = ((), (), s32[]{:S(2)}) async-start(), calls=%async_computation.4 | async-start | bytes 2433024 | tf_op jit(solution)/shard_map/all_gather | solution.py:76
  9.3 382.2 %reduce-scatter.4.cloned.1.call-start = ((), (), s32[]{:S(2)}) async-start(), calls=%async_computation.5 | async-start | bytes 884736
  183.6 84.9 %collective-permute-start.1 = (bf16[128,2,384]{2,0,1:T(8,128)(2,1)S(1)}, bf16[128,2,384]{2,0,1:T(8,128)(2,1)S(1)}, u32[]{:S(2)}, u32[]{:S(2)}) collective-permute-start(bf16[128,2,384]{2,0,1:T(8,128)(2,1)S(1)} %pad_maximum_fusion.1), channel_id=1, source_target_pairs={{16,0},{32,16},{48,32},{64,48},{80,64},{96,80},{112,96},{128,112},... | collective-permute-start | bytes 589832 | tf_op jit(solution)/shard_map/ppermute | solution.py:18
  184.9 83.6 %collective-permute-start = (bf16[128,2,384]{2,0,1:T(8,128)(2,1)S(1)}, bf16[128,2,384]{2,0,1:T(8,128)(2,1)S(1)}, u32[]{:S(2)}, u32[]{:S(2)}) collective-permute-start(bf16[128,2,384]{2,0,1:T(8,128)(2,1)S(1)} %pad_maximum_fusion.1), channel_id=1, source_target_pairs={{0,16},{16,32},{32,48},{48,64},{64,80},{80,96},{96,112},{112,128},... | collective-permute-start | bytes 589832 | tf_op jit(solution)/shard_map/ppermute | solution.py:15
Sparse Core Ops, SparseCore 0:
  10.5 86.3 all-gather.6
  100.1 81.2 all-gather.8
  184.5 81.2 all-gather.4
  268.8 81.2 all-gather.10
  354.0 37.4 reduce-scatter.3
where the time goes:
time: 402 us; the launch traced here: 400 us
  waiting for transfers between devices  341 us (85%)
  blocking collectives  22.6 us (6%)
  between operations  13.4 us (3%)
  matrix products  10.8 us (3%)
  local copies, waits for them, and re-layouts  5.53 us (1%)
  starting transfers between devices  5.44 us (1%)
    all_gather x1, waiting for transfers between devices, on_device(): value = add_rows(lax.all_gather(v_weight, 'slab', axis=0, tiled=True))  81.8 us
    all_gather x1, waiting for transfers between devices, on_device(): lax.all_gather(out_weight, 'slab', axis=1, tiled=True)  78.7 us
    all_gather x1, waiting for transfers between devices, on_device(): query = add_rows(lax.all_gather(q_weight, 'slab', axis=0, tiled=True))  76.8 us
    all_gather x1, waiting for transfers between devices, on_device(): key = add_rows(lax.all_gather(k_weight, 'slab', axis=0, tiled=True))  63.1 us
    unnamed x6, waiting for transfers between devices  40.3 us
    all_gather x1, blocking collectives, on_device(): whole = lax.all_gather(tokens, 'head', axis=1, tiled=True)  22.6 us
  transfers between devices with their start and end apart: 7, of which 5 were waited for; matrix products, arithmetic and copies ran while one was open for 3% of the time, Pallas kernels for 0%

commit v1 on v0

v1 whole, which is shorter than its diff:
```python
import jax
import jax.numpy as jnp
from jax import lax
from jax.sharding import Mesh
from jax.sharding import PartitionSpec as P

HDIM = 128
TILE = 64
HEAD = ("y", "core")
SLAB = ("z", "x")


def head_norm(shaped, gain):
    scaled = shaped * lax.rsqrt(jnp.mean(shaped * shaped, axis=-1, keepdims=True) + 1e-06) * gain
    return scaled.astype(jnp.bfloat16)


def neighbours(block):
    count = lax.axis_size(SLAB)
    forward = [(i, i + 1) for i in range(count - 1)]
    backward = [(i + 1, i) for i in range(count - 1)]
    low = lax.ppermute(block, SLAB, forward)
    high = lax.ppermute(block, SLAB, backward)
    return jnp.concatenate([low, block, high], axis=0)


def allowed_mask(key_tiles, tiles_here):
    slab_pos = lax.axis_index(SLAB)
    near_ids = (slab_pos - 1) * tiles_here + jnp.arange(3 * tiles_here, dtype=jnp.int32)
    live = jnp.any(key_tiles[:, :, :, None] == near_ids[None, None, None, :], axis=2)
    return jnp.repeat(jnp.repeat(live, TILE, axis=1), TILE, axis=2)


def attention(q_norm, k_all, v_all, allowed):
    score = jnp.einsum("qhd,khd->hqk", q_norm, k_all, preferred_element_type=jnp.float32)
    score = score * (1.0 / HDIM**0.5)
    weight = jnp.where(allowed, jnp.exp(score), jnp.zeros_like(score))
    summed = jnp.einsum(
        "hqk,khd->hqd", weight.astype(jnp.bfloat16), v_all, preferred_element_type=jnp.float32
    )
    total = jnp.sum(weight, axis=2)
    return (summed / total[:, :, None]).astype(jnp.bfloat16)


def on_device(tokens, q_weight, k_weight, v_weight, out_weight, q_gain, k_gain, key_tiles):
    rows, width = tokens.shape
    heads = width // HDIM
    n_x = lax.axis_size("x")
    n_z = lax.axis_size("z")
    n_head = lax.axis_size(HEAD)
    part = width // n_x

    stacked = jnp.concatenate([q_weight, k_weight, v_weight], axis=1)
    weights = lax.all_gather(stacked, "z", axis=0, tiled=True)

    pieces = tokens.reshape(rows, n_x, part).transpose(1, 0, 2)
    pieces = lax.all_to_all(pieces, "x", split_axis=0, concat_axis=0, tiled=True)
    pieces = lax.all_gather(pieces.reshape(n_x * rows, part), HEAD, axis=0, tiled=False)
    group = pieces.transpose(1, 0, 2).reshape(n_x * rows, n_head * part)

    turned = [(z * n_head + h, h * n_z + z) for z in range(n_z) for h in range(n_head)]
    columns = lax.ppermute(out_weight.T, ("z",) + HEAD, turned)
    columns = lax.all_gather(columns, "x", axis=0, tiled=True).T
    projection = lax.all_gather(columns, "z", axis=0, tiled=True)
    weights, _ = lax.optimization_barrier((weights, columns))

    partial = jnp.dot(group, weights, preferred_element_type=jnp.float32).astype(jnp.bfloat16)
    partial = lax.all_to_all(
        partial.reshape(n_x, rows, 3 * width), "x", split_axis=0, concat_axis=0, tiled=True
    )
    whole = jnp.sum(partial.astype(jnp.float32), axis=0).reshape(rows, 3, heads, HDIM)
    q_norm = head_norm(whole[:, 0], q_gain)
    k_norm = head_norm(whole[:, 1], k_gain)
    v_cast = whole[:, 2].astype(jnp.bfloat16)
    near = neighbours(jnp.stack([k_norm, v_cast], axis=1))
    allowed = allowed_mask(key_tiles, rows // TILE)
    attended = attention(q_norm, near[:, 0], near[:, 1], allowed)
    attended = attended.transpose(1, 0, 2).reshape(rows, width)
    everyone = lax.all_gather(attended, HEAD, axis=1, tiled=True)
    return jnp.dot(everyone, projection, preferred_element_type=jnp.float32).astype(jnp.bfloat16)


def solution(mesh):
    n_slab, n_head, n_cfg = (mesh.shape[a] for a in ("slab", "head", "cfg"))
    fine = Mesh(
        mesh.devices.reshape(n_slab // 4, 4, n_head // 2, 2, n_cfg), ("z", "x", "y", "core", "cfg")
    )
    placed = (
        P(("cfg", "z", "x"), HEAD),
        P(SLAB, HEAD),
        P(SLAB, HEAD),
        P(SLAB, HEAD),
        P(HEAD, SLAB),
        P(),
        P(),
        P(HEAD, SLAB, None),
    )
    return jax.shard_map(
        on_device, mesh=fine, in_specs=placed, out_specs=P(("cfg", "z", "x"), HEAD), check_vma=False
    )
```

time: 402 us -> 133 us (0.33)
  the two profiles are of different devices: /device:TPU:1 before, /device:TPU:127 now
where the time goes in v1:
time: 133 us; the launch traced here: 132 us
  blocking collectives  54.7 us (41%)
  starting transfers between devices  27.1 us (20%)
  waiting for transfers between devices  25.8 us (19%)
  between operations  13.6 us (10%)
  matrix products  7.65 us (6%)
  other arithmetic  2.31 us (2%)
  local copies, waits for them, and re-layouts  1.34 us (1%)
    all_gather x1, blocking collectives, on_device(): lax.all_gather(pieces.reshape(n_x * rows, part), HEAD, axis=0, tiled=False)  20.9 us
    all_gather x1, blocking collectives, on_device(): everyone = lax.all_gather(attended, HEAD, axis=1, tiled=True)  17 us
    all_to_all x1, waiting for transfers between devices, on_device(): lax.all_to_all(partial.reshape(n_x, rows, 3 * width), 'x', split_axis=0,...  14 us
    ppermute x1, starting transfers between devices, on_device(): columns = lax.ppermute(out_weight.T, ('z',) + HEAD, turned)  12.1 us
    all_gather x1, blocking collectives, on_device(): columns = lax.all_gather(columns, 'x', axis=0, tiled=True).T  10.2 us
    ppermute x1, starting transfers between devices, neighbours(): low = lax.ppermute(block, SLAB, forward)  7.75 us
    all_to_all x1, blocking collectives, on_device(): lax.all_to_all(pieces, 'x', split_axis=0, concat_axis=0, tiled=True)  6.61 us
    all_to_all x1, starting transfers between devices, on_device(): lax.all_to_all(partial.reshape(n_x, rows, 3 * width), 'x', split_axis=0,...  5.31 us
  transfers between devices with their start and end apart: 6, of which 4 were waited for; matrix products, arithmetic and copies ran while one was open for 5% of the time, Pallas kernels for 0%

profile of v1, /device:TPU:127, one launch (start us, length us, event | category | flops | bytes accessed | tf_op | source)
XLA Modules:
  0.0 132.5 jit_solution(11662723083546253791)
XLA Ops:
  6.5 1.7 %pad_maximum_fusion.1 = bf16[96,1152]{1,0:T(8,128)(2,1)} fusion(bf16[96,384]{1,0:T(8,128)(2,1)} %param.11, bf16[96,384]{1,0:T(8,128)(2,1)} %param.10, bf16[96,384]{1,0:T(8,128)(2,1)} %param.9), kind=kLoop, calls=%fused_computation.13 | loop fusion | flops 663552 | bytes 442368 | tf_op jit(solution)/shard_map/concatenate | solution.py:53
  8.3 12.1 %collective-permute-start = (bf16[96,384]{1,0:T(8,128)(2,1)}, bf16[96,384]{1,0:T(8,128)(2,1)S(1)}, u32[]{:S(2)}, u32[]{:S(2)}) collective-permute-start(bf16[96,384]{1,0:T(8,128)(2,1)} %bitcast.56), channel_id=1, source_target_pairs={{0,0},{2,64},{4,128},{6,192},{8,256},{10,320},{12,384},{14,448},{6... | collective-permute-start | bytes 221192 | tf_op jit(solution)/shard_map/ppermute | solution.py:62
  20.4 3.0 %collective-permute-done = bf16[96,384]{1,0:T(8,128)(2,1)S(1)} collective-permute-done((bf16[96,384]{1,0:T(8,128)(2,1)}, bf16[96,384]{1,0:T(8,128)(2,1)S(1)}, u32[]{:S(2)}, u32[]{:S(2)}) %collective-permute-start) | collective-permute-done | bytes 73760 | tf_op jit(solution)/shard_map/ppermute | solution.py:62
  23.4 10.2 %all_gather.16 = bf16[384,384]{1,0:T(8,128)(2,1)} all-gather(bf16[96,384]{1,0:T(8,128)(2,1)S(1)} %collective-permute-done), channel_id=1, replica_groups=mesh['z'=8,'x'=4,'y'=4,'core'=2,'cfg'=2] {'x'}, dimensions={0}, use_global_device_ids=true | all-gather | bytes 368640 | tf_op jit(solution)/shard_map/all_gather | solution.py:63
  33.8 6.6 %all_to_all.10 = bf16[4,128,96]{1,2,0:T(8,128)(2,1)S(1)} all-to-all(bf16[4,128,96]{1,2,0:T(8,128)(2,1)S(1)} %bitcast.54), channel_id=1, replica_groups=mesh['z'=8,'x'=4,'y'=4,'core'=2,'cfg'=2] {'x'}, dimensions={0} | all-to-all | bytes 196608 | tf_op jit(solution)/shard_map/all_to_all | solution.py:57
  40.5 20.9 %all_gather.17 = bf16[8,512,96]{1,2,0:T(8,128)(2,1)S(1)} all-gather(bf16[1,512,96]{1,2,0:T(8,128)(2,1)S(1)} %all_gather_reshape.3), channel_id=1, replica_groups=mesh['z'=8,'x'=4,'y'=4,'core'=2,'cfg'=2] {'y','core'}, dimensions={0}, use_global_device_ids=true | all-gather | bytes 884736 | tf_op jit(solution)/shard_map/all_gather | solution.py:58
  61.4 3.7 %convolution_convert_fusion = bf16[1152,512]{0,1:T(8,128)(2,1)} fusion(bf16[768,1152]{1,0:T(8,128)(2,1)} %all-gather.3.cloned.1.call-done, bf16[512,768]{0,1:T(8,128)(2,1)S(1)} %bitcast.52), kind=kOutput, calls=%fused_computation | convolution fusion | flops 906559488 | bytes 3735552 | tf_op jit(solution)/shard_map/dot_general | solution.py:67
  65.1 5.3 %all-to-all-start.1 = ((bf16[4,128,1152]{2,1,0:T(8,128)(2,1)}), bf16[4,128,1152]{2,1,0:T(8,128)(2,1)S(1)}, u32[]{:S(2)}, u32[]{:S(2)}) async-start(bf16[4,128,1152]{2,1,0:T(8,128)(2,1)} %bitcast.8), calls=%async_computation.1 | async-start | bytes 2359296 | tf_op jit(solution)/shard_map/all_to_all | solution.py:68
  70.6 0.1 copy.32
  70.9 0.2 copy.39
  71.2 14.0 %all-to-all-done.1 = bf16[4,128,1152]{2,1,0:T(8,128)(2,1)S(1)} async-done(((bf16[4,128,1152]{2,1,0:T(8,128)(2,1)}), bf16[4,128,1152]{2,1,0:T(8,128)(2,1)S(1)}, u32[]{:S(2)}, u32[]{:S(2)}) %all-to-all-start.1) | async-done | bytes 1179680 | tf_op jit(solution)/shard_map/all_to_all | solution.py:68
  85.1 0.2 convert_reduce_fusion
  85.3 0.2 copy.35
  85.6 0.1 copy.43
  85.7 0.1 copy.44
  85.9 0.1 multiply_reduce_fusion
  86.2 7.8 %collective-permute-start.1 = (bf16[128,2,3,128]{3,0,2,1:T(8,128)(2,1)S(1)}, bf16[128,2,3,128]{3,0,2,1:T(8,128)(2,1)S(1)}, u32[]{:S(2)}, u32[]{:S(2)}) collective-permute-start(bf16[128,2,3,128]{3,0,2,1:T(8,128)(2,1)S(1)} %pad_maximum_fusion.2), channel_id=1, source_target_pairs={{0,16},{16,32},{32,48},{48,64},{64,80},{80,96},{96,112},{112,128},... | collective-permute-start | bytes 589832 | tf_op jit(solution)/shard_map/ppermute | solution.py:22
  93.9 1.9 %collective-permute-start.2 = (bf16[128,2,3,128]{3,0,2,1:T(8,128)(2,1)S(1)}, bf16[128,2,3,128]{3,0,2,1:T(8,128)(2,1)S(1)}, u32[]{:S(2)}, u32[]{:S(2)}) collective-permute-start(bf16[128,2,3,128]{3,0,2,1:T(8,128)(2,1)S(1)} %pad_maximum_fusion.2), channel_id=1, source_target_pairs={{16,0},{32,16},{48,32},{64,48},{80,64},{96,80},{112,96},{128,112},... | collective-permute-start | bytes 589832 | tf_op jit(solution)/shard_map/ppermute | solution.py:23
  95.9 5.1 %collective-permute-done.1 = bf16[128,2,3,128]{3,0,2,1:T(8,128)(2,1)S(1)} collective-permute-done((bf16[128,2,3,128]{3,0,2,1:T(8,128)(2,1)S(1)}, bf16[128,2,3,128]{3,0,2,1:T(8,128)(2,1)S(1)}, u32[]{:S(2)}, u32[]{:S(2)}) %collective-permute-start.1) | collective-permute-done | bytes 196640 | tf_op jit(solution)/shard_map/ppermute | solution.py:22
  101.0 3.7 %collective-permute-done.2 = bf16[128,2,3,128]{3,0,2,1:T(8,128)(2,1)S(1)} collective-permute-done((bf16[128,2,3,128]{3,0,2,1:T(8,128)(2,1)S(1)}, bf16[128,2,3,128]{3,0,2,1:T(8,128)(2,1)S(1)}, u32[]{:S(2)}, u32[]{:S(2)}) %collective-permute-start.2) | collective-permute-done | bytes 196640 | tf_op jit(solution)/shard_map/ppermute | solution.py:23
  104.7 0.5 fusion.7
  105.2 0.3 fusion.3
  105.5 17.0 %all_gather.18 = bf16[128,3072]{0,1:T(8,128)(2,1)S(1)} all-gather(bf16[128,384]{0,1:T(8,128)(2,1)S(1)} %bitcast.55), channel_id=1, replica_groups=mesh['z'=8,'x'=4,'y'=4,'core'=2,'cfg'=2] {'y','core'}, dimensions={1}, use_global_device_ids=true | all-gather | bytes 884736 | tf_op jit(solution)/shard_map/all_gather | solution.py:79
  122.5 3.1 %convolution_convert_fusion.1 = bf16[128,384]{1,0:T(8,128)(2,1)} fusion(bf16[128,3072]{0,1:T(8,128)(2,1)S(1)} %all_gather.18, bf16[3072,384]{0,1:T(8,128)(2,1)} %all-gather.5.cloned.1.call-done), kind=kOutput, calls=%fused_computation.8 | convolution fusion | flops 302039040 | bytes 3244032 | tf_op jit(solution)/shard_map/dot_general | solution.py:80
  (30 shorter events, 0.9 us)
Async XLA Ops:
  6.5 27.1 %copy-start = (bf16[128,384]{1,0:T(8,128)(2,1)S(1)}, bf16[128,384]{1,0:T(8,128)(2,1)}, u32[]{:S(2)}) copy-start(bf16[128,384]{1,0:T(8,128)(2,1)} %param.8) | copy-start | bytes 294916
  6.5 54.9 %all-gather.3.cloned.1.call-start = ((), (), s32[]{:S(2)}) async-start(), calls=%async_computation.2 | async-start | bytes 1990656 | tf_op jit(solution)/shard_map/all_gather | solution.py:54
  8.2 114.2 %all-gather.5.cloned.1.call-start = ((), (), s32[]{:S(2)}) async-start(), calls=%async_computation.3 | async-start | bytes 2654208 | tf_op jit(solution)/shard_map/all_gather | solution.py:64
  8.3 15.1 %collective-permute-start = (bf16[96,384]{1,0:T(8,128)(2,1)}, bf16[96,384]{1,0:T(8,128)(2,1)S(1)}, u32[]{:S(2)}, u32[]{:S(2)}) collective-permute-start(bf16[96,384]{1,0:T(8,128)(2,1)} %bitcast.56), channel_id=1, source_target_pairs={{0,0},{2,64},{4,128},{6,192},{8,256},{10,320},{12,384},{14,448},{6... | collective-permute-start | bytes 221192 | tf_op jit(solution)/shard_map/ppermute | solution.py:62
  65.1 5.3 %copy-start.1 = (s32[3,2,6]{2,1,0:T(2,128)S(1)}, s32[3,2,6]{2,1,0:T(2,128)}, u32[]{:S(2)}) copy-start(s32[3,2,6]{2,1,0:T(2,128)} %param.15) | copy-start | bytes 436
  65.1 20.0 %all-to-all-start.1 = ((bf16[4,128,1152]{2,1,0:T(8,128)(2,1)}), bf16[4,128,1152]{2,1,0:T(8,128)(2,1)S(1)}, u32[]{:S(2)}, u32[]{:S(2)}) async-start(bf16[4,128,1152]{2,1,0:T(8,128)(2,1)} %bitcast.8), calls=%async_computation.1 | async-start | bytes 2359296 | tf_op jit(solution)/shard_map/all_to_all | solution.py:68
  85.3 0.7 copy-start.2
  85.9 18.9 %copy-start.3 = (f32[128]{0:T(128)S(1)}, f32[128]{0:T(128)}, u32[]{:S(2)}) copy-start(f32[128]{0:T(128)} %param.13) | copy-start | bytes 1540
  86.2 14.8 %collective-permute-start.1 = (bf16[128,2,3,128]{3,0,2,1:T(8,128)(2,1)S(1)}, bf16[128,2,3,128]{3,0,2,1:T(8,128)(2,1)S(1)}, u32[]{:S(2)}, u32[]{:S(2)}) collective-permute-start(bf16[128,2,3,128]{3,0,2,1:T(8,128)(2,1)S(1)} %pad_maximum_fusion.2), channel_id=1, source_target_pairs={{0,16},{16,32},{32,48},{48,64},{64,80},{80,96},{96,112},{112,128},... | collective-permute-start | bytes 589832 | tf_op jit(solution)/shard_map/ppermute | solution.py:22
  93.9 10.7 %collective-permute-start.2 = (bf16[128,2,3,128]{3,0,2,1:T(8,128)(2,1)S(1)}, bf16[128,2,3,128]{3,0,2,1:T(8,128)(2,1)S(1)}, u32[]{:S(2)}, u32[]{:S(2)}) collective-permute-start(bf16[128,2,3,128]{3,0,2,1:T(8,128)(2,1)S(1)} %pad_maximum_fusion.2), channel_id=1, source_target_pairs={{16,0},{32,16},{48,32},{64,48},{80,64},{96,80},{112,96},{128,112},... | collective-permute-start | bytes 589832 | tf_op jit(solution)/shard_map/ppermute | solution.py:23
Sparse Core Ops, SparseCore 0:
  9.4 42.0 all-gather.2
  53.7 49.1 all-gather.4

commit v2 on v1

--- a/solution.py
+++ b/solution.py
@@ -53,26 +53,35 @@
     stacked = jnp.concatenate([q_weight, k_weight, v_weight], axis=1)
     weights = lax.all_gather(stacked, "z", axis=0, tiled=True)
 
+    turned = [(z * n_head + h, h * n_z + z) for z in range(n_z) for h in range(n_head)]
+    columns = lax.ppermute(out_weight.T, ("z",) + HEAD, turned)
+
     pieces = tokens.reshape(rows, n_x, part).transpose(1, 0, 2)
     pieces = lax.all_to_all(pieces, "x", split_axis=0, concat_axis=0, tiled=True)
     pieces = lax.all_gather(pieces.reshape(n_x * rows, part), HEAD, axis=0, tiled=False)
+    pieces, columns = lax.optimization_barrier((pieces, columns))
     group = pieces.transpose(1, 0, 2).reshape(n_x * rows, n_head * part)
 
-    turned = [(z * n_head + h, h * n_z + z) for z in range(n_z) for h in range(n_head)]
-    columns = lax.ppermute(out_weight.T, ("z",) + HEAD, turned)
     columns = lax.all_gather(columns, "x", axis=0, tiled=True).T
     projection = lax.all_gather(columns, "z", axis=0, tiled=True)
-    weights, _ = lax.optimization_barrier((weights, columns))
+    weights, group, _ = lax.optimization_barrier((weights, group, columns))
 
-    partial = jnp.dot(group, weights, preferred_element_type=jnp.float32).astype(jnp.bfloat16)
-    partial = lax.all_to_all(
-        partial.reshape(n_x, rows, 3 * width), "x", split_axis=0, concat_axis=0, tiled=True
+    def shares(piece):
+        share = jnp.dot(group, piece, preferred_element_type=jnp.float32).astype(jnp.bfloat16)
+        return share.reshape(n_x, rows, -1)
+
+    def owned(share):
+        share = lax.all_to_all(share, "x", split_axis=0, concat_axis=0, tiled=True)
+        return jnp.sum(share.astype(jnp.float32), axis=0).reshape(rows, -1, heads, HDIM)
+
+    key_value = owned(shares(weights[:, width:]))
+    packed = jnp.stack(
+        [head_norm(key_value[:, 0], k_gain), key_value[:, 1].astype(jnp.bfloat16)], axis=1
     )
-    whole = jnp.sum(partial.astype(jnp.float32), axis=0).reshape(rows, 3, heads, HDIM)
-    q_norm = head_norm(whole[:, 0], q_gain)
-    k_norm = head_norm(whole[:, 1], k_gain)
-    v_cast = whole[:, 2].astype(jnp.bfloat16)
-    near = neighbours(jnp.stack([k_norm, v_cast], axis=1))
+    query = shares(weights[:, :width])
+    query, packed = lax.optimization_barrier((query, packed))
+    near = neighbours(packed)
+    q_norm = head_norm(owned(query)[:, 0], q_gain)
     allowed = allowed_mask(key_tiles, rows // TILE)
     attended = attention(q_norm, near[:, 0], near[:, 1], allowed)
     attended = attended.transpose(1, 0, 2).reshape(rows, width)

time: 133 us -> 123 us (0.925)
  the two profiles are of different devices: /device:TPU:127 before, /device:TPU:1 now
where the time goes in v2:
time: 123 us; the launch traced here: 122 us
  blocking collectives  59.2 us (48%)
  starting transfers between devices  21.6 us (18%)
  between operations  13.6 us (11%)
  waiting for transfers between devices  13.2 us (11%)
  matrix products  9.3 us (8%)
  local copies, waits for them, and re-layouts  2.96 us (2%)
  other arithmetic  2.25 us (2%)
    all_gather x1, blocking collectives, on_device(): lax.all_gather(pieces.reshape(n_x * rows, part), HEAD, axis=0, tiled=False)  23.8 us
    all_gather x1, blocking collectives, on_device(): everyone = lax.all_gather(attended, HEAD, axis=1, tiled=True)  23.7 us
    all_gather x1, blocking collectives, on_device(): columns = lax.all_gather(columns, 'x', axis=0, tiled=True).T  11.8 us
    all_to_all x2, waiting for transfers between devices, owned(): share = lax.all_to_all(share, 'x', split_axis=0, concat_axis=0, tiled=True)  10.7 us
    all_to_all x2, starting transfers between devices, owned(): share = lax.all_to_all(share, 'x', split_axis=0, concat_axis=0, tiled=True)  8.41 us
    dot_general x2, matrix products, shares(): jnp.dot(group, piece, preferred_element_type=jnp.float32)  5.38 us
    all_to_all x1, starting transfers between devices, on_device(): lax.all_to_all(pieces, 'x', split_axis=0, concat_axis=0, tiled=True)  4.84 us
    ppermute x1, starting transfers between devices, on_device(): columns = lax.ppermute(out_weight.T, ('z',) + HEAD, turned)  4.83 us
  transfers between devices with their start and end apart: 8, of which 4 were waited for; matrix products, arithmetic and copies ran while one was open for 8% of the time, Pallas kernels for 0%

profile of v2, /device:TPU:1, one launch (start us, length us, event | category | flops | bytes accessed | tf_op | source)
XLA Modules:
  0.0 122.1 jit_solution(1836005639469245403)
XLA Ops:
  6.5 1.7 %pad_maximum_fusion = bf16[96,1152]{1,0:T(8,128)(2,1)} fusion(bf16[96,384]{1,0:T(8,128)(2,1)} %param.11, bf16[96,384]{1,0:T(8,128)(2,1)} %param.10, bf16[96,384]{1,0:T(8,128)(2,1)} %param.9), kind=kLoop, calls=%fused_computation.16 | loop fusion | flops 663552 | bytes 442368 | tf_op jit(solution)/shard_map/concatenate | solution.py:53
  8.2 1.6 %copy.34 = bf16[128,384]{0,1:T(8,128)(2,1)} copy(bf16[128,384]{1,0:T(8,128)(2,1)} %param.8) | data formatting | bytes 196608 | tf_op args[0]
  9.9 4.8 %all-to-all-start = ((bf16[4,128,96]{1,2,0:T(8,128)(2,1)}), bf16[4,128,96]{1,2,0:T(8,128)(2,1)S(1)}, u32[]{:S(2)}, u32[]{:S(2)}) async-start(bf16[4,128,96]{1,2,0:T(8,128)(2,1)} %bitcast.2), calls=%async_computation | async-start | bytes 196608 | tf_op jit(solution)/shard_map/all_to_all | solution.py:60
  14.7 4.8 %collective-permute-start = (bf16[96,384]{1,0:T(8,128)(2,1)}, bf16[96,384]{1,0:T(8,128)(2,1)S(1)}, u32[]{:S(2)}, u32[]{:S(2)}) collective-permute-start(bf16[96,384]{1,0:T(8,128)(2,1)} %bitcast.47), channel_id=1, source_target_pairs={{0,0},{2,64},{4,128},{6,192},{8,256},{10,320},{12,384},{14,448},{6... | collective-permute-start | bytes 221192 | tf_op jit(solution)/shard_map/ppermute | solution.py:57
  19.7 23.8 %all_gather.16 = bf16[8,512,96]{1,2,0:T(8,128)(2,1)S(1)} all-gather(bf16[1,512,96]{1,2,0:T(8,128)(2,1)S(1)} %all_gather_reshape.3), channel_id=1, replica_groups=mesh['z'=8,'x'=4,'y'=4,'core'=2,'cfg'=2] {'y','core'}, dimensions={0}, use_global_device_ids=true | all-gather | bytes 884736 | tf_op jit(solution)/shard_map/all_gather | solution.py:61
  43.4 11.8 %all_gather.17 = bf16[384,384]{1,0:T(8,128)(2,1)} all-gather(bf16[96,384]{1,0:T(8,128)(2,1)S(1)} %collective-permute-done), channel_id=1, replica_groups=mesh['z'=8,'x'=4,'y'=4,'core'=2,'cfg'=2] {'x'}, dimensions={0}, use_global_device_ids=true | all-gather | bytes 368640 | tf_op jit(solution)/shard_map/all_gather | solution.py:65
  55.2 0.9 all-gather.3.cloned.1.call-done
  56.2 3.0 %convolution_convert_fusion = bf16[512,768]{1,0:T(8,128)(2,1)} fusion(bf16[512,768]{0,1:T(8,128)(2,1)S(1)} %bitcast.41, bf16[768,1152]{1,0:T(8,128)(2,1)} %all-gather.3.cloned.1.call-done), kind=kOutput, calls=%fused_computation.1 | convolution fusion | flops 604372992 | bytes 2752512 | tf_op jit(solution)/shard_map/dot_general | solution.py:70
  59.1 4.4 %all-to-all-start.1 = ((bf16[4,128,768]{2,1,0:T(8,128)(2,1)}), bf16[4,128,768]{2,1,0:T(8,128)(2,1)S(1)}, u32[]{:S(2)}, u32[]{:S(2)}) async-start(bf16[4,128,768]{2,1,0:T(8,128)(2,1)} %bitcast.8), calls=%async_computation.1 | async-start | bytes 1572864 | tf_op jit(solution)/shard_map/all_to_all | solution.py:74
  63.5 2.4 %convolution_convert_fusion.1 = bf16[512,384]{1,0:T(8,128)(2,1)} fusion(bf16[512,768]{0,1:T(8,128)(2,1)S(1)} %bitcast.42, bf16[768,1152]{1,0:T(8,128)(2,1)} %all-gather.3.cloned.1.call-done), kind=kOutput, calls=%fused_computation.3 | convolution fusion | flops 302186496 | bytes 1769472 | tf_op jit(solution)/shard_map/dot_general | solution.py:70
  65.9 5.9 %all-to-all-done.1 = bf16[4,128,768]{2,1,0:T(8,128)(2,1)S(1)} async-done(((bf16[4,128,768]{2,1,0:T(8,128)(2,1)}), bf16[4,128,768]{2,1,0:T(8,128)(2,1)S(1)}, u32[]{:S(2)}, u32[]{:S(2)}) %all-to-all-start.1) | async-done | bytes 786464 | tf_op jit(solution)/shard_map/all_to_all | solution.py:74
  71.9 0.2 copy.36
  72.3 0.1 copy.45
  72.4 0.1 multiply_reduce_fusion.1
  72.7 2.2 %collective-permute-start.1 = (bf16[128,2,3,128]{3,0,2,1:T(8,128)(2,1)S(1)}, bf16[128,2,3,128]{3,0,2,1:T(8,128)(2,1)S(1)}, u32[]{:S(2)}, u32[]{:S(2)}) collective-permute-start(bf16[128,2,3,128]{3,0,2,1:T(8,128)(2,1)S(1)} %pad_maximum_fusion.1), channel_id=1, source_target_pairs={{0,16},{16,32},{32,48},{48,64},{64,80},{80,96},{96,112},{112,128},... | collective-permute-start | bytes 589832 | tf_op jit(solution)/shard_map/ppermute | solution.py:22
  75.5 0.2 copy.41
  75.7 1.3 %collective-permute-start.2 = (bf16[128,2,3,128]{3,0,2,1:T(8,128)(2,1)S(1)}, bf16[128,2,3,128]{3,0,2,1:T(8,128)(2,1)S(1)}, u32[]{:S(2)}, u32[]{:S(2)}) collective-permute-start(bf16[128,2,3,128]{3,0,2,1:T(8,128)(2,1)S(1)} %pad_maximum_fusion.1), channel_id=1, source_target_pairs={{16,0},{32,16},{48,32},{64,48},{80,64},{96,80},{112,96},{128,112},... | collective-permute-start | bytes 589832 | tf_op jit(solution)/shard_map/ppermute | solution.py:23
  77.0 4.0 %all-to-all-start.2 = ((bf16[4,128,384]{2,1,0:T(8,128)(2,1)}), bf16[4,128,384]{2,1,0:T(8,128)(2,1)S(1)}, u32[]{:S(2)}, u32[]{:S(2)}) async-start(bf16[4,128,384]{2,1,0:T(8,128)(2,1)} %bitcast.7), calls=%async_computation.2 | async-start | bytes 786432 | tf_op jit(solution)/shard_map/all_to_all | solution.py:74
  81.1 1.4 %collective-permute-done.2 = bf16[128,2,3,128]{3,0,2,1:T(8,128)(2,1)S(1)} collective-permute-done((bf16[128,2,3,128]{3,0,2,1:T(8,128)(2,1)S(1)}, bf16[128,2,3,128]{3,0,2,1:T(8,128)(2,1)S(1)}, u32[]{:S(2)}, u32[]{:S(2)}) %collective-permute-start.2) | collective-permute-done | bytes 196640 | tf_op jit(solution)/shard_map/ppermute | solution.py:23
  82.6 4.8 %all-to-all-done.2 = bf16[4,128,384]{2,1,0:T(8,128)(2,1)S(1)} async-done(((bf16[4,128,384]{2,1,0:T(8,128)(2,1)}), bf16[4,128,384]{2,1,0:T(8,128)(2,1)S(1)}, u32[]{:S(2)}, u32[]{:S(2)}) %all-to-all-start.2) | async-done | bytes 393248 | tf_op jit(solution)/shard_map/all_to_all | solution.py:74
  87.6 0.5 fusion.9
  88.1 0.3 fusion.4
  88.4 23.7 %all_gather.18 = bf16[128,3072]{0,1:T(8,128)(2,1)S(1)} all-gather(bf16[128,384]{0,1:T(8,128)(2,1)S(1)} %bitcast.46), channel_id=1, replica_groups=mesh['z'=8,'x'=4,'y'=4,'core'=2,'cfg'=2] {'y','core'}, dimensions={1}, use_global_device_ids=true | all-gather | bytes 884736 | tf_op jit(solution)/shard_map/all_gather | solution.py:88
  112.1 3.1 %convolution_convert_fusion.2 = bf16[128,384]{1,0:T(8,128)(2,1)} fusion(bf16[128,3072]{0,1:T(8,128)(2,1)S(1)} %all_gather.18, bf16[3072,384]{0,1:T(8,128)(2,1)} %all-gather.5.cloned.1.call-done), kind=kOutput, calls=%fused_computation.10 | convolution fusion | flops 302039040 | bytes 3244032 | tf_op jit(solution)/shard_map/dot_general | solution.py:89
  (36 shorter events, 1.3 us)
Async XLA Ops:
  6.5 49.6 %all-gather.3.cloned.1.call-start = ((), (), s32[]{:S(2)}) async-start(), calls=%async_computation.3 | async-start | bytes 1990656 | tf_op jit(solution)/shard_map/all_gather | solution.py:54
  9.9 9.7 %all-to-all-start = ((bf16[4,128,96]{1,2,0:T(8,128)(2,1)}), bf16[4,128,96]{1,2,0:T(8,128)(2,1)S(1)}, u32[]{:S(2)}, u32[]{:S(2)}) async-start(bf16[4,128,96]{1,2,0:T(8,128)(2,1)} %bitcast.2), calls=%async_computation | async-start | bytes 196608 | tf_op jit(solution)/shard_map/all_to_all | solution.py:60
  14.7 97.4 %all-gather.5.cloned.1.call-start = ((), (), s32[]{:S(2)}) async-start(), calls=%async_computation.4 | async-start | bytes 2654208 | tf_op jit(solution)/shard_map/all_gather | solution.py:66
  14.7 28.7 %collective-permute-start = (bf16[96,384]{1,0:T(8,128)(2,1)}, bf16[96,384]{1,0:T(8,128)(2,1)S(1)}, u32[]{:S(2)}, u32[]{:S(2)}) collective-permute-start(bf16[96,384]{1,0:T(8,128)(2,1)} %bitcast.47), channel_id=1, source_target_pairs={{0,0},{2,64},{4,128},{6,192},{8,256},{10,320},{12,384},{14,448},{6... | collective-permute-start | bytes 221192 | tf_op jit(solution)/shard_map/ppermute | solution.py:57
  59.1 12.7 %all-to-all-start.1 = ((bf16[4,128,768]{2,1,0:T(8,128)(2,1)}), bf16[4,128,768]{2,1,0:T(8,128)(2,1)S(1)}, u32[]{:S(2)}, u32[]{:S(2)}) async-start(bf16[4,128,768]{2,1,0:T(8,128)(2,1)} %bitcast.8), calls=%async_computation.1 | async-start | bytes 1572864 | tf_op jit(solution)/shard_map/all_to_all | solution.py:74
  65.9 6.7 %copy-start.1 = (f32[128]{0:T(128)S(1)}, f32[128]{0:T(128)}, u32[]{:S(2)}) copy-start(f32[128]{0:T(128)} %param.14) | copy-start | bytes 1540
  65.9 9.1 %copy-start = (s32[3,2,6]{2,1,0:T(2,128)S(1)}, s32[3,2,6]{2,1,0:T(2,128)}, u32[]{:S(2)}) copy-start(s32[3,2,6]{2,1,0:T(2,128)} %param.15) | copy-start | bytes 436
  72.7 8.3 %collective-permute-start.1 = (bf16[128,2,3,128]{3,0,2,1:T(8,128)(2,1)S(1)}, bf16[128,2,3,128]{3,0,2,1:T(8,128)(2,1)S(1)}, u32[]{:S(2)}, u32[]{:S(2)}) collective-permute-start(bf16[128,2,3,128]{3,0,2,1:T(8,128)(2,1)S(1)} %pad_maximum_fusion.1), channel_id=1, source_target_pairs={{0,16},{16,32},{32,48},{48,64},{64,80},{80,96},{96,112},{112,128},... | collective-permute-start | bytes 589832 | tf_op jit(solution)/shard_map/ppermute | solution.py:22
  75.4 12.2 %copy-start.2 = (f32[128]{0:T(128)S(1)}, f32[128]{0:T(128)}, u32[]{:S(2)}) copy-start(f32[128]{0:T(128)} %param.13) | copy-start | bytes 1540
  75.7 6.8 %collective-permute-start.2 = (bf16[128,2,3,128]{3,0,2,1:T(8,128)(2,1)S(1)}, bf16[128,2,3,128]{3,0,2,1:T(8,128)(2,1)S(1)}, u32[]{:S(2)}, u32[]{:S(2)}) collective-permute-start(bf16[128,2,3,128]{3,0,2,1:T(8,128)(2,1)S(1)} %pad_maximum_fusion.1), channel_id=1, source_target_pairs={{16,0},{32,16},{48,32},{64,48},{80,64},{96,80},{112,96},{128,112},... | collective-permute-start | bytes 589832 | tf_op jit(solution)/shard_map/ppermute | solution.py:23
  77.0 10.4 %all-to-all-start.2 = ((bf16[4,128,384]{2,1,0:T(8,128)(2,1)}), bf16[4,128,384]{2,1,0:T(8,128)(2,1)S(1)}, u32[]{:S(2)}, u32[]{:S(2)}) async-start(bf16[4,128,384]{2,1,0:T(8,128)(2,1)} %bitcast.7), calls=%async_computation.2 | async-start | bytes 786432 | tf_op jit(solution)/shard_map/all_to_all | solution.py:74
Sparse Core Ops, SparseCore 0:
  9.4 46.6 all-gather.2
  58.2 46.7 all-gather.4

commit v3 on v1

v3 whole, which is shorter than its diff:
```python
import functools

import jax
import jax.numpy as jnp
from jax import lax
from jax.experimental import pallas as pl
from jax.experimental.pallas import tpu as pltpu
from jax.sharding import Mesh
from jax.sharding import PartitionSpec as P

HDIM = 128
TILE = 64
HEAD = ("y", "core")
Z = ("zq", "zp")
SLAB = ("zq", "zp", "x")
MIB = 1024 * 1024


def whole_block(array):
    rank = len(array.shape)
    return pl.BlockSpec(array.shape, lambda *_: (0,) * rank)


def params(mib):
    return pltpu.CompilerParams(vmem_limit_bytes=mib * MIB)


def shares_kernel(group_ref, weight_ref, out_ref):
    share = jnp.dot(group_ref[...], weight_ref[...], preferred_element_type=jnp.float32)
    out_ref[...] = share.astype(jnp.bfloat16).reshape(out_ref.shape)


def shares(group, weights, first, count, n_x):
    rows, depth = group.shape
    wide = 3 * HDIM
    return pl.pallas_call(
        shares_kernel,
        grid=(count,),
        in_specs=[whole_block(group), pl.BlockSpec((depth, wide), lambda i: (0, first + i))],
        out_specs=pl.BlockSpec((n_x, rows // n_x, wide), lambda i: (0, 0, i)),
        out_shape=jax.ShapeDtypeStruct((n_x, rows // n_x, count * wide), jnp.bfloat16),
        compiler_params=params(16),
    )(group, weights)


def normed(total, gain):
    return total * lax.rsqrt(jnp.mean(total * total, axis=-1, keepdims=True) + 1e-06) * gain


def summed(ref, low, high):
    return jnp.sum(ref[:, :, low:high].astype(jnp.float32), axis=0)


def pack_kernel(share_ref, gain_ref, out_ref):
    width = out_ref.shape[1] // 2
    for low in range(0, width, HDIM):
        total = summed(share_ref, low, low + HDIM)
        out_ref[:, low : low + HDIM] = normed(total, gain_ref[...]).astype(jnp.bfloat16)
    out_ref[:, width:] = summed(share_ref, width, 2 * width).astype(jnp.bfloat16)


def pack(share, gain):
    return pl.pallas_call(
        pack_kernel,
        out_shape=jax.ShapeDtypeStruct(share.shape[1:], jnp.bfloat16),
        compiler_params=params(16),
    )(share, gain.reshape(1, HDIM))


def attention_kernel(share_ref, gain_ref, live_ref, before_ref, own_ref, after_ref, out_ref):
    rows, width = out_ref.shape
    near = (before_ref, own_ref, after_ref)
    scale = 1.0 / HDIM**0.5
    for low in range(0, width, HDIM):
        query = normed(summed(share_ref, low, low + HDIM), gain_ref[...]).astype(jnp.bfloat16)
        keys = jnp.concatenate([r[:, low : low + HDIM] for r in near], axis=0)
        values = jnp.concatenate([r[:, width + low : width + low + HDIM] for r in near], axis=0)
        score = lax.dot_general(
            query, keys, (((1,), (1,)), ((), ())), preferred_element_type=jnp.float32
        )
        allowed = jnp.concatenate(
            [
                jnp.broadcast_to(live_ref[pl.ds(low // HDIM * (rows // TILE) + t, 1), :], (TILE, 3 * rows))
                for t in range(rows // TILE)
            ],
            axis=0,
        )
        weight = jnp.where(allowed > 0, jnp.exp(score * scale), 0.0)
        total = jnp.sum(weight, axis=1, keepdims=True)
        mixed = jnp.dot(weight.astype(jnp.bfloat16), values, preferred_element_type=jnp.float32)
        out_ref[:, low : low + HDIM] = (mixed / total).astype(jnp.bfloat16)


def attention(share, gain, live, before, own, after):
    rows, width = share.shape[1:]
    return pl.pallas_call(
        attention_kernel,
        out_shape=jax.ShapeDtypeStruct((rows, width), jnp.bfloat16),
        compiler_params=params(16),
    )(share, gain.reshape(1, HDIM), live, before, own, after)


def project_kernel(steps, left_ref, right_ref, out_ref, total_ref):
    step = pl.program_id(0)
    part = jnp.dot(left_ref[0], right_ref[0], preferred_element_type=jnp.float32)
    for piece in range(1, left_ref.shape[0]):
        part += jnp.dot(left_ref[piece], right_ref[piece], preferred_element_type=jnp.float32)

    @pl.when(step == 0)
    def _():
        total_ref[...] = part

    @pl.when(step > 0)
    def _():
        total_ref[...] += part

    @pl.when(step == steps - 1)
    def _():
        out_ref[...] = total_ref[...].astype(jnp.bfloat16)


def project(left, right):
    pieces, rows, depth = left.shape
    width = right.shape[2]
    steps = 4
    each = pieces // steps
    return pl.pallas_call(
        functools.partial(project_kernel, steps),
        grid=(steps,),
        in_specs=[
            pl.BlockSpec((each, rows, depth), lambda i: (i, 0, 0)),
            pl.BlockSpec((each, depth, width), lambda i: (i, 0, 0)),
        ],
        out_specs=pl.BlockSpec((rows, width), lambda i: (0, 0)),
        out_shape=jax.ShapeDtypeStruct((rows, width), jnp.bfloat16),
        scratch_shapes=[pltpu.VMEM((rows, width), jnp.float32)],
        compiler_params=params(16),
    )(left, right)


def live_rows(key_tiles, tiles_here):
    near_ids = (lax.axis_index(SLAB) - 1) * tiles_here + jnp.arange(3 * tiles_here, dtype=jnp.int32)
    live = jnp.any(key_tiles[:, :, :, None] == near_ids[None, None, None, :], axis=2)
    live = live.reshape(-1, 3 * tiles_here).astype(jnp.float32)
    return jnp.repeat(live, TILE, axis=1)


def on_device(tokens, q_weight, k_weight, v_weight, out_weight, q_gain, k_gain, key_tiles):
    rows, width = tokens.shape
    n_x, n_z, n_head = (lax.axis_size(a) for a in ("x", Z, HEAD))
    part = width // n_x

    stacked = jnp.concatenate([q_weight, k_weight, v_weight], axis=1)
    weights = lax.all_gather(stacked, Z, axis=0, tiled=True)

    turned = [(z * n_head + h, h * n_z + z) for z in range(n_z) for h in range(n_head)]
    columns = lax.ppermute(out_weight.T, Z + HEAD, turned)

    pieces = tokens.reshape(rows, n_x, part).transpose(1, 0, 2)
    pieces = lax.all_to_all(pieces, "x", split_axis=0, concat_axis=0, tiled=True)
    columns = lax.all_to_all(
        jnp.broadcast_to(columns[None], (n_x,) + columns.shape),
        "x",
        split_axis=0,
        concat_axis=0,
        tiled=True,
    )
    pieces, columns = lax.optimization_barrier((pieces, columns))
    pieces = lax.all_gather(pieces.reshape(n_x * rows, part), HEAD, axis=0, tiled=False)
    group = pieces.transpose(1, 0, 2).reshape(n_x * rows, n_head * part)

    columns = columns.reshape(width, width).T
    other = lax.ppermute(columns, "zp", [(0, 1), (1, 0)])
    first = lax.axis_index("zp") == 0
    pair = jnp.stack([jnp.where(first, columns, other), jnp.where(first, other, columns)])
    projection = lax.all_gather(pair, "zq", axis=0, tiled=True)
    weights, group, _ = lax.optimization_barrier((weights, group, pair))

    key_value = shares(group, weights, 1, 2, n_x)
    query = shares(group, weights, 0, 1, n_x)
    key_value = lax.all_to_all(key_value, "x", split_axis=0, concat_axis=0, tiled=True)
    query = lax.all_to_all(query, "x", split_axis=0, concat_axis=0, tiled=True)
    packed = pack(key_value, k_gain)
    count = lax.axis_size(SLAB)
    before = lax.ppermute(packed, SLAB, [(i, i + 1) for i in range(count - 1)])
    after = lax.ppermute(packed, SLAB, [(i + 1, i) for i in range(count - 1)])
    live = live_rows(key_tiles, rows // TILE)
    attended = attention(query, q_gain, live, before, packed, after)
    everyone = lax.all_gather(attended, HEAD, axis=0, tiled=False)
    return project(everyone, projection)


def solution(mesh):
    n_slab, n_head, n_cfg = (mesh.shape[a] for a in ("slab", "head", "cfg"))
    fine = Mesh(
        mesh.devices.reshape(n_slab // 8, 2, 4, n_head // 2, 2, n_cfg),
        ("zq", "zp", "x", "y", "core", "cfg"),
    )
    placed = (
        P(("cfg",) + SLAB, HEAD),
        P(SLAB, HEAD),
        P(SLAB, HEAD),
        P(SLAB, HEAD),
        P(HEAD, SLAB),
        P(),
        P(),
        P(HEAD, SLAB, None),
    )
    return jax.shard_map(
        on_device, mesh=fine, in_specs=placed, out_specs=P(("cfg",) + SLAB, HEAD), check_vma=False
    )
```

time: 133 us -> 150 us (1.13)
  the two profiles are of different devices: /device:TPU:127 before, /device:TPU:73 now
where the time goes in v3:
time: 150 us; the launch traced here: 149 us
  blocking collectives  46.5 us (31%)
  waiting for transfers between devices  44.1 us (29%)
  starting transfers between devices  30.1 us (20%)
  between operations  13.6 us (9%)
  local copies, waits for them, and re-layouts  8.08 us (5%)
  Pallas kernels  4.72 us (3%)
  other arithmetic  1.93 us (1%)
    all_gather x1, blocking collectives, on_device(): lax.all_gather(pieces.reshape(n_x * rows, part), HEAD, axis=0, tiled=False)  20.1 us
    ppermute x1, waiting for transfers between devices, on_device(): before = lax.ppermute(packed, SLAB, [(i, i + 1) for i in range(count - 1)])  17.4 us
    all_gather x1, blocking collectives, on_device(): everyone = lax.all_gather(attended, HEAD, axis=0, tiled=False)  16.6 us
    ppermute x1, waiting for transfers between devices, on_device(): other = lax.ppermute(columns, 'zp', [(0, 1), (1, 0)])  13 us
    all_to_all x1, waiting for transfers between devices, on_device(): lax.all_to_all(key_value, 'x', split_axis=0, concat_axis=0, tiled=True)  11 us
    all_to_all x1, blocking collectives, on_device(): lax.all_to_all(jnp.broadcast_to(columns[None], (n_x,) + columns.shape), '...  9.74 us
    unnamed x17, local copies, waits for them, and re-layouts  6.44 us
    ppermute x1, starting transfers between devices, on_device(): columns = lax.ppermute(out_weight.T, Z + HEAD, turned)  5.69 us
  transfers between devices with their start and end apart: 9, of which 4 were waited for; matrix products, arithmetic and copies ran while one was open for 2% of the time, Pallas kernels for 2%

profile of v3, /device:TPU:73, one launch (start us, length us, event | category | flops | bytes accessed | tf_op | source)
XLA Modules:
  0.0 149.1 jit_solution(9575756747707848222)
XLA Ops:
  6.5 1.7 %pad_maximum_fusion.1 = bf16[96,1152]{1,0:T(8,128)(2,1)} fusion(bf16[96,384]{1,0:T(8,128)(2,1)} %param.11, bf16[96,384]{1,0:T(8,128)(2,1)} %param.10, bf16[96,384]{1,0:T(8,128)(2,1)} %param.9), kind=kLoop, calls=%fused_computation.3 | loop fusion | flops 663552 | bytes 442368 | tf_op jit(solution)/shard_map/concatenate | solution.py:153
  8.2 1.6 %copy.21 = bf16[128,384]{0,1:T(8,128)(2,1)} copy(bf16[128,384]{1,0:T(8,128)(2,1)} %param.8) | data formatting | bytes 196608 | tf_op args[0]
  9.9 4.0 %all-to-all-start = ((bf16[4,128,96]{1,2,0:T(8,128)(2,1)}), bf16[4,128,96]{1,2,0:T(8,128)(2,1)S(1)}, u32[]{:S(2)}, u32[]{:S(2)}) async-start(bf16[4,128,96]{1,2,0:T(8,128)(2,1)} %bitcast.1), calls=%async_computation | async-start | bytes 196608 | tf_op jit(solution)/shard_map/all_to_all | solution.py:160
  13.9 5.7 %collective-permute-start = (bf16[96,384]{1,0:T(8,128)(2,1)}, bf16[96,384]{1,0:T(8,128)(2,1)S(1)}, u32[]{:S(2)}, u32[]{:S(2)}) collective-permute-start(bf16[96,384]{1,0:T(8,128)(2,1)} %bitcast.26), channel_id=1, source_target_pairs={{0,0},{2,64},{4,128},{6,192},{8,256},{10,320},{12,384},{14,448},{6... | collective-permute-start | bytes 221192 | tf_op jit(solution)/shard_map/ppermute | solution.py:157
  19.6 2.7 %collective-permute-done = bf16[96,384]{1,0:T(8,128)(2,1)S(1)} collective-permute-done((bf16[96,384]{1,0:T(8,128)(2,1)}, bf16[96,384]{1,0:T(8,128)(2,1)S(1)}, u32[]{:S(2)}, u32[]{:S(2)}) %collective-permute-start) | collective-permute-done | bytes 73760 | tf_op jit(solution)/shard_map/ppermute | solution.py:157
  22.3 9.7 %all_to_all.20 = bf16[4,96,384]{2,1,0:T(8,128)(2,1)S(1)} all-to-all(bf16[4,96,384]{2,1,0:T(8,128)(2,1)S(1)} %broadcast_in_dim.4), channel_id=1, replica_groups=mesh['zq'=4,'zp'=2,'x'=4,'y'=4,'core'=2,'cfg'=2] {'x'}, dimensions={0} | all-to-all | bytes 589824 | tf_op jit(solution)/shard_map/all_to_all | solution.py:161
  32.1 5.7 %collective-permute-start.1 = (bf16[384,384]{0,1:T(8,128)(2,1)S(1)}, bf16[384,384]{0,1:T(8,128)(2,1)S(1)}, u32[]{:S(2)}, u32[]{:S(2)}) collective-permute-start(bf16[384,384]{0,1:T(8,128)(2,1)S(1)} %bitcast.25), channel_id=1, source_target_pairs={{0,64},{64,0},{1,65},{65,1},{2,66},{66,2},{3,67},{67,3},{4,68},{68... | collective-permute-start | bytes 884744 | tf_op jit(solution)/shard_map/ppermute | solution.py:173
  37.8 13.0 %collective-permute-done.1 = bf16[384,384]{0,1:T(8,128)(2,1)S(1)} collective-permute-done((bf16[384,384]{0,1:T(8,128)(2,1)S(1)}, bf16[384,384]{0,1:T(8,128)(2,1)S(1)}, u32[]{:S(2)}, u32[]{:S(2)}) %collective-permute-start.1) | collective-permute-done | bytes 294944 | tf_op jit(solution)/shard_map/ppermute | solution.py:173
  51.0 1.1 copy.25
  52.2 20.1 %all_gather.16 = bf16[8,512,96]{1,2,0:T(8,128)(2,1)S(1)} all-gather(bf16[1,512,96]{1,2,0:T(8,128)(2,1)S(1)} %all_gather_reshape.3), channel_id=1, replica_groups=mesh['zq'=4,'zp'=2,'x'=4,'y'=4,'core'=2,'cfg'=2] {'y','core'}, dimensions={0}, use_global_device_ids=true | all-gather | bytes 884736 | tf_op jit(solution)/shard_map/all_gather | solution.py:169
  72.6 1.5 copy-done
  74.1 1.4 shard_map.83
  75.5 0.9 copy-done.2
  76.3 3.6 %all-to-all-start.3 = ((bf16[4,128,768]{2,1,0:T(8,128)(2,1)}), bf16[4,128,768]{2,1,0:T(8,128)(2,1)S(1)}, u32[]{:S(2)}, u32[]{:S(2)}) async-start(bf16[4,128,768]{2,1,0:T(8,128)(2,1)} %copy-done.2), calls=%async_computation.3 | async-start | bytes 1572864 | tf_op jit(solution)/shard_map/all_to_all | solution.py:181
  80.6 0.8 copy-done.4
  81.4 11.0 %all-to-all-done.3.share_ref = bf16[4,128,768]{2,1,0:T(8,128)(2,1)S(1)} async-done(((bf16[4,128,768]{2,1,0:T(8,128)(2,1)}), bf16[4,128,768]{2,1,0:T(8,128)(2,1)S(1)}, u32[]{:S(2)}, u32[]{:S(2)}) %all-to-all-start.3) | async-done | bytes 786464 | tf_op jit(solution)/shard_map/all_to_all | solution.py:181
  92.3 3.5 %all-to-all-start.2 = ((bf16[4,128,384]{2,1,0:T(8,128)(2,1)}), bf16[4,128,384]{2,1,0:T(8,128)(2,1)S(1)}, u32[]{:S(2)}, u32[]{:S(2)}) async-start(bf16[4,128,384]{2,1,0:T(8,128)(2,1)} %copy-done.4), calls=%async_computation.2 | async-start | bytes 786432 | tf_op jit(solution)/shard_map/all_to_all | solution.py:182
  96.0 3.3 %collective-permute-start.2 = (bf16[128,768]{1,0:T(8,128)(2,1)S(1)}, bf16[128,768]{1,0:T(8,128)(2,1)S(1)}, u32[]{:S(2)}, u32[]{:S(2)}) collective-permute-start(bf16[128,768]{1,0:T(8,128)(2,1)S(1)} %shard_map.84.own_ref), channel_id=1, source_target_pairs={{0,16},{16,32},{32,48},{48,64},{64,80},{80,96},{96,112},{112,128},... | collective-permute-start | bytes 589832 | tf_op jit(solution)/shard_map/ppermute | solution.py:185
  99.3 4.3 %collective-permute-start.3 = (bf16[128,768]{1,0:T(8,128)(2,1)S(1)}, bf16[128,768]{1,0:T(8,128)(2,1)S(1)}, u32[]{:S(2)}, u32[]{:S(2)}) collective-permute-start(bf16[128,768]{1,0:T(8,128)(2,1)S(1)} %shard_map.84.own_ref), channel_id=1, source_target_pairs={{16,0},{32,16},{48,32},{64,48},{80,64},{96,80},{112,96},{128,112},... | collective-permute-start | bytes 589832 | tf_op jit(solution)/shard_map/ppermute | solution.py:186
  104.0 17.4 %collective-permute-done.2.before_ref = bf16[128,768]{1,0:T(8,128)(2,1)S(1)} collective-permute-done((bf16[128,768]{1,0:T(8,128)(2,1)S(1)}, bf16[128,768]{1,0:T(8,128)(2,1)S(1)}, u32[]{:S(2)}, u32[]{:S(2)}) %collective-permute-start.2) | collective-permute-done | bytes 196640 | tf_op jit(solution)/shard_map/ppermute | solution.py:185
  121.4 0.7 shard_map.85
  122.1 16.6 %all-gather = bf16[1024,384]{1,0:T(8,128)(2,1)S(1)} all-gather(bf16[128,384]{1,0:T(8,128)(2,1)S(1)} %shard_map.85), channel_id=2, replica_groups=mesh['zq'=4,'zp'=2,'x'=4,'y'=4,'core'=2,'cfg'=2] {'y','core'}, dimensions={0}, use_global_device_ids=true | all-gather | bytes 884736 | tf_op jit(solution)/shard_map/all_gather | solution.py:189
  138.7 1.7 %copy-done.3 = bf16[8,384,384]{2,1,0:T(8,128)(2,1)S(1)} copy-done((bf16[8,384,384]{2,1,0:T(8,128)(2,1)S(1)}, bf16[8,384,384]{2,1,0:T(8,128)(2,1)}, u32[]{:S(2)}) %copy-start.3) | copy-done | bytes 2359320
  140.4 1.8 %shard_map.86 = bf16[128,384]{1,0:T(8,128)(2,1)} custom-call(bf16[8,128,384]{2,1,0:T(8,128)(2,1)S(1)} %bitcast.21, bf16[8,384,384]{2,1,0:T(8,128)(2,1)S(1)} %copy-done.3), custom_call_target="tpu_custom_call" | custom-call | tf_op jit(solution)/shard_map/pallas_call | solution.py:127
  (35 shorter events, 1.7 us)
Async XLA Ops:
  6.5 65.8 %all-gather.4.cloned.1.call-start = ((), (), s32[]{:S(2)}) async-start(), calls=%async_computation.4 | async-start | bytes 1990656 | tf_op jit(solution)/shard_map/all_gather | solution.py:154
  9.9 9.7 %all-to-all-start = ((bf16[4,128,96]{1,2,0:T(8,128)(2,1)}), bf16[4,128,96]{1,2,0:T(8,128)(2,1)S(1)}, u32[]{:S(2)}, u32[]{:S(2)}) async-start(bf16[4,128,96]{1,2,0:T(8,128)(2,1)} %bitcast.1), calls=%async_computation | async-start | bytes 196608 | tf_op jit(solution)/shard_map/all_to_all | solution.py:160
  13.9 124.8 %all-gather.6.cloned.1.call-start = ((), (), s32[]{:S(2)}) async-start(), calls=%async_computation.5 | async-start | bytes 2949120 | tf_op jit(solution)/shard_map/all_gather | solution.py:176
  13.9 8.4 %collective-permute-start = (bf16[96,384]{1,0:T(8,128)(2,1)}, bf16[96,384]{1,0:T(8,128)(2,1)S(1)}, u32[]{:S(2)}, u32[]{:S(2)}) collective-permute-start(bf16[96,384]{1,0:T(8,128)(2,1)} %bitcast.26), channel_id=1, source_target_pairs={{0,0},{2,64},{4,128},{6,192},{8,256},{10,320},{12,384},{14,448},{6... | collective-permute-start | bytes 221192 | tf_op jit(solution)/shard_map/ppermute | solution.py:157
  32.1 18.7 %collective-permute-start.1 = (bf16[384,384]{0,1:T(8,128)(2,1)S(1)}, bf16[384,384]{0,1:T(8,128)(2,1)S(1)}, u32[]{:S(2)}, u32[]{:S(2)}) collective-permute-start(bf16[384,384]{0,1:T(8,128)(2,1)S(1)} %bitcast.25), channel_id=1, source_target_pairs={{0,64},{64,0},{1,65},{65,1},{2,66},{66,2},{3,67},{67,3},{4,68},{68... | collective-permute-start | bytes 884744 | tf_op jit(solution)/shard_map/ppermute | solution.py:173
  72.6 1.5 copy-start
  74.1 5.9 %copy-start.1 = (bf16[768,1152]{1,0:T(8,128)(2,1)S(1)}, bf16[768,1152]{1,0:T(8,128)(2,1)}, u32[]{:S(2)}) copy-start(bf16[768,1152]{1,0:T(8,128)(2,1)} %all-gather.4.cloned.1.call-done.weight_ref) | copy-start | bytes 5308420
  75.4 0.9 copy-start.2
  76.3 19.5 %copy-start.5 = (f32[128]{0:T(128)S(1)}, f32[128]{0:T(128)}, u32[]{:S(2)}) copy-start(f32[128]{0:T(128)} %param.14) | copy-start | bytes 1540
  76.3 16.0 %all-to-all-start.3 = ((bf16[4,128,768]{2,1,0:T(8,128)(2,1)}), bf16[4,128,768]{2,1,0:T(8,128)(2,1)S(1)}, u32[]{:S(2)}, u32[]{:S(2)}) async-start(bf16[4,128,768]{2,1,0:T(8,128)(2,1)} %copy-done.2), calls=%async_computation.3 | async-start | bytes 1572864 | tf_op jit(solution)/shard_map/all_to_all | solution.py:181
  80.0 23.7 %copy-start.7 = (s32[3,2,6]{2,1,0:T(2,128)S(1)}, s32[3,2,6]{2,1,0:T(2,128)}, u32[]{:S(2)}) copy-start(s32[3,2,6]{2,1,0:T(2,128)} %param.15) | copy-start | bytes 436
  80.0 41.4 %copy-start.6 = (f32[128]{0:T(128)S(1)}, f32[128]{0:T(128)}, u32[]{:S(2)}) copy-start(f32[128]{0:T(128)} %param.13) | copy-start | bytes 1540
  80.6 0.8 copy-start.4
  92.3 11.6 %all-to-all-start.2 = ((bf16[4,128,384]{2,1,0:T(8,128)(2,1)}), bf16[4,128,384]{2,1,0:T(8,128)(2,1)S(1)}, u32[]{:S(2)}, u32[]{:S(2)}) async-start(bf16[4,128,384]{2,1,0:T(8,128)(2,1)} %copy-done.4), calls=%async_computation.2 | async-start | bytes 786432 | tf_op jit(solution)/shard_map/all_to_all | solution.py:182
  96.0 25.4 %collective-permute-start.2 = (bf16[128,768]{1,0:T(8,128)(2,1)S(1)}, bf16[128,768]{1,0:T(8,128)(2,1)S(1)}, u32[]{:S(2)}, u32[]{:S(2)}) collective-permute-start(bf16[128,768]{1,0:T(8,128)(2,1)S(1)} %shard_map.84.own_ref), channel_id=1, source_target_pairs={{0,16},{16,32},{32,48},{48,64},{64,80},{80,96},{96,112},{112,128},... | collective-permute-start | bytes 589832 | tf_op jit(solution)/shard_map/ppermute | solution.py:185
  99.3 22.0 %collective-permute-start.3 = (bf16[128,768]{1,0:T(8,128)(2,1)S(1)}, bf16[128,768]{1,0:T(8,128)(2,1)S(1)}, u32[]{:S(2)}, u32[]{:S(2)}) collective-permute-start(bf16[128,768]{1,0:T(8,128)(2,1)S(1)} %shard_map.84.own_ref), channel_id=1, source_target_pairs={{16,0},{32,16},{48,32},{64,48},{80,64},{96,80},{112,96},{128,112},... | collective-permute-start | bytes 589832 | tf_op jit(solution)/shard_map/ppermute | solution.py:186
  138.7 1.7 %copy-start.3 = (bf16[8,384,384]{2,1,0:T(8,128)(2,1)S(1)}, bf16[8,384,384]{2,1,0:T(8,128)(2,1)}, u32[]{:S(2)}) copy-start(bf16[8,384,384]{2,1,0:T(8,128)(2,1)} %all-gather.6.cloned.1.call-done.right_ref) | copy-start | bytes 7077892
Sparse Core Ops, SparseCore 0:
  9.4 46.8 all-gather.3
  58.4 64.1 all-gather.5

commit v4 on v3

--- a/solution.py
+++ b/solution.py
@@ -11,8 +11,7 @@
 HDIM = 128
 TILE = 64
 HEAD = ("y", "core")
-Z = ("zq", "zp")
-SLAB = ("zq", "zp", "x")
+SLAB = ("z", "x")
 MIB = 1024 * 1024
 
 
@@ -39,8 +38,35 @@
         in_specs=[whole_block(group), pl.BlockSpec((depth, wide), lambda i: (0, first + i))],
         out_specs=pl.BlockSpec((n_x, rows // n_x, wide), lambda i: (0, 0, i)),
         out_shape=jax.ShapeDtypeStruct((n_x, rows // n_x, count * wide), jnp.bfloat16),
-        compiler_params=params(16),
+        compiler_params=params(56),
     )(group, weights)
+
+
+def turned_shares_kernel(place_ref, group_ref, weight_ref, *out_refs):
+    rows = out_refs[0].shape[0]
+    for step, out_ref in enumerate(out_refs):
+        slab = jnp.bitwise_xor(place_ref[0], step)
+        group = group_ref[pl.ds(pl.multiple_of(slab * rows, rows), rows), :]
+        share = jnp.dot(group, weight_ref[...], preferred_element_type=jnp.float32)
+        out_ref[...] = share.astype(jnp.bfloat16)
+
+
+def turned_shares(group, weights, n_x):
+    rows, depth = group.shape
+    wide = 3 * HDIM
+    place = lax.axis_index("x").astype(jnp.int32).reshape(1)
+    block = (rows // n_x, wide)
+    return pl.pallas_call(
+        turned_shares_kernel,
+        grid_spec=pltpu.PrefetchScalarGridSpec(
+            num_scalar_prefetch=1,
+            grid=(1,),
+            in_specs=[whole_block(group), pl.BlockSpec((depth, wide), lambda i, p: (0, 0))],
+            out_specs=[pl.BlockSpec(block, lambda i, p: (0, 0))] * n_x,
+        ),
+        out_shape=[jax.ShapeDtypeStruct(block, jnp.bfloat16)] * n_x,
+        compiler_params=params(56),
+    )(place, group, weights)
 
 
 def normed(total, gain):
@@ -67,12 +93,14 @@
     )(share, gain.reshape(1, HDIM))
 
 
-def attention_kernel(share_ref, gain_ref, live_ref, before_ref, own_ref, after_ref, out_ref):
+def attention_kernel(*refs):
+    *share_refs, gain_ref, live_ref, before_ref, own_ref, after_ref, out_ref = refs
     rows, width = out_ref.shape
     near = (before_ref, own_ref, after_ref)
     scale = 1.0 / HDIM**0.5
     for low in range(0, width, HDIM):
-        query = normed(summed(share_ref, low, low + HDIM), gain_ref[...]).astype(jnp.bfloat16)
+        query = sum(r[:, low : low + HDIM].astype(jnp.float32) for r in share_refs)
+        query = normed(query, gain_ref[...]).astype(jnp.bfloat16)
         keys = jnp.concatenate([r[:, low : low + HDIM] for r in near], axis=0)
         values = jnp.concatenate([r[:, width + low : width + low + HDIM] for r in near], axis=0)
         score = lax.dot_general(
@@ -91,20 +119,26 @@
         out_ref[:, low : low + HDIM] = (mixed / total).astype(jnp.bfloat16)
 
 
-def attention(share, gain, live, before, own, after):
-    rows, width = share.shape[1:]
+def attention(query, gain, live, before, own, after):
+    rows, width = query[0].shape
     return pl.pallas_call(
         attention_kernel,
         out_shape=jax.ShapeDtypeStruct((rows, width), jnp.bfloat16),
         compiler_params=params(16),
-    )(share, gain.reshape(1, HDIM), live, before, own, after)
+    )(*query, gain.reshape(1, HDIM), live, before, own, after)
 
 
 def project_kernel(steps, left_ref, right_ref, out_ref, total_ref):
     step = pl.program_id(0)
-    part = jnp.dot(left_ref[0], right_ref[0], preferred_element_type=jnp.float32)
-    for piece in range(1, left_ref.shape[0]):
-        part += jnp.dot(left_ref[piece], right_ref[piece], preferred_element_type=jnp.float32)
+    part = sum(
+        lax.dot_general(
+            left_ref[piece],
+            right_ref[piece],
+            (((1,), (1,)), ((), ())),
+            preferred_element_type=jnp.float32,
+        )
+        for piece in range(left_ref.shape[0])
+    )
 
     @pl.when(step == 0)
     def _():
@@ -121,7 +155,7 @@
 
 def project(left, right):
     pieces, rows, depth = left.shape
-    width = right.shape[2]
+    width = right.shape[1]
     steps = 4
     each = pieces // steps
     return pl.pallas_call(
@@ -129,12 +163,12 @@
         grid=(steps,),
         in_specs=[
             pl.BlockSpec((each, rows, depth), lambda i: (i, 0, 0)),
-            pl.BlockSpec((each, depth, width), lambda i: (i, 0, 0)),
+            pl.BlockSpec((each, width, depth), lambda i: (i, 0, 0)),
         ],
         out_specs=pl.BlockSpec((rows, width), lambda i: (0, 0)),
         out_shape=jax.ShapeDtypeStruct((rows, width), jnp.bfloat16),
         scratch_shapes=[pltpu.VMEM((rows, width), jnp.float32)],
-        compiler_params=params(16),
+        compiler_params=params(56),
     )(left, right)
 
 
@@ -147,39 +181,33 @@
 
 def on_device(tokens, q_weight, k_weight, v_weight, out_weight, q_gain, k_gain, key_tiles):
     rows, width = tokens.shape
-    n_x, n_z, n_head = (lax.axis_size(a) for a in ("x", Z, HEAD))
+    n_x, n_z, n_head = (lax.axis_size(a) for a in ("x", "z", HEAD))
     part = width // n_x
 
     stacked = jnp.concatenate([q_weight, k_weight, v_weight], axis=1)
-    weights = lax.all_gather(stacked, Z, axis=0, tiled=True)
+    weights = lax.all_gather(stacked, "z", axis=0, tiled=True)
 
     turned = [(z * n_head + h, h * n_z + z) for z in range(n_z) for h in range(n_head)]
-    columns = lax.ppermute(out_weight.T, Z + HEAD, turned)
+    columns = lax.ppermute(out_weight.T, ("z",) + HEAD, turned)
 
     pieces = tokens.reshape(rows, n_x, part).transpose(1, 0, 2)
     pieces = lax.all_to_all(pieces, "x", split_axis=0, concat_axis=0, tiled=True)
-    columns = lax.all_to_all(
-        jnp.broadcast_to(columns[None], (n_x,) + columns.shape),
-        "x",
-        split_axis=0,
-        concat_axis=0,
-        tiled=True,
-    )
+    pieces = lax.all_gather(pieces.reshape(n_x * rows, part), HEAD, axis=0, tiled=False)
     pieces, columns = lax.optimization_barrier((pieces, columns))
-    pieces = lax.all_gather(pieces.reshape(n_x * rows, part), HEAD, axis=0, tiled=False)
     group = pieces.transpose(1, 0, 2).reshape(n_x * rows, n_head * part)
 
-    columns = columns.reshape(width, width).T
-    other = lax.ppermute(columns, "zp", [(0, 1), (1, 0)])
-    first = lax.axis_index("zp") == 0
-    pair = jnp.stack([jnp.where(first, columns, other), jnp.where(first, other, columns)])
-    projection = lax.all_gather(pair, "zq", axis=0, tiled=True)
-    weights, group, _ = lax.optimization_barrier((weights, group, pair))
+    columns = lax.all_gather(columns, "x", axis=0, tiled=True)
+    projection = lax.all_gather(columns, "z", axis=0, tiled=False)
+    weights, group, _ = lax.optimization_barrier((weights, group, columns))
 
     key_value = shares(group, weights, 1, 2, n_x)
-    query = shares(group, weights, 0, 1, n_x)
     key_value = lax.all_to_all(key_value, "x", split_axis=0, concat_axis=0, tiled=True)
-    query = lax.all_to_all(query, "x", split_axis=0, concat_axis=0, tiled=True)
+    query = turned_shares(group, weights, n_x)
+    key_value, *query = lax.optimization_barrier((key_value, *query))
+    query = [
+        lax.ppermute(share, "x", [(i, i ^ step) for i in range(n_x)]) if step else share
+        for step, share in enumerate(query)
+    ]
     packed = pack(key_value, k_gain)
     count = lax.axis_size(SLAB)
     before = lax.ppermute(packed, SLAB, [(i, i + 1) for i in range(count - 1)])
@@ -193,8 +221,7 @@
 def solution(mesh):
     n_slab, n_head, n_cfg = (mesh.shape[a] for a in ("slab", "head", "cfg"))
     fine = Mesh(
-        mesh.devices.reshape(n_slab // 8, 2, 4, n_head // 2, 2, n_cfg),
-        ("zq", "zp", "x", "y", "core", "cfg"),
+        mesh.devices.reshape(n_slab // 4, 4, n_head // 2, 2, n_cfg), ("z", "x", "y", "core", "cfg")
     )
     placed = (
         P(("cfg",) + SLAB, HEAD),

time: 150 us -> 131 us (0.87)
  the two profiles are of different devices: /device:TPU:73 before, /device:TPU:1 now
where the time goes in v4:
time: 131 us; the launch traced here: 130 us
  blocking collectives  60.8 us (46%)
  starting transfers between devices  27.9 us (21%)
  between operations  13.5 us (10%)
  waiting for transfers between devices  11.2 us (9%)
  Pallas kernels  10.8 us (8%)
  local copies, waits for them, and re-layouts  3.99 us (3%)
  other arithmetic  1.78 us (1%)
    all_gather x1, blocking collectives, on_device(): everyone = lax.all_gather(attended, HEAD, axis=0, tiled=False)  25.2 us
    all_gather x1, blocking collectives, on_device(): lax.all_gather(pieces.reshape(n_x * rows, part), HEAD, axis=0, tiled=False)  23.8 us
    all_gather x1, blocking collectives, on_device(): columns = lax.all_gather(columns, 'x', axis=0, tiled=True)  11.8 us
    ppermute x3, starting transfers between devices, on_device(): lax.ppermute(share, 'x', [(i, i ^ step) for i in range(n_x)])  10.2 us
    all_to_all x1, waiting for transfers between devices, on_device(): lax.all_to_all(key_value, 'x', split_axis=0, concat_axis=0, tiled=True)  5.84 us
    all_to_all x1, starting transfers between devices, on_device(): lax.all_to_all(pieces, 'x', split_axis=0, concat_axis=0, tiled=True)  4.84 us
    ppermute x1, starting transfers between devices, on_device(): columns = lax.ppermute(out_weight.T, ('z',) + HEAD, turned)  4.83 us
    all_to_all x1, starting transfers between devices, on_device(): lax.all_to_all(key_value, 'x', split_axis=0, concat_axis=0, tiled=True)  4.52 us
  transfers between devices with their start and end apart: 10, of which 4 were waited for; matrix products, arithmetic and copies ran while one was open for 2% of the time, Pallas kernels for 5%

profile of v4, /device:TPU:1, one launch (start us, length us, event | category | flops | bytes accessed | tf_op | source)
XLA Modules:
  0.0 130.0 jit_solution(7216105374009513398)
XLA Ops:
  6.5 1.7 %pad_maximum_fusion = bf16[96,1152]{1,0:T(8,128)(2,1)} fusion(bf16[96,384]{1,0:T(8,128)(2,1)} %param.11, bf16[96,384]{1,0:T(8,128)(2,1)} %param.10, bf16[96,384]{1,0:T(8,128)(2,1)} %param.9), kind=kLoop, calls=%fused_computation | loop fusion | flops 663552 | bytes 442368 | tf_op jit(solution)/shard_map/concatenate | solution.py:187
  8.2 1.6 %copy.18 = bf16[128,384]{0,1:T(8,128)(2,1)} copy(bf16[128,384]{1,0:T(8,128)(2,1)} %param.8) | data formatting | bytes 196608 | tf_op args[0]
  9.9 4.8 %all-to-all-start = ((bf16[4,128,96]{1,2,0:T(8,128)(2,1)}), bf16[4,128,96]{1,2,0:T(8,128)(2,1)S(1)}, u32[]{:S(2)}, u32[]{:S(2)}) async-start(bf16[4,128,96]{1,2,0:T(8,128)(2,1)} %bitcast.1), calls=%async_computation | async-start | bytes 196608 | tf_op jit(solution)/shard_map/all_to_all | solution.py:194
  14.7 4.8 %collective-permute-start = (bf16[96,384]{1,0:T(8,128)(2,1)}, bf16[96,384]{1,0:T(8,128)(2,1)S(1)}, u32[]{:S(2)}, u32[]{:S(2)}) collective-permute-start(bf16[96,384]{1,0:T(8,128)(2,1)} %bitcast.19), channel_id=1, source_target_pairs={{0,0},{2,64},{4,128},{6,192},{8,256},{10,320},{12,384},{14,448},{6... | collective-permute-start | bytes 221192 | tf_op jit(solution)/shard_map/ppermute | solution.py:191
  19.7 23.8 %all_gather.22 = bf16[8,512,96]{1,2,0:T(8,128)(2,1)S(1)} all-gather(bf16[1,512,96]{1,2,0:T(8,128)(2,1)S(1)} %all_gather_reshape.3), channel_id=1, replica_groups=mesh['z'=8,'x'=4,'y'=4,'core'=2,'cfg'=2] {'y','core'}, dimensions={0}, use_global_device_ids=true | all-gather | bytes 884736 | tf_op jit(solution)/shard_map/all_gather | solution.py:195
  43.4 11.8 %all_gather.23 = bf16[384,384]{1,0:T(8,128)(2,1)} all-gather(bf16[96,384]{1,0:T(8,128)(2,1)S(1)} %collective-permute-done), channel_id=1, replica_groups=mesh['z'=8,'x'=4,'y'=4,'core'=2,'cfg'=2] {'x'}, dimensions={0}, use_global_device_ids=true | all-gather | bytes 368640 | tf_op jit(solution)/shard_map/all_gather | solution.py:199
  55.3 0.9 all-gather.5.cloned.1.call-done.weight_ref
  56.2 1.2 copy.20.group_ref
  57.4 3.3 %shard_map.82 = bf16[4,128,768]{2,1,0:T(8,128)(2,1)} custom-call(bf16[512,768]{1,0:T(8,128)(2,1)} %copy.20.group_ref, bf16[768,1152]{1,0:T(8,128)(2,1)} %all-gather.5.cloned.1.call-done.weight_ref), custom_call_target="tpu_custom_call" | custom-call | tf_op jit(solution)/shard_map/pallas_call | solution.py:35
  60.7 4.5 %all-to-all-start.1 = ((bf16[4,128,768]{2,1,0:T(8,128)(2,1)}), bf16[4,128,768]{2,1,0:T(8,128)(2,1)S(1)}, u32[]{:S(2)}, u32[]{:S(2)}) async-start(bf16[4,128,768]{2,1,0:T(8,128)(2,1)} %shard_map.82), calls=%async_computation.1 | async-start | bytes 1572864 | tf_op jit(solution)/shard_map/all_to_all | solution.py:204
  65.2 2.5 %shard_map.83 = (bf16[128,384]{1,0:T(8,128)(2,1)}, bf16[128,384]{1,0:T(8,128)(2,1)}, bf16[128,384]{1,0:T(8,128)(2,1)}, bf16[128,384]{1,0:T(8,128)(2,1)}) custom-call(s32[1]{0:T(128)} %bitcast.5.place_ref, bf16[512,768]{1,0:T(8,128)(2,1)} %copy.20.group_ref, bf16[768,1152]{1,0:T(8,128)(2,1)} %all-gather.5.cloned.1.call-done.weight_ref), custom_call_target="tpu_custom_call" | custom-call | tf_op jit(solution)/shard_map/pallas_call | solution.py:59
  67.7 5.8 %all-to-all-done.1.share_ref = bf16[4,128,768]{2,1,0:T(8,128)(2,1)S(1)} async-done(((bf16[4,128,768]{2,1,0:T(8,128)(2,1)}), bf16[4,128,768]{2,1,0:T(8,128)(2,1)S(1)}, u32[]{:S(2)}, u32[]{:S(2)}) %all-to-all-start.1) | async-done | bytes 786464 | tf_op jit(solution)/shard_map/all_to_all | solution.py:204
  73.5 0.2 shard_map.84.refs_7_
  73.7 2.2 %collective-permute-start.4 = (bf16[128,768]{1,0:T(8,128)(2,1)S(1)}, bf16[128,768]{1,0:T(8,128)(2,1)S(1)}, u32[]{:S(2)}, u32[]{:S(2)}) collective-permute-start(bf16[128,768]{1,0:T(8,128)(2,1)S(1)} %shard_map.84.refs_7_), channel_id=1, source_target_pairs={{0,16},{16,32},{32,48},{48,64},{64,80},{80,96},{96,112},{112,128},... | collective-permute-start | bytes 589832 | tf_op jit(solution)/shard_map/ppermute | solution.py:213
  76.0 1.3 collective-permute-start.5
  77.3 4.0 %collective-permute-start.1 = (bf16[128,384]{1,0:T(8,128)(2,1)}, bf16[128,384]{1,0:T(8,128)(2,1)S(1)}, u32[]{:S(2)}, u32[]{:S(2)}) collective-permute-start(bf16[128,384]{1,0:T(8,128)(2,1)} %get-tuple-element.27), channel_id=1, source_target_pairs={{0,16},{16,0},{32,48},{48,32},{1,17},{17,1},{33,49},{49,33},{2,18}... | collective-permute-start | bytes 294920 | tf_op jit(solution)/shard_map/ppermute | solution.py:208
  81.3 3.8 %collective-permute-start.2 = (bf16[128,384]{1,0:T(8,128)(2,1)}, bf16[128,384]{1,0:T(8,128)(2,1)S(1)}, u32[]{:S(2)}, u32[]{:S(2)}) collective-permute-start(bf16[128,384]{1,0:T(8,128)(2,1)} %get-tuple-element.28), channel_id=1, source_target_pairs={{0,32},{16,48},{32,0},{48,16},{1,33},{17,49},{33,1},{49,17},{2,34}... | collective-permute-start | bytes 294920 | tf_op jit(solution)/shard_map/ppermute | solution.py:208
  85.0 2.5 %collective-permute-start.3 = (bf16[128,384]{1,0:T(8,128)(2,1)}, bf16[128,384]{1,0:T(8,128)(2,1)S(1)}, u32[]{:S(2)}, u32[]{:S(2)}) collective-permute-start(bf16[128,384]{1,0:T(8,128)(2,1)} %get-tuple-element.29), channel_id=1, source_target_pairs={{0,48},{16,32},{32,16},{48,0},{1,49},{17,33},{33,17},{49,1},{2,50}... | collective-permute-start | bytes 294920 | tf_op jit(solution)/shard_map/ppermute | solution.py:208
  87.8 0.6 collective-permute-done.2.refs_2_
  88.4 3.8 %collective-permute-done.3.refs_3_ = bf16[128,384]{1,0:T(8,128)(2,1)S(1)} collective-permute-done((bf16[128,384]{1,0:T(8,128)(2,1)}, bf16[128,384]{1,0:T(8,128)(2,1)S(1)}, u32[]{:S(2)}, u32[]{:S(2)}) %collective-permute-start.3) | collective-permute-done | bytes 98336 | tf_op jit(solution)/shard_map/ppermute | solution.py:208
  92.2 0.9 copy-done
  93.1 0.7 shard_map.85
  93.8 25.2 %all-gather = bf16[1024,384]{1,0:T(8,128)(2,1)} all-gather(bf16[128,384]{1,0:T(8,128)(2,1)S(1)} %shard_map.85), channel_id=2, replica_groups=mesh['z'=8,'x'=4,'y'=4,'core'=2,'cfg'=2] {'y','core'}, dimensions={0}, use_global_device_ids=true | all-gather | bytes 884736 | tf_op jit(solution)/shard_map/all_gather | solution.py:217
  119.0 4.1 %shard_map.86 = bf16[128,384]{1,0:T(8,128)(2,1)} custom-call(bf16[8,128,384]{2,1,0:T(8,128)(2,1)} %bitcast.17, bf16[8,384,384]{2,1,0:T(8,128)(2,1)} %bitcast.18), custom_call_target="tpu_custom_call" | custom-call | tf_op jit(solution)/shard_map/pallas_call | solution.py:161
  (25 shorter events, 0.4 us)
Async XLA Ops:
  6.5 49.6 %all-gather.5.cloned.1.call-start = ((), (), s32[]{:S(2)}) async-start(), calls=%async_computation.2 | async-start | bytes 1990656 | tf_op jit(solution)/shard_map/all_gather | solution.py:188
  9.9 9.7 %all-to-all-start = ((bf16[4,128,96]{1,2,0:T(8,128)(2,1)}), bf16[4,128,96]{1,2,0:T(8,128)(2,1)S(1)}, u32[]{:S(2)}, u32[]{:S(2)}) async-start(bf16[4,128,96]{1,2,0:T(8,128)(2,1)} %bitcast.1), calls=%async_computation | async-start | bytes 196608 | tf_op jit(solution)/shard_map/all_to_all | solution.py:194
  14.7 104.3 %all-gather.7.cloned.1.call-start = ((), (), s32[]{:S(2)}) async-start(), calls=%async_computation.3 | async-start | bytes 2654208 | tf_op jit(solution)/shard_map/all_gather | solution.py:200
  14.7 28.7 %collective-permute-start = (bf16[96,384]{1,0:T(8,128)(2,1)}, bf16[96,384]{1,0:T(8,128)(2,1)S(1)}, u32[]{:S(2)}, u32[]{:S(2)}) collective-permute-start(bf16[96,384]{1,0:T(8,128)(2,1)} %bitcast.19), channel_id=1, source_target_pairs={{0,0},{2,64},{4,128},{6,192},{8,256},{10,320},{12,384},{14,448},{6... | collective-permute-start | bytes 221192 | tf_op jit(solution)/shard_map/ppermute | solution.py:191
  60.6 12.9 %copy-start.1 = (f32[128]{0:T(128)S(1)}, f32[128]{0:T(128)}, u32[]{:S(2)}) copy-start(f32[128]{0:T(128)} %param.14) | copy-start | bytes 1540
  60.6 26.9 %copy-start.3 = (s32[3,2,6]{2,1,0:T(2,128)S(1)}, s32[3,2,6]{2,1,0:T(2,128)}, u32[]{:S(2)}) copy-start(s32[3,2,6]{2,1,0:T(2,128)} %param.15) | copy-start | bytes 436
  60.6 31.5 %copy-start.2 = (f32[128]{0:T(128)S(1)}, f32[128]{0:T(128)}, u32[]{:S(2)}) copy-start(f32[128]{0:T(128)} %param.13) | copy-start | bytes 1540
  60.7 12.9 %all-to-all-start.1 = ((bf16[4,128,768]{2,1,0:T(8,128)(2,1)}), bf16[4,128,768]{2,1,0:T(8,128)(2,1)S(1)}, u32[]{:S(2)}, u32[]{:S(2)}) async-start(bf16[4,128,768]{2,1,0:T(8,128)(2,1)} %shard_map.82), calls=%async_computation.1 | async-start | bytes 1572864 | tf_op jit(solution)/shard_map/all_to_all | solution.py:204
  73.7 18.4 %collective-permute-start.4 = (bf16[128,768]{1,0:T(8,128)(2,1)S(1)}, bf16[128,768]{1,0:T(8,128)(2,1)S(1)}, u32[]{:S(2)}, u32[]{:S(2)}) collective-permute-start(bf16[128,768]{1,0:T(8,128)(2,1)S(1)} %shard_map.84.refs_7_), channel_id=1, source_target_pairs={{0,16},{16,32},{32,48},{48,64},{64,80},{80,96},{96,112},{112,128},... | collective-permute-start | bytes 589832 | tf_op jit(solution)/shard_map/ppermute | solution.py:213
  76.0 16.2 %collective-permute-start.5 = (bf16[128,768]{1,0:T(8,128)(2,1)S(1)}, bf16[128,768]{1,0:T(8,128)(2,1)S(1)}, u32[]{:S(2)}, u32[]{:S(2)}) collective-permute-start(bf16[128,768]{1,0:T(8,128)(2,1)S(1)} %shard_map.84.refs_7_), channel_id=1, source_target_pairs={{16,0},{32,16},{48,32},{64,48},{80,64},{96,80},{112,96},{128,112},... | collective-permute-start | bytes 589832 | tf_op jit(solution)/shard_map/ppermute | solution.py:214
  77.3 10.5 %collective-permute-start.1 = (bf16[128,384]{1,0:T(8,128)(2,1)}, bf16[128,384]{1,0:T(8,128)(2,1)S(1)}, u32[]{:S(2)}, u32[]{:S(2)}) collective-permute-start(bf16[128,384]{1,0:T(8,128)(2,1)} %get-tuple-element.27), channel_id=1, source_target_pairs={{0,16},{16,0},{32,48},{48,32},{1,17},{17,1},{33,49},{49,33},{2,18}... | collective-permute-start | bytes 294920 | tf_op jit(solution)/shard_map/ppermute | solution.py:208
  81.3 7.1 %collective-permute-start.2 = (bf16[128,384]{1,0:T(8,128)(2,1)}, bf16[128,384]{1,0:T(8,128)(2,1)S(1)}, u32[]{:S(2)}, u32[]{:S(2)}) collective-permute-start(bf16[128,384]{1,0:T(8,128)(2,1)} %get-tuple-element.28), channel_id=1, source_target_pairs={{0,32},{16,48},{32,0},{48,16},{1,33},{17,49},{33,1},{49,17},{2,34}... | collective-permute-start | bytes 294920 | tf_op jit(solution)/shard_map/ppermute | solution.py:208
  85.0 7.1 %collective-permute-start.3 = (bf16[128,384]{1,0:T(8,128)(2,1)}, bf16[128,384]{1,0:T(8,128)(2,1)S(1)}, u32[]{:S(2)}, u32[]{:S(2)}) collective-permute-start(bf16[128,384]{1,0:T(8,128)(2,1)} %get-tuple-element.29), channel_id=1, source_target_pairs={{0,48},{16,32},{32,16},{48,0},{1,49},{17,33},{33,17},{49,1},{2,50}... | collective-permute-start | bytes 294920 | tf_op jit(solution)/shard_map/ppermute | solution.py:208
  92.2 0.9 copy-start
Sparse Core Ops, SparseCore 0:
  9.4 46.6 all-gather.4
  58.2 47.2 all-gather.6

commit v5 on v4

--- a/solution.py
+++ b/solution.py
@@ -24,30 +24,62 @@
     return pltpu.CompilerParams(vmem_limit_bytes=mib * MIB)
 
 
-def shares_kernel(group_ref, weight_ref, out_ref):
-    share = jnp.dot(group_ref[...], weight_ref[...], preferred_element_type=jnp.float32)
-    out_ref[...] = share.astype(jnp.bfloat16).reshape(out_ref.shape)
+def fetches(source, buffer, sems, first):
+    wide = buffer.shape[2]
+    copies = [
+        pltpu.make_async_copy(
+            source.at[:, pl.ds(first + n * wide, wide)], buffer.at[n], sems.at[n]
+        )
+        for n in range(buffer.shape[0])
+    ]
+    for copy in copies:
+        copy.start()
+    return copies
+
+
+def shares_kernel(first, group_ref, weight_ref, out_ref, weights, results, sems, out_sems):
+    wide = weights.shape[2]
+    stores = []
+    for n, copy in enumerate(fetches(weight_ref, weights, sems, first)):
+        copy.wait()
+        share = jnp.dot(group_ref[...], weights[n], preferred_element_type=jnp.float32)
+        results[n] = share.astype(jnp.bfloat16).reshape(results.shape[1:])
+        store = pltpu.make_async_copy(
+            results.at[n], out_ref.at[:, :, pl.ds(n * wide, wide)], out_sems.at[n]
+        )
+        store.start()
+        stores.append(store)
+    for store in stores:
+        store.wait()
 
 
 def shares(group, weights, first, count, n_x):
     rows, depth = group.shape
     wide = 3 * HDIM
     return pl.pallas_call(
-        shares_kernel,
-        grid=(count,),
-        in_specs=[whole_block(group), pl.BlockSpec((depth, wide), lambda i: (0, first + i))],
-        out_specs=pl.BlockSpec((n_x, rows // n_x, wide), lambda i: (0, 0, i)),
+        functools.partial(shares_kernel, first * wide),
+        in_specs=[whole_block(group), pl.BlockSpec(memory_space=pltpu.HBM)],
+        out_specs=pl.BlockSpec(memory_space=pltpu.HBM),
         out_shape=jax.ShapeDtypeStruct((n_x, rows // n_x, count * wide), jnp.bfloat16),
-        compiler_params=params(56),
+        scratch_shapes=[
+            pltpu.VMEM((count, depth, wide), jnp.bfloat16),
+            pltpu.VMEM((count, n_x, rows // n_x, wide), jnp.bfloat16),
+            pltpu.SemaphoreType.DMA((count,)),
+            pltpu.SemaphoreType.DMA((count,)),
+        ],
+        compiler_params=params(16),
     )(group, weights)
 
 
-def turned_shares_kernel(place_ref, group_ref, weight_ref, *out_refs):
+def turned_shares_kernel(place_ref, group_ref, weight_ref, *refs):
+    *out_refs, weights, sems = refs
     rows = out_refs[0].shape[0]
+    (copy,) = fetches(weight_ref, weights, sems, 0)
+    copy.wait()
     for step, out_ref in enumerate(out_refs):
         slab = jnp.bitwise_xor(place_ref[0], step)
         group = group_ref[pl.ds(pl.multiple_of(slab * rows, rows), rows), :]
-        share = jnp.dot(group, weight_ref[...], preferred_element_type=jnp.float32)
+        share = jnp.dot(group, weights[0], preferred_element_type=jnp.float32)
         out_ref[...] = share.astype(jnp.bfloat16)
 
 
@@ -58,14 +90,17 @@
     block = (rows // n_x, wide)
     return pl.pallas_call(
         turned_shares_kernel,
-        grid_spec=pltpu.PrefetchScalarGridSpec(
-            num_scalar_prefetch=1,
-            grid=(1,),
-            in_specs=[whole_block(group), pl.BlockSpec((depth, wide), lambda i, p: (0, 0))],
-            out_specs=[pl.BlockSpec(block, lambda i, p: (0, 0))] * n_x,
-        ),
+        in_specs=[
+            pl.BlockSpec(memory_space=pltpu.SMEM),
+            whole_block(group),
+            pl.BlockSpec(memory_space=pltpu.HBM),
+        ],
         out_shape=[jax.ShapeDtypeStruct(block, jnp.bfloat16)] * n_x,
-        compiler_params=params(56),
+        scratch_shapes=[
+            pltpu.VMEM((1, depth, wide), jnp.bfloat16),
+            pltpu.SemaphoreType.DMA((1,)),
+        ],
+        compiler_params=params(16),
     )(place, group, weights)
 
 
@@ -128,47 +163,34 @@
     )(*query, gain.reshape(1, HDIM), live, before, own, after)
 
 
-def project_kernel(steps, left_ref, right_ref, out_ref, total_ref):
-    step = pl.program_id(0)
-    part = sum(
-        lax.dot_general(
-            left_ref[piece],
-            right_ref[piece],
-            (((1,), (1,)), ((), ())),
-            preferred_element_type=jnp.float32,
-        )
-        for piece in range(left_ref.shape[0])
-    )
-
-    @pl.when(step == 0)
-    def _():
-        total_ref[...] = part
-
-    @pl.when(step > 0)
-    def _():
-        total_ref[...] += part
-
-    @pl.when(step == steps - 1)
-    def _():
-        out_ref[...] = total_ref[...].astype(jnp.bfloat16)
+def project_kernel(left_ref, right_ref, out_ref, rights, sems):
+    copies = [
+        pltpu.make_async_copy(right_ref.at[n], rights.at[n], sems.at[n])
+        for n in range(left_ref.shape[0])
+    ]
+    for copy in copies:
+        copy.start()
+    total = None
+    for n, copy in enumerate(copies):
+        copy.wait()
+        part = lax.dot_general(
+            left_ref[n], rights[n], (((1,), (1,)), ((), ())), preferred_element_type=jnp.float32
+        )
+        total = part if total is None else total + part
+    out_ref[...] = total.astype(jnp.bfloat16)
 
 
 def project(left, right):
-    pieces, rows, depth = left.shape
-    width = right.shape[1]
-    steps = 4
-    each = pieces // steps
-    return pl.pallas_call(
-        functools.partial(project_kernel, steps),
-        grid=(steps,),
-        in_specs=[
-            pl.BlockSpec((each, rows, depth), lambda i: (i, 0, 0)),
-            pl.BlockSpec((each, width, depth), lambda i: (i, 0, 0)),
-        ],
-        out_specs=pl.BlockSpec((rows, width), lambda i: (0, 0)),
-        out_shape=jax.ShapeDtypeStruct((rows, width), jnp.bfloat16),
-        scratch_shapes=[pltpu.VMEM((rows, width), jnp.float32)],
-        compiler_params=params(56),
+    pieces, rows, _ = left.shape
+    return pl.pallas_call(
+        project_kernel,
+        in_specs=[whole_block(left), pl.BlockSpec(memory_space=pltpu.HBM)],
+        out_shape=jax.ShapeDtypeStruct((rows, right.shape[1]), jnp.bfloat16),
+        scratch_shapes=[
+            pltpu.VMEM(right.shape, jnp.bfloat16),
+            pltpu.SemaphoreType.DMA((pieces,)),
+        ],
+        compiler_params=params(16),
     )(left, right)
 
 
@@ -203,7 +225,7 @@
     key_value = shares(group, weights, 1, 2, n_x)
     key_value = lax.all_to_all(key_value, "x", split_axis=0, concat_axis=0, tiled=True)
     query = turned_shares(group, weights, n_x)
-    key_value, *query = lax.optimization_barrier((key_value, *query))
+    key_value, *_ = lax.optimization_barrier((key_value, *query))
     query = [
         lax.ppermute(share, "x", [(i, i ^ step) for i in range(n_x)]) if step else share
         for step, share in enumerate(query)

time: 131 us -> 129 us (0.985)
  Pallas kernels: 10.8 us -> 5.84 us
  local copies, waits for them, and re-layouts: 3.99 us -> 7.47 us
    pallas_call x3, Pallas kernels: 9.91 us -> 4.92 us  [the longest x1 2.89 us: project(): pl.pallas_call(project_kernel, in_specs=[whole_block(left), pl.BlockSpec(...]
    unnamed x9 -> x19, local copies, waits for them, and re-layouts: 2.54 us -> 6.95 us
  transfers between devices with their start and end apart: 10 -> 10, of which waited for: 4 -> 4; matrix products, arithmetic and copies ran while one was open for 2% -> 2% of each run, Pallas kernels for 5% -> 2%
where the time goes in v5:
time: 129 us; the launch traced here: 128 us
  blocking collectives  60 us (47%)
  starting transfers between devices  27.9 us (22%)
  between operations  13.6 us (11%)
  waiting for transfers between devices  11.6 us (9%)
  local copies, waits for them, and re-layouts  7.47 us (6%)
  Pallas kernels  5.84 us (5%)
  other arithmetic  1.77 us (1%)
    all_gather x1, blocking collectives, on_device(): everyone = lax.all_gather(attended, HEAD, axis=0, tiled=False)  24.4 us
    all_gather x1, blocking collectives, on_device(): lax.all_gather(pieces.reshape(n_x * rows, part), HEAD, axis=0, tiled=False)  23.8 us
    all_gather x1, blocking collectives, on_device(): columns = lax.all_gather(columns, 'x', axis=0, tiled=True)  11.8 us
    ppermute x3, starting transfers between devices, on_device(): lax.ppermute(share, 'x', [(i, i ^ step) for i in range(n_x)])  10.2 us
    unnamed x19, local copies, waits for them, and re-layouts  6.95 us
    all_to_all x1, waiting for transfers between devices, on_device(): lax.all_to_all(key_value, 'x', split_axis=0, concat_axis=0, tiled=True)  6.42 us
    all_to_all x1, starting transfers between devices, on_device(): lax.all_to_all(pieces, 'x', split_axis=0, concat_axis=0, tiled=True)  4.84 us
    ppermute x1, starting transfers between devices, on_device(): columns = lax.ppermute(out_weight.T, ('z',) + HEAD, turned)  4.83 us
  transfers between devices with their start and end apart: 10, of which 4 were waited for; matrix products, arithmetic and copies ran while one was open for 2% of the time, Pallas kernels for 2%

profile of v5, /device:TPU:1, one launch (start us, length us, event | category | flops | bytes accessed | tf_op | source)
XLA Modules:
  0.0 128.1 jit_solution(14586730384398416425)
XLA Ops:
  6.5 1.7 %pad_maximum_fusion = bf16[96,1152]{1,0:T(8,128)(2,1)} fusion(bf16[96,384]{1,0:T(8,128)(2,1)} %param.11, bf16[96,384]{1,0:T(8,128)(2,1)} %param.10, bf16[96,384]{1,0:T(8,128)(2,1)} %param.9), kind=kLoop, calls=%fused_computation | loop fusion | flops 663552 | bytes 442368 | tf_op jit(solution)/shard_map/concatenate | solution.py:209
  8.2 1.6 %copy.18 = bf16[128,384]{0,1:T(8,128)(2,1)} copy(bf16[128,384]{1,0:T(8,128)(2,1)} %param.8) | data formatting | bytes 196608 | tf_op args[0]
  9.9 4.8 %all-to-all-start = ((bf16[4,128,96]{1,2,0:T(8,128)(2,1)}), bf16[4,128,96]{1,2,0:T(8,128)(2,1)S(1)}, u32[]{:S(2)}, u32[]{:S(2)}) async-start(bf16[4,128,96]{1,2,0:T(8,128)(2,1)} %bitcast.2), calls=%async_computation | async-start | bytes 196608 | tf_op jit(solution)/shard_map/all_to_all | solution.py:216
  14.7 4.8 %collective-permute-start = (bf16[96,384]{1,0:T(8,128)(2,1)}, bf16[96,384]{1,0:T(8,128)(2,1)S(1)}, u32[]{:S(2)}, u32[]{:S(2)}) collective-permute-start(bf16[96,384]{1,0:T(8,128)(2,1)} %bitcast.19), channel_id=1, source_target_pairs={{0,0},{2,64},{4,128},{6,192},{8,256},{10,320},{12,384},{14,448},{6... | collective-permute-start | bytes 221192 | tf_op jit(solution)/shard_map/ppermute | solution.py:213
  19.7 23.8 %all_gather.22 = bf16[8,512,96]{1,2,0:T(8,128)(2,1)S(1)} all-gather(bf16[1,512,96]{1,2,0:T(8,128)(2,1)S(1)} %all_gather_reshape.3), channel_id=1, replica_groups=mesh['z'=8,'x'=4,'y'=4,'core'=2,'cfg'=2] {'y','core'}, dimensions={0}, use_global_device_ids=true | all-gather | bytes 884736 | tf_op jit(solution)/shard_map/all_gather | solution.py:217
  43.4 11.8 %all_gather.23 = bf16[384,384]{1,0:T(8,128)(2,1)} all-gather(bf16[96,384]{1,0:T(8,128)(2,1)S(1)} %collective-permute-done), channel_id=1, replica_groups=mesh['z'=8,'x'=4,'y'=4,'core'=2,'cfg'=2] {'x'}, dimensions={0}, use_global_device_ids=true | all-gather | bytes 368640 | tf_op jit(solution)/shard_map/all_gather | solution.py:221
  55.3 0.9 all-gather.5.cloned.1.call-done.weight_ref
  56.4 1.5 %copy-done = bf16[768,1152]{1,0:T(8,128)(2,1)S(1)} copy-done((bf16[768,1152]{1,0:T(8,128)(2,1)S(1)}, bf16[768,1152]{1,0:T(8,128)(2,1)}, u32[]{:S(2)}) %copy-start) | copy-done | bytes 1769496
  57.9 1.4 %shard_map.83 = bf16[4,128,768]{2,1,0:T(8,128)(2,1)S(1)} custom-call(bf16[512,768]{1,0:T(8,128)(2,1)S(1)} %copy.20.group_ref, bf16[768,1152]{1,0:T(8,128)(2,1)S(1)} %copy-done), custom_call_target="tpu_custom_call" | custom-call | tf_op jit(solution)/shard_map/pallas_call | solution.py:59
  59.3 0.9 copy-done.2
  60.2 4.5 %all-to-all-start.1 = ((bf16[4,128,768]{2,1,0:T(8,128)(2,1)}), bf16[4,128,768]{2,1,0:T(8,128)(2,1)S(1)}, u32[]{:S(2)}, u32[]{:S(2)}) async-start(bf16[4,128,768]{2,1,0:T(8,128)(2,1)} %copy-done.2), calls=%async_computation.1 | async-start | bytes 1572864 | tf_op jit(solution)/shard_map/all_to_all | solution.py:226
  64.7 0.6 shard_map.82
  66.0 0.6 copy-done.7
  66.7 6.4 %all-to-all-done.1.share_ref = bf16[4,128,768]{2,1,0:T(8,128)(2,1)S(1)} async-done(((bf16[4,128,768]{2,1,0:T(8,128)(2,1)}), bf16[4,128,768]{2,1,0:T(8,128)(2,1)S(1)}, u32[]{:S(2)}, u32[]{:S(2)}) %all-to-all-start.1) | async-done | bytes 786464 | tf_op jit(solution)/shard_map/all_to_all | solution.py:226
  73.3 2.2 %collective-permute-start.4 = (bf16[128,768]{1,0:T(8,128)(2,1)S(1)}, bf16[128,768]{1,0:T(8,128)(2,1)S(1)}, u32[]{:S(2)}, u32[]{:S(2)}) collective-permute-start(bf16[128,768]{1,0:T(8,128)(2,1)S(1)} %shard_map.84.refs_7_), channel_id=1, source_target_pairs={{0,16},{16,32},{32,48},{48,64},{64,80},{80,96},{96,112},{112,128},... | collective-permute-start | bytes 589832 | tf_op jit(solution)/shard_map/ppermute | solution.py:235
  75.5 1.3 %collective-permute-start.5 = (bf16[128,768]{1,0:T(8,128)(2,1)S(1)}, bf16[128,768]{1,0:T(8,128)(2,1)S(1)}, u32[]{:S(2)}, u32[]{:S(2)}) collective-permute-start(bf16[128,768]{1,0:T(8,128)(2,1)S(1)} %shard_map.84.refs_7_), channel_id=1, source_target_pairs={{16,0},{32,16},{48,32},{64,48},{80,64},{96,80},{112,96},{128,112},... | collective-permute-start | bytes 589832 | tf_op jit(solution)/shard_map/ppermute | solution.py:236
  76.8 4.0 %collective-permute-start.1 = (bf16[128,384]{1,0:T(8,128)(2,1)}, bf16[128,384]{1,0:T(8,128)(2,1)S(1)}, u32[]{:S(2)}, u32[]{:S(2)}) collective-permute-start(bf16[128,384]{1,0:T(8,128)(2,1)} %copy-done.7), channel_id=1, source_target_pairs={{0,16},{16,0},{32,48},{48,32},{1,17},{17,1},{33,49},{49,33},{2,18}... | collective-permute-start | bytes 294920 | tf_op jit(solution)/shard_map/ppermute | solution.py:230
  80.8 3.8 %collective-permute-start.2 = (bf16[128,384]{1,0:T(8,128)(2,1)}, bf16[128,384]{1,0:T(8,128)(2,1)S(1)}, u32[]{:S(2)}, u32[]{:S(2)}) collective-permute-start(bf16[128,384]{1,0:T(8,128)(2,1)} %copy-done.6), channel_id=1, source_target_pairs={{0,32},{16,48},{32,0},{48,16},{1,33},{17,49},{33,1},{49,17},{2,34}... | collective-permute-start | bytes 294920 | tf_op jit(solution)/shard_map/ppermute | solution.py:230
  84.6 2.5 %collective-permute-start.3 = (bf16[128,384]{1,0:T(8,128)(2,1)S(1)}, bf16[128,384]{1,0:T(8,128)(2,1)S(1)}, u32[]{:S(2)}, u32[]{:S(2)}) collective-permute-start(bf16[128,384]{1,0:T(8,128)(2,1)S(1)} %get-tuple-element.21), channel_id=1, source_target_pairs={{0,48},{16,32},{32,16},{48,0},{1,49},{17,33},{33,17},{49,1},{2,50}... | collective-permute-start | bytes 294920 | tf_op jit(solution)/shard_map/ppermute | solution.py:230
  87.9 3.6 %collective-permute-done.3.refs_3_ = bf16[128,384]{1,0:T(8,128)(2,1)S(1)} collective-permute-done((bf16[128,384]{1,0:T(8,128)(2,1)S(1)}, bf16[128,384]{1,0:T(8,128)(2,1)S(1)}, u32[]{:S(2)}, u32[]{:S(2)}) %collective-permute-start.3) | collective-permute-done | bytes 98336 | tf_op jit(solution)/shard_map/ppermute | solution.py:230
  91.6 0.7 shard_map.85
  92.3 24.4 %all-gather = bf16[1024,384]{1,0:T(8,128)(2,1)S(1)} all-gather(bf16[128,384]{1,0:T(8,128)(2,1)S(1)} %shard_map.85), channel_id=2, replica_groups=mesh['z'=8,'x'=4,'y'=4,'core'=2,'cfg'=2] {'y','core'}, dimensions={0}, use_global_device_ids=true | all-gather | bytes 884736 | tf_op jit(solution)/shard_map/all_gather | solution.py:239
  116.7 1.7 %copy-done.3 = bf16[3072,384]{1,0:T(8,128)(2,1)S(1)} copy-done((bf16[3072,384]{1,0:T(8,128)(2,1)S(1)}, bf16[3072,384]{1,0:T(8,128)(2,1)}, u32[]{:S(2)}) %copy-start.3) | copy-done | bytes 2359320
  118.4 2.9 %shard_map.86 = bf16[128,384]{1,0:T(8,128)(2,1)} custom-call(bf16[8,128,384]{2,1,0:T(8,128)(2,1)S(1)} %bitcast.14, bf16[8,384,384]{2,1,0:T(8,128)(2,1)S(1)} %bitcast.15), custom_call_target="tpu_custom_call" | custom-call | tf_op jit(solution)/shard_map/pallas_call | solution.py:185
  (35 shorter events, 2.1 us)
Async XLA Ops:
  6.5 49.6 %all-gather.5.cloned.1.call-start = ((), (), s32[]{:S(2)}) async-start(), calls=%async_computation.2 | async-start | bytes 1990656 | tf_op jit(solution)/shard_map/all_gather | solution.py:210
  9.9 9.7 %all-to-all-start = ((bf16[4,128,96]{1,2,0:T(8,128)(2,1)}), bf16[4,128,96]{1,2,0:T(8,128)(2,1)S(1)}, u32[]{:S(2)}, u32[]{:S(2)}) async-start(bf16[4,128,96]{1,2,0:T(8,128)(2,1)} %bitcast.2), calls=%async_computation | async-start | bytes 196608 | tf_op jit(solution)/shard_map/all_to_all | solution.py:216
  14.7 102.0 %all-gather.7.cloned.1.call-start = ((), (), s32[]{:S(2)}) async-start(), calls=%async_computation.3 | async-start | bytes 2654208 | tf_op jit(solution)/shard_map/all_gather | solution.py:222
  14.7 28.7 %collective-permute-start = (bf16[96,384]{1,0:T(8,128)(2,1)}, bf16[96,384]{1,0:T(8,128)(2,1)S(1)}, u32[]{:S(2)}, u32[]{:S(2)}) collective-permute-start(bf16[96,384]{1,0:T(8,128)(2,1)} %bitcast.19), channel_id=1, source_target_pairs={{0,0},{2,64},{4,128},{6,192},{8,256},{10,320},{12,384},{14,448},{6... | collective-permute-start | bytes 221192 | tf_op jit(solution)/shard_map/ppermute | solution.py:213
  56.4 1.5 %copy-start = (bf16[768,1152]{1,0:T(8,128)(2,1)S(1)}, bf16[768,1152]{1,0:T(8,128)(2,1)}, u32[]{:S(2)}) copy-start(bf16[768,1152]{1,0:T(8,128)(2,1)} %all-gather.5.cloned.1.call-done.weight_ref) | copy-start | bytes 5308420
  57.9 6.8 %copy-start.1 = (bf16[768,1152]{1,0:T(8,128)(2,1)S(1)}, bf16[768,1152]{1,0:T(8,128)(2,1)}, u32[]{:S(2)}) copy-start(bf16[768,1152]{1,0:T(8,128)(2,1)} %all-gather.5.cloned.1.call-done.weight_ref) | copy-start | bytes 5308420
  59.3 0.9 copy-start.2
  60.2 12.9 %copy-start.4 = (f32[128]{0:T(128)S(1)}, f32[128]{0:T(128)}, u32[]{:S(2)}) copy-start(f32[128]{0:T(128)} %param.14) | copy-start | bytes 1540
  60.2 26.8 %copy-start.8 = (s32[3,2,6]{2,1,0:T(2,128)S(1)}, s32[3,2,6]{2,1,0:T(2,128)}, u32[]{:S(2)}) copy-start(s32[3,2,6]{2,1,0:T(2,128)} %param.15) | copy-start | bytes 436
  60.2 31.4 %copy-start.5 = (f32[128]{0:T(128)S(1)}, f32[128]{0:T(128)}, u32[]{:S(2)}) copy-start(f32[128]{0:T(128)} %param.13) | copy-start | bytes 1540
  60.2 12.9 %all-to-all-start.1 = ((bf16[4,128,768]{2,1,0:T(8,128)(2,1)}), bf16[4,128,768]{2,1,0:T(8,128)(2,1)S(1)}, u32[]{:S(2)}, u32[]{:S(2)}) async-start(bf16[4,128,768]{2,1,0:T(8,128)(2,1)} %copy-done.2), calls=%async_computation.1 | async-start | bytes 1572864 | tf_op jit(solution)/shard_map/all_to_all | solution.py:226
  65.4 0.6 copy-start.6
  66.0 0.6 copy-start.7
  73.3 18.3 %collective-permute-start.4 = (bf16[128,768]{1,0:T(8,128)(2,1)S(1)}, bf16[128,768]{1,0:T(8,128)(2,1)S(1)}, u32[]{:S(2)}, u32[]{:S(2)}) collective-permute-start(bf16[128,768]{1,0:T(8,128)(2,1)S(1)} %shard_map.84.refs_7_), channel_id=1, source_target_pairs={{0,16},{16,32},{32,48},{48,64},{64,80},{80,96},{96,112},{112,128},... | collective-permute-start | bytes 589832 | tf_op jit(solution)/shard_map/ppermute | solution.py:235
  75.5 16.1 %collective-permute-start.5 = (bf16[128,768]{1,0:T(8,128)(2,1)S(1)}, bf16[128,768]{1,0:T(8,128)(2,1)S(1)}, u32[]{:S(2)}, u32[]{:S(2)}) collective-permute-start(bf16[128,768]{1,0:T(8,128)(2,1)S(1)} %shard_map.84.refs_7_), channel_id=1, source_target_pairs={{16,0},{32,16},{48,32},{64,48},{80,64},{96,80},{112,96},{128,112},... | collective-permute-start | bytes 589832 | tf_op jit(solution)/shard_map/ppermute | solution.py:236
  76.8 10.5 %collective-permute-start.1 = (bf16[128,384]{1,0:T(8,128)(2,1)}, bf16[128,384]{1,0:T(8,128)(2,1)S(1)}, u32[]{:S(2)}, u32[]{:S(2)}) collective-permute-start(bf16[128,384]{1,0:T(8,128)(2,1)} %copy-done.7), channel_id=1, source_target_pairs={{0,16},{16,0},{32,48},{48,32},{1,17},{17,1},{33,49},{49,33},{2,18}... | collective-permute-start | bytes 294920 | tf_op jit(solution)/shard_map/ppermute | solution.py:230
  80.8 7.1 %collective-permute-start.2 = (bf16[128,384]{1,0:T(8,128)(2,1)}, bf16[128,384]{1,0:T(8,128)(2,1)S(1)}, u32[]{:S(2)}, u32[]{:S(2)}) collective-permute-start(bf16[128,384]{1,0:T(8,128)(2,1)} %copy-done.6), channel_id=1, source_target_pairs={{0,32},{16,48},{32,0},{48,16},{1,33},{17,49},{33,1},{49,17},{2,34}... | collective-permute-start | bytes 294920 | tf_op jit(solution)/shard_map/ppermute | solution.py:230
  84.6 7.0 %collective-permute-start.3 = (bf16[128,384]{1,0:T(8,128)(2,1)S(1)}, bf16[128,384]{1,0:T(8,128)(2,1)S(1)}, u32[]{:S(2)}, u32[]{:S(2)}) collective-permute-start(bf16[128,384]{1,0:T(8,128)(2,1)S(1)} %get-tuple-element.21), channel_id=1, source_target_pairs={{0,48},{16,32},{32,16},{48,0},{1,49},{17,33},{33,17},{49,1},{2,50}... | collective-permute-start | bytes 294920 | tf_op jit(solution)/shard_map/ppermute | solution.py:230
  116.7 1.7 %copy-start.3 = (bf16[3072,384]{1,0:T(8,128)(2,1)S(1)}, bf16[3072,384]{1,0:T(8,128)(2,1)}, u32[]{:S(2)}) copy-start(bf16[3072,384]{1,0:T(8,128)(2,1)} %all-gather.7.cloned.1.call-done) | copy-start | bytes 7077892
Sparse Core Ops, SparseCore 0:
  9.4 46.6 all-gather.4
  58.2 46.6 all-gather.6

commit v6 on v4

--- a/solution.py
+++ b/solution.py
@@ -1,5 +1,3 @@
-import functools
-
 import jax
 import jax.numpy as jnp
 from jax import lax
@@ -22,51 +20,6 @@
 
 def params(mib):
     return pltpu.CompilerParams(vmem_limit_bytes=mib * MIB)
-
-
-def shares_kernel(group_ref, weight_ref, out_ref):
-    share = jnp.dot(group_ref[...], weight_ref[...], preferred_element_type=jnp.float32)
-    out_ref[...] = share.astype(jnp.bfloat16).reshape(out_ref.shape)
-
-
-def shares(group, weights, first, count, n_x):
-    rows, depth = group.shape
-    wide = 3 * HDIM
-    return pl.pallas_call(
-        shares_kernel,
-        grid=(count,),
-        in_specs=[whole_block(group), pl.BlockSpec((depth, wide), lambda i: (0, first + i))],
-        out_specs=pl.BlockSpec((n_x, rows // n_x, wide), lambda i: (0, 0, i)),
-        out_shape=jax.ShapeDtypeStruct((n_x, rows // n_x, count * wide), jnp.bfloat16),
-        compiler_params=params(56),
-    )(group, weights)
-
-
-def turned_shares_kernel(place_ref, group_ref, weight_ref, *out_refs):
-    rows = out_refs[0].shape[0]
-    for step, out_ref in enumerate(out_refs):
-        slab = jnp.bitwise_xor(place_ref[0], step)
-        group = group_ref[pl.ds(pl.multiple_of(slab * rows, rows), rows), :]
-        share = jnp.dot(group, weight_ref[...], preferred_element_type=jnp.float32)
-        out_ref[...] = share.astype(jnp.bfloat16)
-
-
-def turned_shares(group, weights, n_x):
-    rows, depth = group.shape
-    wide = 3 * HDIM
-    place = lax.axis_index("x").astype(jnp.int32).reshape(1)
-    block = (rows // n_x, wide)
-    return pl.pallas_call(
-        turned_shares_kernel,
-        grid_spec=pltpu.PrefetchScalarGridSpec(
-            num_scalar_prefetch=1,
-            grid=(1,),
-            in_specs=[whole_block(group), pl.BlockSpec((depth, wide), lambda i, p: (0, 0))],
-            out_specs=[pl.BlockSpec(block, lambda i, p: (0, 0))] * n_x,
-        ),
-        out_shape=[jax.ShapeDtypeStruct(block, jnp.bfloat16)] * n_x,
-        compiler_params=params(56),
-    )(place, group, weights)
 
 
 def normed(total, gain):
@@ -128,50 +81,6 @@
     )(*query, gain.reshape(1, HDIM), live, before, own, after)
 
 
-def project_kernel(steps, left_ref, right_ref, out_ref, total_ref):
-    step = pl.program_id(0)
-    part = sum(
-        lax.dot_general(
-            left_ref[piece],
-            right_ref[piece],
-            (((1,), (1,)), ((), ())),
-            preferred_element_type=jnp.float32,
-        )
-        for piece in range(left_ref.shape[0])
-    )
-
-    @pl.when(step == 0)
-    def _():
-        total_ref[...] = part
-
-    @pl.when(step > 0)
-    def _():
-        total_ref[...] += part
-
-    @pl.when(step == steps - 1)
-    def _():
-        out_ref[...] = total_ref[...].astype(jnp.bfloat16)
-
-
-def project(left, right):
-    pieces, rows, depth = left.shape
-    width = right.shape[1]
-    steps = 4
-    each = pieces // steps
-    return pl.pallas_call(
-        functools.partial(project_kernel, steps),
-        grid=(steps,),
-        in_specs=[
-            pl.BlockSpec((each, rows, depth), lambda i: (i, 0, 0)),
-            pl.BlockSpec((each, width, depth), lambda i: (i, 0, 0)),
-        ],
-        out_specs=pl.BlockSpec((rows, width), lambda i: (0, 0)),
-        out_shape=jax.ShapeDtypeStruct((rows, width), jnp.bfloat16),
-        scratch_shapes=[pltpu.VMEM((rows, width), jnp.float32)],
-        compiler_params=params(56),
-    )(left, right)
-
-
 def live_rows(key_tiles, tiles_here):
     near_ids = (lax.axis_index(SLAB) - 1) * tiles_here + jnp.arange(3 * tiles_here, dtype=jnp.int32)
     live = jnp.any(key_tiles[:, :, :, None] == near_ids[None, None, None, :], axis=2)
@@ -200,14 +109,20 @@
     projection = lax.all_gather(columns, "z", axis=0, tiled=False)
     weights, group, _ = lax.optimization_barrier((weights, group, columns))
 
-    key_value = shares(group, weights, 1, 2, n_x)
+    def shares(piece):
+        share = jnp.dot(group, piece, preferred_element_type=jnp.float32).astype(jnp.bfloat16)
+        return share.reshape(n_x, rows, -1)
+
+    key_value = shares(weights[:, width:])
     key_value = lax.all_to_all(key_value, "x", split_axis=0, concat_axis=0, tiled=True)
-    query = turned_shares(group, weights, n_x)
+    turned = shares(weights[:, :width])
+    place = lax.axis_index("x")
+    query = []
+    for step in range(n_x):
+        share = lax.dynamic_index_in_dim(turned, place ^ step, 0, keepdims=False)
+        pairs = [(i, i ^ step) for i in range(n_x)]
+        query.append(lax.ppermute(share, "x", pairs) if step else share)
     key_value, *query = lax.optimization_barrier((key_value, *query))
-    query = [
-        lax.ppermute(share, "x", [(i, i ^ step) for i in range(n_x)]) if step else share
-        for step, share in enumerate(query)
-    ]
     packed = pack(key_value, k_gain)
     count = lax.axis_size(SLAB)
     before = lax.ppermute(packed, SLAB, [(i, i + 1) for i in range(count - 1)])
@@ -215,7 +130,8 @@
     live = live_rows(key_tiles, rows // TILE)
     attended = attention(query, q_gain, live, before, packed, after)
     everyone = lax.all_gather(attended, HEAD, axis=0, tiled=False)
-    return project(everyone, projection)
+    total = jnp.einsum("hrd,hnd->rn", everyone, projection, preferred_element_type=jnp.float32)
+    return total.astype(jnp.bfloat16)
 
 
 def solution(mesh):

time: 131 us -> 129 us (0.985)
  the two profiles are of different devices: /device:TPU:1 before, /device:TPU:39 now
where the time goes in v6:
time: 129 us; the launch traced here: 128 us
  blocking collectives  58.9 us (46%)
  starting transfers between devices  29.1 us (23%)
  waiting for transfers between devices  13.9 us (11%)
  between operations  13.5 us (10%)
  matrix products  7.81 us (6%)
  local copies, waits for them, and re-layouts  1.96 us (2%)
  other arithmetic  1.78 us (1%)
    all_gather x1, blocking collectives, on_device(): everyone = lax.all_gather(attended, HEAD, axis=0, tiled=False)  24.8 us
    all_gather x1, blocking collectives, on_device(): lax.all_gather(pieces.reshape(n_x * rows, part), HEAD, axis=0, tiled=False)  23.6 us
    all_gather x1, blocking collectives, on_device(): columns = lax.all_gather(columns, 'x', axis=0, tiled=True)  10.5 us
    ppermute x3, starting transfers between devices, on_device(): query.append(lax.ppermute(share, 'x', pairs) if step else share)  9.58 us
    ppermute x1, waiting for transfers between devices, on_device(): after = lax.ppermute(packed, SLAB, [(i + 1, i) for i in range(count - 1)])  5.15 us
    ppermute x1, starting transfers between devices, on_device(): columns = lax.ppermute(out_weight.T, ('z',) + HEAD, turned)  5.11 us
    dot_general x2, matrix products, shares(): jnp.dot(group, piece, preferred_element_type=jnp.float32)  4.68 us
    ppermute x1, waiting for transfers between devices, on_device(): before = lax.ppermute(packed, SLAB, [(i, i + 1) for i in range(count - 1)])  4.35 us
  transfers between devices with their start and end apart: 10, of which 5 were waited for; matrix products, arithmetic and copies ran while one was open for 5% of the time, Pallas kernels for 1%

profile of v6, /device:TPU:39, one launch (start us, length us, event | category | flops | bytes accessed | tf_op | source)
XLA Modules:
  0.0 128.0 jit_solution(3910691833300812541)
XLA Ops:
  6.5 1.7 %pad_maximum_fusion = bf16[96,1152]{1,0:T(8,128)(2,1)} fusion(bf16[96,384]{1,0:T(8,128)(2,1)} %param.11, bf16[96,384]{1,0:T(8,128)(2,1)} %param.10, bf16[96,384]{1,0:T(8,128)(2,1)} %param.9), kind=kLoop, calls=%fused_computation.6 | loop fusion | flops 663552 | bytes 442368 | tf_op jit(solution)/shard_map/concatenate | solution.py:96
  8.2 1.6 %copy.13 = bf16[128,384]{0,1:T(8,128)(2,1)} copy(bf16[128,384]{1,0:T(8,128)(2,1)} %param.8) | data formatting | bytes 196608 | tf_op args[0]
  9.9 4.2 %all-to-all-start = ((bf16[4,128,96]{1,2,0:T(8,128)(2,1)}), bf16[4,128,96]{1,2,0:T(8,128)(2,1)S(1)}, u32[]{:S(2)}, u32[]{:S(2)}) async-start(bf16[4,128,96]{1,2,0:T(8,128)(2,1)} %bitcast.1), calls=%async_computation | async-start | bytes 196608 | tf_op jit(solution)/shard_map/all_to_all | solution.py:103
  14.1 5.1 %collective-permute-start = (bf16[96,384]{1,0:T(8,128)(2,1)}, bf16[96,384]{1,0:T(8,128)(2,1)S(1)}, u32[]{:S(2)}, u32[]{:S(2)}) collective-permute-start(bf16[96,384]{1,0:T(8,128)(2,1)} %bitcast.38), channel_id=1, source_target_pairs={{0,0},{2,64},{4,128},{6,192},{8,256},{10,320},{12,384},{14,448},{6... | collective-permute-start | bytes 221192 | tf_op jit(solution)/shard_map/ppermute | solution.py:100
  19.3 23.6 %all_gather.22 = bf16[8,512,96]{1,2,0:T(8,128)(2,1)S(1)} all-gather(bf16[1,512,96]{1,2,0:T(8,128)(2,1)S(1)} %all_gather_reshape.3), channel_id=1, replica_groups=mesh['z'=8,'x'=4,'y'=4,'core'=2,'cfg'=2] {'y','core'}, dimensions={0}, use_global_device_ids=true | all-gather | bytes 884736 | tf_op jit(solution)/shard_map/all_gather | solution.py:104
  43.0 10.5 %all_gather.23 = bf16[384,384]{1,0:T(8,128)(2,1)} all-gather(bf16[96,384]{1,0:T(8,128)(2,1)S(1)} %collective-permute-done), channel_id=1, replica_groups=mesh['z'=8,'x'=4,'y'=4,'core'=2,'cfg'=2] {'x'}, dimensions={0}, use_global_device_ids=true | all-gather | bytes 368640 | tf_op jit(solution)/shard_map/all_gather | solution.py:108
  53.5 1.8 %all-gather.5.cloned.1.call-done = bf16[768,1152]{1,0:T(8,128)(2,1)} async-done(((bf16[96,1152]{1,0:T(8,128)(2,1)}), bf16[768,1152]{1,0:T(8,128)(2,1)}) %all-gather.5.cloned.1.call-update) | async-done | bytes 1769488 | tf_op jit(solution)/shard_map/all_gather | solution.py:97
  55.3 3.0 %convolution_convert_fusion = bf16[512,768]{1,0:T(8,128)(2,1)} fusion(bf16[512,768]{0,1:T(8,128)(2,1)S(1)} %bitcast.35, bf16[768,1152]{1,0:T(8,128)(2,1)} %all-gather.5.cloned.1.call-done), kind=kOutput, calls=%fused_computation | convolution fusion | flops 604372992 | bytes 2752512 | tf_op jit(solution)/shard_map/dot_general | solution.py:113
  58.3 4.2 %all-to-all-start.1 = ((bf16[4,128,768]{2,1,0:T(8,128)(2,1)}), bf16[4,128,768]{2,1,0:T(8,128)(2,1)S(1)}, u32[]{:S(2)}, u32[]{:S(2)}) async-start(bf16[4,128,768]{2,1,0:T(8,128)(2,1)} %bitcast.5), calls=%async_computation.1 | async-start | bytes 1572864 | tf_op jit(solution)/shard_map/all_to_all | solution.py:117
  62.5 1.7 %convolution_convert_fusion.1 = bf16[512,384]{1,0:T(8,128)(2,1)S(1)} fusion(bf16[512,768]{0,1:T(8,128)(2,1)S(1)} %bitcast.36, bf16[768,1152]{1,0:T(8,128)(2,1)} %all-gather.5.cloned.1.call-done), kind=kOutput, calls=%fused_computation.1 | convolution fusion | flops 302186496 | bytes 1769472 | tf_op jit(solution)/shard_map/dot_general | solution.py:113
  64.3 2.5 %collective-permute-start.1 = (bf16[128,384]{1,0:T(8,128)(2,1)S(1)}, bf16[128,384]{1,0:T(8,128)(2,1)S(1)}, u32[]{:S(2)}, u32[]{:S(2)}) collective-permute-start(bf16[128,384]{1,0:T(8,128)(2,1)S(1)} %get-tuple-element.25), channel_id=1, source_target_pairs={{0,16},{16,0},{32,48},{48,32},{1,17},{17,1},{33,49},{49,33},{2,18}... | collective-permute-start | bytes 294920 | tf_op jit(solution)/shard_map/ppermute | solution.py:124
  66.8 2.5 %collective-permute-start.2 = (bf16[128,384]{1,0:T(8,128)(2,1)S(1)}, bf16[128,384]{1,0:T(8,128)(2,1)S(1)}, u32[]{:S(2)}, u32[]{:S(2)}) collective-permute-start(bf16[128,384]{1,0:T(8,128)(2,1)S(1)} %get-tuple-element.24), channel_id=1, source_target_pairs={{0,32},{16,48},{32,0},{48,16},{1,33},{17,49},{33,1},{49,17},{2,34}... | collective-permute-start | bytes 294920 | tf_op jit(solution)/shard_map/ppermute | solution.py:124
  69.3 4.6 %collective-permute-start.3 = (bf16[128,384]{1,0:T(8,128)(2,1)S(1)}, bf16[128,384]{1,0:T(8,128)(2,1)S(1)}, u32[]{:S(2)}, u32[]{:S(2)}) collective-permute-start(bf16[128,384]{1,0:T(8,128)(2,1)S(1)} %get-tuple-element.23), channel_id=1, source_target_pairs={{0,48},{16,32},{32,16},{48,0},{1,49},{17,33},{33,17},{49,1},{2,50}... | collective-permute-start | bytes 294920 | tf_op jit(solution)/shard_map/ppermute | solution.py:124
  73.9 1.1 collective-permute-done.2.refs_2_
  75.0 1.4 %collective-permute-done.3.refs_3_ = bf16[128,384]{1,0:T(8,128)(2,1)S(1)} collective-permute-done((bf16[128,384]{1,0:T(8,128)(2,1)S(1)}, bf16[128,384]{1,0:T(8,128)(2,1)S(1)}, u32[]{:S(2)}, u32[]{:S(2)}) %collective-permute-start.3) | collective-permute-done | bytes 98336 | tf_op jit(solution)/shard_map/ppermute | solution.py:124
  76.5 0.2 shard_map.82.refs_7_
  76.7 4.0 %collective-permute-start.4 = (bf16[128,768]{1,0:T(8,128)(2,1)S(1)}, bf16[128,768]{1,0:T(8,128)(2,1)S(1)}, u32[]{:S(2)}, u32[]{:S(2)}) collective-permute-start(bf16[128,768]{1,0:T(8,128)(2,1)S(1)} %shard_map.82.refs_7_), channel_id=1, source_target_pairs={{0,16},{16,32},{32,48},{48,64},{64,80},{80,96},{96,112},{112,128},... | collective-permute-start | bytes 589832 | tf_op jit(solution)/shard_map/ppermute | solution.py:128
  80.7 1.9 %collective-permute-start.5 = (bf16[128,768]{1,0:T(8,128)(2,1)S(1)}, bf16[128,768]{1,0:T(8,128)(2,1)S(1)}, u32[]{:S(2)}, u32[]{:S(2)}) collective-permute-start(bf16[128,768]{1,0:T(8,128)(2,1)S(1)} %shard_map.82.refs_7_), channel_id=1, source_target_pairs={{16,0},{32,16},{48,32},{64,48},{80,64},{96,80},{112,96},{128,112},... | collective-permute-start | bytes 589832 | tf_op jit(solution)/shard_map/ppermute | solution.py:129
  82.7 0.1 compare_reduce_fusion
  82.9 4.4 %collective-permute-done.4.refs_6_ = bf16[128,768]{1,0:T(8,128)(2,1)S(1)} collective-permute-done((bf16[128,768]{1,0:T(8,128)(2,1)S(1)}, bf16[128,768]{1,0:T(8,128)(2,1)S(1)}, u32[]{:S(2)}, u32[]{:S(2)}) %collective-permute-start.4) | collective-permute-done | bytes 196640 | tf_op jit(solution)/shard_map/ppermute | solution.py:128
  87.3 5.1 %collective-permute-done.5.refs_8_ = bf16[128,768]{1,0:T(8,128)(2,1)S(1)} collective-permute-done((bf16[128,768]{1,0:T(8,128)(2,1)S(1)}, bf16[128,768]{1,0:T(8,128)(2,1)S(1)}, u32[]{:S(2)}, u32[]{:S(2)}) %collective-permute-start.5) | collective-permute-done | bytes 196640 | tf_op jit(solution)/shard_map/ppermute | solution.py:129
  92.4 0.7 shard_map.83
  93.2 24.8 %all-gather = bf16[1024,384]{1,0:T(8,128)(2,1)S(1)} all-gather(bf16[128,384]{1,0:T(8,128)(2,1)S(1)} %shard_map.83), channel_id=2, replica_groups=mesh['z'=8,'x'=4,'y'=4,'core'=2,'cfg'=2] {'y','core'}, dimensions={0}, use_global_device_ids=true | all-gather | bytes 884736 | tf_op jit(solution)/shard_map/all_gather | solution.py:132
  118.0 3.1 %fusion.1 = bf16[128,384]{1,0:T(8,128)(2,1)} fusion(bf16[8,128,384]{2,1,0:T(8,128)(2,1)S(1)} %bitcast.33, bf16[8,384,384]{2,1,0:T(8,128)(2,1)} %bitcast.34), kind=kOutput, calls=%fused_computation.4 | convolution fusion | flops 302039040 | bytes 3244032 | tf_op jit(solution)/shard_map/hrd,hnd->rn/dot_general | solution.py:133
  (23 shorter events, 0.4 us)
Async XLA Ops:
  6.5 48.8 %all-gather.5.cloned.1.call-start = ((), (), s32[]{:S(2)}) async-start(), calls=%async_computation.2 | async-start | bytes 1990656 | tf_op jit(solution)/shard_map/all_gather | solution.py:97
  9.9 9.3 %all-to-all-start = ((bf16[4,128,96]{1,2,0:T(8,128)(2,1)}), bf16[4,128,96]{1,2,0:T(8,128)(2,1)S(1)}, u32[]{:S(2)}, u32[]{:S(2)}) async-start(bf16[4,128,96]{1,2,0:T(8,128)(2,1)} %bitcast.1), calls=%async_computation | async-start | bytes 196608 | tf_op jit(solution)/shard_map/all_to_all | solution.py:103
  14.1 103.9 %all-gather.7.cloned.1.call-start = ((), (), s32[]{:S(2)}) async-start(), calls=%async_computation.3 | async-start | bytes 2654208 | tf_op jit(solution)/shard_map/all_gather | solution.py:109
  14.1 28.9 %collective-permute-start = (bf16[96,384]{1,0:T(8,128)(2,1)}, bf16[96,384]{1,0:T(8,128)(2,1)S(1)}, u32[]{:S(2)}, u32[]{:S(2)}) collective-permute-start(bf16[96,384]{1,0:T(8,128)(2,1)} %bitcast.38), channel_id=1, source_target_pairs={{0,0},{2,64},{4,128},{6,192},{8,256},{10,320},{12,384},{14,448},{6... | collective-permute-start | bytes 221192 | tf_op jit(solution)/shard_map/ppermute | solution.py:100
  58.3 18.2 %all-to-all-start.1 = ((bf16[4,128,768]{2,1,0:T(8,128)(2,1)}), bf16[4,128,768]{2,1,0:T(8,128)(2,1)S(1)}, u32[]{:S(2)}, u32[]{:S(2)}) async-start(bf16[4,128,768]{2,1,0:T(8,128)(2,1)} %bitcast.5), calls=%async_computation.1 | async-start | bytes 1572864 | tf_op jit(solution)/shard_map/all_to_all | solution.py:117
  62.5 14.0 %copy-start = (f32[128]{0:T(128)S(1)}, f32[128]{0:T(128)}, u32[]{:S(2)}) copy-start(f32[128]{0:T(128)} %param.14) | copy-start | bytes 1540
  62.5 20.2 %copy-start.2 = (s32[3,2,6]{2,1,0:T(2,128)S(1)}, s32[3,2,6]{2,1,0:T(2,128)}, u32[]{:S(2)}) copy-start(s32[3,2,6]{2,1,0:T(2,128)} %param.15) | copy-start | bytes 436
  62.5 29.9 %copy-start.1 = (f32[128]{0:T(128)S(1)}, f32[128]{0:T(128)}, u32[]{:S(2)}) copy-start(f32[128]{0:T(128)} %param.13) | copy-start | bytes 1540
  64.3 9.6 %collective-permute-start.1 = (bf16[128,384]{1,0:T(8,128)(2,1)S(1)}, bf16[128,384]{1,0:T(8,128)(2,1)S(1)}, u32[]{:S(2)}, u32[]{:S(2)}) collective-permute-start(bf16[128,384]{1,0:T(8,128)(2,1)S(1)} %get-tuple-element.25), channel_id=1, source_target_pairs={{0,16},{16,0},{32,48},{48,32},{1,17},{17,1},{33,49},{49,33},{2,18}... | collective-permute-start | bytes 294920 | tf_op jit(solution)/shard_map/ppermute | solution.py:124
  66.8 8.3 %collective-permute-start.2 = (bf16[128,384]{1,0:T(8,128)(2,1)S(1)}, bf16[128,384]{1,0:T(8,128)(2,1)S(1)}, u32[]{:S(2)}, u32[]{:S(2)}) collective-permute-start(bf16[128,384]{1,0:T(8,128)(2,1)S(1)} %get-tuple-element.24), channel_id=1, source_target_pairs={{0,32},{16,48},{32,0},{48,16},{1,33},{17,49},{33,1},{49,17},{2,34}... | collective-permute-start | bytes 294920 | tf_op jit(solution)/shard_map/ppermute | solution.py:124
  69.3 7.2 %collective-permute-start.3 = (bf16[128,384]{1,0:T(8,128)(2,1)S(1)}, bf16[128,384]{1,0:T(8,128)(2,1)S(1)}, u32[]{:S(2)}, u32[]{:S(2)}) collective-permute-start(bf16[128,384]{1,0:T(8,128)(2,1)S(1)} %get-tuple-element.23), channel_id=1, source_target_pairs={{0,48},{16,32},{32,16},{48,0},{1,49},{17,33},{33,17},{49,1},{2,50}... | collective-permute-start | bytes 294920 | tf_op jit(solution)/shard_map/ppermute | solution.py:124
  76.7 10.6 %collective-permute-start.4 = (bf16[128,768]{1,0:T(8,128)(2,1)S(1)}, bf16[128,768]{1,0:T(8,128)(2,1)S(1)}, u32[]{:S(2)}, u32[]{:S(2)}) collective-permute-start(bf16[128,768]{1,0:T(8,128)(2,1)S(1)} %shard_map.82.refs_7_), channel_id=1, source_target_pairs={{0,16},{16,32},{32,48},{48,64},{64,80},{80,96},{96,112},{112,128},... | collective-permute-start | bytes 589832 | tf_op jit(solution)/shard_map/ppermute | solution.py:128
  80.7 11.7 %collective-permute-start.5 = (bf16[128,768]{1,0:T(8,128)(2,1)S(1)}, bf16[128,768]{1,0:T(8,128)(2,1)S(1)}, u32[]{:S(2)}, u32[]{:S(2)}) collective-permute-start(bf16[128,768]{1,0:T(8,128)(2,1)S(1)} %shard_map.82.refs_7_), channel_id=1, source_target_pairs={{16,0},{32,16},{48,32},{64,48},{80,64},{96,80},{112,96},{128,112},... | collective-permute-start | bytes 589832 | tf_op jit(solution)/shard_map/ppermute | solution.py:129
Sparse Core Ops, SparseCore 0:
  9.4 45.8 all-gather.4
  57.4 46.6 all-gather.6

commit v7 on v6

--- a/solution.py
+++ b/solution.py
@@ -46,14 +46,12 @@
     )(share, gain.reshape(1, HDIM))
 
 
-def attention_kernel(*refs):
-    *share_refs, gain_ref, live_ref, before_ref, own_ref, after_ref, out_ref = refs
+def attention_kernel(share_ref, gain_ref, live_ref, before_ref, own_ref, after_ref, out_ref):
     rows, width = out_ref.shape
     near = (before_ref, own_ref, after_ref)
     scale = 1.0 / HDIM**0.5
     for low in range(0, width, HDIM):
-        query = sum(r[:, low : low + HDIM].astype(jnp.float32) for r in share_refs)
-        query = normed(query, gain_ref[...]).astype(jnp.bfloat16)
+        query = normed(summed(share_ref, low, low + HDIM), gain_ref[...]).astype(jnp.bfloat16)
         keys = jnp.concatenate([r[:, low : low + HDIM] for r in near], axis=0)
         values = jnp.concatenate([r[:, width + low : width + low + HDIM] for r in near], axis=0)
         score = lax.dot_general(
@@ -73,12 +71,12 @@
 
 
 def attention(query, gain, live, before, own, after):
-    rows, width = query[0].shape
+    rows, width = query.shape[1:]
     return pl.pallas_call(
         attention_kernel,
         out_shape=jax.ShapeDtypeStruct((rows, width), jnp.bfloat16),
         compiler_params=params(16),
-    )(*query, gain.reshape(1, HDIM), live, before, own, after)
+    )(query, gain.reshape(1, HDIM), live, before, own, after)
 
 
 def live_rows(key_tiles, tiles_here):
@@ -115,14 +113,8 @@
 
     key_value = shares(weights[:, width:])
     key_value = lax.all_to_all(key_value, "x", split_axis=0, concat_axis=0, tiled=True)
-    turned = shares(weights[:, :width])
-    place = lax.axis_index("x")
-    query = []
-    for step in range(n_x):
-        share = lax.dynamic_index_in_dim(turned, place ^ step, 0, keepdims=False)
-        pairs = [(i, i ^ step) for i in range(n_x)]
-        query.append(lax.ppermute(share, "x", pairs) if step else share)
-    key_value, *query = lax.optimization_barrier((key_value, *query))
+    query = shares(weights[:, :width])
+    query = lax.all_to_all(query, "x", split_axis=0, concat_axis=0, tiled=True)
     packed = pack(key_value, k_gain)
     count = lax.axis_size(SLAB)
     before = lax.ppermute(packed, SLAB, [(i, i + 1) for i in range(count - 1)])

time: 129 us -> 124 us (0.961)
  the two profiles are of different devices: /device:TPU:39 before, /device:TPU:7 now
where the time goes in v7:
time: 124 us; the launch traced here: 123 us
  blocking collectives  59.8 us (48%)
  starting transfers between devices  23.7 us (19%)
  between operations  13.5 us (11%)
  waiting for transfers between devices  13 us (10%)
  matrix products  8.55 us (7%)
  local copies, waits for them, and re-layouts  1.91 us (2%)
  other arithmetic  1.77 us (1%)
    all_gather x1, blocking collectives, on_device(): everyone = lax.all_gather(attended, HEAD, axis=0, tiled=False)  25.4 us
    all_gather x1, blocking collectives, on_device(): lax.all_gather(pieces.reshape(n_x * rows, part), HEAD, axis=0, tiled=False)  23.6 us
    all_gather x1, blocking collectives, on_device(): columns = lax.all_gather(columns, 'x', axis=0, tiled=True)  10.8 us
    ppermute x1, waiting for transfers between devices, on_device(): after = lax.ppermute(packed, SLAB, [(i + 1, i) for i in range(count - 1)])  5.49 us
    dot_general x2, matrix products, shares(): jnp.dot(group, piece, preferred_element_type=jnp.float32)  5.43 us
    all_to_all x1, starting transfers between devices, on_device(): query = lax.all_to_all(query, 'x', split_axis=0, concat_axis=0, tiled=True)  5.14 us
    ppermute x1, starting transfers between devices, on_device(): columns = lax.ppermute(out_weight.T, ('z',) + HEAD, turned)  5.11 us
    all_to_all x1, starting transfers between devices, on_device(): lax.all_to_all(pieces, 'x', split_axis=0, concat_axis=0, tiled=True)  4.21 us
  transfers between devices with their start and end apart: 8, of which 4 were waited for; matrix products, arithmetic and copies ran while one was open for 6% of the time, Pallas kernels for 1%

profile of v7, /device:TPU:7, one launch (start us, length us, event | category | flops | bytes accessed | tf_op | source)
XLA Modules:
  0.0 123.1 jit_solution(15940766701516749161)
XLA Ops:
  6.5 1.7 %pad_maximum_fusion = bf16[96,1152]{1,0:T(8,128)(2,1)} fusion(bf16[96,384]{1,0:T(8,128)(2,1)} %param.11, bf16[96,384]{1,0:T(8,128)(2,1)} %param.10, bf16[96,384]{1,0:T(8,128)(2,1)} %param.9), kind=kLoop, calls=%fused_computation.6 | loop fusion | flops 663552 | bytes 442368 | tf_op jit(solution)/shard_map/concatenate | solution.py:94
  8.2 1.6 %copy.13 = bf16[128,384]{0,1:T(8,128)(2,1)} copy(bf16[128,384]{1,0:T(8,128)(2,1)} %param.8) | data formatting | bytes 196608 | tf_op args[0]
  9.9 4.2 %all-to-all-start = ((bf16[4,128,96]{1,2,0:T(8,128)(2,1)}), bf16[4,128,96]{1,2,0:T(8,128)(2,1)S(1)}, u32[]{:S(2)}, u32[]{:S(2)}) async-start(bf16[4,128,96]{1,2,0:T(8,128)(2,1)} %bitcast.1), calls=%async_computation | async-start | bytes 196608 | tf_op jit(solution)/shard_map/all_to_all | solution.py:101
  14.1 5.1 %collective-permute-start = (bf16[96,384]{1,0:T(8,128)(2,1)}, bf16[96,384]{1,0:T(8,128)(2,1)S(1)}, u32[]{:S(2)}, u32[]{:S(2)}) collective-permute-start(bf16[96,384]{1,0:T(8,128)(2,1)} %bitcast.29), channel_id=1, source_target_pairs={{0,0},{2,64},{4,128},{6,192},{8,256},{10,320},{12,384},{14,448},{6... | collective-permute-start | bytes 221192 | tf_op jit(solution)/shard_map/ppermute | solution.py:98
  19.2 0.1 copy.14
  19.3 23.6 %all_gather.22 = bf16[8,512,96]{1,2,0:T(8,128)(2,1)S(1)} all-gather(bf16[1,512,96]{1,2,0:T(8,128)(2,1)S(1)} %all_gather_reshape.3), channel_id=1, replica_groups=mesh['z'=8,'x'=4,'y'=4,'core'=2,'cfg'=2] {'y','core'}, dimensions={0}, use_global_device_ids=true | all-gather | bytes 884736 | tf_op jit(solution)/shard_map/all_gather | solution.py:102
  42.9 10.8 %all_gather.23 = bf16[384,384]{1,0:T(8,128)(2,1)} all-gather(bf16[96,384]{1,0:T(8,128)(2,1)S(1)} %collective-permute-done), channel_id=1, replica_groups=mesh['z'=8,'x'=4,'y'=4,'core'=2,'cfg'=2] {'x'}, dimensions={0}, use_global_device_ids=true | all-gather | bytes 368640 | tf_op jit(solution)/shard_map/all_gather | solution.py:106
  53.8 2.1 %all-gather.5.cloned.1.call-done = bf16[768,1152]{1,0:T(8,128)(2,1)} async-done(((bf16[96,1152]{1,0:T(8,128)(2,1)}), bf16[768,1152]{1,0:T(8,128)(2,1)}) %all-gather.5.cloned.1.call-update) | async-done | bytes 1769488 | tf_op jit(solution)/shard_map/all_gather | solution.py:95
  55.9 3.0 %convolution_convert_fusion = bf16[512,768]{1,0:T(8,128)(2,1)} fusion(bf16[512,768]{0,1:T(8,128)(2,1)S(1)} %bitcast.27, bf16[768,1152]{1,0:T(8,128)(2,1)} %all-gather.5.cloned.1.call-done), kind=kOutput, calls=%fused_computation | convolution fusion | flops 604372992 | bytes 2752512 | tf_op jit(solution)/shard_map/dot_general | solution.py:111
  58.9 4.0 %all-to-all-start.2 = ((bf16[4,128,768]{2,1,0:T(8,128)(2,1)}), bf16[4,128,768]{2,1,0:T(8,128)(2,1)S(1)}, u32[]{:S(2)}, u32[]{:S(2)}) async-start(bf16[4,128,768]{2,1,0:T(8,128)(2,1)} %bitcast.7), calls=%async_computation.2 | async-start | bytes 1572864 | tf_op jit(solution)/shard_map/all_to_all | solution.py:115
  62.9 2.5 %convolution_convert_fusion.1 = bf16[512,384]{1,0:T(8,128)(2,1)} fusion(bf16[512,768]{0,1:T(8,128)(2,1)S(1)} %bitcast.28, bf16[768,1152]{1,0:T(8,128)(2,1)} %all-gather.5.cloned.1.call-done), kind=kOutput, calls=%fused_computation.1 | convolution fusion | flops 302186496 | bytes 1769472 | tf_op jit(solution)/shard_map/dot_general | solution.py:111
  65.3 4.2 %all-to-all-done.2.share_ref = bf16[4,128,768]{2,1,0:T(8,128)(2,1)S(1)} async-done(((bf16[4,128,768]{2,1,0:T(8,128)(2,1)}), bf16[4,128,768]{2,1,0:T(8,128)(2,1)S(1)}, u32[]{:S(2)}, u32[]{:S(2)}) %all-to-all-start.2) | async-done | bytes 786464 | tf_op jit(solution)/shard_map/all_to_all | solution.py:115
  69.5 5.1 %all-to-all-start.1 = ((bf16[4,128,384]{2,1,0:T(8,128)(2,1)}), bf16[4,128,384]{2,1,0:T(8,128)(2,1)S(1)}, u32[]{:S(2)}, u32[]{:S(2)}) async-start(bf16[4,128,384]{2,1,0:T(8,128)(2,1)} %bitcast.5), calls=%async_computation.1 | async-start | bytes 786432 | tf_op jit(solution)/shard_map/all_to_all | solution.py:117
  74.7 0.2 shard_map.82.own_ref
  74.9 1.9 %collective-permute-start.1 = (bf16[128,768]{1,0:T(8,128)(2,1)S(1)}, bf16[128,768]{1,0:T(8,128)(2,1)S(1)}, u32[]{:S(2)}, u32[]{:S(2)}) collective-permute-start(bf16[128,768]{1,0:T(8,128)(2,1)S(1)} %shard_map.82.own_ref), channel_id=1, source_target_pairs={{0,16},{16,32},{32,48},{48,64},{64,80},{80,96},{96,112},{112,128},... | collective-permute-start | bytes 589832 | tf_op jit(solution)/shard_map/ppermute | solution.py:120
  76.8 3.4 %collective-permute-start.2 = (bf16[128,768]{1,0:T(8,128)(2,1)S(1)}, bf16[128,768]{1,0:T(8,128)(2,1)S(1)}, u32[]{:S(2)}, u32[]{:S(2)}) collective-permute-start(bf16[128,768]{1,0:T(8,128)(2,1)S(1)} %shard_map.82.own_ref), channel_id=1, source_target_pairs={{16,0},{32,16},{48,32},{64,48},{80,64},{96,80},{112,96},{128,112},... | collective-permute-start | bytes 589832 | tf_op jit(solution)/shard_map/ppermute | solution.py:121
  80.2 0.1 compare_reduce_fusion
  80.3 0.1 broadcast_in_dim.2
  80.4 0.1 reshape.33.live_ref
  80.5 1.1 collective-permute-done.1.before_ref
  81.6 5.5 %collective-permute-done.2.after_ref = bf16[128,768]{1,0:T(8,128)(2,1)S(1)} collective-permute-done((bf16[128,768]{1,0:T(8,128)(2,1)S(1)}, bf16[128,768]{1,0:T(8,128)(2,1)S(1)}, u32[]{:S(2)}, u32[]{:S(2)}) %collective-permute-start.2) | collective-permute-done | bytes 196640 | tf_op jit(solution)/shard_map/ppermute | solution.py:121
  87.1 0.7 shard_map.83
  87.8 25.4 %all-gather = bf16[1024,384]{1,0:T(8,128)(2,1)S(1)} all-gather(bf16[128,384]{1,0:T(8,128)(2,1)S(1)} %shard_map.83), channel_id=2, replica_groups=mesh['z'=8,'x'=4,'y'=4,'core'=2,'cfg'=2] {'y','core'}, dimensions={0}, use_global_device_ids=true | all-gather | bytes 884736 | tf_op jit(solution)/shard_map/all_gather | solution.py:124
  113.2 3.1 %fusion.1 = bf16[128,384]{1,0:T(8,128)(2,1)} fusion(bf16[8,128,384]{2,1,0:T(8,128)(2,1)S(1)} %bitcast.25, bf16[8,384,384]{2,1,0:T(8,128)(2,1)} %bitcast.26), kind=kOutput, calls=%fused_computation.4 | convolution fusion | flops 302039040 | bytes 3244032 | tf_op jit(solution)/shard_map/hrd,hnd->rn/dot_general | solution.py:125
  (18 shorter events, 0.1 us)
Async XLA Ops:
  6.5 49.4 %all-gather.5.cloned.1.call-start = ((), (), s32[]{:S(2)}) async-start(), calls=%async_computation.3 | async-start | bytes 1990656 | tf_op jit(solution)/shard_map/all_gather | solution.py:95
  9.9 9.3 %all-to-all-start = ((bf16[4,128,96]{1,2,0:T(8,128)(2,1)}), bf16[4,128,96]{1,2,0:T(8,128)(2,1)S(1)}, u32[]{:S(2)}, u32[]{:S(2)}) async-start(bf16[4,128,96]{1,2,0:T(8,128)(2,1)} %bitcast.1), calls=%async_computation | async-start | bytes 196608 | tf_op jit(solution)/shard_map/all_to_all | solution.py:101
  14.1 99.1 %all-gather.7.cloned.1.call-start = ((), (), s32[]{:S(2)}) async-start(), calls=%async_computation.4 | async-start | bytes 2654208 | tf_op jit(solution)/shard_map/all_gather | solution.py:107
  14.1 28.9 %collective-permute-start = (bf16[96,384]{1,0:T(8,128)(2,1)}, bf16[96,384]{1,0:T(8,128)(2,1)S(1)}, u32[]{:S(2)}, u32[]{:S(2)}) collective-permute-start(bf16[96,384]{1,0:T(8,128)(2,1)} %bitcast.29), channel_id=1, source_target_pairs={{0,0},{2,64},{4,128},{6,192},{8,256},{10,320},{12,384},{14,448},{6... | collective-permute-start | bytes 221192 | tf_op jit(solution)/shard_map/ppermute | solution.py:98
  58.9 10.6 %all-to-all-start.2 = ((bf16[4,128,768]{2,1,0:T(8,128)(2,1)}), bf16[4,128,768]{2,1,0:T(8,128)(2,1)S(1)}, u32[]{:S(2)}, u32[]{:S(2)}) async-start(bf16[4,128,768]{2,1,0:T(8,128)(2,1)} %bitcast.7), calls=%async_computation.2 | async-start | bytes 1572864 | tf_op jit(solution)/shard_map/all_to_all | solution.py:115
  62.9 11.8 %copy-start = (f32[128]{0:T(128)S(1)}, f32[128]{0:T(128)}, u32[]{:S(2)}) copy-start(f32[128]{0:T(128)} %param.14) | copy-start | bytes 1540
  62.9 17.3 %copy-start.2 = (s32[3,2,6]{2,1,0:T(2,128)S(1)}, s32[3,2,6]{2,1,0:T(2,128)}, u32[]{:S(2)}) copy-start(s32[3,2,6]{2,1,0:T(2,128)} %param.15) | copy-start | bytes 436
  62.9 24.2 %copy-start.1 = (f32[128]{0:T(128)S(1)}, f32[128]{0:T(128)}, u32[]{:S(2)}) copy-start(f32[128]{0:T(128)} %param.13) | copy-start | bytes 1540
  69.5 10.9 %all-to-all-start.1 = ((bf16[4,128,384]{2,1,0:T(8,128)(2,1)}), bf16[4,128,384]{2,1,0:T(8,128)(2,1)S(1)}, u32[]{:S(2)}, u32[]{:S(2)}) async-start(bf16[4,128,384]{2,1,0:T(8,128)(2,1)} %bitcast.5), calls=%async_computation.1 | async-start | bytes 786432 | tf_op jit(solution)/shard_map/all_to_all | solution.py:117
  74.9 6.7 %collective-permute-start.1 = (bf16[128,768]{1,0:T(8,128)(2,1)S(1)}, bf16[128,768]{1,0:T(8,128)(2,1)S(1)}, u32[]{:S(2)}, u32[]{:S(2)}) collective-permute-start(bf16[128,768]{1,0:T(8,128)(2,1)S(1)} %shard_map.82.own_ref), channel_id=1, source_target_pairs={{0,16},{16,32},{32,48},{48,64},{64,80},{80,96},{96,112},{112,128},... | collective-permute-start | bytes 589832 | tf_op jit(solution)/shard_map/ppermute | solution.py:120
  76.8 10.3 %collective-permute-start.2 = (bf16[128,768]{1,0:T(8,128)(2,1)S(1)}, bf16[128,768]{1,0:T(8,128)(2,1)S(1)}, u32[]{:S(2)}, u32[]{:S(2)}) collective-permute-start(bf16[128,768]{1,0:T(8,128)(2,1)S(1)} %shard_map.82.own_ref), channel_id=1, source_target_pairs={{16,0},{32,16},{48,32},{64,48},{80,64},{96,80},{112,96},{128,112},... | collective-permute-start | bytes 589832 | tf_op jit(solution)/shard_map/ppermute | solution.py:121
Sparse Core Ops, SparseCore 0:
  9.4 46.4 all-gather.4
  58.0 46.5 all-gather.6

commit v8 on v7

--- a/solution.py
+++ b/solution.py
@@ -111,10 +111,11 @@
         share = jnp.dot(group, piece, preferred_element_type=jnp.float32).astype(jnp.bfloat16)
         return share.reshape(n_x, rows, -1)
 
-    key_value = shares(weights[:, width:])
-    key_value = lax.all_to_all(key_value, "x", split_axis=0, concat_axis=0, tiled=True)
     query = shares(weights[:, :width])
     query = lax.all_to_all(query, "x", split_axis=0, concat_axis=0, tiled=True)
+    key_value = shares(weights[:, width:])
+    query, key_value = lax.optimization_barrier((query, key_value))
+    key_value = lax.all_to_all(key_value, "x", split_axis=0, concat_axis=0, tiled=True)
     packed = pack(key_value, k_gain)
     count = lax.axis_size(SLAB)
     before = lax.ppermute(packed, SLAB, [(i, i + 1) for i in range(count - 1)])

time: 124 us -> 132 us (1.065)
  the two profiles are of different devices: /device:TPU:7 before, /device:TPU:39 now
where the time goes in v8:
time: 132 us; the launch traced here: 131 us
  blocking collectives  59.7 us (45%)
  starting transfers between devices  24.1 us (18%)
  waiting for transfers between devices  21.7 us (16%)
  between operations  13.5 us (10%)
  matrix products  7.42 us (6%)
  local copies, waits for them, and re-layouts  1.91 us (1%)
  other arithmetic  1.77 us (1%)
    all_gather x1, blocking collectives, on_device(): everyone = lax.all_gather(attended, HEAD, axis=0, tiled=False)  25.6 us
    all_gather x1, blocking collectives, on_device(): lax.all_gather(pieces.reshape(n_x * rows, part), HEAD, axis=0, tiled=False)  23.7 us
    all_gather x1, blocking collectives, on_device(): columns = lax.all_gather(columns, 'x', axis=0, tiled=True)  10.5 us
    all_to_all x1, waiting for transfers between devices, on_device(): lax.all_to_all(key_value, 'x', split_axis=0, concat_axis=0, tiled=True)  6.59 us
    ppermute x1, waiting for transfers between devices, on_device(): after = lax.ppermute(packed, SLAB, [(i + 1, i) for i in range(count - 1)])  6.46 us
    all_to_all x1, starting transfers between devices, on_device(): lax.all_to_all(key_value, 'x', split_axis=0, concat_axis=0, tiled=True)  5.25 us
    ppermute x1, starting transfers between devices, on_device(): columns = lax.ppermute(out_weight.T, ('z',) + HEAD, turned)  5.11 us
    dot_general x2, matrix products, shares(): jnp.dot(group, piece, preferred_element_type=jnp.float32)  4.3 us
  transfers between devices with their start and end apart: 8, of which 5 were waited for; matrix products, arithmetic and copies ran while one was open for 5% of the time, Pallas kernels for 1%

profile of v8, /device:TPU:39, one launch (start us, length us, event | category | flops | bytes accessed | tf_op | source)
XLA Modules:
  0.0 131.1 jit_solution(15594519896514191569)
XLA Ops:
  6.5 1.7 %pad_maximum_fusion = bf16[96,1152]{1,0:T(8,128)(2,1)} fusion(bf16[96,384]{1,0:T(8,128)(2,1)} %param.11, bf16[96,384]{1,0:T(8,128)(2,1)} %param.10, bf16[96,384]{1,0:T(8,128)(2,1)} %param.9), kind=kLoop, calls=%fused_computation.6 | loop fusion | flops 663552 | bytes 442368 | tf_op jit(solution)/shard_map/concatenate | solution.py:94
  8.2 1.6 %copy.13 = bf16[128,384]{0,1:T(8,128)(2,1)} copy(bf16[128,384]{1,0:T(8,128)(2,1)} %param.8) | data formatting | bytes 196608 | tf_op args[0]
  9.9 4.2 %all-to-all-start = ((bf16[4,128,96]{1,2,0:T(8,128)(2,1)}), bf16[4,128,96]{1,2,0:T(8,128)(2,1)S(1)}, u32[]{:S(2)}, u32[]{:S(2)}) async-start(bf16[4,128,96]{1,2,0:T(8,128)(2,1)} %bitcast.1), calls=%async_computation | async-start | bytes 196608 | tf_op jit(solution)/shard_map/all_to_all | solution.py:101
  14.1 5.1 %collective-permute-start = (bf16[96,384]{1,0:T(8,128)(2,1)}, bf16[96,384]{1,0:T(8,128)(2,1)S(1)}, u32[]{:S(2)}, u32[]{:S(2)}) collective-permute-start(bf16[96,384]{1,0:T(8,128)(2,1)} %bitcast.29), channel_id=1, source_target_pairs={{0,0},{2,64},{4,128},{6,192},{8,256},{10,320},{12,384},{14,448},{6... | collective-permute-start | bytes 221192 | tf_op jit(solution)/shard_map/ppermute | solution.py:98
  19.3 23.7 %all_gather.22 = bf16[8,512,96]{1,2,0:T(8,128)(2,1)S(1)} all-gather(bf16[1,512,96]{1,2,0:T(8,128)(2,1)S(1)} %all_gather_reshape.3), channel_id=1, replica_groups=mesh['z'=8,'x'=4,'y'=4,'core'=2,'cfg'=2] {'y','core'}, dimensions={0}, use_global_device_ids=true | all-gather | bytes 884736 | tf_op jit(solution)/shard_map/all_gather | solution.py:102
  43.0 10.5 %all_gather.23 = bf16[384,384]{1,0:T(8,128)(2,1)} all-gather(bf16[96,384]{1,0:T(8,128)(2,1)S(1)} %collective-permute-done), channel_id=1, replica_groups=mesh['z'=8,'x'=4,'y'=4,'core'=2,'cfg'=2] {'x'}, dimensions={0}, use_global_device_ids=true | all-gather | bytes 368640 | tf_op jit(solution)/shard_map/all_gather | solution.py:106
  53.5 1.8 %all-gather.5.cloned.1.call-done = bf16[768,1152]{1,0:T(8,128)(2,1)} async-done(((bf16[96,1152]{1,0:T(8,128)(2,1)}), bf16[768,1152]{1,0:T(8,128)(2,1)}) %all-gather.5.cloned.1.call-update) | async-done | bytes 1769488 | tf_op jit(solution)/shard_map/all_gather | solution.py:95
  55.3 2.6 %convolution_convert_fusion.1 = bf16[512,384]{1,0:T(8,128)(2,1)} fusion(bf16[512,768]{0,1:T(8,128)(2,1)S(1)} %bitcast.27, bf16[768,1152]{1,0:T(8,128)(2,1)} %all-gather.5.cloned.1.call-done), kind=kOutput, calls=%fused_computation.1 | convolution fusion | flops 302186496 | bytes 1769472 | tf_op jit(solution)/shard_map/dot_general | solution.py:111
  57.9 4.2 %all-to-all-start.1 = ((bf16[4,128,384]{2,1,0:T(8,128)(2,1)}), bf16[4,128,384]{2,1,0:T(8,128)(2,1)S(1)}, u32[]{:S(2)}, u32[]{:S(2)}) async-start(bf16[4,128,384]{2,1,0:T(8,128)(2,1)} %bitcast.5), calls=%async_computation.1 | async-start | bytes 786432 | tf_op jit(solution)/shard_map/all_to_all | solution.py:115
  62.1 1.7 %convolution_convert_fusion = bf16[512,768]{1,0:T(8,128)(2,1)} fusion(bf16[512,768]{0,1:T(8,128)(2,1)S(1)} %bitcast.28, bf16[768,1152]{1,0:T(8,128)(2,1)S(1)} %copy-done.3), kind=kOutput, calls=%fused_computation | convolution fusion | flops 604372992 | bytes 2752512 | tf_op jit(solution)/shard_map/dot_general | solution.py:111
  63.8 2.7 %all-to-all-done.1.share_ref = bf16[4,128,384]{2,1,0:T(8,128)(2,1)S(1)} async-done(((bf16[4,128,384]{2,1,0:T(8,128)(2,1)}), bf16[4,128,384]{2,1,0:T(8,128)(2,1)S(1)}, u32[]{:S(2)}, u32[]{:S(2)}) %all-to-all-start.1) | async-done | bytes 393248 | tf_op jit(solution)/shard_map/all_to_all | solution.py:115
  66.5 5.3 %all-to-all-start.2 = ((bf16[4,128,768]{2,1,0:T(8,128)(2,1)}), bf16[4,128,768]{2,1,0:T(8,128)(2,1)S(1)}, u32[]{:S(2)}, u32[]{:S(2)}) async-start(bf16[4,128,768]{2,1,0:T(8,128)(2,1)} %bitcast.6), calls=%async_computation.2 | async-start | bytes 1572864 | tf_op jit(solution)/shard_map/all_to_all | solution.py:118
  71.8 6.6 %all-to-all-done.2.share_ref = bf16[4,128,768]{2,1,0:T(8,128)(2,1)S(1)} async-done(((bf16[4,128,768]{2,1,0:T(8,128)(2,1)}), bf16[4,128,768]{2,1,0:T(8,128)(2,1)S(1)}, u32[]{:S(2)}, u32[]{:S(2)}) %all-to-all-start.2) | async-done | bytes 786464 | tf_op jit(solution)/shard_map/all_to_all | solution.py:118
  78.4 0.2 shard_map.82.own_ref
  78.6 3.4 %collective-permute-start.1 = (bf16[128,768]{1,0:T(8,128)(2,1)S(1)}, bf16[128,768]{1,0:T(8,128)(2,1)S(1)}, u32[]{:S(2)}, u32[]{:S(2)}) collective-permute-start(bf16[128,768]{1,0:T(8,128)(2,1)S(1)} %shard_map.82.own_ref), channel_id=1, source_target_pairs={{0,16},{16,32},{32,48},{48,64},{64,80},{80,96},{96,112},{112,128},... | collective-permute-start | bytes 589832 | tf_op jit(solution)/shard_map/ppermute | solution.py:121
  82.0 1.9 %collective-permute-start.2 = (bf16[128,768]{1,0:T(8,128)(2,1)S(1)}, bf16[128,768]{1,0:T(8,128)(2,1)S(1)}, u32[]{:S(2)}, u32[]{:S(2)}) collective-permute-start(bf16[128,768]{1,0:T(8,128)(2,1)S(1)} %shard_map.82.own_ref), channel_id=1, source_target_pairs={{16,0},{32,16},{48,32},{64,48},{80,64},{96,80},{112,96},{128,112},... | collective-permute-start | bytes 589832 | tf_op jit(solution)/shard_map/ppermute | solution.py:122
  83.9 0.1 compare_reduce_fusion
  84.1 0.1 broadcast_in_dim.2
  84.1 0.1 reshape.34.live_ref
  84.2 4.0 %collective-permute-done.1.before_ref = bf16[128,768]{1,0:T(8,128)(2,1)S(1)} collective-permute-done((bf16[128,768]{1,0:T(8,128)(2,1)S(1)}, bf16[128,768]{1,0:T(8,128)(2,1)S(1)}, u32[]{:S(2)}, u32[]{:S(2)}) %collective-permute-start.1) | collective-permute-done | bytes 196640 | tf_op jit(solution)/shard_map/ppermute | solution.py:121
  88.3 6.5 %collective-permute-done.2.after_ref = bf16[128,768]{1,0:T(8,128)(2,1)S(1)} collective-permute-done((bf16[128,768]{1,0:T(8,128)(2,1)S(1)}, bf16[128,768]{1,0:T(8,128)(2,1)S(1)}, u32[]{:S(2)}, u32[]{:S(2)}) %collective-permute-start.2) | collective-permute-done | bytes 196640 | tf_op jit(solution)/shard_map/ppermute | solution.py:122
  94.7 0.7 shard_map.83
  95.5 25.6 %all-gather = bf16[1024,384]{1,0:T(8,128)(2,1)S(1)} all-gather(bf16[128,384]{1,0:T(8,128)(2,1)S(1)} %shard_map.83), channel_id=2, replica_groups=mesh['z'=8,'x'=4,'y'=4,'core'=2,'cfg'=2] {'y','core'}, dimensions={0}, use_global_device_ids=true | all-gather | bytes 884736 | tf_op jit(solution)/shard_map/all_gather | solution.py:125
  121.1 3.1 %fusion.1 = bf16[128,384]{1,0:T(8,128)(2,1)} fusion(bf16[8,128,384]{2,1,0:T(8,128)(2,1)S(1)} %bitcast.25, bf16[8,384,384]{2,1,0:T(8,128)(2,1)} %bitcast.26), kind=kOutput, calls=%fused_computation.4 | convolution fusion | flops 302039040 | bytes 3244032 | tf_op jit(solution)/shard_map/hrd,hnd->rn/dot_general | solution.py:126
  (20 shorter events, 0.2 us)
Async XLA Ops:
  6.5 48.8 %all-gather.5.cloned.1.call-start = ((), (), s32[]{:S(2)}) async-start(), calls=%async_computation.3 | async-start | bytes 1990656 | tf_op jit(solution)/shard_map/all_gather | solution.py:95
  9.9 9.3 %all-to-all-start = ((bf16[4,128,96]{1,2,0:T(8,128)(2,1)}), bf16[4,128,96]{1,2,0:T(8,128)(2,1)S(1)}, u32[]{:S(2)}, u32[]{:S(2)}) async-start(bf16[4,128,96]{1,2,0:T(8,128)(2,1)} %bitcast.1), calls=%async_computation | async-start | bytes 196608 | tf_op jit(solution)/shard_map/all_to_all | solution.py:101
  14.1 107.0 %all-gather.7.cloned.1.call-start = ((), (), s32[]{:S(2)}) async-start(), calls=%async_computation.4 | async-start | bytes 2654208 | tf_op jit(solution)/shard_map/all_gather | solution.py:107
  14.1 28.9 %collective-permute-start = (bf16[96,384]{1,0:T(8,128)(2,1)}, bf16[96,384]{1,0:T(8,128)(2,1)S(1)}, u32[]{:S(2)}, u32[]{:S(2)}) collective-permute-start(bf16[96,384]{1,0:T(8,128)(2,1)} %bitcast.29), channel_id=1, source_target_pairs={{0,0},{2,64},{4,128},{6,192},{8,256},{10,320},{12,384},{14,448},{6... | collective-permute-start | bytes 221192 | tf_op jit(solution)/shard_map/ppermute | solution.py:98
  55.3 6.8 %copy-start.3 = (bf16[768,1152]{1,0:T(8,128)(2,1)S(1)}, bf16[768,1152]{1,0:T(8,128)(2,1)}, u32[]{:S(2)}) copy-start(bf16[768,1152]{1,0:T(8,128)(2,1)} %all-gather.5.cloned.1.call-done) | copy-start | bytes 5308420
  57.9 8.7 %all-to-all-start.1 = ((bf16[4,128,384]{2,1,0:T(8,128)(2,1)}), bf16[4,128,384]{2,1,0:T(8,128)(2,1)S(1)}, u32[]{:S(2)}, u32[]{:S(2)}) async-start(bf16[4,128,384]{2,1,0:T(8,128)(2,1)} %bitcast.5), calls=%async_computation.1 | async-start | bytes 786432 | tf_op jit(solution)/shard_map/all_to_all | solution.py:115
  62.1 16.3 %copy-start = (f32[128]{0:T(128)S(1)}, f32[128]{0:T(128)}, u32[]{:S(2)}) copy-start(f32[128]{0:T(128)} %param.14) | copy-start | bytes 1540
  63.8 20.1 %copy-start.2 = (s32[3,2,6]{2,1,0:T(2,128)S(1)}, s32[3,2,6]{2,1,0:T(2,128)}, u32[]{:S(2)}) copy-start(s32[3,2,6]{2,1,0:T(2,128)} %param.15) | copy-start | bytes 436
  63.8 30.9 %copy-start.1 = (f32[128]{0:T(128)S(1)}, f32[128]{0:T(128)}, u32[]{:S(2)}) copy-start(f32[128]{0:T(128)} %param.13) | copy-start | bytes 1540
  66.5 11.8 %all-to-all-start.2 = ((bf16[4,128,768]{2,1,0:T(8,128)(2,1)}), bf16[4,128,768]{2,1,0:T(8,128)(2,1)S(1)}, u32[]{:S(2)}, u32[]{:S(2)}) async-start(bf16[4,128,768]{2,1,0:T(8,128)(2,1)} %bitcast.6), calls=%async_computation.2 | async-start | bytes 1572864 | tf_op jit(solution)/shard_map/all_to_all | solution.py:118
  78.6 9.7 %collective-permute-start.1 = (bf16[128,768]{1,0:T(8,128)(2,1)S(1)}, bf16[128,768]{1,0:T(8,128)(2,1)S(1)}, u32[]{:S(2)}, u32[]{:S(2)}) collective-permute-start(bf16[128,768]{1,0:T(8,128)(2,1)S(1)} %shard_map.82.own_ref), channel_id=1, source_target_pairs={{0,16},{16,32},{32,48},{48,64},{64,80},{80,96},{96,112},{112,128},... | collective-permute-start | bytes 589832 | tf_op jit(solution)/shard_map/ppermute | solution.py:121
  82.0 12.7 %collective-permute-start.2 = (bf16[128,768]{1,0:T(8,128)(2,1)S(1)}, bf16[128,768]{1,0:T(8,128)(2,1)S(1)}, u32[]{:S(2)}, u32[]{:S(2)}) collective-permute-start(bf16[128,768]{1,0:T(8,128)(2,1)S(1)} %shard_map.82.own_ref), channel_id=1, source_target_pairs={{16,0},{32,16},{48,32},{64,48},{80,64},{96,80},{112,96},{128,112},... | collective-permute-start | bytes 589832 | tf_op jit(solution)/shard_map/ppermute | solution.py:122
Sparse Core Ops, SparseCore 0:
  9.4 45.8 all-gather.4
  57.4 47.5 all-gather.6

commit v9 on v7

--- a/solution.py
+++ b/solution.py
@@ -46,9 +46,9 @@
     )(share, gain.reshape(1, HDIM))
 
 
-def attention_kernel(share_ref, gain_ref, live_ref, before_ref, own_ref, after_ref, out_ref):
+def attention_kernel(share_ref, gain_ref, live_ref, odd_ref, own_ref, even_ref, out_ref):
     rows, width = out_ref.shape
-    near = (before_ref, own_ref, after_ref)
+    near = (odd_ref, own_ref, even_ref)
     scale = 1.0 / HDIM**0.5
     for low in range(0, width, HDIM):
         query = normed(summed(share_ref, low, low + HDIM), gain_ref[...]).astype(jnp.bfloat16)
@@ -70,17 +70,21 @@
         out_ref[:, low : low + HDIM] = (mixed / total).astype(jnp.bfloat16)
 
 
-def attention(query, gain, live, before, own, after):
+def attention(query, gain, live, odd, own, even):
     rows, width = query.shape[1:]
     return pl.pallas_call(
         attention_kernel,
         out_shape=jax.ShapeDtypeStruct((rows, width), jnp.bfloat16),
         compiler_params=params(16),
-    )(query, gain.reshape(1, HDIM), live, before, own, after)
+    )(query, gain.reshape(1, HDIM), live, odd, own, even)
 
 
 def live_rows(key_tiles, tiles_here):
-    near_ids = (lax.axis_index(SLAB) - 1) * tiles_here + jnp.arange(3 * tiles_here, dtype=jnp.int32)
+    slab = lax.axis_index(SLAB)
+    even_at = jnp.where(slab % 2 == 0, slab + 1, slab - 1)
+    slabs = jnp.stack([2 * slab - even_at, slab, even_at])
+    near_ids = slabs[:, None] * tiles_here + jnp.arange(tiles_here, dtype=jnp.int32)
+    near_ids = near_ids.reshape(-1)
     live = jnp.any(key_tiles[:, :, :, None] == near_ids[None, None, None, :], axis=2)
     live = live.reshape(-1, 3 * tiles_here).astype(jnp.float32)
     return jnp.repeat(live, TILE, axis=1)
@@ -117,10 +121,13 @@
     query = lax.all_to_all(query, "x", split_axis=0, concat_axis=0, tiled=True)
     packed = pack(key_value, k_gain)
     count = lax.axis_size(SLAB)
-    before = lax.ppermute(packed, SLAB, [(i, i + 1) for i in range(count - 1)])
-    after = lax.ppermute(packed, SLAB, [(i + 1, i) for i in range(count - 1)])
+    swaps = [
+        [pair for i in range(first, count - 1, 2) for pair in ((i, i + 1), (i + 1, i))]
+        for first in (1, 0)
+    ]
+    odd, even = (lax.ppermute(packed, SLAB, pairs) for pairs in swaps)
     live = live_rows(key_tiles, rows // TILE)
-    attended = attention(query, q_gain, live, before, packed, after)
+    attended = attention(query, q_gain, live, odd, packed, even)
     everyone = lax.all_gather(attended, HEAD, axis=0, tiled=False)
     total = jnp.einsum("hrd,hnd->rn", everyone, projection, preferred_element_type=jnp.float32)
     return total.astype(jnp.bfloat16)

time: 124 us -> 121 us (0.976)
  the two profiles are of different devices: /device:TPU:7 before, /device:TPU:71 now
where the time goes in v9:
time: 121 us; the launch traced here: 120 us
  blocking collectives  59.3 us (49%)
  starting transfers between devices  20.3 us (17%)
  waiting for transfers between devices  13.5 us (11%)
  between operations  13.4 us (11%)
  matrix products  8.54 us (7%)
  local copies, waits for them, and re-layouts  1.99 us (2%)
  other arithmetic  1.91 us (2%)
    all_gather x1, blocking collectives, on_device(): everyone = lax.all_gather(attended, HEAD, axis=0, tiled=False)  24.9 us
    all_gather x1, blocking collectives, on_device(): lax.all_gather(pieces.reshape(n_x * rows, part), HEAD, axis=0, tiled=False)  24.3 us
    all_gather x1, blocking collectives, on_device(): columns = lax.all_gather(columns, 'x', axis=0, tiled=True)  10.2 us
    ppermute x2, waiting for transfers between devices, on_device(): odd, even = (lax.ppermute(packed, SLAB, pairs) for pairs in swaps)  5.99 us
    dot_general x2, matrix products, shares(): jnp.dot(group, piece, preferred_element_type=jnp.float32)  5.42 us
    all_to_all x1, starting transfers between devices, on_device(): query = lax.all_to_all(query, 'x', split_axis=0, concat_axis=0, tiled=True)  5.22 us
    ppermute x2, starting transfers between devices, on_device(): odd, even = (lax.ppermute(packed, SLAB, pairs) for pairs in swaps)  5.1 us
    all_to_all x1, starting transfers between devices, on_device(): lax.all_to_all(key_value, 'x', split_axis=0, concat_axis=0, tiled=True)  4.24 us
  transfers between devices with their start and end apart: 8, of which 4 were waited for; matrix products, arithmetic and copies ran while one was open for 6% of the time, Pallas kernels for 1%

profile of v9, /device:TPU:71, one launch (start us, length us, event | category | flops | bytes accessed | tf_op | source)
XLA Modules:
  0.0 119.9 jit_solution(3308448917690740016)
XLA Ops:
  6.5 1.7 %pad_maximum_fusion = bf16[96,1152]{1,0:T(8,128)(2,1)} fusion(bf16[96,384]{1,0:T(8,128)(2,1)} %param.11, bf16[96,384]{1,0:T(8,128)(2,1)} %param.10, bf16[96,384]{1,0:T(8,128)(2,1)} %param.9), kind=kLoop, calls=%fused_computation.6 | loop fusion | flops 663552 | bytes 442368 | tf_op jit(solution)/shard_map/concatenate | solution.py:98
  8.2 1.6 %copy.13 = bf16[128,384]{0,1:T(8,128)(2,1)} copy(bf16[128,384]{1,0:T(8,128)(2,1)} %param.8) | data formatting | bytes 196608 | tf_op args[0]
  9.9 4.2 %all-to-all-start = ((bf16[4,128,96]{1,2,0:T(8,128)(2,1)}), bf16[4,128,96]{1,2,0:T(8,128)(2,1)S(1)}, u32[]{:S(2)}, u32[]{:S(2)}) async-start(bf16[4,128,96]{1,2,0:T(8,128)(2,1)} %bitcast.1), calls=%async_computation | async-start | bytes 196608 | tf_op jit(solution)/shard_map/all_to_all | solution.py:105
  14.1 1.5 %collective-permute-start = (bf16[96,384]{1,0:T(8,128)(2,1)}, bf16[96,384]{1,0:T(8,128)(2,1)S(1)}, u32[]{:S(2)}, u32[]{:S(2)}) collective-permute-start(bf16[96,384]{1,0:T(8,128)(2,1)} %bitcast.32), channel_id=1, source_target_pairs={{0,0},{2,64},{4,128},{6,192},{8,256},{10,320},{12,384},{14,448},{6... | collective-permute-start | bytes 221192 | tf_op jit(solution)/shard_map/ppermute | solution.py:102
  15.6 1.3 %all-to-all-done = bf16[4,128,96]{1,2,0:T(8,128)(2,1)S(1)} async-done(((bf16[4,128,96]{1,2,0:T(8,128)(2,1)}), bf16[4,128,96]{1,2,0:T(8,128)(2,1)S(1)}, u32[]{:S(2)}, u32[]{:S(2)}) %all-to-all-start) | async-done | bytes 98336 | tf_op jit(solution)/shard_map/all_to_all | solution.py:105
  17.0 24.3 %all_gather.22 = bf16[8,512,96]{1,2,0:T(8,128)(2,1)S(1)} all-gather(bf16[1,512,96]{1,2,0:T(8,128)(2,1)S(1)} %all_gather_reshape.3), channel_id=1, replica_groups=mesh['z'=8,'x'=4,'y'=4,'core'=2,'cfg'=2] {'y','core'}, dimensions={0}, use_global_device_ids=true | all-gather | bytes 884736 | tf_op jit(solution)/shard_map/all_gather | solution.py:106
  41.3 10.2 %all_gather.23 = bf16[384,384]{1,0:T(8,128)(2,1)} all-gather(bf16[96,384]{1,0:T(8,128)(2,1)S(1)} %collective-permute-done), channel_id=1, replica_groups=mesh['z'=8,'x'=4,'y'=4,'core'=2,'cfg'=2] {'x'}, dimensions={0}, use_global_device_ids=true | all-gather | bytes 368640 | tf_op jit(solution)/shard_map/all_gather | solution.py:110
  51.5 2.1 %all-gather.5.cloned.1.call-done = bf16[768,1152]{1,0:T(8,128)(2,1)} async-done(((bf16[96,1152]{1,0:T(8,128)(2,1)}), bf16[768,1152]{1,0:T(8,128)(2,1)}) %all-gather.5.cloned.1.call-update) | async-done | bytes 1769488 | tf_op jit(solution)/shard_map/all_gather | solution.py:99
  53.6 3.0 %convolution_convert_fusion = bf16[512,768]{1,0:T(8,128)(2,1)} fusion(bf16[512,768]{0,1:T(8,128)(2,1)S(1)} %bitcast.30, bf16[768,1152]{1,0:T(8,128)(2,1)} %all-gather.5.cloned.1.call-done), kind=kOutput, calls=%fused_computation | convolution fusion | flops 604372992 | bytes 2752512 | tf_op jit(solution)/shard_map/dot_general | solution.py:115
  56.6 4.2 %all-to-all-start.2 = ((bf16[4,128,768]{2,1,0:T(8,128)(2,1)}), bf16[4,128,768]{2,1,0:T(8,128)(2,1)S(1)}, u32[]{:S(2)}, u32[]{:S(2)}) async-start(bf16[4,128,768]{2,1,0:T(8,128)(2,1)} %bitcast.10), calls=%async_computation.2 | async-start | bytes 1572864 | tf_op jit(solution)/shard_map/all_to_all | solution.py:119
  60.8 0.1 add_multiply_fusion
  60.9 2.5 %convolution_convert_fusion.1 = bf16[512,384]{1,0:T(8,128)(2,1)} fusion(bf16[512,768]{0,1:T(8,128)(2,1)S(1)} %bitcast.31, bf16[768,1152]{1,0:T(8,128)(2,1)} %all-gather.5.cloned.1.call-done), kind=kOutput, calls=%fused_computation.1 | convolution fusion | flops 302186496 | bytes 1769472 | tf_op jit(solution)/shard_map/dot_general | solution.py:115
  63.4 4.0 %all-to-all-done.2.share_ref = bf16[4,128,768]{2,1,0:T(8,128)(2,1)S(1)} async-done(((bf16[4,128,768]{2,1,0:T(8,128)(2,1)}), bf16[4,128,768]{2,1,0:T(8,128)(2,1)S(1)}, u32[]{:S(2)}, u32[]{:S(2)}) %all-to-all-start.2) | async-done | bytes 786464 | tf_op jit(solution)/shard_map/all_to_all | solution.py:119
  67.4 5.2 %all-to-all-start.1 = ((bf16[4,128,384]{2,1,0:T(8,128)(2,1)}), bf16[4,128,384]{2,1,0:T(8,128)(2,1)S(1)}, u32[]{:S(2)}, u32[]{:S(2)}) async-start(bf16[4,128,384]{2,1,0:T(8,128)(2,1)} %bitcast.5), calls=%async_computation.1 | async-start | bytes 786432 | tf_op jit(solution)/shard_map/all_to_all | solution.py:121
  72.6 0.2 shard_map.82.own_ref
  72.8 3.2 %collective-permute-start.1 = (bf16[128,768]{1,0:T(8,128)(2,1)S(1)}, bf16[128,768]{1,0:T(8,128)(2,1)S(1)}, u32[]{:S(2)}, u32[]{:S(2)}) collective-permute-start(bf16[128,768]{1,0:T(8,128)(2,1)S(1)} %shard_map.82.own_ref), channel_id=1, source_target_pairs={{16,32},{32,16},{48,64},{64,48},{80,96},{96,80},{112,128},{128,112... | collective-permute-start | bytes 589832 | tf_op jit(solution)/shard_map/ppermute | solution.py:128
  76.0 1.9 %collective-permute-start.2 = (bf16[128,768]{1,0:T(8,128)(2,1)S(1)}, bf16[128,768]{1,0:T(8,128)(2,1)S(1)}, u32[]{:S(2)}, u32[]{:S(2)}) collective-permute-start(bf16[128,768]{1,0:T(8,128)(2,1)S(1)} %shard_map.82.own_ref), channel_id=1, source_target_pairs={{0,16},{16,0},{32,48},{48,32},{64,80},{80,64},{96,112},{112,96},{1... | collective-permute-start | bytes 589832 | tf_op jit(solution)/shard_map/ppermute | solution.py:128
  78.0 0.1 add.37
  78.1 0.1 compare_reduce_fusion
  78.3 0.1 reshape.69.live_ref
  78.3 6.0 %collective-permute-done.1.odd_ref = bf16[128,768]{1,0:T(8,128)(2,1)S(1)} collective-permute-done((bf16[128,768]{1,0:T(8,128)(2,1)S(1)}, bf16[128,768]{1,0:T(8,128)(2,1)S(1)}, u32[]{:S(2)}, u32[]{:S(2)}) %collective-permute-start.1) | collective-permute-done | bytes 196640 | tf_op jit(solution)/shard_map/ppermute | solution.py:128
  84.3 0.7 shard_map.83
  85.1 24.9 %all-gather = bf16[1024,384]{1,0:T(8,128)(2,1)S(1)} all-gather(bf16[128,384]{1,0:T(8,128)(2,1)S(1)} %shard_map.83), channel_id=2, replica_groups=mesh['z'=8,'x'=4,'y'=4,'core'=2,'cfg'=2] {'y','core'}, dimensions={0}, use_global_device_ids=true | all-gather | bytes 884736 | tf_op jit(solution)/shard_map/all_gather | solution.py:131
  110.0 3.1 %fusion.1 = bf16[128,384]{1,0:T(8,128)(2,1)} fusion(bf16[8,128,384]{2,1,0:T(8,128)(2,1)S(1)} %bitcast.28, bf16[8,384,384]{2,1,0:T(8,128)(2,1)} %bitcast.29), kind=kOutput, calls=%fused_computation.4 | convolution fusion | flops 302039040 | bytes 3244032 | tf_op jit(solution)/shard_map/hrd,hnd->rn/dot_general | solution.py:132
  (20 shorter events, 0.3 us)
Async XLA Ops:
  6.5 47.1 %all-gather.5.cloned.1.call-start = ((), (), s32[]{:S(2)}) async-start(), calls=%async_computation.3 | async-start | bytes 1990656 | tf_op jit(solution)/shard_map/all_gather | solution.py:99
  9.9 7.1 %all-to-all-start = ((bf16[4,128,96]{1,2,0:T(8,128)(2,1)}), bf16[4,128,96]{1,2,0:T(8,128)(2,1)S(1)}, u32[]{:S(2)}, u32[]{:S(2)}) async-start(bf16[4,128,96]{1,2,0:T(8,128)(2,1)} %bitcast.1), calls=%async_computation | async-start | bytes 196608 | tf_op jit(solution)/shard_map/all_to_all | solution.py:105
  14.1 95.9 %all-gather.7.cloned.1.call-start = ((), (), s32[]{:S(2)}) async-start(), calls=%async_computation.4 | async-start | bytes 2654208 | tf_op jit(solution)/shard_map/all_gather | solution.py:111
  14.1 27.2 %collective-permute-start = (bf16[96,384]{1,0:T(8,128)(2,1)}, bf16[96,384]{1,0:T(8,128)(2,1)S(1)}, u32[]{:S(2)}, u32[]{:S(2)}) collective-permute-start(bf16[96,384]{1,0:T(8,128)(2,1)} %bitcast.32), channel_id=1, source_target_pairs={{0,0},{2,64},{4,128},{6,192},{8,256},{10,320},{12,384},{14,448},{6... | collective-permute-start | bytes 221192 | tf_op jit(solution)/shard_map/ppermute | solution.py:102
  56.6 10.8 %all-to-all-start.2 = ((bf16[4,128,768]{2,1,0:T(8,128)(2,1)}), bf16[4,128,768]{2,1,0:T(8,128)(2,1)S(1)}, u32[]{:S(2)}, u32[]{:S(2)}) async-start(bf16[4,128,768]{2,1,0:T(8,128)(2,1)} %bitcast.10), calls=%async_computation.2 | async-start | bytes 1572864 | tf_op jit(solution)/shard_map/all_to_all | solution.py:119
  60.8 11.8 %copy-start = (f32[128]{0:T(128)S(1)}, f32[128]{0:T(128)}, u32[]{:S(2)}) copy-start(f32[128]{0:T(128)} %param.14) | copy-start | bytes 1540
  60.9 17.2 %copy-start.2 = (s32[3,2,6]{2,1,0:T(2,128)S(1)}, s32[3,2,6]{2,1,0:T(2,128)}, u32[]{:S(2)}) copy-start(s32[3,2,6]{2,1,0:T(2,128)} %param.15) | copy-start | bytes 436
  60.9 23.4 %copy-start.1 = (f32[128]{0:T(128)S(1)}, f32[128]{0:T(128)}, u32[]{:S(2)}) copy-start(f32[128]{0:T(128)} %param.13) | copy-start | bytes 1540
  67.4 11.0 %all-to-all-start.1 = ((bf16[4,128,384]{2,1,0:T(8,128)(2,1)}), bf16[4,128,384]{2,1,0:T(8,128)(2,1)S(1)}, u32[]{:S(2)}, u32[]{:S(2)}) async-start(bf16[4,128,384]{2,1,0:T(8,128)(2,1)} %bitcast.5), calls=%async_computation.1 | async-start | bytes 786432 | tf_op jit(solution)/shard_map/all_to_all | solution.py:121
  72.8 11.5 %collective-permute-start.1 = (bf16[128,768]{1,0:T(8,128)(2,1)S(1)}, bf16[128,768]{1,0:T(8,128)(2,1)S(1)}, u32[]{:S(2)}, u32[]{:S(2)}) collective-permute-start(bf16[128,768]{1,0:T(8,128)(2,1)S(1)} %shard_map.82.own_ref), channel_id=1, source_target_pairs={{16,32},{32,16},{48,64},{64,48},{80,96},{96,80},{112,128},{128,112... | collective-permute-start | bytes 589832 | tf_op jit(solution)/shard_map/ppermute | solution.py:128
  76.0 8.3 %collective-permute-start.2 = (bf16[128,768]{1,0:T(8,128)(2,1)S(1)}, bf16[128,768]{1,0:T(8,128)(2,1)S(1)}, u32[]{:S(2)}, u32[]{:S(2)}) collective-permute-start(bf16[128,768]{1,0:T(8,128)(2,1)S(1)} %shard_map.82.own_ref), channel_id=1, source_target_pairs={{0,16},{16,0},{32,48},{48,32},{64,80},{80,64},{96,112},{112,96},{1... | collective-permute-start | bytes 589832 | tf_op jit(solution)/shard_map/ppermute | solution.py:128
Sparse Core Ops, SparseCore 0:
  9.4 44.1 all-gather.4
  55.7 47.2 all-gather.6

commit v10 on v9

--- a/solution.py
+++ b/solution.py
@@ -118,8 +118,9 @@
     key_value = shares(weights[:, width:])
     key_value = lax.all_to_all(key_value, "x", split_axis=0, concat_axis=0, tiled=True)
     query = shares(weights[:, :width])
+    packed = pack(key_value, k_gain)
+    query, packed = lax.optimization_barrier((query, packed))
     query = lax.all_to_all(query, "x", split_axis=0, concat_axis=0, tiled=True)
-    packed = pack(key_value, k_gain)
     count = lax.axis_size(SLAB)
     swaps = [
         [pair for i in range(first, count - 1, 2) for pair in ((i, i + 1), (i + 1, i))]

time: 121 us -> 123 us (1.017)
  the two profiles are of different devices: /device:TPU:71 before, /device:TPU:1 now
where the time goes in v10:
time: 123 us; the launch traced here: 122 us
  blocking collectives  59.6 us (48%)
  starting transfers between devices  22.9 us (19%)
  between operations  13.5 us (11%)
  waiting for transfers between devices  12.6 us (10%)
  matrix products  8.54 us (7%)
  local copies, waits for them, and re-layouts  1.99 us (2%)
  other arithmetic  1.91 us (2%)
    all_gather x1, blocking collectives, on_device(): everyone = lax.all_gather(attended, HEAD, axis=0, tiled=False)  24.1 us
    all_gather x1, blocking collectives, on_device(): lax.all_gather(pieces.reshape(n_x * rows, part), HEAD, axis=0, tiled=False)  23.8 us
    all_gather x1, blocking collectives, on_device(): columns = lax.all_gather(columns, 'x', axis=0, tiled=True)  11.8 us
    all_to_all x1, waiting for transfers between devices, on_device(): query = lax.all_to_all(query, 'x', split_axis=0, concat_axis=0, tiled=True)  5.84 us
    all_to_all x1, waiting for transfers between devices, on_device(): lax.all_to_all(key_value, 'x', split_axis=0, concat_axis=0, tiled=True)  5.81 us
    dot_general x2, matrix products, shares(): jnp.dot(group, piece, preferred_element_type=jnp.float32)  5.41 us
    all_to_all x1, starting transfers between devices, on_device(): lax.all_to_all(pieces, 'x', split_axis=0, concat_axis=0, tiled=True)  4.84 us
    ppermute x1, starting transfers between devices, on_device(): columns = lax.ppermute(out_weight.T, ('z',) + HEAD, turned)  4.83 us
  transfers between devices with their start and end apart: 8, of which 3 were waited for; matrix products, arithmetic and copies ran while one was open for 6% of the time, Pallas kernels for 1%

profile of v10, /device:TPU:1, one launch (start us, length us, event | category | flops | bytes accessed | tf_op | source)
XLA Modules:
  0.0 122.0 jit_solution(2479837352262857207)
XLA Ops:
  6.5 1.7 %pad_maximum_fusion = bf16[96,1152]{1,0:T(8,128)(2,1)} fusion(bf16[96,384]{1,0:T(8,128)(2,1)} %param.11, bf16[96,384]{1,0:T(8,128)(2,1)} %param.10, bf16[96,384]{1,0:T(8,128)(2,1)} %param.9), kind=kLoop, calls=%fused_computation.6 | loop fusion | flops 663552 | bytes 442368 | tf_op jit(solution)/shard_map/concatenate | solution.py:98
  8.2 1.6 %copy.13 = bf16[128,384]{0,1:T(8,128)(2,1)} copy(bf16[128,384]{1,0:T(8,128)(2,1)} %param.8) | data formatting | bytes 196608 | tf_op args[0]
  9.9 4.8 %all-to-all-start = ((bf16[4,128,96]{1,2,0:T(8,128)(2,1)}), bf16[4,128,96]{1,2,0:T(8,128)(2,1)S(1)}, u32[]{:S(2)}, u32[]{:S(2)}) async-start(bf16[4,128,96]{1,2,0:T(8,128)(2,1)} %bitcast.1), calls=%async_computation | async-start | bytes 196608 | tf_op jit(solution)/shard_map/all_to_all | solution.py:105
  14.7 4.8 %collective-permute-start = (bf16[96,384]{1,0:T(8,128)(2,1)}, bf16[96,384]{1,0:T(8,128)(2,1)S(1)}, u32[]{:S(2)}, u32[]{:S(2)}) collective-permute-start(bf16[96,384]{1,0:T(8,128)(2,1)} %bitcast.32), channel_id=1, source_target_pairs={{0,0},{2,64},{4,128},{6,192},{8,256},{10,320},{12,384},{14,448},{6... | collective-permute-start | bytes 221192 | tf_op jit(solution)/shard_map/ppermute | solution.py:102
  19.7 23.8 %all_gather.22 = bf16[8,512,96]{1,2,0:T(8,128)(2,1)S(1)} all-gather(bf16[1,512,96]{1,2,0:T(8,128)(2,1)S(1)} %all_gather_reshape.3), channel_id=1, replica_groups=mesh['z'=8,'x'=4,'y'=4,'core'=2,'cfg'=2] {'y','core'}, dimensions={0}, use_global_device_ids=true | all-gather | bytes 884736 | tf_op jit(solution)/shard_map/all_gather | solution.py:106
  43.4 11.8 %all_gather.23 = bf16[384,384]{1,0:T(8,128)(2,1)} all-gather(bf16[96,384]{1,0:T(8,128)(2,1)S(1)} %collective-permute-done), channel_id=1, replica_groups=mesh['z'=8,'x'=4,'y'=4,'core'=2,'cfg'=2] {'x'}, dimensions={0}, use_global_device_ids=true | all-gather | bytes 368640 | tf_op jit(solution)/shard_map/all_gather | solution.py:110
  55.3 0.9 all-gather.5.cloned.1.call-done
  56.2 3.0 %convolution_convert_fusion = bf16[512,768]{1,0:T(8,128)(2,1)} fusion(bf16[512,768]{0,1:T(8,128)(2,1)S(1)} %bitcast.30, bf16[768,1152]{1,0:T(8,128)(2,1)} %all-gather.5.cloned.1.call-done), kind=kOutput, calls=%fused_computation | convolution fusion | flops 604372992 | bytes 2752512 | tf_op jit(solution)/shard_map/dot_general | solution.py:115
  59.1 4.5 %all-to-all-start.1 = ((bf16[4,128,768]{2,1,0:T(8,128)(2,1)}), bf16[4,128,768]{2,1,0:T(8,128)(2,1)S(1)}, u32[]{:S(2)}, u32[]{:S(2)}) async-start(bf16[4,128,768]{2,1,0:T(8,128)(2,1)} %bitcast.6), calls=%async_computation.1 | async-start | bytes 1572864 | tf_op jit(solution)/shard_map/all_to_all | solution.py:119
  63.6 0.1 add_multiply_fusion
  63.7 2.5 %convolution_convert_fusion.1 = bf16[512,384]{1,0:T(8,128)(2,1)} fusion(bf16[512,768]{0,1:T(8,128)(2,1)S(1)} %bitcast.31, bf16[768,1152]{1,0:T(8,128)(2,1)} %all-gather.5.cloned.1.call-done), kind=kOutput, calls=%fused_computation.1 | convolution fusion | flops 302186496 | bytes 1769472 | tf_op jit(solution)/shard_map/dot_general | solution.py:115
  66.2 5.8 %all-to-all-done.1.share_ref = bf16[4,128,768]{2,1,0:T(8,128)(2,1)S(1)} async-done(((bf16[4,128,768]{2,1,0:T(8,128)(2,1)}), bf16[4,128,768]{2,1,0:T(8,128)(2,1)S(1)}, u32[]{:S(2)}, u32[]{:S(2)}) %all-to-all-start.1) | async-done | bytes 786464 | tf_op jit(solution)/shard_map/all_to_all | solution.py:119
  72.0 0.2 shard_map.82.own_ref
  72.2 0.7 collective-permute-start.1
  72.9 3.5 %collective-permute-start.2 = (bf16[128,768]{1,0:T(8,128)(2,1)S(1)}, bf16[128,768]{1,0:T(8,128)(2,1)S(1)}, u32[]{:S(2)}, u32[]{:S(2)}) collective-permute-start(bf16[128,768]{1,0:T(8,128)(2,1)S(1)} %shard_map.82.own_ref), channel_id=1, source_target_pairs={{0,16},{16,0},{32,48},{48,32},{64,80},{80,64},{96,112},{112,96},{1... | collective-permute-start | bytes 589832 | tf_op jit(solution)/shard_map/ppermute | solution.py:129
  76.3 4.6 %all-to-all-start.2 = ((bf16[4,128,384]{2,1,0:T(8,128)(2,1)}), bf16[4,128,384]{2,1,0:T(8,128)(2,1)S(1)}, u32[]{:S(2)}, u32[]{:S(2)}) async-start(bf16[4,128,384]{2,1,0:T(8,128)(2,1)} %bitcast.5), calls=%async_computation.2 | async-start | bytes 786432 | tf_op jit(solution)/shard_map/all_to_all | solution.py:123
  81.0 0.1 add.37
  81.1 0.1 compare_reduce_fusion
  81.2 0.1 broadcast_in_dim.2
  81.3 0.1 reshape.71.live_ref
  81.3 5.8 %all-to-all-done.2.share_ref = bf16[4,128,384]{2,1,0:T(8,128)(2,1)S(1)} async-done(((bf16[4,128,384]{2,1,0:T(8,128)(2,1)}), bf16[4,128,384]{2,1,0:T(8,128)(2,1)S(1)}, u32[]{:S(2)}, u32[]{:S(2)}) %all-to-all-start.2) | async-done | bytes 393248 | tf_op jit(solution)/shard_map/all_to_all | solution.py:123
  87.2 0.7 shard_map.83
  87.9 24.1 %all-gather = bf16[1024,384]{1,0:T(8,128)(2,1)S(1)} all-gather(bf16[128,384]{1,0:T(8,128)(2,1)S(1)} %shard_map.83), channel_id=2, replica_groups=mesh['z'=8,'x'=4,'y'=4,'core'=2,'cfg'=2] {'y','core'}, dimensions={0}, use_global_device_ids=true | all-gather | bytes 884736 | tf_op jit(solution)/shard_map/all_gather | solution.py:132
  112.0 3.1 %fusion.1 = bf16[128,384]{1,0:T(8,128)(2,1)} fusion(bf16[8,128,384]{2,1,0:T(8,128)(2,1)S(1)} %bitcast.28, bf16[8,384,384]{2,1,0:T(8,128)(2,1)} %bitcast.29), kind=kOutput, calls=%fused_computation.4 | convolution fusion | flops 302039040 | bytes 3244032 | tf_op jit(solution)/shard_map/hrd,hnd->rn/dot_general | solution.py:133
  (20 shorter events, 0.2 us)
Async XLA Ops:
  6.5 49.6 %all-gather.5.cloned.1.call-start = ((), (), s32[]{:S(2)}) async-start(), calls=%async_computation.3 | async-start | bytes 1990656 | tf_op jit(solution)/shard_map/all_gather | solution.py:99
  9.9 9.7 %all-to-all-start = ((bf16[4,128,96]{1,2,0:T(8,128)(2,1)}), bf16[4,128,96]{1,2,0:T(8,128)(2,1)S(1)}, u32[]{:S(2)}, u32[]{:S(2)}) async-start(bf16[4,128,96]{1,2,0:T(8,128)(2,1)} %bitcast.1), calls=%async_computation | async-start | bytes 196608 | tf_op jit(solution)/shard_map/all_to_all | solution.py:105
  14.7 97.3 %all-gather.7.cloned.1.call-start = ((), (), s32[]{:S(2)}) async-start(), calls=%async_computation.4 | async-start | bytes 2654208 | tf_op jit(solution)/shard_map/all_gather | solution.py:111
  14.7 28.7 %collective-permute-start = (bf16[96,384]{1,0:T(8,128)(2,1)}, bf16[96,384]{1,0:T(8,128)(2,1)S(1)}, u32[]{:S(2)}, u32[]{:S(2)}) collective-permute-start(bf16[96,384]{1,0:T(8,128)(2,1)} %bitcast.32), channel_id=1, source_target_pairs={{0,0},{2,64},{4,128},{6,192},{8,256},{10,320},{12,384},{14,448},{6... | collective-permute-start | bytes 221192 | tf_op jit(solution)/shard_map/ppermute | solution.py:102
  59.1 12.9 %copy-start = (f32[128]{0:T(128)S(1)}, f32[128]{0:T(128)}, u32[]{:S(2)}) copy-start(f32[128]{0:T(128)} %param.14) | copy-start | bytes 1540
  59.1 12.9 %all-to-all-start.1 = ((bf16[4,128,768]{2,1,0:T(8,128)(2,1)}), bf16[4,128,768]{2,1,0:T(8,128)(2,1)S(1)}, u32[]{:S(2)}, u32[]{:S(2)}) async-start(bf16[4,128,768]{2,1,0:T(8,128)(2,1)} %bitcast.6), calls=%async_computation.1 | async-start | bytes 1572864 | tf_op jit(solution)/shard_map/all_to_all | solution.py:119
  63.7 17.4 %copy-start.2 = (s32[3,2,6]{2,1,0:T(2,128)S(1)}, s32[3,2,6]{2,1,0:T(2,128)}, u32[]{:S(2)}) copy-start(s32[3,2,6]{2,1,0:T(2,128)} %param.15) | copy-start | bytes 436
  63.7 23.5 %copy-start.1 = (f32[128]{0:T(128)S(1)}, f32[128]{0:T(128)}, u32[]{:S(2)}) copy-start(f32[128]{0:T(128)} %param.13) | copy-start | bytes 1540
  72.2 9.2 %collective-permute-start.1 = (bf16[128,768]{1,0:T(8,128)(2,1)S(1)}, bf16[128,768]{1,0:T(8,128)(2,1)S(1)}, u32[]{:S(2)}, u32[]{:S(2)}) collective-permute-start(bf16[128,768]{1,0:T(8,128)(2,1)S(1)} %shard_map.82.own_ref), channel_id=1, source_target_pairs={{16,32},{32,16},{48,64},{64,48},{80,96},{96,80},{112,128},{128,112... | collective-permute-start | bytes 589832 | tf_op jit(solution)/shard_map/ppermute | solution.py:129
  72.9 8.5 %collective-permute-start.2 = (bf16[128,768]{1,0:T(8,128)(2,1)S(1)}, bf16[128,768]{1,0:T(8,128)(2,1)S(1)}, u32[]{:S(2)}, u32[]{:S(2)}) collective-permute-start(bf16[128,768]{1,0:T(8,128)(2,1)S(1)} %shard_map.82.own_ref), channel_id=1, source_target_pairs={{0,16},{16,0},{32,48},{48,32},{64,80},{80,64},{96,112},{112,96},{1... | collective-permute-start | bytes 589832 | tf_op jit(solution)/shard_map/ppermute | solution.py:129
  76.3 10.9 %all-to-all-start.2 = ((bf16[4,128,384]{2,1,0:T(8,128)(2,1)}), bf16[4,128,384]{2,1,0:T(8,128)(2,1)S(1)}, u32[]{:S(2)}, u32[]{:S(2)}) async-start(bf16[4,128,384]{2,1,0:T(8,128)(2,1)} %bitcast.5), calls=%async_computation.2 | async-start | bytes 786432 | tf_op jit(solution)/shard_map/all_to_all | solution.py:123
Sparse Core Ops, SparseCore 0:
  9.4 46.6 all-gather.4
  58.2 46.3 all-gather.6

commit v11 on v9

--- a/solution.py
+++ b/solution.py
@@ -46,12 +46,14 @@
     )(share, gain.reshape(1, HDIM))
 
 
-def attention_kernel(share_ref, gain_ref, live_ref, odd_ref, own_ref, even_ref, out_ref):
+def attention_kernel(kept_ref, came_ref, gain_ref, live_ref, odd_ref, own_ref, even_ref, out_ref):
     rows, width = out_ref.shape
     near = (odd_ref, own_ref, even_ref)
     scale = 1.0 / HDIM**0.5
     for low in range(0, width, HDIM):
-        query = normed(summed(share_ref, low, low + HDIM), gain_ref[...]).astype(jnp.bfloat16)
+        head = slice(low, low + HDIM)
+        query = kept_ref[:, head] + came_ref[:, head].astype(jnp.float32)
+        query = normed(query, gain_ref[...]).astype(jnp.bfloat16)
         keys = jnp.concatenate([r[:, low : low + HDIM] for r in near], axis=0)
         values = jnp.concatenate([r[:, width + low : width + low + HDIM] for r in near], axis=0)
         score = lax.dot_general(
@@ -70,13 +72,13 @@
         out_ref[:, low : low + HDIM] = (mixed / total).astype(jnp.bfloat16)
 
 
-def attention(query, gain, live, odd, own, even):
-    rows, width = query.shape[1:]
+def attention(kept, came, gain, live, odd, own, even):
+    rows, width = kept.shape
     return pl.pallas_call(
         attention_kernel,
         out_shape=jax.ShapeDtypeStruct((rows, width), jnp.bfloat16),
         compiler_params=params(16),
-    )(query, gain.reshape(1, HDIM), live, odd, own, even)
+    )(kept, came, gain.reshape(1, HDIM), live, odd, own, even)
 
 
 def live_rows(key_tiles, tiles_here):
@@ -117,8 +119,19 @@
 
     key_value = shares(weights[:, width:])
     key_value = lax.all_to_all(key_value, "x", split_axis=0, concat_axis=0, tiled=True)
-    query = shares(weights[:, :width])
-    query = lax.all_to_all(query, "x", split_axis=0, concat_axis=0, tiled=True)
+    query = shares(weights[:, :width]).reshape(n_x // 2, 2, rows, width)
+    place = lax.axis_index("x")
+    kept, sent = (
+        lax.dynamic_index_in_dim(query, side, 1, keepdims=False)
+        for side in (place % 2, 1 - place % 2)
+    )
+    came = lax.ppermute(sent, "x", [(i, i ^ 1) for i in range(n_x)])
+    pair = kept.astype(jnp.float32) + came.astype(jnp.float32)
+    kept, sent = (
+        lax.dynamic_index_in_dim(pair, side, 0, keepdims=False)
+        for side in (place // 2, 1 - place // 2)
+    )
+    came = lax.ppermute(sent.astype(jnp.bfloat16), "x", [(i, i ^ 2) for i in range(n_x)])
     packed = pack(key_value, k_gain)
     count = lax.axis_size(SLAB)
     swaps = [
@@ -127,7 +140,7 @@
     ]
     odd, even = (lax.ppermute(packed, SLAB, pairs) for pairs in swaps)
     live = live_rows(key_tiles, rows // TILE)
-    attended = attention(query, q_gain, live, odd, packed, even)
+    attended = attention(kept, came, q_gain, live, odd, packed, even)
     everyone = lax.all_gather(attended, HEAD, axis=0, tiled=False)
     total = jnp.einsum("hrd,hnd->rn", everyone, projection, preferred_element_type=jnp.float32)
     return total.astype(jnp.bfloat16)

time: 121 us -> 121 us (level)
  the two profiles are of different devices: /device:TPU:71 before, /device:TPU:1 now
where the time goes in v11:
time: 121 us; the launch traced here: 120 us
  blocking collectives  57.6 us (48%)
  starting transfers between devices  26.4 us (22%)
  between operations  13.6 us (11%)
  waiting for transfers between devices  10.1 us (8%)
  matrix products  7.77 us (6%)
  local copies, waits for them, and re-layouts  2.07 us (2%)
  other arithmetic  1.96 us (2%)
    all_gather x1, blocking collectives, on_device(): lax.all_gather(pieces.reshape(n_x * rows, part), HEAD, axis=0, tiled=False)  23.8 us
    all_gather x1, blocking collectives, on_device(): everyone = lax.all_gather(attended, HEAD, axis=0, tiled=False)  22 us
    all_gather x1, blocking collectives, on_device(): columns = lax.all_gather(columns, 'x', axis=0, tiled=True)  11.8 us
    ppermute x2, starting transfers between devices, on_device(): odd, even = (lax.ppermute(packed, SLAB, pairs) for pairs in swaps)  5.89 us
    ppermute x1, waiting for transfers between devices, on_device(): came = lax.ppermute(sent, 'x', [(i, i ^ 1) for i in range(n_x)])  5.54 us
    all_to_all x1, starting transfers between devices, on_device(): lax.all_to_all(pieces, 'x', split_axis=0, concat_axis=0, tiled=True)  4.84 us
    ppermute x1, starting transfers between devices, on_device(): columns = lax.ppermute(out_weight.T, ('z',) + HEAD, turned)  4.83 us
    dot_general x2, matrix products, shares(): jnp.dot(group, piece, preferred_element_type=jnp.float32)  4.65 us
  transfers between devices with their start and end apart: 9, of which 3 were waited for; matrix products, arithmetic and copies ran while one was open for 6% of the time, Pallas kernels for 1%

profile of v11, /device:TPU:1, one launch (start us, length us, event | category | flops | bytes accessed | tf_op | source)
XLA Modules:
  0.0 120.4 jit_solution(18075074672963064169)
XLA Ops:
  6.5 1.7 %pad_maximum_fusion = bf16[96,1152]{1,0:T(8,128)(2,1)} fusion(bf16[96,384]{1,0:T(8,128)(2,1)} %param.11, bf16[96,384]{1,0:T(8,128)(2,1)} %param.10, bf16[96,384]{1,0:T(8,128)(2,1)} %param.9), kind=kLoop, calls=%fused_computation.7 | loop fusion | flops 663552 | bytes 442368 | tf_op jit(solution)/shard_map/concatenate | solution.py:100
  8.2 1.6 %copy.15 = bf16[128,384]{0,1:T(8,128)(2,1)} copy(bf16[128,384]{1,0:T(8,128)(2,1)} %param.8) | data formatting | bytes 196608 | tf_op args[0]
  9.9 4.8 %all-to-all-start = ((bf16[4,128,96]{1,2,0:T(8,128)(2,1)}), bf16[4,128,96]{1,2,0:T(8,128)(2,1)S(1)}, u32[]{:S(2)}, u32[]{:S(2)}) async-start(bf16[4,128,96]{1,2,0:T(8,128)(2,1)} %bitcast.1), calls=%async_computation | async-start | bytes 196608 | tf_op jit(solution)/shard_map/all_to_all | solution.py:107
  14.7 4.8 %collective-permute-start = (bf16[96,384]{1,0:T(8,128)(2,1)}, bf16[96,384]{1,0:T(8,128)(2,1)S(1)}, u32[]{:S(2)}, u32[]{:S(2)}) collective-permute-start(bf16[96,384]{1,0:T(8,128)(2,1)} %bitcast.45), channel_id=1, source_target_pairs={{0,0},{2,64},{4,128},{6,192},{8,256},{10,320},{12,384},{14,448},{6... | collective-permute-start | bytes 221192 | tf_op jit(solution)/shard_map/ppermute | solution.py:104
  19.7 23.8 %all_gather.22 = bf16[8,512,96]{1,2,0:T(8,128)(2,1)S(1)} all-gather(bf16[1,512,96]{1,2,0:T(8,128)(2,1)S(1)} %all_gather_reshape.3), channel_id=1, replica_groups=mesh['z'=8,'x'=4,'y'=4,'core'=2,'cfg'=2] {'y','core'}, dimensions={0}, use_global_device_ids=true | all-gather | bytes 884736 | tf_op jit(solution)/shard_map/all_gather | solution.py:108
  43.4 11.8 %all_gather.23 = bf16[384,384]{1,0:T(8,128)(2,1)} all-gather(bf16[96,384]{1,0:T(8,128)(2,1)S(1)} %collective-permute-done), channel_id=1, replica_groups=mesh['z'=8,'x'=4,'y'=4,'core'=2,'cfg'=2] {'x'}, dimensions={0}, use_global_device_ids=true | all-gather | bytes 368640 | tf_op jit(solution)/shard_map/all_gather | solution.py:112
  55.3 0.1 add_multiply_fusion
  55.4 0.8 all-gather.5.cloned.1.call-done
  56.2 3.0 %convolution_convert_fusion = bf16[512,768]{1,0:T(8,128)(2,1)} fusion(bf16[512,768]{0,1:T(8,128)(2,1)S(1)} %bitcast.41, bf16[768,1152]{1,0:T(8,128)(2,1)} %all-gather.5.cloned.1.call-done), kind=kOutput, calls=%fused_computation | convolution fusion | flops 604372992 | bytes 2752512 | tf_op jit(solution)/shard_map/dot_general | solution.py:117
  59.1 4.4 %all-to-all-start.1 = ((bf16[4,128,768]{2,1,0:T(8,128)(2,1)}), bf16[4,128,768]{2,1,0:T(8,128)(2,1)S(1)}, u32[]{:S(2)}, u32[]{:S(2)}) async-start(bf16[4,128,768]{2,1,0:T(8,128)(2,1)} %bitcast.14), calls=%async_computation.1 | async-start | bytes 1572864 | tf_op jit(solution)/shard_map/all_to_all | solution.py:121
  63.5 1.7 %convolution_convert_fusion.1 = bf16[512,384]{1,0:T(8,128)(2,1)S(1)} fusion(bf16[512,768]{0,1:T(8,128)(2,1)S(1)} %bitcast.42, bf16[768,1152]{1,0:T(8,128)(2,1)} %all-gather.5.cloned.1.call-done), kind=kOutput, calls=%fused_computation.1 | convolution fusion | flops 302186496 | bytes 1769472 | tf_op jit(solution)/shard_map/dot_general | solution.py:117
  65.3 3.4 %collective-permute-start.1 = (bf16[2,128,384]{2,1,0:T(8,128)(2,1)S(1)}, bf16[2,128,384]{2,1,0:T(8,128)(2,1)S(1)}, u32[]{:S(2)}, u32[]{:S(2)}) collective-permute-start(bf16[2,128,384]{2,1,0:T(8,128)(2,1)S(1)} %dynamic-slice_bitcast_fusion.1), channel_id=1, source_target_pairs={{0,16},{16,0},{32,48},{48,32},{1,17},{17,1},{33,49},{49,33},{2,18}... | collective-permute-start | bytes 589832 | tf_op jit(solution)/shard_map/ppermute | solution.py:128
  68.7 0.1 add.67
  68.8 0.1 compare_reduce_fusion
  69.0 0.1 reshape.68.live_ref
  69.1 5.5 %collective-permute-done.1 = bf16[2,128,384]{2,1,0:T(8,128)(2,1)S(1)} collective-permute-done((bf16[2,128,384]{2,1,0:T(8,128)(2,1)S(1)}, bf16[2,128,384]{2,1,0:T(8,128)(2,1)S(1)}, u32[]{:S(2)}, u32[]{:S(2)}) %collective-permute-start.1) | collective-permute-done | bytes 196640 | tf_op jit(solution)/shard_map/ppermute | solution.py:128
  74.7 0.2 shard_map.82.own_ref
  74.9 0.7 collective-permute-start.3
  75.5 5.2 %collective-permute-start.4 = (bf16[128,768]{1,0:T(8,128)(2,1)S(1)}, bf16[128,768]{1,0:T(8,128)(2,1)S(1)}, u32[]{:S(2)}, u32[]{:S(2)}) collective-permute-start(bf16[128,768]{1,0:T(8,128)(2,1)S(1)} %shard_map.82.own_ref), channel_id=1, source_target_pairs={{0,16},{16,0},{32,48},{48,32},{64,80},{80,64},{96,112},{112,96},{1... | collective-permute-start | bytes 589832 | tf_op jit(solution)/shard_map/ppermute | solution.py:141
  80.8 3.1 %collective-permute-start.2 = (bf16[128,384]{1,0:T(8,128)(2,1)S(1)}, bf16[128,384]{1,0:T(8,128)(2,1)S(1)}, u32[]{:S(2)}, u32[]{:S(2)}) collective-permute-start(bf16[128,384]{1,0:T(8,128)(2,1)S(1)} %fusion.3), channel_id=1, source_target_pairs={{0,32},{16,48},{32,0},{48,16},{1,33},{17,49},{33,1},{49,17},{2,34}... | collective-permute-start | bytes 294920 | tf_op jit(solution)/shard_map/ppermute | solution.py:134
  84.0 3.8 %collective-permute-done.2.came_ref = bf16[128,384]{1,0:T(8,128)(2,1)S(1)} collective-permute-done((bf16[128,384]{1,0:T(8,128)(2,1)S(1)}, bf16[128,384]{1,0:T(8,128)(2,1)S(1)}, u32[]{:S(2)}, u32[]{:S(2)}) %collective-permute-start.2) | collective-permute-done | bytes 98336 | tf_op jit(solution)/shard_map/ppermute | solution.py:134
  87.7 0.7 shard_map.83
  88.5 22.0 %all-gather = bf16[1024,384]{1,0:T(8,128)(2,1)S(1)} all-gather(bf16[128,384]{1,0:T(8,128)(2,1)S(1)} %shard_map.83), channel_id=2, replica_groups=mesh['z'=8,'x'=4,'y'=4,'core'=2,'cfg'=2] {'y','core'}, dimensions={0}, use_global_device_ids=true | all-gather | bytes 884736 | tf_op jit(solution)/shard_map/all_gather | solution.py:144
  110.5 3.1 %fusion.1 = bf16[128,384]{1,0:T(8,128)(2,1)} fusion(bf16[8,128,384]{2,1,0:T(8,128)(2,1)S(1)} %bitcast.39, bf16[8,384,384]{2,1,0:T(8,128)(2,1)} %bitcast.40), kind=kOutput, calls=%fused_computation.4 | convolution fusion | flops 302039040 | bytes 3244032 | tf_op jit(solution)/shard_map/hrd,hnd->rn/dot_general | solution.py:145
  (26 shorter events, 0.4 us)
Async XLA Ops:
  6.5 49.6 %all-gather.5.cloned.1.call-start = ((), (), s32[]{:S(2)}) async-start(), calls=%async_computation.2 | async-start | bytes 1990656 | tf_op jit(solution)/shard_map/all_gather | solution.py:101
  9.9 9.7 %all-to-all-start = ((bf16[4,128,96]{1,2,0:T(8,128)(2,1)}), bf16[4,128,96]{1,2,0:T(8,128)(2,1)S(1)}, u32[]{:S(2)}, u32[]{:S(2)}) async-start(bf16[4,128,96]{1,2,0:T(8,128)(2,1)} %bitcast.1), calls=%async_computation | async-start | bytes 196608 | tf_op jit(solution)/shard_map/all_to_all | solution.py:107
  14.7 95.8 %all-gather.7.cloned.1.call-start = ((), (), s32[]{:S(2)}) async-start(), calls=%async_computation.3 | async-start | bytes 2654208 | tf_op jit(solution)/shard_map/all_gather | solution.py:113
  14.7 28.7 %collective-permute-start = (bf16[96,384]{1,0:T(8,128)(2,1)}, bf16[96,384]{1,0:T(8,128)(2,1)S(1)}, u32[]{:S(2)}, u32[]{:S(2)}) collective-permute-start(bf16[96,384]{1,0:T(8,128)(2,1)} %bitcast.45), channel_id=1, source_target_pairs={{0,0},{2,64},{4,128},{6,192},{8,256},{10,320},{12,384},{14,448},{6... | collective-permute-start | bytes 221192 | tf_op jit(solution)/shard_map/ppermute | solution.py:104
  59.1 15.5 %all-to-all-start.1 = ((bf16[4,128,768]{2,1,0:T(8,128)(2,1)}), bf16[4,128,768]{2,1,0:T(8,128)(2,1)S(1)}, u32[]{:S(2)}, u32[]{:S(2)}) async-start(bf16[4,128,768]{2,1,0:T(8,128)(2,1)} %bitcast.14), calls=%async_computation.1 | async-start | bytes 1572864 | tf_op jit(solution)/shard_map/all_to_all | solution.py:121
  63.5 5.3 %copy-start.2 = (s32[3,2,6]{2,1,0:T(2,128)S(1)}, s32[3,2,6]{2,1,0:T(2,128)}, u32[]{:S(2)}) copy-start(s32[3,2,6]{2,1,0:T(2,128)} %param.15) | copy-start | bytes 436
  63.5 11.2 %copy-start = (f32[128]{0:T(128)S(1)}, f32[128]{0:T(128)}, u32[]{:S(2)}) copy-start(f32[128]{0:T(128)} %param.14) | copy-start | bytes 1540
  65.2 22.5 %copy-start.1 = (f32[128]{0:T(128)S(1)}, f32[128]{0:T(128)}, u32[]{:S(2)}) copy-start(f32[128]{0:T(128)} %param.13) | copy-start | bytes 1540
  65.3 9.4 %collective-permute-start.1 = (bf16[2,128,384]{2,1,0:T(8,128)(2,1)S(1)}, bf16[2,128,384]{2,1,0:T(8,128)(2,1)S(1)}, u32[]{:S(2)}, u32[]{:S(2)}) collective-permute-start(bf16[2,128,384]{2,1,0:T(8,128)(2,1)S(1)} %dynamic-slice_bitcast_fusion.1), channel_id=1, source_target_pairs={{0,16},{16,0},{32,48},{48,32},{1,17},{17,1},{33,49},{49,33},{2,18}... | collective-permute-start | bytes 589832 | tf_op jit(solution)/shard_map/ppermute | solution.py:128
  74.9 12.8 %collective-permute-start.3 = (bf16[128,768]{1,0:T(8,128)(2,1)S(1)}, bf16[128,768]{1,0:T(8,128)(2,1)S(1)}, u32[]{:S(2)}, u32[]{:S(2)}) collective-permute-start(bf16[128,768]{1,0:T(8,128)(2,1)S(1)} %shard_map.82.own_ref), channel_id=1, source_target_pairs={{16,32},{32,16},{48,64},{64,48},{80,96},{96,80},{112,128},{128,112... | collective-permute-start | bytes 589832 | tf_op jit(solution)/shard_map/ppermute | solution.py:141
  75.5 12.2 %collective-permute-start.4 = (bf16[128,768]{1,0:T(8,128)(2,1)S(1)}, bf16[128,768]{1,0:T(8,128)(2,1)S(1)}, u32[]{:S(2)}, u32[]{:S(2)}) collective-permute-start(bf16[128,768]{1,0:T(8,128)(2,1)S(1)} %shard_map.82.own_ref), channel_id=1, source_target_pairs={{0,16},{16,0},{32,48},{48,32},{64,80},{80,64},{96,112},{112,96},{1... | collective-permute-start | bytes 589832 | tf_op jit(solution)/shard_map/ppermute | solution.py:141
  80.8 6.9 %collective-permute-start.2 = (bf16[128,384]{1,0:T(8,128)(2,1)S(1)}, bf16[128,384]{1,0:T(8,128)(2,1)S(1)}, u32[]{:S(2)}, u32[]{:S(2)}) collective-permute-start(bf16[128,384]{1,0:T(8,128)(2,1)S(1)} %fusion.3), channel_id=1, source_target_pairs={{0,32},{16,48},{32,0},{48,16},{1,33},{17,49},{33,1},{49,17},{2,34}... | collective-permute-start | bytes 294920 | tf_op jit(solution)/shard_map/ppermute | solution.py:134
Sparse Core Ops, SparseCore 0:
  9.4 46.6 all-gather.4
  58.2 47.2 all-gather.6

commit v12 on v10

--- a/solution.py
+++ b/solution.py
@@ -44,6 +44,18 @@
         out_shape=jax.ShapeDtypeStruct(share.shape[1:], jnp.bfloat16),
         compiler_params=params(16),
     )(share, gain.reshape(1, HDIM))
+
+
+def copy_kernel(source_ref, out_ref):
+    out_ref[...] = source_ref[...]
+
+
+def copied(array):
+    return pl.pallas_call(
+        copy_kernel,
+        out_shape=jax.ShapeDtypeStruct(array.shape, array.dtype),
+        compiler_params=params(16),
+    )(array)
 
 
 def attention_kernel(share_ref, gain_ref, live_ref, odd_ref, own_ref, even_ref, out_ref):
@@ -126,7 +138,8 @@
         [pair for i in range(first, count - 1, 2) for pair in ((i, i + 1), (i + 1, i))]
         for first in (1, 0)
     ]
-    odd, even = (lax.ppermute(packed, SLAB, pairs) for pairs in swaps)
+    odd = lax.ppermute(packed, SLAB, swaps[0])
+    even = lax.ppermute(copied(packed), SLAB, swaps[1])
     live = live_rows(key_tiles, rows // TILE)
     attended = attention(query, q_gain, live, odd, packed, even)
     everyone = lax.all_gather(attended, HEAD, axis=0, tiled=False)

time: 123 us -> 120 us (0.976)
  waiting for transfers between devices: 12.6 us -> 10.2 us
    all_to_all x1, waiting for transfers between devices: 5.84 us -> 0.01 us  [on_device(): query = lax.all_to_all(query, 'x', split_axis=0, concat_axis=0, tiled=True)]
    ppermute x2, waiting for transfers between devices: 0.01 us -> 3.44 us  [the longest x1 3.44 us: on_device(): even = lax.ppermute(copied(packed), SLAB, swaps[1])]
where the time goes in v12:
time: 120 us; the launch traced here: 119 us
  blocking collectives  59 us (49%)
  starting transfers between devices  23.2 us (19%)
  between operations  13.5 us (11%)
  waiting for transfers between devices  10.2 us (8%)
  matrix products  8.54 us (7%)
  local copies, waits for them, and re-layouts  1.99 us (2%)
  other arithmetic  1.91 us (2%)
    all_gather x1, blocking collectives, on_device(): lax.all_gather(pieces.reshape(n_x * rows, part), HEAD, axis=0, tiled=False)  23.8 us
    all_gather x1, blocking collectives, on_device(): everyone = lax.all_gather(attended, HEAD, axis=0, tiled=False)  23.4 us
    all_gather x1, blocking collectives, on_device(): columns = lax.all_gather(columns, 'x', axis=0, tiled=True)  11.8 us
    all_to_all x1, waiting for transfers between devices, on_device(): lax.all_to_all(key_value, 'x', split_axis=0, concat_axis=0, tiled=True)  5.81 us
    dot_general x2, matrix products, shares(): jnp.dot(group, piece, preferred_element_type=jnp.float32)  5.41 us
    all_to_all x1, starting transfers between devices, on_device(): query = lax.all_to_all(query, 'x', split_axis=0, concat_axis=0, tiled=True)  4.96 us
    all_to_all x1, starting transfers between devices, on_device(): lax.all_to_all(pieces, 'x', split_axis=0, concat_axis=0, tiled=True)  4.84 us
    ppermute x1, starting transfers between devices, on_device(): columns = lax.ppermute(out_weight.T, ('z',) + HEAD, turned)  4.83 us
  transfers between devices with their start and end apart: 8, of which 3 were waited for; matrix products, arithmetic and copies ran while one was open for 6% of the time, Pallas kernels for 1%

profile of v12, /device:TPU:1, one launch (start us, length us, event | category | flops | bytes accessed | tf_op | source)
XLA Modules:
  0.0 119.2 jit_solution(12735762625173416000)
XLA Ops:
  6.5 1.7 %pad_maximum_fusion = bf16[96,1152]{1,0:T(8,128)(2,1)} fusion(bf16[96,384]{1,0:T(8,128)(2,1)} %param.11, bf16[96,384]{1,0:T(8,128)(2,1)} %param.10, bf16[96,384]{1,0:T(8,128)(2,1)} %param.9), kind=kLoop, calls=%fused_computation.6 | loop fusion | flops 663552 | bytes 442368 | tf_op jit(solution)/shard_map/concatenate | solution.py:110
  8.2 1.6 %copy.13 = bf16[128,384]{0,1:T(8,128)(2,1)} copy(bf16[128,384]{1,0:T(8,128)(2,1)} %param.8) | data formatting | bytes 196608 | tf_op args[0]
  9.9 4.8 %all-to-all-start = ((bf16[4,128,96]{1,2,0:T(8,128)(2,1)}), bf16[4,128,96]{1,2,0:T(8,128)(2,1)S(1)}, u32[]{:S(2)}, u32[]{:S(2)}) async-start(bf16[4,128,96]{1,2,0:T(8,128)(2,1)} %bitcast.1), calls=%async_computation | async-start | bytes 196608 | tf_op jit(solution)/shard_map/all_to_all | solution.py:117
  14.7 4.8 %collective-permute-start = (bf16[96,384]{1,0:T(8,128)(2,1)}, bf16[96,384]{1,0:T(8,128)(2,1)S(1)}, u32[]{:S(2)}, u32[]{:S(2)}) collective-permute-start(bf16[96,384]{1,0:T(8,128)(2,1)} %bitcast.32), channel_id=1, source_target_pairs={{0,0},{2,64},{4,128},{6,192},{8,256},{10,320},{12,384},{14,448},{6... | collective-permute-start | bytes 221192 | tf_op jit(solution)/shard_map/ppermute | solution.py:114
  19.7 23.8 %all_gather.22 = bf16[8,512,96]{1,2,0:T(8,128)(2,1)S(1)} all-gather(bf16[1,512,96]{1,2,0:T(8,128)(2,1)S(1)} %all_gather_reshape.3), channel_id=1, replica_groups=mesh['z'=8,'x'=4,'y'=4,'core'=2,'cfg'=2] {'y','core'}, dimensions={0}, use_global_device_ids=true | all-gather | bytes 884736 | tf_op jit(solution)/shard_map/all_gather | solution.py:118
  43.4 11.8 %all_gather.23 = bf16[384,384]{1,0:T(8,128)(2,1)} all-gather(bf16[96,384]{1,0:T(8,128)(2,1)S(1)} %collective-permute-done), channel_id=1, replica_groups=mesh['z'=8,'x'=4,'y'=4,'core'=2,'cfg'=2] {'x'}, dimensions={0}, use_global_device_ids=true | all-gather | bytes 368640 | tf_op jit(solution)/shard_map/all_gather | solution.py:122
  55.3 0.9 all-gather.5.cloned.1.call-done
  56.2 3.0 %convolution_convert_fusion = bf16[512,768]{1,0:T(8,128)(2,1)} fusion(bf16[512,768]{0,1:T(8,128)(2,1)S(1)} %bitcast.30, bf16[768,1152]{1,0:T(8,128)(2,1)} %all-gather.5.cloned.1.call-done), kind=kOutput, calls=%fused_computation | convolution fusion | flops 604372992 | bytes 2752512 | tf_op jit(solution)/shard_map/dot_general | solution.py:127
  59.1 4.5 %all-to-all-start.1 = ((bf16[4,128,768]{2,1,0:T(8,128)(2,1)}), bf16[4,128,768]{2,1,0:T(8,128)(2,1)S(1)}, u32[]{:S(2)}, u32[]{:S(2)}) async-start(bf16[4,128,768]{2,1,0:T(8,128)(2,1)} %bitcast.6), calls=%async_computation.1 | async-start | bytes 1572864 | tf_op jit(solution)/shard_map/all_to_all | solution.py:131
  63.6 0.1 add_multiply_fusion
  63.7 2.5 %convolution_convert_fusion.1 = bf16[512,384]{1,0:T(8,128)(2,1)} fusion(bf16[512,768]{0,1:T(8,128)(2,1)S(1)} %bitcast.31, bf16[768,1152]{1,0:T(8,128)(2,1)} %all-gather.5.cloned.1.call-done), kind=kOutput, calls=%fused_computation.1 | convolution fusion | flops 302186496 | bytes 1769472 | tf_op jit(solution)/shard_map/dot_general | solution.py:127
  66.2 5.8 %all-to-all-done.1.share_ref = bf16[4,128,768]{2,1,0:T(8,128)(2,1)S(1)} async-done(((bf16[4,128,768]{2,1,0:T(8,128)(2,1)}), bf16[4,128,768]{2,1,0:T(8,128)(2,1)S(1)}, u32[]{:S(2)}, u32[]{:S(2)}) %all-to-all-start.1) | async-done | bytes 786464 | tf_op jit(solution)/shard_map/all_to_all | solution.py:131
  72.0 0.2 shard_map.82.source_ref.own_ref
  72.2 0.7 collective-permute-start.1
  72.9 5.0 %all-to-all-start.2 = ((bf16[4,128,384]{2,1,0:T(8,128)(2,1)}), bf16[4,128,384]{2,1,0:T(8,128)(2,1)S(1)}, u32[]{:S(2)}, u32[]{:S(2)}) async-start(bf16[4,128,384]{2,1,0:T(8,128)(2,1)} %bitcast.5), calls=%async_computation.2 | async-start | bytes 786432 | tf_op jit(solution)/shard_map/all_to_all | solution.py:135
  77.8 3.4 %collective-permute-start.2 = (bf16[128,768]{1,0:T(8,128)(2,1)S(1)}, bf16[128,768]{1,0:T(8,128)(2,1)S(1)}, u32[]{:S(2)}, u32[]{:S(2)}) collective-permute-start(bf16[128,768]{1,0:T(8,128)(2,1)S(1)} %shard_map.83), channel_id=1, source_target_pairs={{0,16},{16,0},{32,48},{48,32},{64,80},{80,64},{96,112},{112,96},{1... | collective-permute-start | bytes 589832 | tf_op jit(solution)/shard_map/ppermute | solution.py:142
  81.3 0.1 add.37
  81.4 0.1 compare_reduce_fusion
  81.5 0.1 broadcast_in_dim.2
  81.6 0.1 reshape.71.live_ref
  81.6 3.4 %collective-permute-done.2.even_ref = bf16[128,768]{1,0:T(8,128)(2,1)S(1)} collective-permute-done((bf16[128,768]{1,0:T(8,128)(2,1)S(1)}, bf16[128,768]{1,0:T(8,128)(2,1)S(1)}, u32[]{:S(2)}, u32[]{:S(2)}) %collective-permute-start.2) | collective-permute-done | bytes 196640 | tf_op jit(solution)/shard_map/ppermute | solution.py:142
  85.1 0.7 shard_map.84
  85.8 23.4 %all-gather = bf16[1024,384]{1,0:T(8,128)(2,1)S(1)} all-gather(bf16[128,384]{1,0:T(8,128)(2,1)S(1)} %shard_map.84), channel_id=2, replica_groups=mesh['z'=8,'x'=4,'y'=4,'core'=2,'cfg'=2] {'y','core'}, dimensions={0}, use_global_device_ids=true | all-gather | bytes 884736 | tf_op jit(solution)/shard_map/all_gather | solution.py:145
  109.3 3.1 %fusion.1 = bf16[128,384]{1,0:T(8,128)(2,1)} fusion(bf16[8,128,384]{2,1,0:T(8,128)(2,1)S(1)} %bitcast.28, bf16[8,384,384]{2,1,0:T(8,128)(2,1)} %bitcast.29), kind=kOutput, calls=%fused_computation.4 | convolution fusion | flops 302039040 | bytes 3244032 | tf_op jit(solution)/shard_map/hrd,hnd->rn/dot_general | solution.py:146
  (21 shorter events, 0.3 us)
Async XLA Ops:
  6.5 49.6 %all-gather.5.cloned.1.call-start = ((), (), s32[]{:S(2)}) async-start(), calls=%async_computation.3 | async-start | bytes 1990656 | tf_op jit(solution)/shard_map/all_gather | solution.py:111
  9.9 9.7 %all-to-all-start = ((bf16[4,128,96]{1,2,0:T(8,128)(2,1)}), bf16[4,128,96]{1,2,0:T(8,128)(2,1)S(1)}, u32[]{:S(2)}, u32[]{:S(2)}) async-start(bf16[4,128,96]{1,2,0:T(8,128)(2,1)} %bitcast.1), calls=%async_computation | async-start | bytes 196608 | tf_op jit(solution)/shard_map/all_to_all | solution.py:117
  14.7 94.6 %all-gather.7.cloned.1.call-start = ((), (), s32[]{:S(2)}) async-start(), calls=%async_computation.4 | async-start | bytes 2654208 | tf_op jit(solution)/shard_map/all_gather | solution.py:123
  14.7 28.7 %collective-permute-start = (bf16[96,384]{1,0:T(8,128)(2,1)}, bf16[96,384]{1,0:T(8,128)(2,1)S(1)}, u32[]{:S(2)}, u32[]{:S(2)}) collective-permute-start(bf16[96,384]{1,0:T(8,128)(2,1)} %bitcast.32), channel_id=1, source_target_pairs={{0,0},{2,64},{4,128},{6,192},{8,256},{10,320},{12,384},{14,448},{6... | collective-permute-start | bytes 221192 | tf_op jit(solution)/shard_map/ppermute | solution.py:114
  59.1 12.9 %copy-start = (f32[128]{0:T(128)S(1)}, f32[128]{0:T(128)}, u32[]{:S(2)}) copy-start(f32[128]{0:T(128)} %param.14) | copy-start | bytes 1540
  59.1 12.9 %all-to-all-start.1 = ((bf16[4,128,768]{2,1,0:T(8,128)(2,1)}), bf16[4,128,768]{2,1,0:T(8,128)(2,1)S(1)}, u32[]{:S(2)}, u32[]{:S(2)}) async-start(bf16[4,128,768]{2,1,0:T(8,128)(2,1)} %bitcast.6), calls=%async_computation.1 | async-start | bytes 1572864 | tf_op jit(solution)/shard_map/all_to_all | solution.py:131
  63.7 17.7 %copy-start.2 = (s32[3,2,6]{2,1,0:T(2,128)S(1)}, s32[3,2,6]{2,1,0:T(2,128)}, u32[]{:S(2)}) copy-start(s32[3,2,6]{2,1,0:T(2,128)} %param.15) | copy-start | bytes 436
  63.7 21.4 %copy-start.1 = (f32[128]{0:T(128)S(1)}, f32[128]{0:T(128)}, u32[]{:S(2)}) copy-start(f32[128]{0:T(128)} %param.13) | copy-start | bytes 1540
  72.2 9.5 %collective-permute-start.1 = (bf16[128,768]{1,0:T(8,128)(2,1)S(1)}, bf16[128,768]{1,0:T(8,128)(2,1)S(1)}, u32[]{:S(2)}, u32[]{:S(2)}) collective-permute-start(bf16[128,768]{1,0:T(8,128)(2,1)S(1)} %shard_map.82.source_ref.own_ref), channel_id=1, source_target_pairs={{16,32},{32,16},{48,64},{64,48},{80,96},{96,80},{112,128},{128,112... | collective-permute-start | bytes 589832 | tf_op jit(solution)/shard_map/ppermute | solution.py:141
  72.9 12.2 %all-to-all-start.2 = ((bf16[4,128,384]{2,1,0:T(8,128)(2,1)}), bf16[4,128,384]{2,1,0:T(8,128)(2,1)S(1)}, u32[]{:S(2)}, u32[]{:S(2)}) async-start(bf16[4,128,384]{2,1,0:T(8,128)(2,1)} %bitcast.5), calls=%async_computation.2 | async-start | bytes 786432 | tf_op jit(solution)/shard_map/all_to_all | solution.py:135
  77.8 7.2 %collective-permute-start.2 = (bf16[128,768]{1,0:T(8,128)(2,1)S(1)}, bf16[128,768]{1,0:T(8,128)(2,1)S(1)}, u32[]{:S(2)}, u32[]{:S(2)}) collective-permute-start(bf16[128,768]{1,0:T(8,128)(2,1)S(1)} %shard_map.83), channel_id=1, source_target_pairs={{0,16},{16,0},{32,48},{48,32},{64,80},{80,64},{96,112},{112,96},{1... | collective-permute-start | bytes 589832 | tf_op jit(solution)/shard_map/ppermute | solution.py:142
Sparse Core Ops, SparseCore 0:
  9.4 46.6 all-gather.4
  58.2 46.5 all-gather.6

commit v13 on v12

--- a/solution.py
+++ b/solution.py
@@ -110,7 +110,9 @@
     stacked = jnp.concatenate([q_weight, k_weight, v_weight], axis=1)
     weights = lax.all_gather(stacked, "z", axis=0, tiled=True)
 
-    turned = [(z * n_head + h, h * n_z + z) for z in range(n_z) for h in range(n_head)]
+    n_core = lax.axis_size("core")
+    rank = [h % n_core * (n_head // n_core) + h // n_core for h in range(n_head)]
+    turned = [(z * n_head + h, rank[h] * n_z + z) for z in range(n_z) for h in range(n_head)]
     columns = lax.ppermute(out_weight.T, ("z",) + HEAD, turned)
 
     pieces = tokens.reshape(rows, n_x, part).transpose(1, 0, 2)
@@ -142,7 +144,7 @@
     even = lax.ppermute(copied(packed), SLAB, swaps[1])
     live = live_rows(key_tiles, rows // TILE)
     attended = attention(query, q_gain, live, odd, packed, even)
-    everyone = lax.all_gather(attended, HEAD, axis=0, tiled=False)
+    everyone = lax.all_gather(attended, ("core", "y"), axis=0, tiled=False)
     total = jnp.einsum("hrd,hnd->rn", everyone, projection, preferred_element_type=jnp.float32)
     return total.astype(jnp.bfloat16)
 

time: 120 us -> 131 us (1.092)
  starting transfers between devices: 23.2 us -> 29 us
  blocking collectives: 59 us -> 62.9 us
    all_gather x1, blocking collectives: 23.4 us -> 35.2 us  [on_device(): everyone = lax.all_gather(attended, ('core', 'y'), axis=0, tiled=False)]
    all_gather x1, blocking collectives: 23.8 us -> 16 us  [on_device(): lax.all_gather(pieces.reshape(n_x * rows, part), HEAD, axis=0, tiled=False)]
    ppermute x1, starting transfers between devices: 4.83 us -> 11.5 us  [on_device(): columns = lax.ppermute(out_weight.T, ('z',) + HEAD, turned)]
where the time goes in v13:
time: 131 us; the launch traced here: 130 us
  blocking collectives  62.9 us (48%)
  starting transfers between devices  29 us (22%)
  between operations  13.5 us (10%)
  waiting for transfers between devices  11.3 us (9%)
  matrix products  8.54 us (7%)
  local copies, waits for them, and re-layouts  1.99 us (2%)
  other arithmetic  1.91 us (1%)
    all_gather x1, blocking collectives, on_device(): everyone = lax.all_gather(attended, ('core', 'y'), axis=0, tiled=False)  35.2 us
    all_gather x1, blocking collectives, on_device(): lax.all_gather(pieces.reshape(n_x * rows, part), HEAD, axis=0, tiled=False)  16 us
    all_gather x1, blocking collectives, on_device(): columns = lax.all_gather(columns, 'x', axis=0, tiled=True)  11.8 us
    ppermute x1, starting transfers between devices, on_device(): columns = lax.ppermute(out_weight.T, ('z',) + HEAD, turned)  11.5 us
    all_to_all x1, waiting for transfers between devices, on_device(): lax.all_to_all(key_value, 'x', split_axis=0, concat_axis=0, tiled=True)  5.75 us
    dot_general x2, matrix products, shares(): jnp.dot(group, piece, preferred_element_type=jnp.float32)  5.42 us
    all_to_all x1, starting transfers between devices, on_device(): query = lax.all_to_all(query, 'x', split_axis=0, concat_axis=0, tiled=True)  5.02 us
    all_to_all x1, starting transfers between devices, on_device(): lax.all_to_all(pieces, 'x', split_axis=0, concat_axis=0, tiled=True)  4.84 us
  transfers between devices with their start and end apart: 8, of which 3 were waited for; matrix products, arithmetic and copies ran while one was open for 6% of the time, Pallas kernels for 1%

profile of v13, /device:TPU:1, one launch (start us, length us, event | category | flops | bytes accessed | tf_op | source)
XLA Modules:
  0.0 130.1 jit_solution(7062247037163973202)
XLA Ops:
  6.5 1.7 %pad_maximum_fusion = bf16[96,1152]{1,0:T(8,128)(2,1)} fusion(bf16[96,384]{1,0:T(8,128)(2,1)} %param.11, bf16[96,384]{1,0:T(8,128)(2,1)} %param.10, bf16[96,384]{1,0:T(8,128)(2,1)} %param.9), kind=kLoop, calls=%fused_computation.6 | loop fusion | flops 663552 | bytes 442368 | tf_op jit(solution)/shard_map/concatenate | solution.py:110
  8.2 1.6 %copy.13 = bf16[128,384]{0,1:T(8,128)(2,1)} copy(bf16[128,384]{1,0:T(8,128)(2,1)} %param.8) | data formatting | bytes 196608 | tf_op args[0]
  9.9 4.8 %all-to-all-start = ((bf16[4,128,96]{1,2,0:T(8,128)(2,1)}), bf16[4,128,96]{1,2,0:T(8,128)(2,1)S(1)}, u32[]{:S(2)}, u32[]{:S(2)}) async-start(bf16[4,128,96]{1,2,0:T(8,128)(2,1)} %bitcast.1), calls=%async_computation | async-start | bytes 196608 | tf_op jit(solution)/shard_map/all_to_all | solution.py:119
  14.7 11.5 %collective-permute-start = (bf16[96,384]{1,0:T(8,128)(2,1)}, bf16[96,384]{1,0:T(8,128)(2,1)S(1)}, u32[]{:S(2)}, u32[]{:S(2)}) collective-permute-start(bf16[96,384]{1,0:T(8,128)(2,1)} %bitcast.32), channel_id=1, source_target_pairs={{0,0},{2,256},{4,64},{6,320},{8,128},{10,384},{12,192},{14,448},{6... | collective-permute-start | bytes 221192 | tf_op jit(solution)/shard_map/ppermute | solution.py:116
  26.3 16.0 %all_gather.22 = bf16[8,512,96]{1,2,0:T(8,128)(2,1)S(1)} all-gather(bf16[1,512,96]{1,2,0:T(8,128)(2,1)S(1)} %all_gather_reshape.3), channel_id=1, replica_groups=mesh['z'=8,'x'=4,'y'=4,'core'=2,'cfg'=2] {'y','core'}, dimensions={0}, use_global_device_ids=true | all-gather | bytes 884736 | tf_op jit(solution)/shard_map/all_gather | solution.py:120
  42.3 11.8 %all_gather.23 = bf16[384,384]{1,0:T(8,128)(2,1)} all-gather(bf16[96,384]{1,0:T(8,128)(2,1)S(1)} %collective-permute-done), channel_id=1, replica_groups=mesh['z'=8,'x'=4,'y'=4,'core'=2,'cfg'=2] {'x'}, dimensions={0}, use_global_device_ids=true | all-gather | bytes 368640 | tf_op jit(solution)/shard_map/all_gather | solution.py:124
  54.1 2.0 %all-gather.5.cloned.1.call-done = bf16[768,1152]{1,0:T(8,128)(2,1)} async-done(((bf16[96,1152]{1,0:T(8,128)(2,1)}), bf16[768,1152]{1,0:T(8,128)(2,1)}) %all-gather.5.cloned.1.call-update) | async-done | bytes 1769488 | tf_op jit(solution)/shard_map/all_gather | solution.py:111
  56.1 3.0 %convolution_convert_fusion = bf16[512,768]{1,0:T(8,128)(2,1)} fusion(bf16[512,768]{0,1:T(8,128)(2,1)S(1)} %bitcast.30, bf16[768,1152]{1,0:T(8,128)(2,1)} %all-gather.5.cloned.1.call-done), kind=kOutput, calls=%fused_computation | convolution fusion | flops 604372992 | bytes 2752512 | tf_op jit(solution)/shard_map/dot_general | solution.py:129
  59.1 3.6 %all-to-all-start.1 = ((bf16[4,128,768]{2,1,0:T(8,128)(2,1)}), bf16[4,128,768]{2,1,0:T(8,128)(2,1)S(1)}, u32[]{:S(2)}, u32[]{:S(2)}) async-start(bf16[4,128,768]{2,1,0:T(8,128)(2,1)} %bitcast.6), calls=%async_computation.1 | async-start | bytes 1572864 | tf_op jit(solution)/shard_map/all_to_all | solution.py:133
  62.8 0.1 add_multiply_fusion
  62.8 2.5 %convolution_convert_fusion.1 = bf16[512,384]{1,0:T(8,128)(2,1)} fusion(bf16[512,768]{0,1:T(8,128)(2,1)S(1)} %bitcast.31, bf16[768,1152]{1,0:T(8,128)(2,1)} %all-gather.5.cloned.1.call-done), kind=kOutput, calls=%fused_computation.1 | convolution fusion | flops 302186496 | bytes 1769472 | tf_op jit(solution)/shard_map/dot_general | solution.py:129
  65.3 5.7 %all-to-all-done.1.share_ref = bf16[4,128,768]{2,1,0:T(8,128)(2,1)S(1)} async-done(((bf16[4,128,768]{2,1,0:T(8,128)(2,1)}), bf16[4,128,768]{2,1,0:T(8,128)(2,1)S(1)}, u32[]{:S(2)}, u32[]{:S(2)}) %all-to-all-start.1) | async-done | bytes 786464 | tf_op jit(solution)/shard_map/all_to_all | solution.py:133
  71.0 0.2 shard_map.82.source_ref.own_ref
  71.2 0.7 collective-permute-start.1
  71.9 5.0 %all-to-all-start.2 = ((bf16[4,128,384]{2,1,0:T(8,128)(2,1)}), bf16[4,128,384]{2,1,0:T(8,128)(2,1)S(1)}, u32[]{:S(2)}, u32[]{:S(2)}) async-start(bf16[4,128,384]{2,1,0:T(8,128)(2,1)} %bitcast.5), calls=%async_computation.2 | async-start | bytes 786432 | tf_op jit(solution)/shard_map/all_to_all | solution.py:137
  77.0 3.4 %collective-permute-start.2 = (bf16[128,768]{1,0:T(8,128)(2,1)S(1)}, bf16[128,768]{1,0:T(8,128)(2,1)S(1)}, u32[]{:S(2)}, u32[]{:S(2)}) collective-permute-start(bf16[128,768]{1,0:T(8,128)(2,1)S(1)} %shard_map.83), channel_id=1, source_target_pairs={{0,16},{16,0},{32,48},{48,32},{64,80},{80,64},{96,112},{112,96},{1... | collective-permute-start | bytes 589832 | tf_op jit(solution)/shard_map/ppermute | solution.py:144
  80.4 0.1 add.37
  80.5 0.1 compare_reduce_fusion
  80.6 0.1 broadcast_in_dim.2
  80.7 0.1 reshape.71.live_ref
  80.8 3.4 %collective-permute-done.2.even_ref = bf16[128,768]{1,0:T(8,128)(2,1)S(1)} collective-permute-done((bf16[128,768]{1,0:T(8,128)(2,1)S(1)}, bf16[128,768]{1,0:T(8,128)(2,1)S(1)}, u32[]{:S(2)}, u32[]{:S(2)}) %collective-permute-start.2) | collective-permute-done | bytes 196640 | tf_op jit(solution)/shard_map/ppermute | solution.py:144
  84.2 0.7 shard_map.84
  84.9 35.2 %all-gather = bf16[1024,384]{1,0:T(8,128)(2,1)S(1)} all-gather(bf16[128,384]{1,0:T(8,128)(2,1)S(1)} %shard_map.84), channel_id=2, replica_groups=mesh['z'=8,'x'=4,'y'=4,'core'=2,'cfg'=2] {'core','y'}, dimensions={0}, use_global_device_ids=true | all-gather | bytes 884736 | tf_op jit(solution)/shard_map/all_gather | solution.py:147
  120.1 3.1 %fusion.1 = bf16[128,384]{1,0:T(8,128)(2,1)} fusion(bf16[8,128,384]{2,1,0:T(8,128)(2,1)S(1)} %bitcast.28, bf16[8,384,384]{2,1,0:T(8,128)(2,1)} %bitcast.29), kind=kOutput, calls=%fused_computation.4 | convolution fusion | flops 302039040 | bytes 3244032 | tf_op jit(solution)/shard_map/hrd,hnd->rn/dot_general | solution.py:148
  (21 shorter events, 0.3 us)
Async XLA Ops:
  6.5 49.6 %all-gather.5.cloned.1.call-start = ((), (), s32[]{:S(2)}) async-start(), calls=%async_computation.3 | async-start | bytes 1990656 | tf_op jit(solution)/shard_map/all_gather | solution.py:111
  9.9 16.3 %all-to-all-start = ((bf16[4,128,96]{1,2,0:T(8,128)(2,1)}), bf16[4,128,96]{1,2,0:T(8,128)(2,1)S(1)}, u32[]{:S(2)}, u32[]{:S(2)}) async-start(bf16[4,128,96]{1,2,0:T(8,128)(2,1)} %bitcast.1), calls=%async_computation | async-start | bytes 196608 | tf_op jit(solution)/shard_map/all_to_all | solution.py:119
  14.7 105.4 %all-gather.7.cloned.1.call-start = ((), (), s32[]{:S(2)}) async-start(), calls=%async_computation.4 | async-start | bytes 2654208 | tf_op jit(solution)/shard_map/all_gather | solution.py:125
  14.7 27.6 %collective-permute-start = (bf16[96,384]{1,0:T(8,128)(2,1)}, bf16[96,384]{1,0:T(8,128)(2,1)S(1)}, u32[]{:S(2)}, u32[]{:S(2)}) collective-permute-start(bf16[96,384]{1,0:T(8,128)(2,1)} %bitcast.32), channel_id=1, source_target_pairs={{0,0},{2,256},{4,64},{6,320},{8,128},{10,384},{12,192},{14,448},{6... | collective-permute-start | bytes 221192 | tf_op jit(solution)/shard_map/ppermute | solution.py:116
  59.1 11.9 %copy-start = (f32[128]{0:T(128)S(1)}, f32[128]{0:T(128)}, u32[]{:S(2)}) copy-start(f32[128]{0:T(128)} %param.14) | copy-start | bytes 1540
  59.1 11.9 %all-to-all-start.1 = ((bf16[4,128,768]{2,1,0:T(8,128)(2,1)}), bf16[4,128,768]{2,1,0:T(8,128)(2,1)S(1)}, u32[]{:S(2)}, u32[]{:S(2)}) async-start(bf16[4,128,768]{2,1,0:T(8,128)(2,1)} %bitcast.6), calls=%async_computation.1 | async-start | bytes 1572864 | tf_op jit(solution)/shard_map/all_to_all | solution.py:133
  62.8 17.6 %copy-start.2 = (s32[3,2,6]{2,1,0:T(2,128)S(1)}, s32[3,2,6]{2,1,0:T(2,128)}, u32[]{:S(2)}) copy-start(s32[3,2,6]{2,1,0:T(2,128)} %param.15) | copy-start | bytes 436
  62.8 21.4 %copy-start.1 = (f32[128]{0:T(128)S(1)}, f32[128]{0:T(128)}, u32[]{:S(2)}) copy-start(f32[128]{0:T(128)} %param.13) | copy-start | bytes 1540
  71.2 9.5 %collective-permute-start.1 = (bf16[128,768]{1,0:T(8,128)(2,1)S(1)}, bf16[128,768]{1,0:T(8,128)(2,1)S(1)}, u32[]{:S(2)}, u32[]{:S(2)}) collective-permute-start(bf16[128,768]{1,0:T(8,128)(2,1)S(1)} %shard_map.82.source_ref.own_ref), channel_id=1, source_target_pairs={{16,32},{32,16},{48,64},{64,48},{80,96},{96,80},{112,128},{128,112... | collective-permute-start | bytes 589832 | tf_op jit(solution)/shard_map/ppermute | solution.py:143
  71.9 12.3 %all-to-all-start.2 = ((bf16[4,128,384]{2,1,0:T(8,128)(2,1)}), bf16[4,128,384]{2,1,0:T(8,128)(2,1)S(1)}, u32[]{:S(2)}, u32[]{:S(2)}) async-start(bf16[4,128,384]{2,1,0:T(8,128)(2,1)} %bitcast.5), calls=%async_computation.2 | async-start | bytes 786432 | tf_op jit(solution)/shard_map/all_to_all | solution.py:137
  77.0 7.2 %collective-permute-start.2 = (bf16[128,768]{1,0:T(8,128)(2,1)S(1)}, bf16[128,768]{1,0:T(8,128)(2,1)S(1)}, u32[]{:S(2)}, u32[]{:S(2)}) collective-permute-start(bf16[128,768]{1,0:T(8,128)(2,1)S(1)} %shard_map.83), channel_id=1, source_target_pairs={{0,16},{16,0},{32,48},{48,32},{64,80},{80,64},{96,112},{112,96},{1... | collective-permute-start | bytes 589832 | tf_op jit(solution)/shard_map/ppermute | solution.py:144
Sparse Core Ops, SparseCore 0:
  9.4 46.6 all-gather.4
  58.2 45.2 all-gather.6

commit v14 on v12

--- a/solution.py
+++ b/solution.py
@@ -8,7 +8,6 @@
 
 HDIM = 128
 TILE = 64
-HEAD = ("y", "core")
 SLAB = ("z", "x")
 MIB = 1024 * 1024
 
@@ -104,18 +103,19 @@
 
 def on_device(tokens, q_weight, k_weight, v_weight, out_weight, q_gain, k_gain, key_tiles):
     rows, width = tokens.shape
-    n_x, n_z, n_head = (lax.axis_size(a) for a in ("x", "z", HEAD))
+    n_x, n_z, n_head = (lax.axis_size(a) for a in ("x", "z", "head"))
     part = width // n_x
 
     stacked = jnp.concatenate([q_weight, k_weight, v_weight], axis=1)
     weights = lax.all_gather(stacked, "z", axis=0, tiled=True)
 
-    turned = [(z * n_head + h, h * n_z + z) for z in range(n_z) for h in range(n_head)]
-    columns = lax.ppermute(out_weight.T, ("z",) + HEAD, turned)
+    ring = [*range(0, n_head, 2), *range(n_head - 1, 0, -2)]
+    turned = [(z * n_head + h, ring.index(h) * n_z + z) for z in range(n_z) for h in range(n_head)]
+    columns = lax.ppermute(out_weight.T, ("z", "head"), turned)
 
     pieces = tokens.reshape(rows, n_x, part).transpose(1, 0, 2)
     pieces = lax.all_to_all(pieces, "x", split_axis=0, concat_axis=0, tiled=True)
-    pieces = lax.all_gather(pieces.reshape(n_x * rows, part), HEAD, axis=0, tiled=False)
+    pieces = lax.all_gather(pieces.reshape(n_x * rows, part), "head", axis=0, tiled=False)
     pieces, columns = lax.optimization_barrier((pieces, columns))
     group = pieces.transpose(1, 0, 2).reshape(n_x * rows, n_head * part)
 
@@ -142,7 +142,7 @@
     even = lax.ppermute(copied(packed), SLAB, swaps[1])
     live = live_rows(key_tiles, rows // TILE)
     attended = attention(query, q_gain, live, odd, packed, even)
-    everyone = lax.all_gather(attended, HEAD, axis=0, tiled=False)
+    everyone = lax.all_gather(attended, "head", axis=0, tiled=False, axis_index_groups=[ring])
     total = jnp.einsum("hrd,hnd->rn", everyone, projection, preferred_element_type=jnp.float32)
     return total.astype(jnp.bfloat16)
 
@@ -150,18 +150,18 @@
 def solution(mesh):
     n_slab, n_head, n_cfg = (mesh.shape[a] for a in ("slab", "head", "cfg"))
     fine = Mesh(
-        mesh.devices.reshape(n_slab // 4, 4, n_head // 2, 2, n_cfg), ("z", "x", "y", "core", "cfg")
+        mesh.devices.reshape(n_slab // 4, 4, n_head, n_cfg), ("z", "x", "head", "cfg")
     )
     placed = (
-        P(("cfg",) + SLAB, HEAD),
-        P(SLAB, HEAD),
-        P(SLAB, HEAD),
-        P(SLAB, HEAD),
-        P(HEAD, SLAB),
+        P(("cfg",) + SLAB, "head"),
+        P(SLAB, "head"),
+        P(SLAB, "head"),
+        P(SLAB, "head"),
+        P("head", SLAB),
         P(),
         P(),
-        P(HEAD, SLAB, None),
+        P("head", SLAB, None),
     )
     return jax.shard_map(
-        on_device, mesh=fine, in_specs=placed, out_specs=P(("cfg",) + SLAB, HEAD), check_vma=False
+        on_device, mesh=fine, in_specs=placed, out_specs=P(("cfg",) + SLAB, "head"), check_vma=False
     )

time: 120 us -> 124 us (1.033)
  starting transfers between devices: 23.2 us -> 29.7 us
  blocking collectives: 59 us -> 56.3 us
    ppermute x1, starting transfers between devices: 4.83 us -> 11.5 us  [on_device(): columns = lax.ppermute(out_weight.T, ('z', 'head'), turned)]
    all_gather x2, blocking collectives: 47.2 us -> 44.6 us  [the longest x1 28.7 us: on_device(): lax.all_gather(attended, 'head', axis=0, tiled=False, axis_index_groups=[...]
where the time goes in v14:
time: 124 us; the launch traced here: 123 us
  blocking collectives  56.3 us (45%)
  starting transfers between devices  29.7 us (24%)
  between operations  13.5 us (11%)
  waiting for transfers between devices  10.4 us (8%)
  matrix products  8.55 us (7%)
  local copies, waits for them, and re-layouts  1.99 us (2%)
  other arithmetic  1.91 us (2%)
    all_gather x1, blocking collectives, on_device(): lax.all_gather(attended, 'head', axis=0, tiled=False, axis_index_groups=[...  28.7 us
    all_gather x1, blocking collectives, on_device(): lax.all_gather(pieces.reshape(n_x * rows, part), 'head', axis=0, tiled=Fa...  15.9 us
    all_gather x1, blocking collectives, on_device(): columns = lax.all_gather(columns, 'x', axis=0, tiled=True)  11.6 us
    ppermute x1, starting transfers between devices, on_device(): columns = lax.ppermute(out_weight.T, ('z', 'head'), turned)  11.5 us
    all_to_all x1, waiting for transfers between devices, on_device(): lax.all_to_all(key_value, 'x', split_axis=0, concat_axis=0, tiled=True)  5.8 us
    dot_general x2, matrix products, shares(): jnp.dot(group, piece, preferred_element_type=jnp.float32)  5.43 us
    all_to_all x1, starting transfers between devices, on_device(): query = lax.all_to_all(query, 'x', split_axis=0, concat_axis=0, tiled=True)  5.37 us
    all_to_all x1, starting transfers between devices, on_device(): lax.all_to_all(pieces, 'x', split_axis=0, concat_axis=0, tiled=True)  4.84 us
  transfers between devices with their start and end apart: 8, of which 3 were waited for; matrix products, arithmetic and copies ran while one was open for 6% of the time, Pallas kernels for 1%

profile of v14, /device:TPU:1, one launch (start us, length us, event | category | flops | bytes accessed | tf_op | source)
XLA Modules:
  0.0 123.2 jit_solution(14568357626726468961)
XLA Ops:
  6.5 1.7 %pad_maximum_fusion = bf16[96,1152]{1,0:T(8,128)(2,1)} fusion(bf16[96,384]{1,0:T(8,128)(2,1)} %param.11, bf16[96,384]{1,0:T(8,128)(2,1)} %param.10, bf16[96,384]{1,0:T(8,128)(2,1)} %param.9), kind=kLoop, calls=%fused_computation.6 | loop fusion | flops 663552 | bytes 442368 | tf_op jit(solution)/shard_map/concatenate | solution.py:109
  8.2 1.6 %copy.13 = bf16[128,384]{0,1:T(8,128)(2,1)} copy(bf16[128,384]{1,0:T(8,128)(2,1)} %param.8) | data formatting | bytes 196608 | tf_op args[0]
  9.9 4.8 %all-to-all-start = ((bf16[4,128,96]{1,2,0:T(8,128)(2,1)}), bf16[4,128,96]{1,2,0:T(8,128)(2,1)S(1)}, u32[]{:S(2)}, u32[]{:S(2)}) async-start(bf16[4,128,96]{1,2,0:T(8,128)(2,1)} %bitcast.1), calls=%async_computation | async-start | bytes 196608 | tf_op jit(solution)/shard_map/all_to_all | solution.py:117
  14.7 11.5 %collective-permute-start = (bf16[96,384]{1,0:T(8,128)(2,1)}, bf16[96,384]{1,0:T(8,128)(2,1)S(1)}, u32[]{:S(2)}, u32[]{:S(2)}) collective-permute-start(bf16[96,384]{1,0:T(8,128)(2,1)} %bitcast.32), channel_id=1, source_target_pairs={{0,0},{2,448},{4,64},{6,384},{8,128},{10,320},{12,192},{14,256},{6... | collective-permute-start | bytes 221192 | tf_op jit(solution)/shard_map/ppermute | solution.py:114
  26.3 15.9 %all_gather.22 = bf16[8,512,96]{1,2,0:T(8,128)(2,1)S(1)} all-gather(bf16[1,512,96]{1,2,0:T(8,128)(2,1)S(1)} %all_gather_reshape.3), channel_id=1, replica_groups=mesh['z'=8,'x'=4,'head'=8,'cfg'=2] {'head'}, dimensions={0}, use_global_device_ids=true | all-gather | bytes 884736 | tf_op jit(solution)/shard_map/all_gather | solution.py:118
  42.3 11.6 %all_gather.23 = bf16[384,384]{1,0:T(8,128)(2,1)} all-gather(bf16[96,384]{1,0:T(8,128)(2,1)S(1)} %collective-permute-done), channel_id=1, replica_groups=mesh['z'=8,'x'=4,'head'=8,'cfg'=2] {'x'}, dimensions={0}, use_global_device_ids=true | all-gather | bytes 368640 | tf_op jit(solution)/shard_map/all_gather | solution.py:122
  53.9 1.1 all-gather.5.cloned.1.call-done
  55.1 3.0 %convolution_convert_fusion = bf16[512,768]{1,0:T(8,128)(2,1)} fusion(bf16[512,768]{0,1:T(8,128)(2,1)S(1)} %bitcast.30, bf16[768,1152]{1,0:T(8,128)(2,1)} %all-gather.5.cloned.1.call-done), kind=kOutput, calls=%fused_computation | convolution fusion | flops 604372992 | bytes 2752512 | tf_op jit(solution)/shard_map/dot_general | solution.py:127
  58.0 3.9 %all-to-all-start.1 = ((bf16[4,128,768]{2,1,0:T(8,128)(2,1)}), bf16[4,128,768]{2,1,0:T(8,128)(2,1)S(1)}, u32[]{:S(2)}, u32[]{:S(2)}) async-start(bf16[4,128,768]{2,1,0:T(8,128)(2,1)} %bitcast.6), calls=%async_computation.1 | async-start | bytes 1572864 | tf_op jit(solution)/shard_map/all_to_all | solution.py:131
  62.0 0.1 add_multiply_fusion
  62.1 2.5 %convolution_convert_fusion.1 = bf16[512,384]{1,0:T(8,128)(2,1)} fusion(bf16[512,768]{0,1:T(8,128)(2,1)S(1)} %bitcast.31, bf16[768,1152]{1,0:T(8,128)(2,1)} %all-gather.5.cloned.1.call-done), kind=kOutput, calls=%fused_computation.1 | convolution fusion | flops 302186496 | bytes 1769472 | tf_op jit(solution)/shard_map/dot_general | solution.py:127
  64.5 5.8 %all-to-all-done.1.share_ref = bf16[4,128,768]{2,1,0:T(8,128)(2,1)S(1)} async-done(((bf16[4,128,768]{2,1,0:T(8,128)(2,1)}), bf16[4,128,768]{2,1,0:T(8,128)(2,1)S(1)}, u32[]{:S(2)}, u32[]{:S(2)}) %all-to-all-start.1) | async-done | bytes 786464 | tf_op jit(solution)/shard_map/all_to_all | solution.py:131
  70.3 0.2 shard_map.82.source_ref.own_ref
  70.5 0.7 collective-permute-start.1
  71.2 5.4 %all-to-all-start.2 = ((bf16[4,128,384]{2,1,0:T(8,128)(2,1)}), bf16[4,128,384]{2,1,0:T(8,128)(2,1)S(1)}, u32[]{:S(2)}, u32[]{:S(2)}) async-start(bf16[4,128,384]{2,1,0:T(8,128)(2,1)} %bitcast.5), calls=%async_computation.2 | async-start | bytes 786432 | tf_op jit(solution)/shard_map/all_to_all | solution.py:135
  76.6 3.4 %collective-permute-start.2 = (bf16[128,768]{1,0:T(8,128)(2,1)S(1)}, bf16[128,768]{1,0:T(8,128)(2,1)S(1)}, u32[]{:S(2)}, u32[]{:S(2)}) collective-permute-start(bf16[128,768]{1,0:T(8,128)(2,1)S(1)} %shard_map.83), channel_id=1, source_target_pairs={{0,16},{16,0},{32,48},{48,32},{64,80},{80,64},{96,112},{112,96},{1... | collective-permute-start | bytes 589832 | tf_op jit(solution)/shard_map/ppermute | solution.py:142
  80.0 0.1 add.37
  80.1 0.1 compare_reduce_fusion
  80.2 0.1 broadcast_in_dim.2
  80.3 0.1 reshape.71.live_ref
  80.4 3.4 %collective-permute-done.2.even_ref = bf16[128,768]{1,0:T(8,128)(2,1)S(1)} collective-permute-done((bf16[128,768]{1,0:T(8,128)(2,1)S(1)}, bf16[128,768]{1,0:T(8,128)(2,1)S(1)}, u32[]{:S(2)}, u32[]{:S(2)}) %collective-permute-start.2) | collective-permute-done | bytes 196640 | tf_op jit(solution)/shard_map/ppermute | solution.py:142
  83.8 0.7 shard_map.84
  84.6 28.7 %all-gather = bf16[1024,384]{1,0:T(8,128)(2,1)S(1)} all-gather(bf16[128,384]{1,0:T(8,128)(2,1)S(1)} %shard_map.84), channel_id=2, replica_groups={{0,4,8,12,14,10,6,2},{1,5,9,13,15,11,7,3},{16,20,24,28,30,26,22,18},{17..., dimensions={0}, use_global_device_ids=true | all-gather | bytes 884736 | tf_op jit(solution)/shard_map/all_gather | solution.py:145
  113.3 3.1 %fusion.1 = bf16[128,384]{1,0:T(8,128)(2,1)} fusion(bf16[8,128,384]{2,1,0:T(8,128)(2,1)S(1)} %bitcast.28, bf16[8,384,384]{2,1,0:T(8,128)(2,1)} %bitcast.29), kind=kOutput, calls=%fused_computation.4 | convolution fusion | flops 302039040 | bytes 3244032 | tf_op jit(solution)/shard_map/hrd,hnd->rn/dot_general | solution.py:146
  (21 shorter events, 0.3 us)
Async XLA Ops:
  6.5 48.5 %all-gather.5.cloned.1.call-start = ((), (), s32[]{:S(2)}) async-start(), calls=%async_computation.3 | async-start | bytes 1990656 | tf_op jit(solution)/shard_map/all_gather | solution.py:110
  9.9 16.4 %all-to-all-start = ((bf16[4,128,96]{1,2,0:T(8,128)(2,1)}), bf16[4,128,96]{1,2,0:T(8,128)(2,1)S(1)}, u32[]{:S(2)}, u32[]{:S(2)}) async-start(bf16[4,128,96]{1,2,0:T(8,128)(2,1)} %bitcast.1), calls=%async_computation | async-start | bytes 196608 | tf_op jit(solution)/shard_map/all_to_all | solution.py:117
  14.7 98.6 %all-gather.7.cloned.1.call-start = ((), (), s32[]{:S(2)}) async-start(), calls=%async_computation.4 | async-start | bytes 2654208 | tf_op jit(solution)/shard_map/all_gather | solution.py:123
  14.7 27.6 %collective-permute-start = (bf16[96,384]{1,0:T(8,128)(2,1)}, bf16[96,384]{1,0:T(8,128)(2,1)S(1)}, u32[]{:S(2)}, u32[]{:S(2)}) collective-permute-start(bf16[96,384]{1,0:T(8,128)(2,1)} %bitcast.32), channel_id=1, source_target_pairs={{0,0},{2,448},{4,64},{6,384},{8,128},{10,320},{12,192},{14,256},{6... | collective-permute-start | bytes 221192 | tf_op jit(solution)/shard_map/ppermute | solution.py:114
  58.0 12.3 %copy-start = (f32[128]{0:T(128)S(1)}, f32[128]{0:T(128)}, u32[]{:S(2)}) copy-start(f32[128]{0:T(128)} %param.14) | copy-start | bytes 1540
  58.0 12.3 %all-to-all-start.1 = ((bf16[4,128,768]{2,1,0:T(8,128)(2,1)}), bf16[4,128,768]{2,1,0:T(8,128)(2,1)S(1)}, u32[]{:S(2)}, u32[]{:S(2)}) async-start(bf16[4,128,768]{2,1,0:T(8,128)(2,1)} %bitcast.6), calls=%async_computation.1 | async-start | bytes 1572864 | tf_op jit(solution)/shard_map/all_to_all | solution.py:131
  62.1 18.0 %copy-start.2 = (s32[3,2,6]{2,1,0:T(2,128)S(1)}, s32[3,2,6]{2,1,0:T(2,128)}, u32[]{:S(2)}) copy-start(s32[3,2,6]{2,1,0:T(2,128)} %param.15) | copy-start | bytes 436
  62.1 21.8 %copy-start.1 = (f32[128]{0:T(128)S(1)}, f32[128]{0:T(128)}, u32[]{:S(2)}) copy-start(f32[128]{0:T(128)} %param.13) | copy-start | bytes 1540
  70.5 9.9 %collective-permute-start.1 = (bf16[128,768]{1,0:T(8,128)(2,1)S(1)}, bf16[128,768]{1,0:T(8,128)(2,1)S(1)}, u32[]{:S(2)}, u32[]{:S(2)}) collective-permute-start(bf16[128,768]{1,0:T(8,128)(2,1)S(1)} %shard_map.82.source_ref.own_ref), channel_id=1, source_target_pairs={{16,32},{32,16},{48,64},{64,48},{80,96},{96,80},{112,128},{128,112... | collective-permute-start | bytes 589832 | tf_op jit(solution)/shard_map/ppermute | solution.py:141
  71.2 12.6 %all-to-all-start.2 = ((bf16[4,128,384]{2,1,0:T(8,128)(2,1)}), bf16[4,128,384]{2,1,0:T(8,128)(2,1)S(1)}, u32[]{:S(2)}, u32[]{:S(2)}) async-start(bf16[4,128,384]{2,1,0:T(8,128)(2,1)} %bitcast.5), calls=%async_computation.2 | async-start | bytes 786432 | tf_op jit(solution)/shard_map/all_to_all | solution.py:135
  76.6 7.2 %collective-permute-start.2 = (bf16[128,768]{1,0:T(8,128)(2,1)S(1)}, bf16[128,768]{1,0:T(8,128)(2,1)S(1)}, u32[]{:S(2)}, u32[]{:S(2)}) collective-permute-start(bf16[128,768]{1,0:T(8,128)(2,1)S(1)} %shard_map.83), channel_id=1, source_target_pairs={{0,16},{16,0},{32,48},{48,32},{64,80},{80,64},{96,112},{112,96},{1... | collective-permute-start | bytes 589832 | tf_op jit(solution)/shard_map/ppermute | solution.py:142
Sparse Core Ops, SparseCore 0:
  9.4 45.5 all-gather.4
  57.2 45.9 all-gather.6

commit v15 on v13

--- a/solution.py
+++ b/solution.py
@@ -59,7 +59,7 @@
 
 
 def attention_kernel(share_ref, gain_ref, live_ref, odd_ref, own_ref, even_ref, out_ref):
-    rows, width = out_ref.shape
+    rows, width = out_ref.shape[1:]
     near = (odd_ref, own_ref, even_ref)
     scale = 1.0 / HDIM**0.5
     for low in range(0, width, HDIM):
@@ -79,14 +79,16 @@
         weight = jnp.where(allowed > 0, jnp.exp(score * scale), 0.0)
         total = jnp.sum(weight, axis=1, keepdims=True)
         mixed = jnp.dot(weight.astype(jnp.bfloat16), values, preferred_element_type=jnp.float32)
-        out_ref[:, low : low + HDIM] = (mixed / total).astype(jnp.bfloat16)
+        mixed = (mixed / total).astype(jnp.bfloat16)
+        for copy in range(out_ref.shape[0]):
+            out_ref[copy, :, low : low + HDIM] = mixed
 
 
-def attention(query, gain, live, odd, own, even):
+def attention(copies, query, gain, live, odd, own, even):
     rows, width = query.shape[1:]
     return pl.pallas_call(
         attention_kernel,
-        out_shape=jax.ShapeDtypeStruct((rows, width), jnp.bfloat16),
+        out_shape=jax.ShapeDtypeStruct((copies, rows, width), jnp.bfloat16),
         compiler_params=params(16),
     )(query, gain.reshape(1, HDIM), live, odd, own, even)
 
@@ -143,8 +145,9 @@
     odd = lax.ppermute(packed, SLAB, swaps[0])
     even = lax.ppermute(copied(packed), SLAB, swaps[1])
     live = live_rows(key_tiles, rows // TILE)
-    attended = attention(query, q_gain, live, odd, packed, even)
-    everyone = lax.all_gather(attended, ("core", "y"), axis=0, tiled=False)
+    attended = attention(n_head // n_core, query, q_gain, live, odd, packed, even)
+    everyone = lax.all_to_all(attended, "y", split_axis=0, concat_axis=0, tiled=True)
+    everyone = lax.all_gather(everyone, "core", axis=0, tiled=True)
     total = jnp.einsum("hrd,hnd->rn", everyone, projection, preferred_element_type=jnp.float32)
     return total.astype(jnp.bfloat16)
 

time: 131 us -> 118 us (0.901)
  blocking collectives: 62.9 us -> 50.4 us
    all_gather x1, blocking collectives: 35.2 us -> 10.7 us  [on_device(): everyone = lax.all_gather(everyone, 'core', axis=0, tiled=True)]
    all_to_all x0 -> x1, blocking collectives: none -> 11.9 us  [on_device(): lax.all_to_all(attended, 'y', split_axis=0, concat_axis=0, tiled=True)]
  transfers between devices with their start and end apart: 8 -> 8, of which waited for: 3 -> 3; matrix products, arithmetic and copies ran while one was open for 6% -> 7% of each run, Pallas kernels for 1% -> 1%
where the time goes in v15:
time: 118 us
  blocking collectives  50.4 us (43%)
  starting transfers between devices  29 us (25%)
  between operations  13.5 us (11%)
  waiting for transfers between devices  11.3 us (10%)
  matrix products  8.54 us (7%)
  local copies, waits for them, and re-layouts  1.99 us (2%)
  other arithmetic  1.91 us (2%)
    all_gather x1, blocking collectives, on_device(): lax.all_gather(pieces.reshape(n_x * rows, part), HEAD, axis=0, tiled=False)  16 us
    all_to_all x1, blocking collectives, on_device(): lax.all_to_all(attended, 'y', split_axis=0, concat_axis=0, tiled=True)  11.9 us
    all_gather x1, blocking collectives, on_device(): columns = lax.all_gather(columns, 'x', axis=0, tiled=True)  11.8 us
    ppermute x1, starting transfers between devices, on_device(): columns = lax.ppermute(out_weight.T, ('z',) + HEAD, turned)  11.5 us
    all_gather x1, blocking collectives, on_device(): everyone = lax.all_gather(everyone, 'core', axis=0, tiled=True)  10.7 us
    all_to_all x1, waiting for transfers between devices, on_device(): lax.all_to_all(key_value, 'x', split_axis=0, concat_axis=0, tiled=True)  5.75 us
    dot_general x2, matrix products, shares(): jnp.dot(group, piece, preferred_element_type=jnp.float32)  5.42 us
    all_to_all x1, starting transfers between devices, on_device(): query = lax.all_to_all(query, 'x', split_axis=0, concat_axis=0, tiled=True)  5.02 us
  transfers between devices with their start and end apart: 8, of which 3 were waited for; matrix products, arithmetic and copies ran while one was open for 7% of the time, Pallas kernels for 1%

profile of v15, /device:TPU:1, one launch (start us, length us, event | category | flops | bytes accessed | tf_op | source)
XLA Modules:
  0.0 117.5 jit_solution(7700151427906595449)
XLA Ops:
  6.5 1.7 %pad_maximum_fusion = bf16[96,1152]{1,0:T(8,128)(2,1)} fusion(bf16[96,384]{1,0:T(8,128)(2,1)} %param.11, bf16[96,384]{1,0:T(8,128)(2,1)} %param.10, bf16[96,384]{1,0:T(8,128)(2,1)} %param.9), kind=kLoop, calls=%fused_computation.6 | loop fusion | flops 663552 | bytes 442368 | tf_op jit(solution)/shard_map/concatenate | solution.py:112
  8.2 1.6 %copy.13 = bf16[128,384]{0,1:T(8,128)(2,1)} copy(bf16[128,384]{1,0:T(8,128)(2,1)} %param.8) | data formatting | bytes 196608 | tf_op args[0]
  9.9 4.8 %all-to-all-start = ((bf16[4,128,96]{1,2,0:T(8,128)(2,1)}), bf16[4,128,96]{1,2,0:T(8,128)(2,1)S(1)}, u32[]{:S(2)}, u32[]{:S(2)}) async-start(bf16[4,128,96]{1,2,0:T(8,128)(2,1)} %bitcast.1), calls=%async_computation | async-start | bytes 196608 | tf_op jit(solution)/shard_map/all_to_all | solution.py:121
  14.7 11.5 %collective-permute-start = (bf16[96,384]{1,0:T(8,128)(2,1)}, bf16[96,384]{1,0:T(8,128)(2,1)S(1)}, u32[]{:S(2)}, u32[]{:S(2)}) collective-permute-start(bf16[96,384]{1,0:T(8,128)(2,1)} %bitcast.30), channel_id=1, source_target_pairs={{0,0},{2,256},{4,64},{6,320},{8,128},{10,384},{12,192},{14,448},{6... | collective-permute-start | bytes 221192 | tf_op jit(solution)/shard_map/ppermute | solution.py:118
  26.3 16.0 %all_gather.19 = bf16[8,512,96]{1,2,0:T(8,128)(2,1)S(1)} all-gather(bf16[1,512,96]{1,2,0:T(8,128)(2,1)S(1)} %all_gather_reshape.3), channel_id=1, replica_groups=mesh['z'=8,'x'=4,'y'=4,'core'=2,'cfg'=2] {'y','core'}, dimensions={0}, use_global_device_ids=true | all-gather | bytes 884736 | tf_op jit(solution)/shard_map/all_gather | solution.py:122
  42.3 11.8 %all_gather.20 = bf16[384,384]{1,0:T(8,128)(2,1)} all-gather(bf16[96,384]{1,0:T(8,128)(2,1)S(1)} %collective-permute-done), channel_id=1, replica_groups=mesh['z'=8,'x'=4,'y'=4,'core'=2,'cfg'=2] {'x'}, dimensions={0}, use_global_device_ids=true | all-gather | bytes 368640 | tf_op jit(solution)/shard_map/all_gather | solution.py:126
  54.1 2.0 %all-gather.4.cloned.1.call-done = bf16[768,1152]{1,0:T(8,128)(2,1)} async-done(((bf16[96,1152]{1,0:T(8,128)(2,1)}), bf16[768,1152]{1,0:T(8,128)(2,1)}) %all-gather.4.cloned.1.call-update) | async-done | bytes 1769488 | tf_op jit(solution)/shard_map/all_gather | solution.py:113
  56.1 3.0 %convolution_convert_fusion = bf16[512,768]{1,0:T(8,128)(2,1)} fusion(bf16[512,768]{0,1:T(8,128)(2,1)S(1)} %bitcast.28, bf16[768,1152]{1,0:T(8,128)(2,1)} %all-gather.4.cloned.1.call-done), kind=kOutput, calls=%fused_computation | convolution fusion | flops 604372992 | bytes 2752512 | tf_op jit(solution)/shard_map/dot_general | solution.py:131
  59.1 3.6 %all-to-all-start.1 = ((bf16[4,128,768]{2,1,0:T(8,128)(2,1)}), bf16[4,128,768]{2,1,0:T(8,128)(2,1)S(1)}, u32[]{:S(2)}, u32[]{:S(2)}) async-start(bf16[4,128,768]{2,1,0:T(8,128)(2,1)} %bitcast.6), calls=%async_computation.1 | async-start | bytes 1572864 | tf_op jit(solution)/shard_map/all_to_all | solution.py:135
  62.8 0.1 add_multiply_fusion
  62.8 2.5 %convolution_convert_fusion.1 = bf16[512,384]{1,0:T(8,128)(2,1)} fusion(bf16[512,768]{0,1:T(8,128)(2,1)S(1)} %bitcast.29, bf16[768,1152]{1,0:T(8,128)(2,1)} %all-gather.4.cloned.1.call-done), kind=kOutput, calls=%fused_computation.1 | convolution fusion | flops 302186496 | bytes 1769472 | tf_op jit(solution)/shard_map/dot_general | solution.py:131
  65.3 5.7 %all-to-all-done.1.share_ref = bf16[4,128,768]{2,1,0:T(8,128)(2,1)S(1)} async-done(((bf16[4,128,768]{2,1,0:T(8,128)(2,1)}), bf16[4,128,768]{2,1,0:T(8,128)(2,1)S(1)}, u32[]{:S(2)}, u32[]{:S(2)}) %all-to-all-start.1) | async-done | bytes 786464 | tf_op jit(solution)/shard_map/all_to_all | solution.py:135
  71.0 0.2 shard_map.82.source_ref.own_ref
  71.2 0.7 collective-permute-start.1
  71.9 5.0 %all-to-all-start.2 = ((bf16[4,128,384]{2,1,0:T(8,128)(2,1)}), bf16[4,128,384]{2,1,0:T(8,128)(2,1)S(1)}, u32[]{:S(2)}, u32[]{:S(2)}) async-start(bf16[4,128,384]{2,1,0:T(8,128)(2,1)} %bitcast.5), calls=%async_computation.2 | async-start | bytes 786432 | tf_op jit(solution)/shard_map/all_to_all | solution.py:139
  77.0 3.4 %collective-permute-start.2 = (bf16[128,768]{1,0:T(8,128)(2,1)S(1)}, bf16[128,768]{1,0:T(8,128)(2,1)S(1)}, u32[]{:S(2)}, u32[]{:S(2)}) collective-permute-start(bf16[128,768]{1,0:T(8,128)(2,1)S(1)} %shard_map.83), channel_id=1, source_target_pairs={{0,16},{16,0},{32,48},{48,32},{64,80},{80,64},{96,112},{112,96},{1... | collective-permute-start | bytes 589832 | tf_op jit(solution)/shard_map/ppermute | solution.py:146
  80.4 0.1 add.37
  80.5 0.1 compare_reduce_fusion
  80.7 0.1 reshape.71.live_ref
  80.8 3.4 %collective-permute-done.2.even_ref = bf16[128,768]{1,0:T(8,128)(2,1)S(1)} collective-permute-done((bf16[128,768]{1,0:T(8,128)(2,1)S(1)}, bf16[128,768]{1,0:T(8,128)(2,1)S(1)}, u32[]{:S(2)}, u32[]{:S(2)}) %collective-permute-start.2) | collective-permute-done | bytes 196640 | tf_op jit(solution)/shard_map/ppermute | solution.py:146
  84.2 0.7 shard_map.84
  84.9 11.9 %all_to_all.20 = bf16[4,128,384]{2,1,0:T(8,128)(2,1)S(1)} all-to-all(bf16[4,128,384]{2,1,0:T(8,128)(2,1)S(1)} %shard_map.84), channel_id=1, replica_groups=mesh['z'=8,'x'=4,'y'=4,'core'=2,'cfg'=2] {'y'}, dimensions={0} | all-to-all | bytes 786432 | tf_op jit(solution)/shard_map/all_to_all | solution.py:149
  96.8 10.7 %all_gather.21 = bf16[8,128,384]{2,1,0:T(8,128)(2,1)S(1)} all-gather(bf16[4,128,384]{2,1,0:T(8,128)(2,1)S(1)} %all_to_all.20), channel_id=1, replica_groups=mesh['z'=8,'x'=4,'y'=4,'core'=2,'cfg'=2] {'core'}, dimensions={0}, use_global_device_ids=true | all-gather | bytes 1179648 | tf_op jit(solution)/shard_map/all_gather | solution.py:150
  107.5 3.1 %fusion.1 = bf16[128,384]{1,0:T(8,128)(2,1)} fusion(bf16[8,128,384]{2,1,0:T(8,128)(2,1)S(1)} %all_gather.21, bf16[8,384,384]{2,1,0:T(8,128)(2,1)} %bitcast.27), kind=kOutput, calls=%fused_computation.4 | convolution fusion | flops 302039040 | bytes 3244032 | tf_op jit(solution)/shard_map/hrd,hnd->rn/dot_general | solution.py:151
  (22 shorter events, 0.3 us)
Async XLA Ops:
  6.5 49.6 %all-gather.4.cloned.1.call-start = ((), (), s32[]{:S(2)}) async-start(), calls=%async_computation.4 | async-start | bytes 1990656 | tf_op jit(solution)/shard_map/all_gather | solution.py:113
  9.9 16.3 %all-to-all-start = ((bf16[4,128,96]{1,2,0:T(8,128)(2,1)}), bf16[4,128,96]{1,2,0:T(8,128)(2,1)S(1)}, u32[]{:S(2)}, u32[]{:S(2)}) async-start(bf16[4,128,96]{1,2,0:T(8,128)(2,1)} %bitcast.1), calls=%async_computation | async-start | bytes 196608 | tf_op jit(solution)/shard_map/all_to_all | solution.py:121
  14.7 92.8 %all-gather.6.cloned.1.call-start = ((), (), s32[]{:S(2)}) async-start(), calls=%async_computation.5 | async-start | bytes 2654208 | tf_op jit(solution)/shard_map/all_gather | solution.py:127
  14.7 27.6 %collective-permute-start = (bf16[96,384]{1,0:T(8,128)(2,1)}, bf16[96,384]{1,0:T(8,128)(2,1)S(1)}, u32[]{:S(2)}, u32[]{:S(2)}) collective-permute-start(bf16[96,384]{1,0:T(8,128)(2,1)} %bitcast.30), channel_id=1, source_target_pairs={{0,0},{2,256},{4,64},{6,320},{8,128},{10,384},{12,192},{14,448},{6... | collective-permute-start | bytes 221192 | tf_op jit(solution)/shard_map/ppermute | solution.py:118
  59.1 11.9 %copy-start = (f32[128]{0:T(128)S(1)}, f32[128]{0:T(128)}, u32[]{:S(2)}) copy-start(f32[128]{0:T(128)} %param.14) | copy-start | bytes 1540
  59.1 11.9 %all-to-all-start.1 = ((bf16[4,128,768]{2,1,0:T(8,128)(2,1)}), bf16[4,128,768]{2,1,0:T(8,128)(2,1)S(1)}, u32[]{:S(2)}, u32[]{:S(2)}) async-start(bf16[4,128,768]{2,1,0:T(8,128)(2,1)} %bitcast.6), calls=%async_computation.1 | async-start | bytes 1572864 | tf_op jit(solution)/shard_map/all_to_all | solution.py:135
  62.8 17.6 %copy-start.2 = (s32[3,2,6]{2,1,0:T(2,128)S(1)}, s32[3,2,6]{2,1,0:T(2,128)}, u32[]{:S(2)}) copy-start(s32[3,2,6]{2,1,0:T(2,128)} %param.15) | copy-start | bytes 436
  62.8 21.4 %copy-start.1 = (f32[128]{0:T(128)S(1)}, f32[128]{0:T(128)}, u32[]{:S(2)}) copy-start(f32[128]{0:T(128)} %param.13) | copy-start | bytes 1540
  71.2 9.5 %collective-permute-start.1 = (bf16[128,768]{1,0:T(8,128)(2,1)S(1)}, bf16[128,768]{1,0:T(8,128)(2,1)S(1)}, u32[]{:S(2)}, u32[]{:S(2)}) collective-permute-start(bf16[128,768]{1,0:T(8,128)(2,1)S(1)} %shard_map.82.source_ref.own_ref), channel_id=1, source_target_pairs={{16,32},{32,16},{48,64},{64,48},{80,96},{96,80},{112,128},{128,112... | collective-permute-start | bytes 589832 | tf_op jit(solution)/shard_map/ppermute | solution.py:145
  71.9 12.3 %all-to-all-start.2 = ((bf16[4,128,384]{2,1,0:T(8,128)(2,1)}), bf16[4,128,384]{2,1,0:T(8,128)(2,1)S(1)}, u32[]{:S(2)}, u32[]{:S(2)}) async-start(bf16[4,128,384]{2,1,0:T(8,128)(2,1)} %bitcast.5), calls=%async_computation.2 | async-start | bytes 786432 | tf_op jit(solution)/shard_map/all_to_all | solution.py:139
  77.0 7.2 %collective-permute-start.2 = (bf16[128,768]{1,0:T(8,128)(2,1)S(1)}, bf16[128,768]{1,0:T(8,128)(2,1)S(1)}, u32[]{:S(2)}, u32[]{:S(2)}) collective-permute-start(bf16[128,768]{1,0:T(8,128)(2,1)S(1)} %shard_map.83), channel_id=1, source_target_pairs={{0,16},{16,0},{32,48},{48,32},{64,80},{80,64},{96,112},{112,96},{1... | collective-permute-start | bytes 589832 | tf_op jit(solution)/shard_map/ppermute | solution.py:146
Sparse Core Ops, SparseCore 0:
  9.4 46.6 all-gather.3
  58.2 45.2 all-gather.5

commit v16 on v15

--- a/solution.py
+++ b/solution.py
@@ -147,6 +147,7 @@
     live = live_rows(key_tiles, rows // TILE)
     attended = attention(n_head // n_core, query, q_gain, live, odd, packed, even)
     everyone = lax.all_to_all(attended, "y", split_axis=0, concat_axis=0, tiled=True)
+    everyone, projection = lax.optimization_barrier((everyone, projection))
     everyone = lax.all_gather(everyone, "core", axis=0, tiled=True)
     total = jnp.einsum("hrd,hnd->rn", everyone, projection, preferred_element_type=jnp.float32)
     return total.astype(jnp.bfloat16)

time: 118 us -> 119 us (level)
  blocking collectives: 50.4 us -> 32.7 us
  waiting for transfers between devices: 11.3 us -> 25.2 us
  starting transfers between devices: 29 us -> 33 us
    all_gather x1, waiting for transfers between devices: 0.01 us -> 13.9 us  [on_device(): projection = lax.all_gather(columns, 'z', axis=0, tiled=False)]
    all_to_all x1 -> x0, blocking collectives: 11.9 us -> none  [on_device(): lax.all_to_all(attended, 'y', split_axis=0, concat_axis=0, tiled=True)]
    all_gather x1, blocking collectives: 10.7 us -> 4.93 us  [on_device(): everyone = lax.all_gather(everyone, 'core', axis=0, tiled=True)]
    all_to_all x0 -> x1, starting transfers between devices: none -> 3.98 us  [on_device(): lax.all_to_all(attended, 'y', split_axis=0, concat_axis=0, tiled=True)]
  transfers between devices with their start and end apart: 8 -> 9, of which waited for: 3 -> 4; matrix products, arithmetic and copies ran while one was open for 7% -> 6% of each run, Pallas kernels for 1% -> 1%
where the time goes in v16:
time: 119 us; the launch traced here: 118 us
  starting transfers between devices  33 us (28%)
  blocking collectives  32.7 us (27%)
  waiting for transfers between devices  25.2 us (21%)
  between operations  13.5 us (11%)
  matrix products  8.53 us (7%)
  local copies, waits for them, and re-layouts  1.99 us (2%)
  other arithmetic  1.92 us (2%)
  Pallas kernels  1.69 us (1%)
    all_gather x1, blocking collectives, on_device(): lax.all_gather(pieces.reshape(n_x * rows, part), HEAD, axis=0, tiled=False)  16 us
    all_gather x1, waiting for transfers between devices, on_device(): projection = lax.all_gather(columns, 'z', axis=0, tiled=False)  13.9 us
    all_gather x1, blocking collectives, on_device(): columns = lax.all_gather(columns, 'x', axis=0, tiled=True)  11.8 us
    ppermute x1, starting transfers between devices, on_device(): columns = lax.ppermute(out_weight.T, ('z',) + HEAD, turned)  11.5 us
    all_to_all x1, waiting for transfers between devices, on_device(): lax.all_to_all(key_value, 'x', split_axis=0, concat_axis=0, tiled=True)  5.76 us
    dot_general x2, matrix products, shares(): jnp.dot(group, piece, preferred_element_type=jnp.float32)  5.41 us
    all_to_all x1, starting transfers between devices, on_device(): query = lax.all_to_all(query, 'x', split_axis=0, concat_axis=0, tiled=True)  5.01 us
    all_gather x1, blocking collectives, on_device(): everyone = lax.all_gather(everyone, 'core', axis=0, tiled=True)  4.93 us
  transfers between devices with their start and end apart: 9, of which 4 were waited for; matrix products, arithmetic and copies ran while one was open for 6% of the time, Pallas kernels for 1%

profile of v16, /device:TPU:1, one launch (start us, length us, event | category | flops | bytes accessed | tf_op | source)
XLA Modules:
  0.0 118.5 jit_solution(3793826790105020307)
XLA Ops:
  6.5 1.7 %pad_maximum_fusion = bf16[96,1152]{1,0:T(8,128)(2,1)} fusion(bf16[96,384]{1,0:T(8,128)(2,1)} %param.11, bf16[96,384]{1,0:T(8,128)(2,1)} %param.10, bf16[96,384]{1,0:T(8,128)(2,1)} %param.9), kind=kLoop, calls=%fused_computation.6 | loop fusion | flops 663552 | bytes 442368 | tf_op jit(solution)/shard_map/concatenate | solution.py:112
  8.2 1.6 %copy.13 = bf16[128,384]{0,1:T(8,128)(2,1)} copy(bf16[128,384]{1,0:T(8,128)(2,1)} %param.8) | data formatting | bytes 196608 | tf_op args[0]
  9.9 4.8 %all-to-all-start = ((bf16[4,128,96]{1,2,0:T(8,128)(2,1)}), bf16[4,128,96]{1,2,0:T(8,128)(2,1)S(1)}, u32[]{:S(2)}, u32[]{:S(2)}) async-start(bf16[4,128,96]{1,2,0:T(8,128)(2,1)} %bitcast.1), calls=%async_computation | async-start | bytes 196608 | tf_op jit(solution)/shard_map/all_to_all | solution.py:121
  14.7 11.5 %collective-permute-start = (bf16[96,384]{1,0:T(8,128)(2,1)}, bf16[96,384]{1,0:T(8,128)(2,1)S(1)}, u32[]{:S(2)}, u32[]{:S(2)}) collective-permute-start(bf16[96,384]{1,0:T(8,128)(2,1)} %bitcast.30), channel_id=1, source_target_pairs={{0,0},{2,256},{4,64},{6,320},{8,128},{10,384},{12,192},{14,448},{6... | collective-permute-start | bytes 221192 | tf_op jit(solution)/shard_map/ppermute | solution.py:118
  26.3 16.0 %all_gather.19 = bf16[8,512,96]{1,2,0:T(8,128)(2,1)S(1)} all-gather(bf16[1,512,96]{1,2,0:T(8,128)(2,1)S(1)} %all_gather_reshape.3), channel_id=1, replica_groups=mesh['z'=8,'x'=4,'y'=4,'core'=2,'cfg'=2] {'y','core'}, dimensions={0}, use_global_device_ids=true | all-gather | bytes 884736 | tf_op jit(solution)/shard_map/all_gather | solution.py:122
  42.3 11.8 %all_gather.20 = bf16[384,384]{1,0:T(8,128)(2,1)} all-gather(bf16[96,384]{1,0:T(8,128)(2,1)S(1)} %collective-permute-done), channel_id=1, replica_groups=mesh['z'=8,'x'=4,'y'=4,'core'=2,'cfg'=2] {'x'}, dimensions={0}, use_global_device_ids=true | all-gather | bytes 368640 | tf_op jit(solution)/shard_map/all_gather | solution.py:126
  54.1 2.0 %all-gather.4.cloned.1.call-done = bf16[768,1152]{1,0:T(8,128)(2,1)} async-done(((bf16[96,1152]{1,0:T(8,128)(2,1)}), bf16[768,1152]{1,0:T(8,128)(2,1)}) %all-gather.4.cloned.1.call-update) | async-done | bytes 1769488 | tf_op jit(solution)/shard_map/all_gather | solution.py:113
  56.2 3.0 %convolution_convert_fusion = bf16[512,768]{1,0:T(8,128)(2,1)} fusion(bf16[512,768]{0,1:T(8,128)(2,1)S(1)} %bitcast.28, bf16[768,1152]{1,0:T(8,128)(2,1)} %all-gather.4.cloned.1.call-done), kind=kOutput, calls=%fused_computation | convolution fusion | flops 604372992 | bytes 2752512 | tf_op jit(solution)/shard_map/dot_general | solution.py:131
  59.1 3.6 %all-to-all-start.1 = ((bf16[4,128,768]{2,1,0:T(8,128)(2,1)}), bf16[4,128,768]{2,1,0:T(8,128)(2,1)S(1)}, u32[]{:S(2)}, u32[]{:S(2)}) async-start(bf16[4,128,768]{2,1,0:T(8,128)(2,1)} %bitcast.6), calls=%async_computation.1 | async-start | bytes 1572864 | tf_op jit(solution)/shard_map/all_to_all | solution.py:135
  62.8 0.1 add_multiply_fusion
  62.9 2.4 %convolution_convert_fusion.1 = bf16[512,384]{1,0:T(8,128)(2,1)} fusion(bf16[512,768]{0,1:T(8,128)(2,1)S(1)} %bitcast.29, bf16[768,1152]{1,0:T(8,128)(2,1)} %all-gather.4.cloned.1.call-done), kind=kOutput, calls=%fused_computation.1 | convolution fusion | flops 302186496 | bytes 1769472 | tf_op jit(solution)/shard_map/dot_general | solution.py:131
  65.3 5.8 %all-to-all-done.1.share_ref = bf16[4,128,768]{2,1,0:T(8,128)(2,1)S(1)} async-done(((bf16[4,128,768]{2,1,0:T(8,128)(2,1)}), bf16[4,128,768]{2,1,0:T(8,128)(2,1)S(1)}, u32[]{:S(2)}, u32[]{:S(2)}) %all-to-all-start.1) | async-done | bytes 786464 | tf_op jit(solution)/shard_map/all_to_all | solution.py:135
  71.1 0.2 shard_map.82.source_ref.own_ref
  71.3 0.7 collective-permute-start.1
  72.0 5.0 %all-to-all-start.2 = ((bf16[4,128,384]{2,1,0:T(8,128)(2,1)}), bf16[4,128,384]{2,1,0:T(8,128)(2,1)S(1)}, u32[]{:S(2)}, u32[]{:S(2)}) async-start(bf16[4,128,384]{2,1,0:T(8,128)(2,1)} %bitcast.5), calls=%async_computation.2 | async-start | bytes 786432 | tf_op jit(solution)/shard_map/all_to_all | solution.py:139
  77.0 3.4 %collective-permute-start.2 = (bf16[128,768]{1,0:T(8,128)(2,1)S(1)}, bf16[128,768]{1,0:T(8,128)(2,1)S(1)}, u32[]{:S(2)}, u32[]{:S(2)}) collective-permute-start(bf16[128,768]{1,0:T(8,128)(2,1)S(1)} %shard_map.83), channel_id=1, source_target_pairs={{0,16},{16,0},{32,48},{48,32},{64,80},{80,64},{96,112},{112,96},{1... | collective-permute-start | bytes 589832 | tf_op jit(solution)/shard_map/ppermute | solution.py:146
  80.4 0.1 add.37
  80.5 0.1 compare_reduce_fusion
  80.8 3.4 %collective-permute-done.2.even_ref = bf16[128,768]{1,0:T(8,128)(2,1)S(1)} collective-permute-done((bf16[128,768]{1,0:T(8,128)(2,1)S(1)}, bf16[128,768]{1,0:T(8,128)(2,1)S(1)}, u32[]{:S(2)}, u32[]{:S(2)}) %collective-permute-start.2) | collective-permute-done | bytes 196640 | tf_op jit(solution)/shard_map/ppermute | solution.py:146
  84.2 1.5 %shard_map.84 = bf16[4,128,384]{2,1,0:T(8,128)(2,1)} custom-call(bf16[4,128,384]{2,1,0:T(8,128)(2,1)S(1)} %all-to-all-done.2.share_ref, f32[1,128]{1,0:T(1,128)S(1)} %bitcast.26, f32[6,384]{1,0:T(8,128)S(1)} %reshape.71.live_ref, bf16[128,768]{1,0:T(8,128)(2,1)S(1)} %collective-permute-done.1.odd_ref, bf16[128,768]{1,0:T(8,128)(2,1)S(1)} %shard_map.82.source_ref.own_ref, ...), custom_call_target="tpu_custom_call" | custom-call | tf_op jit(solution)/shard_map/pallas_call | solution.py:89
  85.7 4.0 %all-to-all-start.3 = ((bf16[4,128,384]{2,1,0:T(8,128)(2,1)}), bf16[4,128,384]{2,1,0:T(8,128)(2,1)S(1)}, u32[]{:S(2)}, u32[]{:S(2)}) async-start(bf16[4,128,384]{2,1,0:T(8,128)(2,1)} %shard_map.84), calls=%async_computation.3 | async-start | bytes 786432 | tf_op jit(solution)/shard_map/all_to_all | solution.py:149
  89.7 13.9 %all-gather.6.cloned.1.call-done = bf16[3072,384]{1,0:T(8,128)(2,1)} async-done(((bf16[384,384]{1,0:T(8,128)(2,1)}), bf16[3072,384]{1,0:T(8,128)(2,1)}) %all-gather.6.cloned.1.call-update) | async-done | bytes 2359312 | tf_op jit(solution)/shard_map/all_gather | solution.py:127
  103.6 4.9 %all_gather.23 = bf16[8,128,384]{2,1,0:T(8,128)(2,1)S(1)} all-gather(bf16[4,128,384]{2,1,0:T(8,128)(2,1)S(1)} %all-to-all-done.3), channel_id=1, replica_groups=mesh['z'=8,'x'=4,'y'=4,'core'=2,'cfg'=2] {'core'}, dimensions={0}, use_global_device_ids=true | all-gather | bytes 1179648 | tf_op jit(solution)/shard_map/all_gather | solution.py:151
  108.5 3.1 %fusion.1 = bf16[128,384]{1,0:T(8,128)(2,1)} fusion(bf16[8,128,384]{2,1,0:T(8,128)(2,1)S(1)} %all_gather.23, bf16[8,384,384]{2,1,0:T(8,128)(2,1)} %bitcast.27), kind=kOutput, calls=%fused_computation.4 | convolution fusion | flops 302039040 | bytes 3244032 | tf_op jit(solution)/shard_map/hrd,hnd->rn/dot_general | solution.py:152
  (23 shorter events, 0.4 us)
Async XLA Ops:
  6.5 49.6 %all-gather.4.cloned.1.call-start = ((), (), s32[]{:S(2)}) async-start(), calls=%async_computation.4 | async-start | bytes 1990656 | tf_op jit(solution)/shard_map/all_gather | solution.py:113
  9.9 16.3 %all-to-all-start = ((bf16[4,128,96]{1,2,0:T(8,128)(2,1)}), bf16[4,128,96]{1,2,0:T(8,128)(2,1)S(1)}, u32[]{:S(2)}, u32[]{:S(2)}) async-start(bf16[4,128,96]{1,2,0:T(8,128)(2,1)} %bitcast.1), calls=%async_computation | async-start | bytes 196608 | tf_op jit(solution)/shard_map/all_to_all | solution.py:121
  14.7 88.9 %all-gather.6.cloned.1.call-start = ((), (), s32[]{:S(2)}) async-start(), calls=%async_computation.5 | async-start | bytes 2654208 | tf_op jit(solution)/shard_map/all_gather | solution.py:127
  14.7 27.6 %collective-permute-start = (bf16[96,384]{1,0:T(8,128)(2,1)}, bf16[96,384]{1,0:T(8,128)(2,1)S(1)}, u32[]{:S(2)}, u32[]{:S(2)}) collective-permute-start(bf16[96,384]{1,0:T(8,128)(2,1)} %bitcast.30), channel_id=1, source_target_pairs={{0,0},{2,256},{4,64},{6,320},{8,128},{10,384},{12,192},{14,448},{6... | collective-permute-start | bytes 221192 | tf_op jit(solution)/shard_map/ppermute | solution.py:118
  59.1 11.9 %copy-start = (f32[128]{0:T(128)S(1)}, f32[128]{0:T(128)}, u32[]{:S(2)}) copy-start(f32[128]{0:T(128)} %param.14) | copy-start | bytes 1540
  59.1 11.9 %all-to-all-start.1 = ((bf16[4,128,768]{2,1,0:T(8,128)(2,1)}), bf16[4,128,768]{2,1,0:T(8,128)(2,1)S(1)}, u32[]{:S(2)}, u32[]{:S(2)}) async-start(bf16[4,128,768]{2,1,0:T(8,128)(2,1)} %bitcast.6), calls=%async_computation.1 | async-start | bytes 1572864 | tf_op jit(solution)/shard_map/all_to_all | solution.py:135
  62.9 17.6 %copy-start.2 = (s32[3,2,6]{2,1,0:T(2,128)S(1)}, s32[3,2,6]{2,1,0:T(2,128)}, u32[]{:S(2)}) copy-start(s32[3,2,6]{2,1,0:T(2,128)} %param.15) | copy-start | bytes 436
  62.9 21.3 %copy-start.1 = (f32[128]{0:T(128)S(1)}, f32[128]{0:T(128)}, u32[]{:S(2)}) copy-start(f32[128]{0:T(128)} %param.13) | copy-start | bytes 1540
  71.3 9.5 %collective-permute-start.1 = (bf16[128,768]{1,0:T(8,128)(2,1)S(1)}, bf16[128,768]{1,0:T(8,128)(2,1)S(1)}, u32[]{:S(2)}, u32[]{:S(2)}) collective-permute-start(bf16[128,768]{1,0:T(8,128)(2,1)S(1)} %shard_map.82.source_ref.own_ref), channel_id=1, source_target_pairs={{16,32},{32,16},{48,64},{64,48},{80,96},{96,80},{112,128},{128,112... | collective-permute-start | bytes 589832 | tf_op jit(solution)/shard_map/ppermute | solution.py:145
  72.0 12.2 %all-to-all-start.2 = ((bf16[4,128,384]{2,1,0:T(8,128)(2,1)}), bf16[4,128,384]{2,1,0:T(8,128)(2,1)S(1)}, u32[]{:S(2)}, u32[]{:S(2)}) async-start(bf16[4,128,384]{2,1,0:T(8,128)(2,1)} %bitcast.5), calls=%async_computation.2 | async-start | bytes 786432 | tf_op jit(solution)/shard_map/all_to_all | solution.py:139
  77.0 7.2 %collective-permute-start.2 = (bf16[128,768]{1,0:T(8,128)(2,1)S(1)}, bf16[128,768]{1,0:T(8,128)(2,1)S(1)}, u32[]{:S(2)}, u32[]{:S(2)}) collective-permute-start(bf16[128,768]{1,0:T(8,128)(2,1)S(1)} %shard_map.83), channel_id=1, source_target_pairs={{0,16},{16,0},{32,48},{48,32},{64,80},{80,64},{96,112},{112,96},{1... | collective-permute-start | bytes 589832 | tf_op jit(solution)/shard_map/ppermute | solution.py:146
  85.7 17.9 %all-to-all-start.3 = ((bf16[4,128,384]{2,1,0:T(8,128)(2,1)}), bf16[4,128,384]{2,1,0:T(8,128)(2,1)S(1)}, u32[]{:S(2)}, u32[]{:S(2)}) async-start(bf16[4,128,384]{2,1,0:T(8,128)(2,1)} %shard_map.84), calls=%async_computation.3 | async-start | bytes 786432 | tf_op jit(solution)/shard_map/all_to_all | solution.py:149
Sparse Core Ops, SparseCore 0:
  9.4 46.6 all-gather.3
  58.2 45.2 all-gather.5

commit v17 on v15

--- a/solution.py
+++ b/solution.py
@@ -113,8 +113,14 @@
     weights = lax.all_gather(stacked, "z", axis=0, tiled=True)
 
     n_core = lax.axis_size("core")
-    rank = [h % n_core * (n_head // n_core) + h // n_core for h in range(n_head)]
-    turned = [(z * n_head + h, rank[h] * n_z + z) for z in range(n_z) for h in range(n_head)]
+    n_y = n_head // n_core
+
+    def place_of(head, column):
+        return (head % n_core + column) % n_core * n_y + head // n_core
+
+    turned = [
+        (z * n_head + h, place_of(h, z) * n_z + z) for z in range(n_z) for h in range(n_head)
+    ]
     columns = lax.ppermute(out_weight.T, ("z",) + HEAD, turned)
 
     pieces = tokens.reshape(rows, n_x, part).transpose(1, 0, 2)
@@ -145,10 +151,14 @@
     odd = lax.ppermute(packed, SLAB, swaps[0])
     even = lax.ppermute(copied(packed), SLAB, swaps[1])
     live = live_rows(key_tiles, rows // TILE)
-    attended = attention(n_head // n_core, query, q_gain, live, odd, packed, even)
-    everyone = lax.all_to_all(attended, "y", split_axis=0, concat_axis=0, tiled=True)
-    everyone = lax.all_gather(everyone, "core", axis=0, tiled=True)
-    total = jnp.einsum("hrd,hnd->rn", everyone, projection, preferred_element_type=jnp.float32)
+    attended = attention(n_y, query, q_gain, live, odd, packed, even)
+    mine = lax.all_to_all(attended, "y", split_axis=0, concat_axis=0, tiled=True)
+    other = lax.ppermute(mine, "core", [(i, (i + 1) % n_core) for i in range(n_core)])
+
+    def projected(part, rows_of):
+        return jnp.einsum("hrd,hnd->rn", part, rows_of, preferred_element_type=jnp.float32)
+
+    total = projected(mine, projection[:n_y]) + projected(other, projection[n_y:])
     return total.astype(jnp.bfloat16)
 
 

time: 118 us -> 121 us (1.025)
  blocking collectives: 50.4 us -> 39.2 us
  starting transfers between devices: 29 us -> 39.7 us
  waiting for transfers between devices: 11.3 us -> 14.3 us
  local copies, waits for them, and re-layouts: 1.99 us -> 3.85 us
  matrix products: 8.54 us -> 7.07 us
    ppermute x0 -> x1, starting transfers between devices: none -> 11.3 us  [on_device(): lax.ppermute(mine, 'core', [(i, (i + 1) % n_core) for i in range(n_core)])]
    all_gather x1 -> x0, blocking collectives: 10.7 us -> none  [on_device(): everyone = lax.all_gather(everyone, 'core', axis=0, tiled=True)]
    all_to_all x1, waiting for transfers between devices: 0.01 us -> 5.81 us  [on_device(): query = lax.all_to_all(query, 'x', split_axis=0, concat_axis=0, tiled=True)]
    ppermute x1, waiting for transfers between devices: 3.44 us -> 0.01 us  [on_device(): even = lax.ppermute(copied(packed), SLAB, swaps[1])]
    slice x0 -> x1, local copies, waits for them, and re-layouts: none -> 1.86 us  [on_device(): projection[:n_y]]
    all_to_all x1, starting transfers between devices: 5.02 us -> 3.47 us  [on_device(): query = lax.all_to_all(query, 'x', split_axis=0, concat_axis=0, tiled=True)]
    dot_general x1 -> x2, matrix products: 3.12 us -> 1.67 us  [projected(): jnp.einsum('hrd,hnd->rn', part, rows_of, preferred_element_type=jnp.float32)]
  transfers between devices with their start and end apart: 8 -> 9, of which waited for: 3 -> 3; matrix products, arithmetic and copies ran while one was open for 7% -> 8% of each run, Pallas kernels for 1% -> 1%
where the time goes in v17:
time: 121 us
  starting transfers between devices  39.7 us (33%)
  blocking collectives  39.2 us (32%)
  waiting for transfers between devices  14.3 us (12%)
  between operations  13.5 us (11%)
  matrix products  7.07 us (6%)
  local copies, waits for them, and re-layouts  3.85 us (3%)
  other arithmetic  1.92 us (2%)
    all_gather x1, blocking collectives, on_device(): lax.all_gather(pieces.reshape(n_x * rows, part), HEAD, axis=0, tiled=False)  15.8 us
    all_gather x1, blocking collectives, on_device(): columns = lax.all_gather(columns, 'x', axis=0, tiled=True)  12.1 us
    ppermute x1, starting transfers between devices, on_device(): columns = lax.ppermute(out_weight.T, ('z',) + HEAD, turned)  11.5 us
    all_to_all x1, blocking collectives, on_device(): lax.all_to_all(attended, 'y', split_axis=0, concat_axis=0, tiled=True)  11.3 us
    ppermute x1, starting transfers between devices, on_device(): lax.ppermute(mine, 'core', [(i, (i + 1) % n_core) for i in range(n_core)])  11.3 us
    all_to_all x1, waiting for transfers between devices, on_device(): lax.all_to_all(key_value, 'x', split_axis=0, concat_axis=0, tiled=True)  6.42 us
    all_to_all x1, waiting for transfers between devices, on_device(): query = lax.all_to_all(query, 'x', split_axis=0, concat_axis=0, tiled=True)  5.81 us
    dot_general x2, matrix products, shares(): jnp.dot(group, piece, preferred_element_type=jnp.float32)  5.4 us
  transfers between devices with their start and end apart: 9, of which 3 were waited for; matrix products, arithmetic and copies ran while one was open for 8% of the time, Pallas kernels for 1%

profile of v17, /device:TPU:1, one launch (start us, length us, event | category | flops | bytes accessed | tf_op | source)
XLA Modules:
  0.0 120.5 jit_solution(611047520908757607)
XLA Ops:
  6.5 1.7 %pad_maximum_fusion = bf16[96,1152]{1,0:T(8,128)(2,1)} fusion(bf16[96,384]{1,0:T(8,128)(2,1)} %param.11, bf16[96,384]{1,0:T(8,128)(2,1)} %param.10, bf16[96,384]{1,0:T(8,128)(2,1)} %param.9), kind=kLoop, calls=%fused_computation.8 | loop fusion | flops 663552 | bytes 442368 | tf_op jit(solution)/shard_map/concatenate | solution.py:112
  8.2 1.6 %copy.13 = bf16[128,384]{0,1:T(8,128)(2,1)} copy(bf16[128,384]{1,0:T(8,128)(2,1)} %param.8) | data formatting | bytes 196608 | tf_op args[0]
  9.9 4.8 %all-to-all-start = ((bf16[4,128,96]{1,2,0:T(8,128)(2,1)}), bf16[4,128,96]{1,2,0:T(8,128)(2,1)S(1)}, u32[]{:S(2)}, u32[]{:S(2)}) async-start(bf16[4,128,96]{1,2,0:T(8,128)(2,1)} %bitcast.1), calls=%async_computation | async-start | bytes 196608 | tf_op jit(solution)/shard_map/all_to_all | solution.py:127
  14.7 11.5 %collective-permute-start = (bf16[96,384]{1,0:T(8,128)(2,1)}, bf16[96,384]{1,0:T(8,128)(2,1)S(1)}, u32[]{:S(2)}, u32[]{:S(2)}) collective-permute-start(bf16[96,384]{1,0:T(8,128)(2,1)} %bitcast.38), channel_id=1, source_target_pairs={{0,0},{2,256},{4,64},{6,320},{8,128},{10,384},{12,192},{14,448},{6... | collective-permute-start | bytes 221192 | tf_op jit(solution)/shard_map/ppermute | solution.py:124
  26.3 15.8 %all_gather.16 = bf16[8,512,96]{1,2,0:T(8,128)(2,1)S(1)} all-gather(bf16[1,512,96]{1,2,0:T(8,128)(2,1)S(1)} %all_gather_reshape.3), channel_id=1, replica_groups=mesh['z'=8,'x'=4,'y'=4,'core'=2,'cfg'=2] {'y','core'}, dimensions={0}, use_global_device_ids=true | all-gather | bytes 884736 | tf_op jit(solution)/shard_map/all_gather | solution.py:128
  42.1 12.1 %all_gather.17 = bf16[384,384]{1,0:T(8,128)(2,1)} all-gather(bf16[96,384]{1,0:T(8,128)(2,1)S(1)} %collective-permute-done), channel_id=1, replica_groups=mesh['z'=8,'x'=4,'y'=4,'core'=2,'cfg'=2] {'x'}, dimensions={0}, use_global_device_ids=true | all-gather | bytes 368640 | tf_op jit(solution)/shard_map/all_gather | solution.py:132
  54.2 2.0 %all-gather.4.cloned.1.call-done = bf16[768,1152]{1,0:T(8,128)(2,1)} async-done(((bf16[96,1152]{1,0:T(8,128)(2,1)}), bf16[768,1152]{1,0:T(8,128)(2,1)}) %all-gather.4.cloned.1.call-update) | async-done | bytes 1769488 | tf_op jit(solution)/shard_map/all_gather | solution.py:113
  56.2 3.0 %convolution_convert_fusion = bf16[512,768]{1,0:T(8,128)(2,1)} fusion(bf16[512,768]{0,1:T(8,128)(2,1)S(1)} %bitcast.36, bf16[768,1152]{1,0:T(8,128)(2,1)} %all-gather.4.cloned.1.call-done), kind=kOutput, calls=%fused_computation | convolution fusion | flops 604372992 | bytes 2752512 | tf_op jit(solution)/shard_map/dot_general | solution.py:137
  59.2 4.5 %all-to-all-start.1 = ((bf16[4,128,768]{2,1,0:T(8,128)(2,1)}), bf16[4,128,768]{2,1,0:T(8,128)(2,1)S(1)}, u32[]{:S(2)}, u32[]{:S(2)}) async-start(bf16[4,128,768]{2,1,0:T(8,128)(2,1)} %bitcast.6), calls=%async_computation.1 | async-start | bytes 1572864 | tf_op jit(solution)/shard_map/all_to_all | solution.py:141
  63.8 2.4 %convolution_convert_fusion.1 = bf16[512,384]{1,0:T(8,128)(2,1)} fusion(bf16[512,768]{0,1:T(8,128)(2,1)S(1)} %bitcast.37, bf16[768,1152]{1,0:T(8,128)(2,1)} %all-gather.4.cloned.1.call-done), kind=kOutput, calls=%fused_computation.1 | convolution fusion | flops 302186496 | bytes 1769472 | tf_op jit(solution)/shard_map/dot_general | solution.py:137
  66.3 6.4 %all-to-all-done.1.share_ref = bf16[4,128,768]{2,1,0:T(8,128)(2,1)S(1)} async-done(((bf16[4,128,768]{2,1,0:T(8,128)(2,1)}), bf16[4,128,768]{2,1,0:T(8,128)(2,1)S(1)}, u32[]{:S(2)}, u32[]{:S(2)}) %all-to-all-start.1) | async-done | bytes 786464 | tf_op jit(solution)/shard_map/all_to_all | solution.py:141
  72.7 0.2 shard_map.82.source_ref.own_ref
  72.9 0.7 collective-permute-start.1
  73.6 3.4 %collective-permute-start.2 = (bf16[128,768]{1,0:T(8,128)(2,1)S(1)}, bf16[128,768]{1,0:T(8,128)(2,1)S(1)}, u32[]{:S(2)}, u32[]{:S(2)}) collective-permute-start(bf16[128,768]{1,0:T(8,128)(2,1)S(1)} %shard_map.83), channel_id=1, source_target_pairs={{0,16},{16,0},{32,48},{48,32},{64,80},{80,64},{96,112},{112,96},{1... | collective-permute-start | bytes 589832 | tf_op jit(solution)/shard_map/ppermute | solution.py:152
  77.0 3.5 %all-to-all-start.2 = ((bf16[4,128,384]{2,1,0:T(8,128)(2,1)}), bf16[4,128,384]{2,1,0:T(8,128)(2,1)S(1)}, u32[]{:S(2)}, u32[]{:S(2)}) async-start(bf16[4,128,384]{2,1,0:T(8,128)(2,1)} %bitcast.5), calls=%async_computation.2 | async-start | bytes 786432 | tf_op jit(solution)/shard_map/all_to_all | solution.py:145
  80.6 0.1 add.40
  80.7 0.1 compare_reduce_fusion
  80.9 5.8 %all-to-all-done.2.share_ref = bf16[4,128,384]{2,1,0:T(8,128)(2,1)S(1)} async-done(((bf16[4,128,384]{2,1,0:T(8,128)(2,1)}), bf16[4,128,384]{2,1,0:T(8,128)(2,1)S(1)}, u32[]{:S(2)}, u32[]{:S(2)}) %all-to-all-start.2) | async-done | bytes 393248 | tf_op jit(solution)/shard_map/all_to_all | solution.py:145
  86.7 0.7 shard_map.84
  87.5 11.3 %all_to_all.20 = bf16[4,128,384]{2,1,0:T(8,128)(2,1)S(1)} all-to-all(bf16[4,128,384]{2,1,0:T(8,128)(2,1)S(1)} %shard_map.84), channel_id=1, replica_groups=mesh['z'=8,'x'=4,'y'=4,'core'=2,'cfg'=2] {'y'}, dimensions={0} | all-to-all | bytes 786432 | tf_op jit(solution)/shard_map/all_to_all | solution.py:155
  98.8 11.3 %collective-permute-start.3 = (bf16[4,128,384]{2,1,0:T(8,128)(2,1)S(1)}, bf16[4,128,384]{2,1,0:T(8,128)(2,1)S(1)}, u32[]{:S(2)}, u32[]{:S(2)}) collective-permute-start(bf16[4,128,384]{2,1,0:T(8,128)(2,1)S(1)} %all_to_all.20), channel_id=1, source_target_pairs={{0,2},{2,0},{1,3},{3,1},{4,6},{6,4},{5,7},{7,5},{8,10},{10,8},{9,1... | collective-permute-start | bytes 1179656 | tf_op jit(solution)/shard_map/ppermute | solution.py:156
  110.1 1.9 %fusion.4 = (bf16[1536,384]{1,0:T(8,128)(2,1)S(1)}, bf16[1536,384]{1,0:T(8,128)(2,1)S(1)}) fusion(bf16[3072,384]{1,0:T(8,128)(2,1)} %all-gather.6.cloned.1.call-done), kind=kLoop, calls=%fused_computation.12 | loop fusion | bytes 4718592 | tf_op jit(solution)/shard_map/slice | solution.py:161
  112.0 0.5 convolution_bitcast_fusion
  112.5 1.2 fusion.2
  (25 shorter events, 0.5 us)
Async XLA Ops:
  6.5 49.7 %all-gather.4.cloned.1.call-start = ((), (), s32[]{:S(2)}) async-start(), calls=%async_computation.4 | async-start | bytes 1990656 | tf_op jit(solution)/shard_map/all_gather | solution.py:113
  9.9 16.3 %all-to-all-start = ((bf16[4,128,96]{1,2,0:T(8,128)(2,1)}), bf16[4,128,96]{1,2,0:T(8,128)(2,1)S(1)}, u32[]{:S(2)}, u32[]{:S(2)}) async-start(bf16[4,128,96]{1,2,0:T(8,128)(2,1)} %bitcast.1), calls=%async_computation | async-start | bytes 196608 | tf_op jit(solution)/shard_map/all_to_all | solution.py:127
  14.7 95.4 %all-gather.6.cloned.1.call-start = ((), (), s32[]{:S(2)}) async-start(), calls=%async_computation.5 | async-start | bytes 2654208 | tf_op jit(solution)/shard_map/all_gather | solution.py:133
  14.7 27.4 %collective-permute-start = (bf16[96,384]{1,0:T(8,128)(2,1)}, bf16[96,384]{1,0:T(8,128)(2,1)S(1)}, u32[]{:S(2)}, u32[]{:S(2)}) collective-permute-start(bf16[96,384]{1,0:T(8,128)(2,1)} %bitcast.38), channel_id=1, source_target_pairs={{0,0},{2,256},{4,64},{6,320},{8,128},{10,384},{12,192},{14,448},{6... | collective-permute-start | bytes 221192 | tf_op jit(solution)/shard_map/ppermute | solution.py:124
  59.2 13.5 %all-to-all-start.1 = ((bf16[4,128,768]{2,1,0:T(8,128)(2,1)}), bf16[4,128,768]{2,1,0:T(8,128)(2,1)S(1)}, u32[]{:S(2)}, u32[]{:S(2)}) async-start(bf16[4,128,768]{2,1,0:T(8,128)(2,1)} %bitcast.6), calls=%async_computation.1 | async-start | bytes 1572864 | tf_op jit(solution)/shard_map/all_to_all | solution.py:141
  63.8 8.9 %copy-start = (f32[128]{0:T(128)S(1)}, f32[128]{0:T(128)}, u32[]{:S(2)}) copy-start(f32[128]{0:T(128)} %param.14) | copy-start | bytes 1540
  66.3 14.4 %copy-start.2 = (s32[3,2,6]{2,1,0:T(2,128)S(1)}, s32[3,2,6]{2,1,0:T(2,128)}, u32[]{:S(2)}) copy-start(s32[3,2,6]{2,1,0:T(2,128)} %param.15) | copy-start | bytes 436
  66.3 20.5 %copy-start.1 = (f32[128]{0:T(128)S(1)}, f32[128]{0:T(128)}, u32[]{:S(2)}) copy-start(f32[128]{0:T(128)} %param.13) | copy-start | bytes 1540
  72.9 8.0 %collective-permute-start.1 = (bf16[128,768]{1,0:T(8,128)(2,1)S(1)}, bf16[128,768]{1,0:T(8,128)(2,1)S(1)}, u32[]{:S(2)}, u32[]{:S(2)}) collective-permute-start(bf16[128,768]{1,0:T(8,128)(2,1)S(1)} %shard_map.82.source_ref.own_ref), channel_id=1, source_target_pairs={{16,32},{32,16},{48,64},{64,48},{80,96},{96,80},{112,128},{128,112... | collective-permute-start | bytes 589832 | tf_op jit(solution)/shard_map/ppermute | solution.py:151
  73.6 7.4 %collective-permute-start.2 = (bf16[128,768]{1,0:T(8,128)(2,1)S(1)}, bf16[128,768]{1,0:T(8,128)(2,1)S(1)}, u32[]{:S(2)}, u32[]{:S(2)}) collective-permute-start(bf16[128,768]{1,0:T(8,128)(2,1)S(1)} %shard_map.83), channel_id=1, source_target_pairs={{0,16},{16,0},{32,48},{48,32},{64,80},{80,64},{96,112},{112,96},{1... | collective-permute-start | bytes 589832 | tf_op jit(solution)/shard_map/ppermute | solution.py:152
  77.0 9.7 %all-to-all-start.2 = ((bf16[4,128,384]{2,1,0:T(8,128)(2,1)}), bf16[4,128,384]{2,1,0:T(8,128)(2,1)S(1)}, u32[]{:S(2)}, u32[]{:S(2)}) async-start(bf16[4,128,384]{2,1,0:T(8,128)(2,1)} %bitcast.5), calls=%async_computation.2 | async-start | bytes 786432 | tf_op jit(solution)/shard_map/all_to_all | solution.py:145
  98.8 13.2 %collective-permute-start.3 = (bf16[4,128,384]{2,1,0:T(8,128)(2,1)S(1)}, bf16[4,128,384]{2,1,0:T(8,128)(2,1)S(1)}, u32[]{:S(2)}, u32[]{:S(2)}) collective-permute-start(bf16[4,128,384]{2,1,0:T(8,128)(2,1)S(1)} %all_to_all.20), channel_id=1, source_target_pairs={{0,2},{2,0},{1,3},{3,1},{4,6},{6,4},{5,7},{7,5},{8,10},{10,8},{9,1... | collective-permute-start | bytes 1179656 | tf_op jit(solution)/shard_map/ppermute | solution.py:156
Sparse Core Ops, SparseCore 0:
  9.4 46.7 all-gather.3
  58.3 46.0 all-gather.5

commit v18 on v15

--- a/solution.py
+++ b/solution.py
@@ -134,9 +134,8 @@
     key_value = shares(weights[:, width:])
     key_value = lax.all_to_all(key_value, "x", split_axis=0, concat_axis=0, tiled=True)
     query = shares(weights[:, :width])
+    query = lax.all_to_all(query, "x", split_axis=0, concat_axis=0, tiled=True)
     packed = pack(key_value, k_gain)
-    query, packed = lax.optimization_barrier((query, packed))
-    query = lax.all_to_all(query, "x", split_axis=0, concat_axis=0, tiled=True)
     count = lax.axis_size(SLAB)
     swaps = [
         [pair for i in range(first, count - 1, 2) for pair in ((i, i + 1), (i + 1, i))]

time: 118 us -> 119 us (level)
  the two profiles are of different devices: /device:TPU:1 before, /device:TPU:7 now
where the time goes in v18:
time: 119 us
  blocking collectives  49.7 us (42%)
  starting transfers between devices  29.8 us (25%)
  between operations  13.5 us (11%)
  waiting for transfers between devices  12.4 us (10%)
  matrix products  8.54 us (7%)
  local copies, waits for them, and re-layouts  1.99 us (2%)
  other arithmetic  1.91 us (2%)
    all_gather x1, blocking collectives, on_device(): lax.all_gather(pieces.reshape(n_x * rows, part), HEAD, axis=0, tiled=False)  16 us
    all_to_all x1, blocking collectives, on_device(): lax.all_to_all(attended, 'y', split_axis=0, concat_axis=0, tiled=True)  12.3 us
    ppermute x1, starting transfers between devices, on_device(): columns = lax.ppermute(out_weight.T, ('z',) + HEAD, turned)  11.7 us
    all_gather x1, blocking collectives, on_device(): columns = lax.all_gather(columns, 'x', axis=0, tiled=True)  10.9 us
    all_gather x1, blocking collectives, on_device(): everyone = lax.all_gather(everyone, 'core', axis=0, tiled=True)  10.5 us
    ppermute x1, waiting for transfers between devices, on_device(): odd = lax.ppermute(packed, SLAB, swaps[0])  6.1 us
    dot_general x2, matrix products, shares(): jnp.dot(group, piece, preferred_element_type=jnp.float32)  5.41 us
    all_to_all x1, starting transfers between devices, on_device(): query = lax.all_to_all(query, 'x', split_axis=0, concat_axis=0, tiled=True)  5.12 us
  transfers between devices with their start and end apart: 8, of which 3 were waited for; matrix products, arithmetic and copies ran while one was open for 6% of the time, Pallas kernels for 1%

profile of v18, /device:TPU:7, one launch (start us, length us, event | category | flops | bytes accessed | tf_op | source)
XLA Modules:
  0.0 118.7 jit_solution(5352161215879740175)
XLA Ops:
  6.5 1.7 %pad_maximum_fusion = bf16[96,1152]{1,0:T(8,128)(2,1)} fusion(bf16[96,384]{1,0:T(8,128)(2,1)} %param.11, bf16[96,384]{1,0:T(8,128)(2,1)} %param.10, bf16[96,384]{1,0:T(8,128)(2,1)} %param.9), kind=kLoop, calls=%fused_computation.6 | loop fusion | flops 663552 | bytes 442368 | tf_op jit(solution)/shard_map/concatenate | solution.py:112
  8.2 1.6 %copy.13 = bf16[128,384]{0,1:T(8,128)(2,1)} copy(bf16[128,384]{1,0:T(8,128)(2,1)} %param.8) | data formatting | bytes 196608 | tf_op args[0]
  9.9 4.2 %all-to-all-start = ((bf16[4,128,96]{1,2,0:T(8,128)(2,1)}), bf16[4,128,96]{1,2,0:T(8,128)(2,1)S(1)}, u32[]{:S(2)}, u32[]{:S(2)}) async-start(bf16[4,128,96]{1,2,0:T(8,128)(2,1)} %bitcast.1), calls=%async_computation | async-start | bytes 196608 | tf_op jit(solution)/shard_map/all_to_all | solution.py:121
  14.1 11.7 %collective-permute-start = (bf16[96,384]{1,0:T(8,128)(2,1)}, bf16[96,384]{1,0:T(8,128)(2,1)S(1)}, u32[]{:S(2)}, u32[]{:S(2)}) collective-permute-start(bf16[96,384]{1,0:T(8,128)(2,1)} %bitcast.30), channel_id=1, source_target_pairs={{0,0},{2,256},{4,64},{6,320},{8,128},{10,384},{12,192},{14,448},{6... | collective-permute-start | bytes 221192 | tf_op jit(solution)/shard_map/ppermute | solution.py:118
  25.9 16.0 %all_gather.19 = bf16[8,512,96]{1,2,0:T(8,128)(2,1)S(1)} all-gather(bf16[1,512,96]{1,2,0:T(8,128)(2,1)S(1)} %all_gather_reshape.3), channel_id=1, replica_groups=mesh['z'=8,'x'=4,'y'=4,'core'=2,'cfg'=2] {'y','core'}, dimensions={0}, use_global_device_ids=true | all-gather | bytes 884736 | tf_op jit(solution)/shard_map/all_gather | solution.py:122
  41.9 10.9 %all_gather.20 = bf16[384,384]{1,0:T(8,128)(2,1)} all-gather(bf16[96,384]{1,0:T(8,128)(2,1)S(1)} %collective-permute-done), channel_id=1, replica_groups=mesh['z'=8,'x'=4,'y'=4,'core'=2,'cfg'=2] {'x'}, dimensions={0}, use_global_device_ids=true | all-gather | bytes 368640 | tf_op jit(solution)/shard_map/all_gather | solution.py:126
  52.8 2.1 %all-gather.4.cloned.1.call-done = bf16[768,1152]{1,0:T(8,128)(2,1)} async-done(((bf16[96,1152]{1,0:T(8,128)(2,1)}), bf16[768,1152]{1,0:T(8,128)(2,1)}) %all-gather.4.cloned.1.call-update) | async-done | bytes 1769488 | tf_op jit(solution)/shard_map/all_gather | solution.py:113
  55.0 3.0 %convolution_convert_fusion = bf16[512,768]{1,0:T(8,128)(2,1)} fusion(bf16[512,768]{0,1:T(8,128)(2,1)S(1)} %bitcast.28, bf16[768,1152]{1,0:T(8,128)(2,1)} %all-gather.4.cloned.1.call-done), kind=kOutput, calls=%fused_computation | convolution fusion | flops 604372992 | bytes 2752512 | tf_op jit(solution)/shard_map/dot_general | solution.py:131
  57.9 4.0 %all-to-all-start.2 = ((bf16[4,128,768]{2,1,0:T(8,128)(2,1)}), bf16[4,128,768]{2,1,0:T(8,128)(2,1)S(1)}, u32[]{:S(2)}, u32[]{:S(2)}) async-start(bf16[4,128,768]{2,1,0:T(8,128)(2,1)} %bitcast.10), calls=%async_computation.2 | async-start | bytes 1572864 | tf_op jit(solution)/shard_map/all_to_all | solution.py:135
  61.9 0.1 add_multiply_fusion
  62.0 2.5 %convolution_convert_fusion.1 = bf16[512,384]{1,0:T(8,128)(2,1)} fusion(bf16[512,768]{0,1:T(8,128)(2,1)S(1)} %bitcast.29, bf16[768,1152]{1,0:T(8,128)(2,1)} %all-gather.4.cloned.1.call-done), kind=kOutput, calls=%fused_computation.1 | convolution fusion | flops 302186496 | bytes 1769472 | tf_op jit(solution)/shard_map/dot_general | solution.py:131
  64.5 4.1 %all-to-all-done.2.share_ref = bf16[4,128,768]{2,1,0:T(8,128)(2,1)S(1)} async-done(((bf16[4,128,768]{2,1,0:T(8,128)(2,1)}), bf16[4,128,768]{2,1,0:T(8,128)(2,1)S(1)}, u32[]{:S(2)}, u32[]{:S(2)}) %all-to-all-start.2) | async-done | bytes 786464 | tf_op jit(solution)/shard_map/all_to_all | solution.py:135
  68.6 5.1 %all-to-all-start.1 = ((bf16[4,128,384]{2,1,0:T(8,128)(2,1)}), bf16[4,128,384]{2,1,0:T(8,128)(2,1)S(1)}, u32[]{:S(2)}, u32[]{:S(2)}) async-start(bf16[4,128,384]{2,1,0:T(8,128)(2,1)} %bitcast.5), calls=%async_computation.1 | async-start | bytes 786432 | tf_op jit(solution)/shard_map/all_to_all | solution.py:137
  73.7 0.2 shard_map.82.source_ref.own_ref
  73.9 1.9 %collective-permute-start.1 = (bf16[128,768]{1,0:T(8,128)(2,1)S(1)}, bf16[128,768]{1,0:T(8,128)(2,1)S(1)}, u32[]{:S(2)}, u32[]{:S(2)}) collective-permute-start(bf16[128,768]{1,0:T(8,128)(2,1)S(1)} %shard_map.82.source_ref.own_ref), channel_id=1, source_target_pairs={{16,32},{32,16},{48,64},{64,48},{80,96},{96,80},{112,128},{128,112... | collective-permute-start | bytes 589832 | tf_op jit(solution)/shard_map/ppermute | solution.py:144
  75.9 2.8 %collective-permute-start.2 = (bf16[128,768]{1,0:T(8,128)(2,1)S(1)}, bf16[128,768]{1,0:T(8,128)(2,1)S(1)}, u32[]{:S(2)}, u32[]{:S(2)}) collective-permute-start(bf16[128,768]{1,0:T(8,128)(2,1)S(1)} %shard_map.83), channel_id=1, source_target_pairs={{0,16},{16,0},{32,48},{48,32},{64,80},{80,64},{96,112},{112,96},{1... | collective-permute-start | bytes 589832 | tf_op jit(solution)/shard_map/ppermute | solution.py:145
  78.7 0.1 add.37
  78.8 0.1 compare_reduce_fusion
  79.0 0.1 reshape.69.live_ref
  79.0 6.1 %collective-permute-done.1.odd_ref = bf16[128,768]{1,0:T(8,128)(2,1)S(1)} collective-permute-done((bf16[128,768]{1,0:T(8,128)(2,1)S(1)}, bf16[128,768]{1,0:T(8,128)(2,1)S(1)}, u32[]{:S(2)}, u32[]{:S(2)}) %collective-permute-start.1) | collective-permute-done | bytes 196640 | tf_op jit(solution)/shard_map/ppermute | solution.py:144
  85.2 0.7 shard_map.84
  85.9 12.3 %all_to_all.20 = bf16[4,128,384]{2,1,0:T(8,128)(2,1)S(1)} all-to-all(bf16[4,128,384]{2,1,0:T(8,128)(2,1)S(1)} %shard_map.84), channel_id=1, replica_groups=mesh['z'=8,'x'=4,'y'=4,'core'=2,'cfg'=2] {'y'}, dimensions={0} | all-to-all | bytes 786432 | tf_op jit(solution)/shard_map/all_to_all | solution.py:148
  98.2 10.5 %all_gather.21 = bf16[8,128,384]{2,1,0:T(8,128)(2,1)S(1)} all-gather(bf16[4,128,384]{2,1,0:T(8,128)(2,1)S(1)} %all_to_all.20), channel_id=1, replica_groups=mesh['z'=8,'x'=4,'y'=4,'core'=2,'cfg'=2] {'core'}, dimensions={0}, use_global_device_ids=true | all-gather | bytes 1179648 | tf_op jit(solution)/shard_map/all_gather | solution.py:149
  108.7 3.1 %fusion.1 = bf16[128,384]{1,0:T(8,128)(2,1)} fusion(bf16[8,128,384]{2,1,0:T(8,128)(2,1)S(1)} %all_gather.21, bf16[8,384,384]{2,1,0:T(8,128)(2,1)} %bitcast.27), kind=kOutput, calls=%fused_computation.4 | convolution fusion | flops 302039040 | bytes 3244032 | tf_op jit(solution)/shard_map/hrd,hnd->rn/dot_general | solution.py:150
  (22 shorter events, 0.3 us)
Async XLA Ops:
  6.5 48.4 %all-gather.4.cloned.1.call-start = ((), (), s32[]{:S(2)}) async-start(), calls=%async_computation.4 | async-start | bytes 1990656 | tf_op jit(solution)/shard_map/all_gather | solution.py:113
  9.9 16.0 %all-to-all-start = ((bf16[4,128,96]{1,2,0:T(8,128)(2,1)}), bf16[4,128,96]{1,2,0:T(8,128)(2,1)S(1)}, u32[]{:S(2)}, u32[]{:S(2)}) async-start(bf16[4,128,96]{1,2,0:T(8,128)(2,1)} %bitcast.1), calls=%async_computation | async-start | bytes 196608 | tf_op jit(solution)/shard_map/all_to_all | solution.py:121
  14.1 94.6 %all-gather.6.cloned.1.call-start = ((), (), s32[]{:S(2)}) async-start(), calls=%async_computation.5 | async-start | bytes 2654208 | tf_op jit(solution)/shard_map/all_gather | solution.py:127
  14.1 27.8 %collective-permute-start = (bf16[96,384]{1,0:T(8,128)(2,1)}, bf16[96,384]{1,0:T(8,128)(2,1)S(1)}, u32[]{:S(2)}, u32[]{:S(2)}) collective-permute-start(bf16[96,384]{1,0:T(8,128)(2,1)} %bitcast.30), channel_id=1, source_target_pairs={{0,0},{2,256},{4,64},{6,320},{8,128},{10,384},{12,192},{14,448},{6... | collective-permute-start | bytes 221192 | tf_op jit(solution)/shard_map/ppermute | solution.py:118
  57.9 10.7 %all-to-all-start.2 = ((bf16[4,128,768]{2,1,0:T(8,128)(2,1)}), bf16[4,128,768]{2,1,0:T(8,128)(2,1)S(1)}, u32[]{:S(2)}, u32[]{:S(2)}) async-start(bf16[4,128,768]{2,1,0:T(8,128)(2,1)} %bitcast.10), calls=%async_computation.2 | async-start | bytes 1572864 | tf_op jit(solution)/shard_map/all_to_all | solution.py:135
  61.9 11.8 %copy-start = (f32[128]{0:T(128)S(1)}, f32[128]{0:T(128)}, u32[]{:S(2)}) copy-start(f32[128]{0:T(128)} %param.14) | copy-start | bytes 1540
  62.0 16.8 %copy-start.2 = (s32[3,2,6]{2,1,0:T(2,128)S(1)}, s32[3,2,6]{2,1,0:T(2,128)}, u32[]{:S(2)}) copy-start(s32[3,2,6]{2,1,0:T(2,128)} %param.15) | copy-start | bytes 436
  62.0 23.1 %copy-start.1 = (f32[128]{0:T(128)S(1)}, f32[128]{0:T(128)}, u32[]{:S(2)}) copy-start(f32[128]{0:T(128)} %param.13) | copy-start | bytes 1540
  68.6 10.4 %all-to-all-start.1 = ((bf16[4,128,384]{2,1,0:T(8,128)(2,1)}), bf16[4,128,384]{2,1,0:T(8,128)(2,1)S(1)}, u32[]{:S(2)}, u32[]{:S(2)}) async-start(bf16[4,128,384]{2,1,0:T(8,128)(2,1)} %bitcast.5), calls=%async_computation.1 | async-start | bytes 786432 | tf_op jit(solution)/shard_map/all_to_all | solution.py:137
  73.9 11.2 %collective-permute-start.1 = (bf16[128,768]{1,0:T(8,128)(2,1)S(1)}, bf16[128,768]{1,0:T(8,128)(2,1)S(1)}, u32[]{:S(2)}, u32[]{:S(2)}) collective-permute-start(bf16[128,768]{1,0:T(8,128)(2,1)S(1)} %shard_map.82.source_ref.own_ref), channel_id=1, source_target_pairs={{16,32},{32,16},{48,64},{64,48},{80,96},{96,80},{112,128},{128,112... | collective-permute-start | bytes 589832 | tf_op jit(solution)/shard_map/ppermute | solution.py:144
  75.9 9.3 %collective-permute-start.2 = (bf16[128,768]{1,0:T(8,128)(2,1)S(1)}, bf16[128,768]{1,0:T(8,128)(2,1)S(1)}, u32[]{:S(2)}, u32[]{:S(2)}) collective-permute-start(bf16[128,768]{1,0:T(8,128)(2,1)S(1)} %shard_map.83), channel_id=1, source_target_pairs={{0,16},{16,0},{32,48},{48,32},{64,80},{80,64},{96,112},{112,96},{1... | collective-permute-start | bytes 589832 | tf_op jit(solution)/shard_map/ppermute | solution.py:145
Sparse Core Ops, SparseCore 0:
  9.4 45.4 all-gather.3
  57.0 46.9 all-gather.5

commit v19 on v15

--- a/solution.py
+++ b/solution.py
@@ -145,8 +145,8 @@
     odd = lax.ppermute(packed, SLAB, swaps[0])
     even = lax.ppermute(copied(packed), SLAB, swaps[1])
     live = live_rows(key_tiles, rows // TILE)
-    attended = attention(n_head // n_core, query, q_gain, live, odd, packed, even)
-    everyone = lax.all_to_all(attended, "y", split_axis=0, concat_axis=0, tiled=True)
+    attended = attention(1, query, q_gain, live, odd, packed, even)
+    everyone = lax.all_gather(attended, "y", axis=0, tiled=True)
     everyone = lax.all_gather(everyone, "core", axis=0, tiled=True)
     total = jnp.einsum("hrd,hnd->rn", everyone, projection, preferred_element_type=jnp.float32)
     return total.astype(jnp.bfloat16)

time: 118 us -> 120 us (1.017)
  blocking collectives: 50.4 us -> 51.9 us
    all_gather x0 -> x1, blocking collectives: none -> 12 us  [on_device(): everyone = lax.all_gather(attended, 'y', axis=0, tiled=True)]
    all_to_all x1 -> x0, blocking collectives: 11.9 us -> none  [on_device(): lax.all_to_all(attended, 'y', split_axis=0, concat_axis=0, tiled=True)]
    all_gather x1, blocking collectives: 10.7 us -> 12.1 us  [on_device(): everyone = lax.all_gather(everyone, 'core', axis=0, tiled=True)]
  transfers between devices with their start and end apart: 8 -> 8, of which waited for: 3 -> 3; matrix products, arithmetic and copies ran while one was open for 7% -> 6% of each run, Pallas kernels for 1% -> 1%
where the time goes in v19:
time: 120 us; the launch traced here: 119 us
  blocking collectives  51.9 us (43%)
  starting transfers between devices  29 us (24%)
  between operations  13.5 us (11%)
  waiting for transfers between devices  11.3 us (9%)
  matrix products  8.54 us (7%)
  local copies, waits for them, and re-layouts  1.99 us (2%)
  other arithmetic  1.91 us (2%)
    all_gather x1, blocking collectives, on_device(): lax.all_gather(pieces.reshape(n_x * rows, part), HEAD, axis=0, tiled=False)  16 us
    all_gather x1, blocking collectives, on_device(): everyone = lax.all_gather(everyone, 'core', axis=0, tiled=True)  12.1 us
    all_gather x1, blocking collectives, on_device(): everyone = lax.all_gather(attended, 'y', axis=0, tiled=True)  12 us
    all_gather x1, blocking collectives, on_device(): columns = lax.all_gather(columns, 'x', axis=0, tiled=True)  11.8 us
    ppermute x1, starting transfers between devices, on_device(): columns = lax.ppermute(out_weight.T, ('z',) + HEAD, turned)  11.5 us
    all_to_all x1, waiting for transfers between devices, on_device(): lax.all_to_all(key_value, 'x', split_axis=0, concat_axis=0, tiled=True)  5.75 us
    dot_general x2, matrix products, shares(): jnp.dot(group, piece, preferred_element_type=jnp.float32)  5.42 us
    all_to_all x1, starting transfers between devices, on_device(): query = lax.all_to_all(query, 'x', split_axis=0, concat_axis=0, tiled=True)  5.02 us
  transfers between devices with their start and end apart: 8, of which 3 were waited for; matrix products, arithmetic and copies ran while one was open for 6% of the time, Pallas kernels for 1%

profile of v19, /device:TPU:1, one launch (start us, length us, event | category | flops | bytes accessed | tf_op | source)
XLA Modules:
  0.0 119.0 jit_solution(1405395477945465226)
XLA Ops:
  6.5 1.7 %pad_maximum_fusion = bf16[96,1152]{1,0:T(8,128)(2,1)} fusion(bf16[96,384]{1,0:T(8,128)(2,1)} %param.11, bf16[96,384]{1,0:T(8,128)(2,1)} %param.10, bf16[96,384]{1,0:T(8,128)(2,1)} %param.9), kind=kLoop, calls=%fused_computation.6 | loop fusion | flops 663552 | bytes 442368 | tf_op jit(solution)/shard_map/concatenate | solution.py:112
  8.2 1.6 %copy.13 = bf16[128,384]{0,1:T(8,128)(2,1)} copy(bf16[128,384]{1,0:T(8,128)(2,1)} %param.8) | data formatting | bytes 196608 | tf_op args[0]
  9.9 4.8 %all-to-all-start = ((bf16[4,128,96]{1,2,0:T(8,128)(2,1)}), bf16[4,128,96]{1,2,0:T(8,128)(2,1)S(1)}, u32[]{:S(2)}, u32[]{:S(2)}) async-start(bf16[4,128,96]{1,2,0:T(8,128)(2,1)} %bitcast.1), calls=%async_computation | async-start | bytes 196608 | tf_op jit(solution)/shard_map/all_to_all | solution.py:121
  14.7 11.5 %collective-permute-start = (bf16[96,384]{1,0:T(8,128)(2,1)}, bf16[96,384]{1,0:T(8,128)(2,1)S(1)}, u32[]{:S(2)}, u32[]{:S(2)}) collective-permute-start(bf16[96,384]{1,0:T(8,128)(2,1)} %bitcast.30), channel_id=1, source_target_pairs={{0,0},{2,256},{4,64},{6,320},{8,128},{10,384},{12,192},{14,448},{6... | collective-permute-start | bytes 221192 | tf_op jit(solution)/shard_map/ppermute | solution.py:118
  26.3 16.0 %all_gather.22 = bf16[8,512,96]{1,2,0:T(8,128)(2,1)S(1)} all-gather(bf16[1,512,96]{1,2,0:T(8,128)(2,1)S(1)} %all_gather_reshape.3), channel_id=1, replica_groups=mesh['z'=8,'x'=4,'y'=4,'core'=2,'cfg'=2] {'y','core'}, dimensions={0}, use_global_device_ids=true | all-gather | bytes 884736 | tf_op jit(solution)/shard_map/all_gather | solution.py:122
  42.3 11.8 %all_gather.23 = bf16[384,384]{1,0:T(8,128)(2,1)} all-gather(bf16[96,384]{1,0:T(8,128)(2,1)S(1)} %collective-permute-done), channel_id=1, replica_groups=mesh['z'=8,'x'=4,'y'=4,'core'=2,'cfg'=2] {'x'}, dimensions={0}, use_global_device_ids=true | all-gather | bytes 368640 | tf_op jit(solution)/shard_map/all_gather | solution.py:126
  54.1 2.0 %all-gather.4.cloned.1.call-done = bf16[768,1152]{1,0:T(8,128)(2,1)} async-done(((bf16[96,1152]{1,0:T(8,128)(2,1)}), bf16[768,1152]{1,0:T(8,128)(2,1)}) %all-gather.4.cloned.1.call-update) | async-done | bytes 1769488 | tf_op jit(solution)/shard_map/all_gather | solution.py:113
  56.1 3.0 %convolution_convert_fusion = bf16[512,768]{1,0:T(8,128)(2,1)} fusion(bf16[512,768]{0,1:T(8,128)(2,1)S(1)} %bitcast.28, bf16[768,1152]{1,0:T(8,128)(2,1)} %all-gather.4.cloned.1.call-done), kind=kOutput, calls=%fused_computation | convolution fusion | flops 604372992 | bytes 2752512 | tf_op jit(solution)/shard_map/dot_general | solution.py:131
  59.1 3.6 %all-to-all-start.1 = ((bf16[4,128,768]{2,1,0:T(8,128)(2,1)}), bf16[4,128,768]{2,1,0:T(8,128)(2,1)S(1)}, u32[]{:S(2)}, u32[]{:S(2)}) async-start(bf16[4,128,768]{2,1,0:T(8,128)(2,1)} %bitcast.6), calls=%async_computation.1 | async-start | bytes 1572864 | tf_op jit(solution)/shard_map/all_to_all | solution.py:135
  62.8 0.1 add_multiply_fusion
  62.8 2.5 %convolution_convert_fusion.1 = bf16[512,384]{1,0:T(8,128)(2,1)} fusion(bf16[512,768]{0,1:T(8,128)(2,1)S(1)} %bitcast.29, bf16[768,1152]{1,0:T(8,128)(2,1)} %all-gather.4.cloned.1.call-done), kind=kOutput, calls=%fused_computation.1 | convolution fusion | flops 302186496 | bytes 1769472 | tf_op jit(solution)/shard_map/dot_general | solution.py:131
  65.3 5.7 %all-to-all-done.1.share_ref = bf16[4,128,768]{2,1,0:T(8,128)(2,1)S(1)} async-done(((bf16[4,128,768]{2,1,0:T(8,128)(2,1)}), bf16[4,128,768]{2,1,0:T(8,128)(2,1)S(1)}, u32[]{:S(2)}, u32[]{:S(2)}) %all-to-all-start.1) | async-done | bytes 786464 | tf_op jit(solution)/shard_map/all_to_all | solution.py:135
  71.0 0.2 shard_map.82.source_ref.own_ref
  71.2 0.7 collective-permute-start.1
  71.9 5.0 %all-to-all-start.2 = ((bf16[4,128,384]{2,1,0:T(8,128)(2,1)}), bf16[4,128,384]{2,1,0:T(8,128)(2,1)S(1)}, u32[]{:S(2)}, u32[]{:S(2)}) async-start(bf16[4,128,384]{2,1,0:T(8,128)(2,1)} %bitcast.5), calls=%async_computation.2 | async-start | bytes 786432 | tf_op jit(solution)/shard_map/all_to_all | solution.py:139
  77.0 3.4 %collective-permute-start.2 = (bf16[128,768]{1,0:T(8,128)(2,1)S(1)}, bf16[128,768]{1,0:T(8,128)(2,1)S(1)}, u32[]{:S(2)}, u32[]{:S(2)}) collective-permute-start(bf16[128,768]{1,0:T(8,128)(2,1)S(1)} %shard_map.83), channel_id=1, source_target_pairs={{0,16},{16,0},{32,48},{48,32},{64,80},{80,64},{96,112},{112,96},{1... | collective-permute-start | bytes 589832 | tf_op jit(solution)/shard_map/ppermute | solution.py:146
  80.4 0.1 add.37
  80.5 0.1 compare_reduce_fusion
  80.7 0.1 reshape.71.live_ref
  80.8 3.4 %collective-permute-done.2.even_ref = bf16[128,768]{1,0:T(8,128)(2,1)S(1)} collective-permute-done((bf16[128,768]{1,0:T(8,128)(2,1)S(1)}, bf16[128,768]{1,0:T(8,128)(2,1)S(1)}, u32[]{:S(2)}, u32[]{:S(2)}) %collective-permute-start.2) | collective-permute-done | bytes 196640 | tf_op jit(solution)/shard_map/ppermute | solution.py:146
  84.2 0.7 shard_map.84
  84.9 12.0 %all_gather.24 = bf16[4,128,384]{2,1,0:T(8,128)(2,1)S(1)} all-gather(bf16[1,128,384]{2,1,0:T(8,128)(2,1)S(1)} %shard_map.84), channel_id=1, replica_groups=mesh['z'=8,'x'=4,'y'=4,'core'=2,'cfg'=2] {'y'}, dimensions={0}, use_global_device_ids=true | all-gather | bytes 491520 | tf_op jit(solution)/shard_map/all_gather | solution.py:149
  97.0 12.1 %all_gather.25 = bf16[8,128,384]{2,1,0:T(8,128)(2,1)S(1)} all-gather(bf16[4,128,384]{2,1,0:T(8,128)(2,1)S(1)} %all_gather.24), channel_id=1, replica_groups=mesh['z'=8,'x'=4,'y'=4,'core'=2,'cfg'=2] {'core'}, dimensions={0}, use_global_device_ids=true | all-gather | bytes 1179648 | tf_op jit(solution)/shard_map/all_gather | solution.py:150
  109.1 3.1 %fusion.1 = bf16[128,384]{1,0:T(8,128)(2,1)} fusion(bf16[8,128,384]{2,1,0:T(8,128)(2,1)S(1)} %all_gather.25, bf16[8,384,384]{2,1,0:T(8,128)(2,1)} %bitcast.27), kind=kOutput, calls=%fused_computation.4 | convolution fusion | flops 302039040 | bytes 3244032 | tf_op jit(solution)/shard_map/hrd,hnd->rn/dot_general | solution.py:151
  (22 shorter events, 0.3 us)
Async XLA Ops:
  6.5 49.6 %all-gather.4.cloned.1.call-start = ((), (), s32[]{:S(2)}) async-start(), calls=%async_computation.3 | async-start | bytes 1990656 | tf_op jit(solution)/shard_map/all_gather | solution.py:113
  9.9 16.3 %all-to-all-start = ((bf16[4,128,96]{1,2,0:T(8,128)(2,1)}), bf16[4,128,96]{1,2,0:T(8,128)(2,1)S(1)}, u32[]{:S(2)}, u32[]{:S(2)}) async-start(bf16[4,128,96]{1,2,0:T(8,128)(2,1)} %bitcast.1), calls=%async_computation | async-start | bytes 196608 | tf_op jit(solution)/shard_map/all_to_all | solution.py:121
  14.7 94.4 %all-gather.6.cloned.1.call-start = ((), (), s32[]{:S(2)}) async-start(), calls=%async_computation.4 | async-start | bytes 2654208 | tf_op jit(solution)/shard_map/all_gather | solution.py:127
  14.7 27.6 %collective-permute-start = (bf16[96,384]{1,0:T(8,128)(2,1)}, bf16[96,384]{1,0:T(8,128)(2,1)S(1)}, u32[]{:S(2)}, u32[]{:S(2)}) collective-permute-start(bf16[96,384]{1,0:T(8,128)(2,1)} %bitcast.30), channel_id=1, source_target_pairs={{0,0},{2,256},{4,64},{6,320},{8,128},{10,384},{12,192},{14,448},{6... | collective-permute-start | bytes 221192 | tf_op jit(solution)/shard_map/ppermute | solution.py:118
  59.1 11.9 %copy-start = (f32[128]{0:T(128)S(1)}, f32[128]{0:T(128)}, u32[]{:S(2)}) copy-start(f32[128]{0:T(128)} %param.14) | copy-start | bytes 1540
  59.1 11.9 %all-to-all-start.1 = ((bf16[4,128,768]{2,1,0:T(8,128)(2,1)}), bf16[4,128,768]{2,1,0:T(8,128)(2,1)S(1)}, u32[]{:S(2)}, u32[]{:S(2)}) async-start(bf16[4,128,768]{2,1,0:T(8,128)(2,1)} %bitcast.6), calls=%async_computation.1 | async-start | bytes 1572864 | tf_op jit(solution)/shard_map/all_to_all | solution.py:135
  62.8 17.6 %copy-start.2 = (s32[3,2,6]{2,1,0:T(2,128)S(1)}, s32[3,2,6]{2,1,0:T(2,128)}, u32[]{:S(2)}) copy-start(s32[3,2,6]{2,1,0:T(2,128)} %param.15) | copy-start | bytes 436
  62.8 21.4 %copy-start.1 = (f32[128]{0:T(128)S(1)}, f32[128]{0:T(128)}, u32[]{:S(2)}) copy-start(f32[128]{0:T(128)} %param.13) | copy-start | bytes 1540
  71.2 9.5 %collective-permute-start.1 = (bf16[128,768]{1,0:T(8,128)(2,1)S(1)}, bf16[128,768]{1,0:T(8,128)(2,1)S(1)}, u32[]{:S(2)}, u32[]{:S(2)}) collective-permute-start(bf16[128,768]{1,0:T(8,128)(2,1)S(1)} %shard_map.82.source_ref.own_ref), channel_id=1, source_target_pairs={{16,32},{32,16},{48,64},{64,48},{80,96},{96,80},{112,128},{128,112... | collective-permute-start | bytes 589832 | tf_op jit(solution)/shard_map/ppermute | solution.py:145
  71.9 12.3 %all-to-all-start.2 = ((bf16[4,128,384]{2,1,0:T(8,128)(2,1)}), bf16[4,128,384]{2,1,0:T(8,128)(2,1)S(1)}, u32[]{:S(2)}, u32[]{:S(2)}) async-start(bf16[4,128,384]{2,1,0:T(8,128)(2,1)} %bitcast.5), calls=%async_computation.2 | async-start | bytes 786432 | tf_op jit(solution)/shard_map/all_to_all | solution.py:139
  77.0 7.2 %collective-permute-start.2 = (bf16[128,768]{1,0:T(8,128)(2,1)S(1)}, bf16[128,768]{1,0:T(8,128)(2,1)S(1)}, u32[]{:S(2)}, u32[]{:S(2)}) collective-permute-start(bf16[128,768]{1,0:T(8,128)(2,1)S(1)} %shard_map.83), channel_id=1, source_target_pairs={{0,16},{16,0},{32,48},{48,32},{64,80},{80,64},{96,112},{112,96},{1... | collective-permute-start | bytes 589832 | tf_op jit(solution)/shard_map/ppermute | solution.py:146
Sparse Core Ops, SparseCore 0:
  9.4 46.6 all-gather.3
  58.2 45.2 all-gather.5

commit v20 on v15

--- a/solution.py
+++ b/solution.py
@@ -46,6 +46,32 @@
     )(share, gain.reshape(1, HDIM))
 
 
+def turn_kernel(source_ref, out_ref):
+    out_ref[...] = source_ref[...].T
+
+
+def turned_over(array):
+    return pl.pallas_call(
+        turn_kernel,
+        out_shape=jax.ShapeDtypeStruct(array.shape[::-1], array.dtype),
+        compiler_params=params(16),
+    )(array)
+
+
+def query_kernel(share_ref, gain_ref, out_ref):
+    for low in range(0, out_ref.shape[1], HDIM):
+        total = summed(share_ref, low, low + HDIM)
+        out_ref[:, low : low + HDIM] = normed(total, gain_ref[...]).astype(jnp.bfloat16)
+
+
+def normed_query(share, gain):
+    return pl.pallas_call(
+        query_kernel,
+        out_shape=jax.ShapeDtypeStruct(share.shape[1:], jnp.bfloat16),
+        compiler_params=params(16),
+    )(share, gain.reshape(1, HDIM))
+
+
 def copy_kernel(source_ref, out_ref):
     out_ref[...] = source_ref[...]
 
@@ -58,12 +84,12 @@
     )(array)
 
 
-def attention_kernel(share_ref, gain_ref, live_ref, odd_ref, own_ref, even_ref, out_ref):
+def attention_kernel(query_ref, live_ref, odd_ref, own_ref, even_ref, out_ref):
     rows, width = out_ref.shape[1:]
     near = (odd_ref, own_ref, even_ref)
     scale = 1.0 / HDIM**0.5
     for low in range(0, width, HDIM):
-        query = normed(summed(share_ref, low, low + HDIM), gain_ref[...]).astype(jnp.bfloat16)
+        query = query_ref[:, low : low + HDIM]
         keys = jnp.concatenate([r[:, low : low + HDIM] for r in near], axis=0)
         values = jnp.concatenate([r[:, width + low : width + low + HDIM] for r in near], axis=0)
         score = lax.dot_general(
@@ -84,13 +110,13 @@
             out_ref[copy, :, low : low + HDIM] = mixed
 
 
-def attention(copies, query, gain, live, odd, own, even):
-    rows, width = query.shape[1:]
+def attention(copies, query, live, odd, own, even):
+    rows, width = query.shape
     return pl.pallas_call(
         attention_kernel,
         out_shape=jax.ShapeDtypeStruct((copies, rows, width), jnp.bfloat16),
         compiler_params=params(16),
-    )(query, gain.reshape(1, HDIM), live, odd, own, even)
+    )(query, live, odd, own, even)
 
 
 def live_rows(key_tiles, tiles_here):
@@ -123,7 +149,7 @@
     pieces, columns = lax.optimization_barrier((pieces, columns))
     group = pieces.transpose(1, 0, 2).reshape(n_x * rows, n_head * part)
 
-    columns = lax.all_gather(columns, "x", axis=0, tiled=True)
+    columns = turned_over(lax.all_gather(columns, "x", axis=0, tiled=True))
     projection = lax.all_gather(columns, "z", axis=0, tiled=False)
     weights, group, _ = lax.optimization_barrier((weights, group, columns))
 
@@ -145,10 +171,10 @@
     odd = lax.ppermute(packed, SLAB, swaps[0])
     even = lax.ppermute(copied(packed), SLAB, swaps[1])
     live = live_rows(key_tiles, rows // TILE)
-    attended = attention(n_head // n_core, query, q_gain, live, odd, packed, even)
+    attended = attention(n_head // n_core, normed_query(query, q_gain), live, odd, packed, even)
     everyone = lax.all_to_all(attended, "y", split_axis=0, concat_axis=0, tiled=True)
     everyone = lax.all_gather(everyone, "core", axis=0, tiled=True)
-    total = jnp.einsum("hrd,hnd->rn", everyone, projection, preferred_element_type=jnp.float32)
+    total = jnp.einsum("hrd,hdn->rn", everyone, projection, preferred_element_type=jnp.float32)
     return total.astype(jnp.bfloat16)
 
 

time: 118 us -> 118 us (level)
    ppermute x1, waiting for transfers between devices: 3.44 us -> 0.84 us  [on_device(): even = lax.ppermute(copied(packed), SLAB, swaps[1])]
    all_to_all x1, waiting for transfers between devices: 0.01 us -> 2.44 us  [on_device(): query = lax.all_to_all(query, 'x', split_axis=0, concat_axis=0, tiled=True)]
  transfers between devices with their start and end apart: 8 -> 8, of which waited for: 3 -> 4; matrix products, arithmetic and copies ran while one was open for 7% -> 7% of each run, Pallas kernels for 1% -> 2%
where the time goes in v20:
time: 118 us; the launch traced here: 117 us
  blocking collectives  50 us (42%)
  starting transfers between devices  29 us (25%)
  between operations  13.5 us (11%)
  waiting for transfers between devices  10.6 us (9%)
  matrix products  8.31 us (7%)
  local copies, waits for them, and re-layouts  1.99 us (2%)
  other arithmetic  1.91 us (2%)
  Pallas kernels  1.87 us (2%)
    all_gather x1, blocking collectives, on_device(): lax.all_gather(pieces.reshape(n_x * rows, part), HEAD, axis=0, tiled=False)  16 us
    all_to_all x1, blocking collectives, on_device(): lax.all_to_all(attended, 'y', split_axis=0, concat_axis=0, tiled=True)  11.9 us
    ppermute x1, starting transfers between devices, on_device(): columns = lax.ppermute(out_weight.T, ('z',) + HEAD, turned)  11.5 us
    all_gather x1, blocking collectives, on_device(): columns = turned_over(lax.all_gather(columns, 'x', axis=0, tiled=True))  11.4 us
    all_gather x1, blocking collectives, on_device(): everyone = lax.all_gather(everyone, 'core', axis=0, tiled=True)  10.7 us
    all_to_all x1, waiting for transfers between devices, on_device(): lax.all_to_all(key_value, 'x', split_axis=0, concat_axis=0, tiled=True)  5.75 us
    dot_general x2, matrix products, shares(): jnp.dot(group, piece, preferred_element_type=jnp.float32)  5.42 us
    all_to_all x1, starting transfers between devices, on_device(): query = lax.all_to_all(query, 'x', split_axis=0, concat_axis=0, tiled=True)  5.02 us
  transfers between devices with their start and end apart: 8, of which 4 were waited for; matrix products, arithmetic and copies ran while one was open for 7% of the time, Pallas kernels for 2%

profile of v20, /device:TPU:1, one launch (start us, length us, event | category | flops | bytes accessed | tf_op | source)
XLA Modules:
  0.0 117.2 jit_solution(1751613366976180663)
XLA Ops:
  6.5 1.7 %pad_maximum_fusion = bf16[96,1152]{1,0:T(8,128)(2,1)} fusion(bf16[96,384]{1,0:T(8,128)(2,1)} %param.11, bf16[96,384]{1,0:T(8,128)(2,1)} %param.10, bf16[96,384]{1,0:T(8,128)(2,1)} %param.9), kind=kLoop, calls=%fused_computation.6 | loop fusion | flops 663552 | bytes 442368 | tf_op jit(solution)/shard_map/concatenate | solution.py:138
  8.2 1.6 %copy.13 = bf16[128,384]{0,1:T(8,128)(2,1)} copy(bf16[128,384]{1,0:T(8,128)(2,1)} %param.8) | data formatting | bytes 196608 | tf_op args[0]
  9.9 4.8 %all-to-all-start = ((bf16[4,128,96]{1,2,0:T(8,128)(2,1)}), bf16[4,128,96]{1,2,0:T(8,128)(2,1)S(1)}, u32[]{:S(2)}, u32[]{:S(2)}) async-start(bf16[4,128,96]{1,2,0:T(8,128)(2,1)} %bitcast.1), calls=%async_computation | async-start | bytes 196608 | tf_op jit(solution)/shard_map/all_to_all | solution.py:147
  14.7 11.5 %collective-permute-start = (bf16[96,384]{1,0:T(8,128)(2,1)}, bf16[96,384]{1,0:T(8,128)(2,1)S(1)}, u32[]{:S(2)}, u32[]{:S(2)}) collective-permute-start(bf16[96,384]{1,0:T(8,128)(2,1)} %bitcast.30), channel_id=1, source_target_pairs={{0,0},{2,256},{4,64},{6,320},{8,128},{10,384},{12,192},{14,448},{6... | collective-permute-start | bytes 221192 | tf_op jit(solution)/shard_map/ppermute | solution.py:144
  26.3 16.0 %all_gather.19 = bf16[8,512,96]{1,2,0:T(8,128)(2,1)S(1)} all-gather(bf16[1,512,96]{1,2,0:T(8,128)(2,1)S(1)} %all_gather_reshape.3), channel_id=1, replica_groups=mesh['z'=8,'x'=4,'y'=4,'core'=2,'cfg'=2] {'y','core'}, dimensions={0}, use_global_device_ids=true | all-gather | bytes 884736 | tf_op jit(solution)/shard_map/all_gather | solution.py:148
  42.3 11.4 %all_gather.20.source_ref = bf16[384,384]{1,0:T(8,128)(2,1)S(1)} all-gather(bf16[96,384]{1,0:T(8,128)(2,1)S(1)} %collective-permute-done), channel_id=1, replica_groups=mesh['z'=8,'x'=4,'y'=4,'core'=2,'cfg'=2] {'x'}, dimensions={0}, use_global_device_ids=true | all-gather | bytes 368640 | tf_op jit(solution)/shard_map/all_gather | solution.py:152
  53.7 0.9 shard_map.82
  54.6 1.6 %all-gather.4.cloned.1.call-done = bf16[768,1152]{1,0:T(8,128)(2,1)} async-done(((bf16[96,1152]{1,0:T(8,128)(2,1)}), bf16[768,1152]{1,0:T(8,128)(2,1)}) %all-gather.4.cloned.1.call-update) | async-done | bytes 1769488 | tf_op jit(solution)/shard_map/all_gather | solution.py:139
  56.1 3.0 %convolution_convert_fusion = bf16[512,768]{1,0:T(8,128)(2,1)} fusion(bf16[512,768]{0,1:T(8,128)(2,1)S(1)} %bitcast.28, bf16[768,1152]{1,0:T(8,128)(2,1)} %all-gather.4.cloned.1.call-done), kind=kOutput, calls=%fused_computation | convolution fusion | flops 604372992 | bytes 2752512 | tf_op jit(solution)/shard_map/dot_general | solution.py:157
  59.1 3.6 %all-to-all-start.1 = ((bf16[4,128,768]{2,1,0:T(8,128)(2,1)}), bf16[4,128,768]{2,1,0:T(8,128)(2,1)S(1)}, u32[]{:S(2)}, u32[]{:S(2)}) async-start(bf16[4,128,768]{2,1,0:T(8,128)(2,1)} %bitcast.6), calls=%async_computation.1 | async-start | bytes 1572864 | tf_op jit(solution)/shard_map/all_to_all | solution.py:161
  62.8 2.5 %convolution_convert_fusion.1 = bf16[512,384]{1,0:T(8,128)(2,1)} fusion(bf16[512,768]{0,1:T(8,128)(2,1)S(1)} %bitcast.29, bf16[768,1152]{1,0:T(8,128)(2,1)} %all-gather.4.cloned.1.call-done), kind=kOutput, calls=%fused_computation.1 | convolution fusion | flops 302186496 | bytes 1769472 | tf_op jit(solution)/shard_map/dot_general | solution.py:157
  65.3 5.7 %all-to-all-done.1.share_ref = bf16[4,128,768]{2,1,0:T(8,128)(2,1)S(1)} async-done(((bf16[4,128,768]{2,1,0:T(8,128)(2,1)}), bf16[4,128,768]{2,1,0:T(8,128)(2,1)S(1)}, u32[]{:S(2)}, u32[]{:S(2)}) %all-to-all-start.1) | async-done | bytes 786464 | tf_op jit(solution)/shard_map/all_to_all | solution.py:161
  71.0 0.2 shard_map.83.source_ref.own_ref
  71.2 0.7 collective-permute-start.1
  71.9 5.0 %all-to-all-start.2 = ((bf16[4,128,384]{2,1,0:T(8,128)(2,1)}), bf16[4,128,384]{2,1,0:T(8,128)(2,1)S(1)}, u32[]{:S(2)}, u32[]{:S(2)}) async-start(bf16[4,128,384]{2,1,0:T(8,128)(2,1)} %bitcast.5), calls=%async_computation.2 | async-start | bytes 786432 | tf_op jit(solution)/shard_map/all_to_all | solution.py:165
  77.0 3.4 %collective-permute-start.2 = (bf16[128,768]{1,0:T(8,128)(2,1)S(1)}, bf16[128,768]{1,0:T(8,128)(2,1)S(1)}, u32[]{:S(2)}, u32[]{:S(2)}) collective-permute-start(bf16[128,768]{1,0:T(8,128)(2,1)S(1)} %shard_map.85), channel_id=1, source_target_pairs={{0,16},{16,0},{32,48},{48,32},{64,80},{80,64},{96,112},{112,96},{1... | collective-permute-start | bytes 589832 | tf_op jit(solution)/shard_map/ppermute | solution.py:172
  80.5 0.1 compare_reduce_fusion
  80.8 2.4 %all-to-all-done.2.share_ref = bf16[4,128,384]{2,1,0:T(8,128)(2,1)S(1)} async-done(((bf16[4,128,384]{2,1,0:T(8,128)(2,1)}), bf16[4,128,384]{2,1,0:T(8,128)(2,1)S(1)}, u32[]{:S(2)}, u32[]{:S(2)}) %all-to-all-start.2) | async-done | bytes 393248 | tf_op jit(solution)/shard_map/all_to_all | solution.py:165
  83.2 0.1 shard_map.84.query_ref
  83.4 0.8 collective-permute-done.2.even_ref
  84.2 0.7 shard_map.86
  84.9 11.9 %all_to_all.20 = bf16[4,128,384]{2,1,0:T(8,128)(2,1)S(1)} all-to-all(bf16[4,128,384]{2,1,0:T(8,128)(2,1)S(1)} %shard_map.86), channel_id=1, replica_groups=mesh['z'=8,'x'=4,'y'=4,'core'=2,'cfg'=2] {'y'}, dimensions={0} | all-to-all | bytes 786432 | tf_op jit(solution)/shard_map/all_to_all | solution.py:175
  96.8 10.7 %all_gather.21 = bf16[8,128,384]{2,1,0:T(8,128)(2,1)S(1)} all-gather(bf16[4,128,384]{2,1,0:T(8,128)(2,1)S(1)} %all_to_all.20), channel_id=1, replica_groups=mesh['z'=8,'x'=4,'y'=4,'core'=2,'cfg'=2] {'core'}, dimensions={0}, use_global_device_ids=true | all-gather | bytes 1179648 | tf_op jit(solution)/shard_map/all_gather | solution.py:176
  107.5 2.9 %fusion.1 = bf16[128,384]{1,0:T(8,128)(2,1)} fusion(bf16[8,128,384]{2,1,0:T(8,128)(2,1)S(1)} %all_gather.21, bf16[8,384,384]{2,1,0:T(8,128)(2,1)} %bitcast.27), kind=kOutput, calls=%fused_computation.4 | convolution fusion | flops 302039040 | bytes 3244032 | tf_op jit(solution)/shard_map/hrd,hdn->rn/dot_general | solution.py:177
  (24 shorter events, 0.6 us)
Async XLA Ops:
  6.5 49.6 %all-gather.4.cloned.1.call-start = ((), (), s32[]{:S(2)}) async-start(), calls=%async_computation.4 | async-start | bytes 1990656 | tf_op jit(solution)/shard_map/all_gather | solution.py:139
  9.9 16.3 %all-to-all-start = ((bf16[4,128,96]{1,2,0:T(8,128)(2,1)}), bf16[4,128,96]{1,2,0:T(8,128)(2,1)S(1)}, u32[]{:S(2)}, u32[]{:S(2)}) async-start(bf16[4,128,96]{1,2,0:T(8,128)(2,1)} %bitcast.1), calls=%async_computation | async-start | bytes 196608 | tf_op jit(solution)/shard_map/all_to_all | solution.py:147
  14.7 92.8 %all-gather.6.cloned.1.call-start = ((), (), s32[]{:S(2)}) async-start(), calls=%async_computation.5 | async-start | bytes 2654208 | tf_op jit(solution)/shard_map/all_gather | solution.py:153
  14.7 27.6 %collective-permute-start = (bf16[96,384]{1,0:T(8,128)(2,1)}, bf16[96,384]{1,0:T(8,128)(2,1)S(1)}, u32[]{:S(2)}, u32[]{:S(2)}) collective-permute-start(bf16[96,384]{1,0:T(8,128)(2,1)} %bitcast.30), channel_id=1, source_target_pairs={{0,0},{2,256},{4,64},{6,320},{8,128},{10,384},{12,192},{14,448},{6... | collective-permute-start | bytes 221192 | tf_op jit(solution)/shard_map/ppermute | solution.py:144
  59.1 11.9 %copy-start = (f32[128]{0:T(128)S(1)}, f32[128]{0:T(128)}, u32[]{:S(2)}) copy-start(f32[128]{0:T(128)} %param.14) | copy-start | bytes 1540
  59.1 11.9 %all-to-all-start.1 = ((bf16[4,128,768]{2,1,0:T(8,128)(2,1)}), bf16[4,128,768]{2,1,0:T(8,128)(2,1)S(1)}, u32[]{:S(2)}, u32[]{:S(2)}) async-start(bf16[4,128,768]{2,1,0:T(8,128)(2,1)} %bitcast.6), calls=%async_computation.1 | async-start | bytes 1572864 | tf_op jit(solution)/shard_map/all_to_all | solution.py:161
  62.8 17.6 %copy-start.2 = (s32[3,2,6]{2,1,0:T(2,128)S(1)}, s32[3,2,6]{2,1,0:T(2,128)}, u32[]{:S(2)}) copy-start(s32[3,2,6]{2,1,0:T(2,128)} %param.15) | copy-start | bytes 436
  62.8 20.4 %copy-start.1 = (f32[128]{0:T(128)S(1)}, f32[128]{0:T(128)}, u32[]{:S(2)}) copy-start(f32[128]{0:T(128)} %param.13) | copy-start | bytes 1540
  71.2 12.1 %collective-permute-start.1 = (bf16[128,768]{1,0:T(8,128)(2,1)S(1)}, bf16[128,768]{1,0:T(8,128)(2,1)S(1)}, u32[]{:S(2)}, u32[]{:S(2)}) collective-permute-start(bf16[128,768]{1,0:T(8,128)(2,1)S(1)} %shard_map.83.source_ref.own_ref), channel_id=1, source_target_pairs={{16,32},{32,16},{48,64},{64,48},{80,96},{96,80},{112,128},{128,112... | collective-permute-start | bytes 589832 | tf_op jit(solution)/shard_map/ppermute | solution.py:171
  71.9 11.3 %all-to-all-start.2 = ((bf16[4,128,384]{2,1,0:T(8,128)(2,1)}), bf16[4,128,384]{2,1,0:T(8,128)(2,1)S(1)}, u32[]{:S(2)}, u32[]{:S(2)}) async-start(bf16[4,128,384]{2,1,0:T(8,128)(2,1)} %bitcast.5), calls=%async_computation.2 | async-start | bytes 786432 | tf_op jit(solution)/shard_map/all_to_all | solution.py:165
  77.0 7.2 %collective-permute-start.2 = (bf16[128,768]{1,0:T(8,128)(2,1)S(1)}, bf16[128,768]{1,0:T(8,128)(2,1)S(1)}, u32[]{:S(2)}, u32[]{:S(2)}) collective-permute-start(bf16[128,768]{1,0:T(8,128)(2,1)S(1)} %shard_map.85), channel_id=1, source_target_pairs={{0,16},{16,0},{32,48},{48,32},{64,80},{80,64},{96,112},{112,96},{1... | collective-permute-start | bytes 589832 | tf_op jit(solution)/shard_map/ppermute | solution.py:172
Sparse Core Ops, SparseCore 0:
  9.4 46.6 all-gather.3
  58.2 45.2 all-gather.5

commit v21 on v20

--- a/solution.py
+++ b/solution.py
@@ -87,24 +87,37 @@
 def attention_kernel(query_ref, live_ref, odd_ref, own_ref, even_ref, out_ref):
     rows, width = out_ref.shape[1:]
     near = (odd_ref, own_ref, even_ref)
+    tiles = rows // TILE
     scale = 1.0 / HDIM**0.5
-    for low in range(0, width, HDIM):
-        query = query_ref[:, low : low + HDIM]
-        keys = jnp.concatenate([r[:, low : low + HDIM] for r in near], axis=0)
-        values = jnp.concatenate([r[:, width + low : width + low + HDIM] for r in near], axis=0)
+    lows = range(0, width, HDIM)
+
+    def weight_of(low, place):
         score = lax.dot_general(
-            query, keys, (((1,), (1,)), ((), ())), preferred_element_type=jnp.float32
+            query_ref[:, low : low + HDIM],
+            near[place][:, low : low + HDIM],
+            (((1,), (1,)), ((), ())),
+            preferred_element_type=jnp.float32,
         )
-        allowed = jnp.concatenate(
-            [
-                jnp.broadcast_to(live_ref[pl.ds(low // HDIM * (rows // TILE) + t, 1), :], (TILE, 3 * rows))
-                for t in range(rows // TILE)
-            ],
-            axis=0,
+        allowed = [
+            jnp.broadcast_to(
+                live_ref[pl.ds(low // HDIM * tiles + t, 1), place * rows : (place + 1) * rows],
+                (TILE, rows),
+            )
+            for t in range(tiles)
+        ]
+        return jnp.where(jnp.concatenate(allowed, axis=0) > 0, jnp.exp(score * scale), 0.0)
+
+    weights = [[weight_of(low, place) for place in range(len(near))] for low in lows]
+    for low, each in zip(lows, weights):
+        total = jnp.sum(sum(each), axis=1, keepdims=True)
+        mixed = sum(
+            jnp.dot(
+                weight.astype(jnp.bfloat16),
+                ref[:, width + low : width + low + HDIM],
+                preferred_element_type=jnp.float32,
+            )
+            for weight, ref in zip(each, near)
         )
-        weight = jnp.where(allowed > 0, jnp.exp(score * scale), 0.0)
-        total = jnp.sum(weight, axis=1, keepdims=True)
-        mixed = jnp.dot(weight.astype(jnp.bfloat16), values, preferred_element_type=jnp.float32)
         mixed = (mixed / total).astype(jnp.bfloat16)
         for copy in range(out_ref.shape[0]):
             out_ref[copy, :, low : low + HDIM] = mixed

time: 118 us -> 118 us (level)
  transfers between devices with their start and end apart: 8 -> 8, of which waited for: 4 -> 4; matrix products, arithmetic and copies ran while one was open for 7% -> 7% of each run, Pallas kernels for 2% -> 1%
where the time goes in v21:
time: 118 us; the launch traced here: 117 us
  blocking collectives  50 us (42%)
  starting transfers between devices  29 us (25%)
  between operations  13.5 us (11%)
  waiting for transfers between devices  10.6 us (9%)
  matrix products  8.3 us (7%)
  local copies, waits for them, and re-layouts  1.99 us (2%)
  other arithmetic  1.91 us (2%)
  Pallas kernels  1.69 us (1%)
    all_gather x1, blocking collectives, on_device(): lax.all_gather(pieces.reshape(n_x * rows, part), HEAD, axis=0, tiled=False)  16 us
    all_to_all x1, blocking collectives, on_device(): lax.all_to_all(attended, 'y', split_axis=0, concat_axis=0, tiled=True)  11.8 us
    ppermute x1, starting transfers between devices, on_device(): columns = lax.ppermute(out_weight.T, ('z',) + HEAD, turned)  11.5 us
    all_gather x1, blocking collectives, on_device(): columns = turned_over(lax.all_gather(columns, 'x', axis=0, tiled=True))  11.4 us
    all_gather x1, blocking collectives, on_device(): everyone = lax.all_gather(everyone, 'core', axis=0, tiled=True)  10.8 us
    all_to_all x1, waiting for transfers between devices, on_device(): lax.all_to_all(key_value, 'x', split_axis=0, concat_axis=0, tiled=True)  5.75 us
    dot_general x2, matrix products, shares(): jnp.dot(group, piece, preferred_element_type=jnp.float32)  5.42 us
    all_to_all x1, starting transfers between devices, on_device(): query = lax.all_to_all(query, 'x', split_axis=0, concat_axis=0, tiled=True)  5.02 us
  transfers between devices with their start and end apart: 8, of which 4 were waited for; matrix products, arithmetic and copies ran while one was open for 7% of the time, Pallas kernels for 1%

profile of v21, /device:TPU:1, one launch (start us, length us, event | category | flops | bytes accessed | tf_op | source)
XLA Modules:
  0.0 117.0 jit_solution(5436272247759467930)
XLA Ops:
  6.5 1.7 %pad_maximum_fusion = bf16[96,1152]{1,0:T(8,128)(2,1)} fusion(bf16[96,384]{1,0:T(8,128)(2,1)} %param.11, bf16[96,384]{1,0:T(8,128)(2,1)} %param.10, bf16[96,384]{1,0:T(8,128)(2,1)} %param.9), kind=kLoop, calls=%fused_computation.6 | loop fusion | flops 663552 | bytes 442368 | tf_op jit(solution)/shard_map/concatenate | solution.py:151
  8.2 1.6 %copy.13 = bf16[128,384]{0,1:T(8,128)(2,1)} copy(bf16[128,384]{1,0:T(8,128)(2,1)} %param.8) | data formatting | bytes 196608 | tf_op args[0]
  9.9 4.8 %all-to-all-start = ((bf16[4,128,96]{1,2,0:T(8,128)(2,1)}), bf16[4,128,96]{1,2,0:T(8,128)(2,1)S(1)}, u32[]{:S(2)}, u32[]{:S(2)}) async-start(bf16[4,128,96]{1,2,0:T(8,128)(2,1)} %bitcast.1), calls=%async_computation | async-start | bytes 196608 | tf_op jit(solution)/shard_map/all_to_all | solution.py:160
  14.7 11.5 %collective-permute-start = (bf16[96,384]{1,0:T(8,128)(2,1)}, bf16[96,384]{1,0:T(8,128)(2,1)S(1)}, u32[]{:S(2)}, u32[]{:S(2)}) collective-permute-start(bf16[96,384]{1,0:T(8,128)(2,1)} %bitcast.30), channel_id=1, source_target_pairs={{0,0},{2,256},{4,64},{6,320},{8,128},{10,384},{12,192},{14,448},{6... | collective-permute-start | bytes 221192 | tf_op jit(solution)/shard_map/ppermute | solution.py:157
  26.3 16.0 %all_gather.19 = bf16[8,512,96]{1,2,0:T(8,128)(2,1)S(1)} all-gather(bf16[1,512,96]{1,2,0:T(8,128)(2,1)S(1)} %all_gather_reshape.3), channel_id=1, replica_groups=mesh['z'=8,'x'=4,'y'=4,'core'=2,'cfg'=2] {'y','core'}, dimensions={0}, use_global_device_ids=true | all-gather | bytes 884736 | tf_op jit(solution)/shard_map/all_gather | solution.py:161
  42.3 11.4 %all_gather.20.source_ref = bf16[384,384]{1,0:T(8,128)(2,1)S(1)} all-gather(bf16[96,384]{1,0:T(8,128)(2,1)S(1)} %collective-permute-done), channel_id=1, replica_groups=mesh['z'=8,'x'=4,'y'=4,'core'=2,'cfg'=2] {'x'}, dimensions={0}, use_global_device_ids=true | all-gather | bytes 368640 | tf_op jit(solution)/shard_map/all_gather | solution.py:165
  53.7 0.9 shard_map.82
  54.6 1.6 %all-gather.4.cloned.1.call-done = bf16[768,1152]{1,0:T(8,128)(2,1)} async-done(((bf16[96,1152]{1,0:T(8,128)(2,1)}), bf16[768,1152]{1,0:T(8,128)(2,1)}) %all-gather.4.cloned.1.call-update) | async-done | bytes 1769488 | tf_op jit(solution)/shard_map/all_gather | solution.py:152
  56.1 3.0 %convolution_convert_fusion = bf16[512,768]{1,0:T(8,128)(2,1)} fusion(bf16[512,768]{0,1:T(8,128)(2,1)S(1)} %bitcast.28, bf16[768,1152]{1,0:T(8,128)(2,1)} %all-gather.4.cloned.1.call-done), kind=kOutput, calls=%fused_computation | convolution fusion | flops 604372992 | bytes 2752512 | tf_op jit(solution)/shard_map/dot_general | solution.py:170
  59.1 3.6 %all-to-all-start.1 = ((bf16[4,128,768]{2,1,0:T(8,128)(2,1)}), bf16[4,128,768]{2,1,0:T(8,128)(2,1)S(1)}, u32[]{:S(2)}, u32[]{:S(2)}) async-start(bf16[4,128,768]{2,1,0:T(8,128)(2,1)} %bitcast.6), calls=%async_computation.1 | async-start | bytes 1572864 | tf_op jit(solution)/shard_map/all_to_all | solution.py:174
  62.8 2.5 %convolution_convert_fusion.1 = bf16[512,384]{1,0:T(8,128)(2,1)} fusion(bf16[512,768]{0,1:T(8,128)(2,1)S(1)} %bitcast.29, bf16[768,1152]{1,0:T(8,128)(2,1)} %all-gather.4.cloned.1.call-done), kind=kOutput, calls=%fused_computation.1 | convolution fusion | flops 302186496 | bytes 1769472 | tf_op jit(solution)/shard_map/dot_general | solution.py:170
  65.3 5.7 %all-to-all-done.1.share_ref = bf16[4,128,768]{2,1,0:T(8,128)(2,1)S(1)} async-done(((bf16[4,128,768]{2,1,0:T(8,128)(2,1)}), bf16[4,128,768]{2,1,0:T(8,128)(2,1)S(1)}, u32[]{:S(2)}, u32[]{:S(2)}) %all-to-all-start.1) | async-done | bytes 786464 | tf_op jit(solution)/shard_map/all_to_all | solution.py:174
  71.0 0.2 shard_map.83.source_ref.own_ref
  71.2 0.7 collective-permute-start.1
  71.9 5.0 %all-to-all-start.2 = ((bf16[4,128,384]{2,1,0:T(8,128)(2,1)}), bf16[4,128,384]{2,1,0:T(8,128)(2,1)S(1)}, u32[]{:S(2)}, u32[]{:S(2)}) async-start(bf16[4,128,384]{2,1,0:T(8,128)(2,1)} %bitcast.5), calls=%async_computation.2 | async-start | bytes 786432 | tf_op jit(solution)/shard_map/all_to_all | solution.py:178
  77.0 3.4 %collective-permute-start.2 = (bf16[128,768]{1,0:T(8,128)(2,1)S(1)}, bf16[128,768]{1,0:T(8,128)(2,1)S(1)}, u32[]{:S(2)}, u32[]{:S(2)}) collective-permute-start(bf16[128,768]{1,0:T(8,128)(2,1)S(1)} %shard_map.85), channel_id=1, source_target_pairs={{0,16},{16,0},{32,48},{48,32},{64,80},{80,64},{96,112},{112,96},{1... | collective-permute-start | bytes 589832 | tf_op jit(solution)/shard_map/ppermute | solution.py:185
  80.5 0.1 compare_reduce_fusion
  80.8 2.4 %all-to-all-done.2.share_ref = bf16[4,128,384]{2,1,0:T(8,128)(2,1)S(1)} async-done(((bf16[4,128,384]{2,1,0:T(8,128)(2,1)}), bf16[4,128,384]{2,1,0:T(8,128)(2,1)S(1)}, u32[]{:S(2)}, u32[]{:S(2)}) %all-to-all-start.2) | async-done | bytes 393248 | tf_op jit(solution)/shard_map/all_to_all | solution.py:178
  83.2 0.1 shard_map.84.query_ref
  83.4 0.8 collective-permute-done.2.even_ref
  84.2 0.5 shard_map.86
  84.7 11.8 %all_to_all.20 = bf16[4,128,384]{2,1,0:T(8,128)(2,1)S(1)} all-to-all(bf16[4,128,384]{2,1,0:T(8,128)(2,1)S(1)} %shard_map.86), channel_id=1, replica_groups=mesh['z'=8,'x'=4,'y'=4,'core'=2,'cfg'=2] {'y'}, dimensions={0} | all-to-all | bytes 786432 | tf_op jit(solution)/shard_map/all_to_all | solution.py:188
  96.5 10.8 %all_gather.21 = bf16[8,128,384]{2,1,0:T(8,128)(2,1)S(1)} all-gather(bf16[4,128,384]{2,1,0:T(8,128)(2,1)S(1)} %all_to_all.20), channel_id=1, replica_groups=mesh['z'=8,'x'=4,'y'=4,'core'=2,'cfg'=2] {'core'}, dimensions={0}, use_global_device_ids=true | all-gather | bytes 1179648 | tf_op jit(solution)/shard_map/all_gather | solution.py:189
  107.3 2.9 %fusion.1 = bf16[128,384]{1,0:T(8,128)(2,1)} fusion(bf16[8,128,384]{2,1,0:T(8,128)(2,1)S(1)} %all_gather.21, bf16[8,384,384]{2,1,0:T(8,128)(2,1)} %bitcast.27), kind=kOutput, calls=%fused_computation.4 | convolution fusion | flops 302039040 | bytes 3244032 | tf_op jit(solution)/shard_map/hrd,hdn->rn/dot_general | solution.py:190
  (24 shorter events, 0.6 us)
Async XLA Ops:
  6.5 49.6 %all-gather.4.cloned.1.call-start = ((), (), s32[]{:S(2)}) async-start(), calls=%async_computation.4 | async-start | bytes 1990656 | tf_op jit(solution)/shard_map/all_gather | solution.py:152
  9.9 16.3 %all-to-all-start = ((bf16[4,128,96]{1,2,0:T(8,128)(2,1)}), bf16[4,128,96]{1,2,0:T(8,128)(2,1)S(1)}, u32[]{:S(2)}, u32[]{:S(2)}) async-start(bf16[4,128,96]{1,2,0:T(8,128)(2,1)} %bitcast.1), calls=%async_computation | async-start | bytes 196608 | tf_op jit(solution)/shard_map/all_to_all | solution.py:160
  14.7 92.6 %all-gather.6.cloned.1.call-start = ((), (), s32[]{:S(2)}) async-start(), calls=%async_computation.5 | async-start | bytes 2654208 | tf_op jit(solution)/shard_map/all_gather | solution.py:166
  14.7 27.6 %collective-permute-start = (bf16[96,384]{1,0:T(8,128)(2,1)}, bf16[96,384]{1,0:T(8,128)(2,1)S(1)}, u32[]{:S(2)}, u32[]{:S(2)}) collective-permute-start(bf16[96,384]{1,0:T(8,128)(2,1)} %bitcast.30), channel_id=1, source_target_pairs={{0,0},{2,256},{4,64},{6,320},{8,128},{10,384},{12,192},{14,448},{6... | collective-permute-start | bytes 221192 | tf_op jit(solution)/shard_map/ppermute | solution.py:157
  59.1 11.9 %copy-start = (f32[128]{0:T(128)S(1)}, f32[128]{0:T(128)}, u32[]{:S(2)}) copy-start(f32[128]{0:T(128)} %param.14) | copy-start | bytes 1540
  59.1 11.9 %all-to-all-start.1 = ((bf16[4,128,768]{2,1,0:T(8,128)(2,1)}), bf16[4,128,768]{2,1,0:T(8,128)(2,1)S(1)}, u32[]{:S(2)}, u32[]{:S(2)}) async-start(bf16[4,128,768]{2,1,0:T(8,128)(2,1)} %bitcast.6), calls=%async_computation.1 | async-start | bytes 1572864 | tf_op jit(solution)/shard_map/all_to_all | solution.py:174
  62.8 17.6 %copy-start.2 = (s32[3,2,6]{2,1,0:T(2,128)S(1)}, s32[3,2,6]{2,1,0:T(2,128)}, u32[]{:S(2)}) copy-start(s32[3,2,6]{2,1,0:T(2,128)} %param.15) | copy-start | bytes 436
  62.8 20.4 %copy-start.1 = (f32[128]{0:T(128)S(1)}, f32[128]{0:T(128)}, u32[]{:S(2)}) copy-start(f32[128]{0:T(128)} %param.13) | copy-start | bytes 1540
  71.2 12.1 %collective-permute-start.1 = (bf16[128,768]{1,0:T(8,128)(2,1)S(1)}, bf16[128,768]{1,0:T(8,128)(2,1)S(1)}, u32[]{:S(2)}, u32[]{:S(2)}) collective-permute-start(bf16[128,768]{1,0:T(8,128)(2,1)S(1)} %shard_map.83.source_ref.own_ref), channel_id=1, source_target_pairs={{16,32},{32,16},{48,64},{64,48},{80,96},{96,80},{112,128},{128,112... | collective-permute-start | bytes 589832 | tf_op jit(solution)/shard_map/ppermute | solution.py:184
  71.9 11.3 %all-to-all-start.2 = ((bf16[4,128,384]{2,1,0:T(8,128)(2,1)}), bf16[4,128,384]{2,1,0:T(8,128)(2,1)S(1)}, u32[]{:S(2)}, u32[]{:S(2)}) async-start(bf16[4,128,384]{2,1,0:T(8,128)(2,1)} %bitcast.5), calls=%async_computation.2 | async-start | bytes 786432 | tf_op jit(solution)/shard_map/all_to_all | solution.py:178
  77.0 7.2 %collective-permute-start.2 = (bf16[128,768]{1,0:T(8,128)(2,1)S(1)}, bf16[128,768]{1,0:T(8,128)(2,1)S(1)}, u32[]{:S(2)}, u32[]{:S(2)}) collective-permute-start(bf16[128,768]{1,0:T(8,128)(2,1)S(1)} %shard_map.85), channel_id=1, source_target_pairs={{0,16},{16,0},{32,48},{48,32},{64,80},{80,64},{96,112},{112,96},{1... | collective-permute-start | bytes 589832 | tf_op jit(solution)/shard_map/ppermute | solution.py:185
Sparse Core Ops, SparseCore 0:
  9.4 46.6 all-gather.3
  58.2 45.2 all-gather.5

commit v22 on v21

--- a/solution.py
+++ b/solution.py
@@ -170,9 +170,9 @@
         share = jnp.dot(group, piece, preferred_element_type=jnp.float32).astype(jnp.bfloat16)
         return share.reshape(n_x, rows, -1)
 
-    key_value = shares(weights[:, width:])
+    both = shares(weights)
+    query, key_value = lax.optimization_barrier((both[:, :, :width], both[:, :, width:]))
     key_value = lax.all_to_all(key_value, "x", split_axis=0, concat_axis=0, tiled=True)
-    query = shares(weights[:, :width])
     packed = pack(key_value, k_gain)
     query, packed = lax.optimization_barrier((query, packed))
     query = lax.all_to_all(query, "x", split_axis=0, concat_axis=0, tiled=True)

time: 118 us -> 119 us (level)
  matrix products: 8.3 us -> 5.57 us
  waiting for transfers between devices: 10.6 us -> 12.9 us
  local copies, waits for them, and re-layouts: 1.99 us -> 3.72 us
    dot_general x2 -> x1, matrix products: 5.42 us -> 2.68 us  [shares(): jnp.dot(group, piece, preferred_element_type=jnp.float32)]
    all_to_all x1, waiting for transfers between devices: 5.75 us -> 8.21 us  [on_device(): lax.all_to_all(key_value, 'x', split_axis=0, concat_axis=0, tiled=True)]
    slice x0 -> x2, local copies, waits for them, and re-layouts: none -> 1.73 us  [the longest x1 0.94 us: on_device(): both[:, :, width:]]
  transfers between devices with their start and end apart: 8 -> 8, of which waited for: 4 -> 4; matrix products, arithmetic and copies ran while one was open for 7% -> 6% of each run, Pallas kernels for 1% -> 1%
where the time goes in v22:
time: 119 us; the launch traced here: 118 us
  blocking collectives  50.2 us (42%)
  starting transfers between devices  29 us (24%)
  between operations  13.5 us (11%)
  waiting for transfers between devices  12.9 us (11%)
  matrix products  5.57 us (5%)
  local copies, waits for them, and re-layouts  3.72 us (3%)
  other arithmetic  1.91 us (2%)
  Pallas kernels  1.66 us (1%)
    all_gather x1, blocking collectives, on_device(): lax.all_gather(pieces.reshape(n_x * rows, part), HEAD, axis=0, tiled=False)  16 us
    all_to_all x1, blocking collectives, on_device(): lax.all_to_all(attended, 'y', split_axis=0, concat_axis=0, tiled=True)  12.1 us
    ppermute x1, starting transfers between devices, on_device(): columns = lax.ppermute(out_weight.T, ('z',) + HEAD, turned)  11.5 us
    all_gather x1, blocking collectives, on_device(): columns = turned_over(lax.all_gather(columns, 'x', axis=0, tiled=True))  11.4 us
    all_gather x1, blocking collectives, on_device(): everyone = lax.all_gather(everyone, 'core', axis=0, tiled=True)  10.7 us
    all_to_all x1, waiting for transfers between devices, on_device(): lax.all_to_all(key_value, 'x', split_axis=0, concat_axis=0, tiled=True)  8.21 us
    all_to_all x1, starting transfers between devices, on_device(): query = lax.all_to_all(query, 'x', split_axis=0, concat_axis=0, tiled=True)  5.02 us
    all_to_all x1, starting transfers between devices, on_device(): lax.all_to_all(pieces, 'x', split_axis=0, concat_axis=0, tiled=True)  4.84 us
  transfers between devices with their start and end apart: 8, of which 4 were waited for; matrix products, arithmetic and copies ran while one was open for 6% of the time, Pallas kernels for 1%

profile of v22, /device:TPU:1, one launch (start us, length us, event | category | flops | bytes accessed | tf_op | source)
XLA Modules:
  0.0 118.5 jit_solution(327178983521336219)
XLA Ops:
  6.5 1.7 %pad_maximum_fusion = bf16[96,1152]{1,0:T(8,128)(2,1)} fusion(bf16[96,384]{1,0:T(8,128)(2,1)} %param.11, bf16[96,384]{1,0:T(8,128)(2,1)} %param.10, bf16[96,384]{1,0:T(8,128)(2,1)} %param.9), kind=kLoop, calls=%fused_computation.3 | loop fusion | flops 663552 | bytes 442368 | tf_op jit(solution)/shard_map/concatenate | solution.py:151
  8.2 1.6 %copy.13 = bf16[128,384]{0,1:T(8,128)(2,1)} copy(bf16[128,384]{1,0:T(8,128)(2,1)} %param.8) | data formatting | bytes 196608 | tf_op args[0]
  9.9 4.8 %all-to-all-start = ((bf16[4,128,96]{1,2,0:T(8,128)(2,1)}), bf16[4,128,96]{1,2,0:T(8,128)(2,1)S(1)}, u32[]{:S(2)}, u32[]{:S(2)}) async-start(bf16[4,128,96]{1,2,0:T(8,128)(2,1)} %bitcast.1), calls=%async_computation | async-start | bytes 196608 | tf_op jit(solution)/shard_map/all_to_all | solution.py:160
  14.7 11.5 %collective-permute-start = (bf16[96,384]{1,0:T(8,128)(2,1)}, bf16[96,384]{1,0:T(8,128)(2,1)S(1)}, u32[]{:S(2)}, u32[]{:S(2)}) collective-permute-start(bf16[96,384]{1,0:T(8,128)(2,1)} %bitcast.30), channel_id=1, source_target_pairs={{0,0},{2,256},{4,64},{6,320},{8,128},{10,384},{12,192},{14,448},{6... | collective-permute-start | bytes 221192 | tf_op jit(solution)/shard_map/ppermute | solution.py:157
  26.3 16.0 %all_gather.19 = bf16[8,512,96]{1,2,0:T(8,128)(2,1)S(1)} all-gather(bf16[1,512,96]{1,2,0:T(8,128)(2,1)S(1)} %all_gather_reshape.3), channel_id=1, replica_groups=mesh['z'=8,'x'=4,'y'=4,'core'=2,'cfg'=2] {'y','core'}, dimensions={0}, use_global_device_ids=true | all-gather | bytes 884736 | tf_op jit(solution)/shard_map/all_gather | solution.py:161
  42.3 11.4 %all_gather.20.source_ref = bf16[384,384]{1,0:T(8,128)(2,1)S(1)} all-gather(bf16[96,384]{1,0:T(8,128)(2,1)S(1)} %collective-permute-done), channel_id=1, replica_groups=mesh['z'=8,'x'=4,'y'=4,'core'=2,'cfg'=2] {'x'}, dimensions={0}, use_global_device_ids=true | all-gather | bytes 368640 | tf_op jit(solution)/shard_map/all_gather | solution.py:165
  53.7 0.8 shard_map.82
  54.6 1.6 %all-gather.4.cloned.1.call-done = bf16[768,1152]{1,0:T(8,128)(2,1)} async-done(((bf16[96,1152]{1,0:T(8,128)(2,1)}), bf16[768,1152]{1,0:T(8,128)(2,1)}) %all-gather.4.cloned.1.call-update) | async-done | bytes 1769488 | tf_op jit(solution)/shard_map/all_gather | solution.py:152
  56.1 2.7 %convolution_convert_fusion = bf16[512,1152]{1,0:T(8,128)(2,1)S(1)} fusion(bf16[512,768]{0,1:T(8,128)(2,1)S(1)} %bitcast.29, bf16[768,1152]{1,0:T(8,128)(2,1)} %all-gather.4.cloned.1.call-done), kind=kOutput, calls=%fused_computation | convolution fusion | flops 906559488 | bytes 3735552 | tf_op jit(solution)/shard_map/dot_general | solution.py:170
  58.8 0.8 slice.8
  59.6 0.9 slice.9
  60.6 3.6 %all-to-all-start.1 = ((bf16[4,128,768]{2,1,0:T(8,128)(2,1)}), bf16[4,128,768]{2,1,0:T(8,128)(2,1)S(1)}, u32[]{:S(2)}, u32[]{:S(2)}) async-start(bf16[4,128,768]{2,1,0:T(8,128)(2,1)} %slice.9), calls=%async_computation.1 | async-start | bytes 1572864 | tf_op jit(solution)/shard_map/all_to_all | solution.py:175
  64.3 8.2 %all-to-all-done.1.share_ref = bf16[4,128,768]{2,1,0:T(8,128)(2,1)S(1)} async-done(((bf16[4,128,768]{2,1,0:T(8,128)(2,1)}), bf16[4,128,768]{2,1,0:T(8,128)(2,1)S(1)}, u32[]{:S(2)}, u32[]{:S(2)}) %all-to-all-start.1) | async-done | bytes 786464 | tf_op jit(solution)/shard_map/all_to_all | solution.py:175
  72.5 0.2 shard_map.83.source_ref.own_ref
  72.7 0.7 collective-permute-start.1
  73.4 5.0 %all-to-all-start.2 = ((bf16[4,128,384]{2,1,0:T(8,128)(2,1)}), bf16[4,128,384]{2,1,0:T(8,128)(2,1)S(1)}, u32[]{:S(2)}, u32[]{:S(2)}) async-start(bf16[4,128,384]{2,1,0:T(8,128)(2,1)} %slice.8), calls=%async_computation.2 | async-start | bytes 786432 | tf_op jit(solution)/shard_map/all_to_all | solution.py:178
  78.4 3.4 %collective-permute-start.2 = (bf16[128,768]{1,0:T(8,128)(2,1)S(1)}, bf16[128,768]{1,0:T(8,128)(2,1)S(1)}, u32[]{:S(2)}, u32[]{:S(2)}) collective-permute-start(bf16[128,768]{1,0:T(8,128)(2,1)S(1)} %shard_map.85), channel_id=1, source_target_pairs={{0,16},{16,0},{32,48},{48,32},{64,80},{80,64},{96,112},{112,96},{1... | collective-permute-start | bytes 589832 | tf_op jit(solution)/shard_map/ppermute | solution.py:185
  82.2 2.4 %all-to-all-done.2.share_ref = bf16[4,128,384]{2,1,0:T(8,128)(2,1)S(1)} async-done(((bf16[4,128,384]{2,1,0:T(8,128)(2,1)}), bf16[4,128,384]{2,1,0:T(8,128)(2,1)S(1)}, u32[]{:S(2)}, u32[]{:S(2)}) %all-to-all-start.2) | async-done | bytes 393248 | tf_op jit(solution)/shard_map/all_to_all | solution.py:178
  84.7 0.1 shard_map.84.query_ref
  84.8 0.7 collective-permute-done.2.even_ref
  85.5 0.5 shard_map.86
  86.0 12.1 %all_to_all.20 = bf16[4,128,384]{2,1,0:T(8,128)(2,1)S(1)} all-to-all(bf16[4,128,384]{2,1,0:T(8,128)(2,1)S(1)} %shard_map.86), channel_id=1, replica_groups=mesh['z'=8,'x'=4,'y'=4,'core'=2,'cfg'=2] {'y'}, dimensions={0} | all-to-all | bytes 786432 | tf_op jit(solution)/shard_map/all_to_all | solution.py:188
  98.1 10.7 %all_gather.21 = bf16[8,128,384]{2,1,0:T(8,128)(2,1)S(1)} all-gather(bf16[4,128,384]{2,1,0:T(8,128)(2,1)S(1)} %all_to_all.20), channel_id=1, replica_groups=mesh['z'=8,'x'=4,'y'=4,'core'=2,'cfg'=2] {'core'}, dimensions={0}, use_global_device_ids=true | all-gather | bytes 1179648 | tf_op jit(solution)/shard_map/all_gather | solution.py:189
  108.7 2.9 %fusion = bf16[128,384]{1,0:T(8,128)(2,1)} fusion(bf16[8,128,384]{2,1,0:T(8,128)(2,1)S(1)} %all_gather.21, bf16[8,384,384]{2,1,0:T(8,128)(2,1)} %bitcast.26), kind=kOutput, calls=%fused_computation.2 | convolution fusion | flops 302039040 | bytes 3244032 | tf_op jit(solution)/shard_map/hrd,hdn->rn/dot_general | solution.py:190
  (25 shorter events, 0.7 us)
Async XLA Ops:
  6.5 49.6 %all-gather.4.cloned.1.call-start = ((), (), s32[]{:S(2)}) async-start(), calls=%async_computation.4 | async-start | bytes 1990656 | tf_op jit(solution)/shard_map/all_gather | solution.py:152
  9.9 16.3 %all-to-all-start = ((bf16[4,128,96]{1,2,0:T(8,128)(2,1)}), bf16[4,128,96]{1,2,0:T(8,128)(2,1)S(1)}, u32[]{:S(2)}, u32[]{:S(2)}) async-start(bf16[4,128,96]{1,2,0:T(8,128)(2,1)} %bitcast.1), calls=%async_computation | async-start | bytes 196608 | tf_op jit(solution)/shard_map/all_to_all | solution.py:160
  14.7 94.0 %all-gather.6.cloned.1.call-start = ((), (), s32[]{:S(2)}) async-start(), calls=%async_computation.5 | async-start | bytes 2654208 | tf_op jit(solution)/shard_map/all_gather | solution.py:166
  14.7 27.6 %collective-permute-start = (bf16[96,384]{1,0:T(8,128)(2,1)}, bf16[96,384]{1,0:T(8,128)(2,1)S(1)}, u32[]{:S(2)}, u32[]{:S(2)}) collective-permute-start(bf16[96,384]{1,0:T(8,128)(2,1)} %bitcast.30), channel_id=1, source_target_pairs={{0,0},{2,256},{4,64},{6,320},{8,128},{10,384},{12,192},{14,448},{6... | collective-permute-start | bytes 221192 | tf_op jit(solution)/shard_map/ppermute | solution.py:157
  59.6 12.9 %copy-start = (f32[128]{0:T(128)S(1)}, f32[128]{0:T(128)}, u32[]{:S(2)}) copy-start(f32[128]{0:T(128)} %param.14) | copy-start | bytes 1540
  60.6 21.4 %copy-start.2 = (s32[3,2,6]{2,1,0:T(2,128)S(1)}, s32[3,2,6]{2,1,0:T(2,128)}, u32[]{:S(2)}) copy-start(s32[3,2,6]{2,1,0:T(2,128)} %param.15) | copy-start | bytes 436
  60.6 24.1 %copy-start.1 = (f32[128]{0:T(128)S(1)}, f32[128]{0:T(128)}, u32[]{:S(2)}) copy-start(f32[128]{0:T(128)} %param.13) | copy-start | bytes 1540
  60.6 11.9 %all-to-all-start.1 = ((bf16[4,128,768]{2,1,0:T(8,128)(2,1)}), bf16[4,128,768]{2,1,0:T(8,128)(2,1)S(1)}, u32[]{:S(2)}, u32[]{:S(2)}) async-start(bf16[4,128,768]{2,1,0:T(8,128)(2,1)} %slice.9), calls=%async_computation.1 | async-start | bytes 1572864 | tf_op jit(solution)/shard_map/all_to_all | solution.py:175
  72.7 12.1 %collective-permute-start.1 = (bf16[128,768]{1,0:T(8,128)(2,1)S(1)}, bf16[128,768]{1,0:T(8,128)(2,1)S(1)}, u32[]{:S(2)}, u32[]{:S(2)}) collective-permute-start(bf16[128,768]{1,0:T(8,128)(2,1)S(1)} %shard_map.83.source_ref.own_ref), channel_id=1, source_target_pairs={{16,32},{32,16},{48,64},{64,48},{80,96},{96,80},{112,128},{128,112... | collective-permute-start | bytes 589832 | tf_op jit(solution)/shard_map/ppermute | solution.py:184
  73.4 11.3 %all-to-all-start.2 = ((bf16[4,128,384]{2,1,0:T(8,128)(2,1)}), bf16[4,128,384]{2,1,0:T(8,128)(2,1)S(1)}, u32[]{:S(2)}, u32[]{:S(2)}) async-start(bf16[4,128,384]{2,1,0:T(8,128)(2,1)} %slice.8), calls=%async_computation.2 | async-start | bytes 786432 | tf_op jit(solution)/shard_map/all_to_all | solution.py:178
  78.4 7.1 %collective-permute-start.2 = (bf16[128,768]{1,0:T(8,128)(2,1)S(1)}, bf16[128,768]{1,0:T(8,128)(2,1)S(1)}, u32[]{:S(2)}, u32[]{:S(2)}) collective-permute-start(bf16[128,768]{1,0:T(8,128)(2,1)S(1)} %shard_map.85), channel_id=1, source_target_pairs={{0,16},{16,0},{32,48},{48,32},{64,80},{80,64},{96,112},{112,96},{1... | collective-permute-start | bytes 589832 | tf_op jit(solution)/shard_map/ppermute | solution.py:185
Sparse Core Ops, SparseCore 0:
  9.4 46.6 all-gather.3
  58.2 46.6 all-gather.5

commit v23 on v22

--- a/solution.py
+++ b/solution.py
@@ -148,7 +148,7 @@
     n_x, n_z, n_head = (lax.axis_size(a) for a in ("x", "z", HEAD))
     part = width // n_x
 
-    stacked = jnp.concatenate([q_weight, k_weight, v_weight], axis=1)
+    stacked = jnp.concatenate([k_weight, v_weight, q_weight], axis=1)
     weights = lax.all_gather(stacked, "z", axis=0, tiled=True)
 
     n_core = lax.axis_size("core")
@@ -170,9 +170,9 @@
         share = jnp.dot(group, piece, preferred_element_type=jnp.float32).astype(jnp.bfloat16)
         return share.reshape(n_x, rows, -1)
 
-    both = shares(weights)
-    query, key_value = lax.optimization_barrier((both[:, :, :width], both[:, :, width:]))
+    key_value = shares(weights[:, : 2 * width])
     key_value = lax.all_to_all(key_value, "x", split_axis=0, concat_axis=0, tiled=True)
+    query = shares(weights[:, 2 * width :])
     packed = pack(key_value, k_gain)
     query, packed = lax.optimization_barrier((query, packed))
     query = lax.all_to_all(query, "x", split_axis=0, concat_axis=0, tiled=True)

time: 119 us -> 118 us (level)
  matrix products: 5.57 us -> 8.3 us
  waiting for transfers between devices: 12.9 us -> 10.6 us
  local copies, waits for them, and re-layouts: 3.72 us -> 1.99 us
    dot_general x1 -> x2, matrix products: 2.68 us -> 5.42 us  [shares(): jnp.dot(group, piece, preferred_element_type=jnp.float32)]
    all_to_all x1, waiting for transfers between devices: 8.21 us -> 5.75 us  [on_device(): lax.all_to_all(key_value, 'x', split_axis=0, concat_axis=0, tiled=True)]
    slice x2 -> x0, local copies, waits for them, and re-layouts: 1.73 us -> none  [the longest x1 0.94 us: on_device(): both[:, :, width:]]
  transfers between devices with their start and end apart: 8 -> 8, of which waited for: 4 -> 4; matrix products, arithmetic and copies ran while one was open for 6% -> 7% of each run, Pallas kernels for 1% -> 1%
where the time goes in v23:
time: 118 us; the launch traced here: 117 us
  blocking collectives  50 us (42%)
  starting transfers between devices  29 us (25%)
  between operations  13.5 us (11%)
  waiting for transfers between devices  10.6 us (9%)
  matrix products  8.3 us (7%)
  local copies, waits for them, and re-layouts  1.99 us (2%)
  other arithmetic  1.91 us (2%)
  Pallas kernels  1.69 us (1%)
    all_gather x1, blocking collectives, on_device(): lax.all_gather(pieces.reshape(n_x * rows, part), HEAD, axis=0, tiled=False)  16 us
    all_to_all x1, blocking collectives, on_device(): lax.all_to_all(attended, 'y', split_axis=0, concat_axis=0, tiled=True)  11.8 us
    ppermute x1, starting transfers between devices, on_device(): columns = lax.ppermute(out_weight.T, ('z',) + HEAD, turned)  11.5 us
    all_gather x1, blocking collectives, on_device(): columns = turned_over(lax.all_gather(columns, 'x', axis=0, tiled=True))  11.4 us
    all_gather x1, blocking collectives, on_device(): everyone = lax.all_gather(everyone, 'core', axis=0, tiled=True)  10.8 us
    all_to_all x1, waiting for transfers between devices, on_device(): lax.all_to_all(key_value, 'x', split_axis=0, concat_axis=0, tiled=True)  5.75 us
    dot_general x2, matrix products, shares(): jnp.dot(group, piece, preferred_element_type=jnp.float32)  5.42 us
    all_to_all x1, starting transfers between devices, on_device(): query = lax.all_to_all(query, 'x', split_axis=0, concat_axis=0, tiled=True)  5.02 us
  transfers between devices with their start and end apart: 8, of which 4 were waited for; matrix products, arithmetic and copies ran while one was open for 7% of the time, Pallas kernels for 1%

profile of v23, /device:TPU:1, one launch (start us, length us, event | category | flops | bytes accessed | tf_op | source)
XLA Modules:
  0.0 117.0 jit_solution(15554441039612155605)
XLA Ops:
  6.5 1.7 %pad_maximum_fusion = bf16[96,1152]{1,0:T(8,128)(2,1)} fusion(bf16[96,384]{1,0:T(8,128)(2,1)} %param.9, bf16[96,384]{1,0:T(8,128)(2,1)} %param.11, bf16[96,384]{1,0:T(8,128)(2,1)} %param.10), kind=kLoop, calls=%fused_computation.6 | loop fusion | flops 663552 | bytes 442368 | tf_op jit(solution)/shard_map/concatenate | solution.py:151
  8.2 1.6 %copy.13 = bf16[128,384]{0,1:T(8,128)(2,1)} copy(bf16[128,384]{1,0:T(8,128)(2,1)} %param.8) | data formatting | bytes 196608 | tf_op args[0]
  9.9 4.8 %all-to-all-start = ((bf16[4,128,96]{1,2,0:T(8,128)(2,1)}), bf16[4,128,96]{1,2,0:T(8,128)(2,1)S(1)}, u32[]{:S(2)}, u32[]{:S(2)}) async-start(bf16[4,128,96]{1,2,0:T(8,128)(2,1)} %bitcast.1), calls=%async_computation | async-start | bytes 196608 | tf_op jit(solution)/shard_map/all_to_all | solution.py:160
  14.7 11.5 %collective-permute-start = (bf16[96,384]{1,0:T(8,128)(2,1)}, bf16[96,384]{1,0:T(8,128)(2,1)S(1)}, u32[]{:S(2)}, u32[]{:S(2)}) collective-permute-start(bf16[96,384]{1,0:T(8,128)(2,1)} %bitcast.30), channel_id=1, source_target_pairs={{0,0},{2,256},{4,64},{6,320},{8,128},{10,384},{12,192},{14,448},{6... | collective-permute-start | bytes 221192 | tf_op jit(solution)/shard_map/ppermute | solution.py:157
  26.3 16.0 %all_gather.19 = bf16[8,512,96]{1,2,0:T(8,128)(2,1)S(1)} all-gather(bf16[1,512,96]{1,2,0:T(8,128)(2,1)S(1)} %all_gather_reshape.3), channel_id=1, replica_groups=mesh['z'=8,'x'=4,'y'=4,'core'=2,'cfg'=2] {'y','core'}, dimensions={0}, use_global_device_ids=true | all-gather | bytes 884736 | tf_op jit(solution)/shard_map/all_gather | solution.py:161
  42.3 11.4 %all_gather.20.source_ref = bf16[384,384]{1,0:T(8,128)(2,1)S(1)} all-gather(bf16[96,384]{1,0:T(8,128)(2,1)S(1)} %collective-permute-done), channel_id=1, replica_groups=mesh['z'=8,'x'=4,'y'=4,'core'=2,'cfg'=2] {'x'}, dimensions={0}, use_global_device_ids=true | all-gather | bytes 368640 | tf_op jit(solution)/shard_map/all_gather | solution.py:165
  53.7 0.9 shard_map.82
  54.6 1.6 %all-gather.4.cloned.1.call-done = bf16[768,1152]{1,0:T(8,128)(2,1)} async-done(((bf16[96,1152]{1,0:T(8,128)(2,1)}), bf16[768,1152]{1,0:T(8,128)(2,1)}) %all-gather.4.cloned.1.call-update) | async-done | bytes 1769488 | tf_op jit(solution)/shard_map/all_gather | solution.py:152
  56.1 3.0 %convolution_convert_fusion = bf16[512,768]{1,0:T(8,128)(2,1)} fusion(bf16[512,768]{0,1:T(8,128)(2,1)S(1)} %bitcast.28, bf16[768,1152]{1,0:T(8,128)(2,1)} %all-gather.4.cloned.1.call-done), kind=kOutput, calls=%fused_computation | convolution fusion | flops 604372992 | bytes 2752512 | tf_op jit(solution)/shard_map/dot_general | solution.py:170
  59.1 3.6 %all-to-all-start.1 = ((bf16[4,128,768]{2,1,0:T(8,128)(2,1)}), bf16[4,128,768]{2,1,0:T(8,128)(2,1)S(1)}, u32[]{:S(2)}, u32[]{:S(2)}) async-start(bf16[4,128,768]{2,1,0:T(8,128)(2,1)} %bitcast.6), calls=%async_computation.1 | async-start | bytes 1572864 | tf_op jit(solution)/shard_map/all_to_all | solution.py:174
  62.8 2.5 %convolution_convert_fusion.1 = bf16[512,384]{1,0:T(8,128)(2,1)} fusion(bf16[512,768]{0,1:T(8,128)(2,1)S(1)} %bitcast.29, bf16[768,1152]{1,0:T(8,128)(2,1)} %all-gather.4.cloned.1.call-done), kind=kOutput, calls=%fused_computation.1 | convolution fusion | flops 302186496 | bytes 1769472 | tf_op jit(solution)/shard_map/dot_general | solution.py:170
  65.3 5.7 %all-to-all-done.1.share_ref = bf16[4,128,768]{2,1,0:T(8,128)(2,1)S(1)} async-done(((bf16[4,128,768]{2,1,0:T(8,128)(2,1)}), bf16[4,128,768]{2,1,0:T(8,128)(2,1)S(1)}, u32[]{:S(2)}, u32[]{:S(2)}) %all-to-all-start.1) | async-done | bytes 786464 | tf_op jit(solution)/shard_map/all_to_all | solution.py:174
  71.0 0.2 shard_map.83.source_ref.own_ref
  71.2 0.7 collective-permute-start.1
  71.9 5.0 %all-to-all-start.2 = ((bf16[4,128,384]{2,1,0:T(8,128)(2,1)}), bf16[4,128,384]{2,1,0:T(8,128)(2,1)S(1)}, u32[]{:S(2)}, u32[]{:S(2)}) async-start(bf16[4,128,384]{2,1,0:T(8,128)(2,1)} %bitcast.5), calls=%async_computation.2 | async-start | bytes 786432 | tf_op jit(solution)/shard_map/all_to_all | solution.py:178
  77.0 3.4 %collective-permute-start.2 = (bf16[128,768]{1,0:T(8,128)(2,1)S(1)}, bf16[128,768]{1,0:T(8,128)(2,1)S(1)}, u32[]{:S(2)}, u32[]{:S(2)}) collective-permute-start(bf16[128,768]{1,0:T(8,128)(2,1)S(1)} %shard_map.85), channel_id=1, source_target_pairs={{0,16},{16,0},{32,48},{48,32},{64,80},{80,64},{96,112},{112,96},{1... | collective-permute-start | bytes 589832 | tf_op jit(solution)/shard_map/ppermute | solution.py:185
  80.5 0.1 compare_reduce_fusion
  80.8 2.4 %all-to-all-done.2.share_ref = bf16[4,128,384]{2,1,0:T(8,128)(2,1)S(1)} async-done(((bf16[4,128,384]{2,1,0:T(8,128)(2,1)}), bf16[4,128,384]{2,1,0:T(8,128)(2,1)S(1)}, u32[]{:S(2)}, u32[]{:S(2)}) %all-to-all-start.2) | async-done | bytes 393248 | tf_op jit(solution)/shard_map/all_to_all | solution.py:178
  83.2 0.1 shard_map.84.query_ref
  83.4 0.8 collective-permute-done.2.even_ref
  84.2 0.5 shard_map.86
  84.7 11.8 %all_to_all.20 = bf16[4,128,384]{2,1,0:T(8,128)(2,1)S(1)} all-to-all(bf16[4,128,384]{2,1,0:T(8,128)(2,1)S(1)} %shard_map.86), channel_id=1, replica_groups=mesh['z'=8,'x'=4,'y'=4,'core'=2,'cfg'=2] {'y'}, dimensions={0} | all-to-all | bytes 786432 | tf_op jit(solution)/shard_map/all_to_all | solution.py:188
  96.5 10.8 %all_gather.21 = bf16[8,128,384]{2,1,0:T(8,128)(2,1)S(1)} all-gather(bf16[4,128,384]{2,1,0:T(8,128)(2,1)S(1)} %all_to_all.20), channel_id=1, replica_groups=mesh['z'=8,'x'=4,'y'=4,'core'=2,'cfg'=2] {'core'}, dimensions={0}, use_global_device_ids=true | all-gather | bytes 1179648 | tf_op jit(solution)/shard_map/all_gather | solution.py:189
  107.3 2.9 %fusion.1 = bf16[128,384]{1,0:T(8,128)(2,1)} fusion(bf16[8,128,384]{2,1,0:T(8,128)(2,1)S(1)} %all_gather.21, bf16[8,384,384]{2,1,0:T(8,128)(2,1)} %bitcast.27), kind=kOutput, calls=%fused_computation.4 | convolution fusion | flops 302039040 | bytes 3244032 | tf_op jit(solution)/shard_map/hrd,hdn->rn/dot_general | solution.py:190
  (24 shorter events, 0.6 us)
Async XLA Ops:
  6.5 49.6 %all-gather.4.cloned.1.call-start = ((), (), s32[]{:S(2)}) async-start(), calls=%async_computation.4 | async-start | bytes 1990656 | tf_op jit(solution)/shard_map/all_gather | solution.py:152
  9.9 16.3 %all-to-all-start = ((bf16[4,128,96]{1,2,0:T(8,128)(2,1)}), bf16[4,128,96]{1,2,0:T(8,128)(2,1)S(1)}, u32[]{:S(2)}, u32[]{:S(2)}) async-start(bf16[4,128,96]{1,2,0:T(8,128)(2,1)} %bitcast.1), calls=%async_computation | async-start | bytes 196608 | tf_op jit(solution)/shard_map/all_to_all | solution.py:160
  14.7 92.6 %all-gather.6.cloned.1.call-start = ((), (), s32[]{:S(2)}) async-start(), calls=%async_computation.5 | async-start | bytes 2654208 | tf_op jit(solution)/shard_map/all_gather | solution.py:166
  14.7 27.6 %collective-permute-start = (bf16[96,384]{1,0:T(8,128)(2,1)}, bf16[96,384]{1,0:T(8,128)(2,1)S(1)}, u32[]{:S(2)}, u32[]{:S(2)}) collective-permute-start(bf16[96,384]{1,0:T(8,128)(2,1)} %bitcast.30), channel_id=1, source_target_pairs={{0,0},{2,256},{4,64},{6,320},{8,128},{10,384},{12,192},{14,448},{6... | collective-permute-start | bytes 221192 | tf_op jit(solution)/shard_map/ppermute | solution.py:157
  59.1 11.9 %copy-start = (f32[128]{0:T(128)S(1)}, f32[128]{0:T(128)}, u32[]{:S(2)}) copy-start(f32[128]{0:T(128)} %param.14) | copy-start | bytes 1540
  59.1 11.9 %all-to-all-start.1 = ((bf16[4,128,768]{2,1,0:T(8,128)(2,1)}), bf16[4,128,768]{2,1,0:T(8,128)(2,1)S(1)}, u32[]{:S(2)}, u32[]{:S(2)}) async-start(bf16[4,128,768]{2,1,0:T(8,128)(2,1)} %bitcast.6), calls=%async_computation.1 | async-start | bytes 1572864 | tf_op jit(solution)/shard_map/all_to_all | solution.py:174
  62.8 17.6 %copy-start.2 = (s32[3,2,6]{2,1,0:T(2,128)S(1)}, s32[3,2,6]{2,1,0:T(2,128)}, u32[]{:S(2)}) copy-start(s32[3,2,6]{2,1,0:T(2,128)} %param.15) | copy-start | bytes 436
  62.8 20.4 %copy-start.1 = (f32[128]{0:T(128)S(1)}, f32[128]{0:T(128)}, u32[]{:S(2)}) copy-start(f32[128]{0:T(128)} %param.13) | copy-start | bytes 1540
  71.2 12.1 %collective-permute-start.1 = (bf16[128,768]{1,0:T(8,128)(2,1)S(1)}, bf16[128,768]{1,0:T(8,128)(2,1)S(1)}, u32[]{:S(2)}, u32[]{:S(2)}) collective-permute-start(bf16[128,768]{1,0:T(8,128)(2,1)S(1)} %shard_map.83.source_ref.own_ref), channel_id=1, source_target_pairs={{16,32},{32,16},{48,64},{64,48},{80,96},{96,80},{112,128},{128,112... | collective-permute-start | bytes 589832 | tf_op jit(solution)/shard_map/ppermute | solution.py:184
  71.9 11.3 %all-to-all-start.2 = ((bf16[4,128,384]{2,1,0:T(8,128)(2,1)}), bf16[4,128,384]{2,1,0:T(8,128)(2,1)S(1)}, u32[]{:S(2)}, u32[]{:S(2)}) async-start(bf16[4,128,384]{2,1,0:T(8,128)(2,1)} %bitcast.5), calls=%async_computation.2 | async-start | bytes 786432 | tf_op jit(solution)/shard_map/all_to_all | solution.py:178
  77.0 7.2 %collective-permute-start.2 = (bf16[128,768]{1,0:T(8,128)(2,1)S(1)}, bf16[128,768]{1,0:T(8,128)(2,1)S(1)}, u32[]{:S(2)}, u32[]{:S(2)}) collective-permute-start(bf16[128,768]{1,0:T(8,128)(2,1)S(1)} %shard_map.85), channel_id=1, source_target_pairs={{0,16},{16,0},{32,48},{48,32},{64,80},{80,64},{96,112},{112,96},{1... | collective-permute-start | bytes 589832 | tf_op jit(solution)/shard_map/ppermute | solution.py:185
Sparse Core Ops, SparseCore 0:
  9.4 46.6 all-gather.3
  58.2 45.2 all-gather.5

commit v24 on v23

--- a/solution.py
+++ b/solution.py
@@ -162,7 +162,9 @@
     pieces, columns = lax.optimization_barrier((pieces, columns))
     group = pieces.transpose(1, 0, 2).reshape(n_x * rows, n_head * part)
 
-    columns = turned_over(lax.all_gather(columns, "x", axis=0, tiled=True))
+    columns = jnp.broadcast_to(columns[None], (n_x,) + columns.shape)
+    columns = lax.all_to_all(columns, "x", split_axis=0, concat_axis=0, tiled=True)
+    columns = turned_over(columns.reshape(width, width))
     projection = lax.all_gather(columns, "z", axis=0, tiled=False)
     weights, group, _ = lax.optimization_barrier((weights, group, columns))
 

time: 118 us -> 118 us (level)
    all_gather x1 -> x0, blocking collectives: 11.4 us -> none  [on_device(): columns = turned_over(lax.all_gather(columns, 'x', axis=0, tiled=True))]
    all_to_all x0 -> x1, blocking collectives: none -> 11 us  [on_device(): lax.all_to_all(columns, 'x', split_axis=0, concat_axis=0, tiled=True)]
where the time goes in v24:
time: 118 us; the launch traced here: 117 us
  blocking collectives  49.6 us (42%)
  starting transfers between devices  29 us (25%)
  between operations  13.5 us (11%)
  waiting for transfers between devices  11 us (9%)
  matrix products  8.3 us (7%)
  local copies, waits for them, and re-layouts  2.02 us (2%)
  other arithmetic  1.91 us (2%)
  Pallas kernels  1.68 us (1%)
    all_gather x1, blocking collectives, on_device(): lax.all_gather(pieces.reshape(n_x * rows, part), HEAD, axis=0, tiled=False)  16 us
    all_to_all x1, blocking collectives, on_device(): lax.all_to_all(attended, 'y', split_axis=0, concat_axis=0, tiled=True)  11.8 us
    ppermute x1, starting transfers between devices, on_device(): columns = lax.ppermute(out_weight.T, ('z',) + HEAD, turned)  11.5 us
    all_to_all x1, blocking collectives, on_device(): lax.all_to_all(columns, 'x', split_axis=0, concat_axis=0, tiled=True)  11 us
    all_gather x1, blocking collectives, on_device(): everyone = lax.all_gather(everyone, 'core', axis=0, tiled=True)  10.8 us
    all_to_all x1, waiting for transfers between devices, on_device(): lax.all_to_all(key_value, 'x', split_axis=0, concat_axis=0, tiled=True)  5.75 us
    dot_general x2, matrix products, shares(): jnp.dot(group, piece, preferred_element_type=jnp.float32)  5.42 us
    all_to_all x1, starting transfers between devices, on_device(): query = lax.all_to_all(query, 'x', split_axis=0, concat_axis=0, tiled=True)  5.02 us
  transfers between devices with their start and end apart: 8, of which 4 were waited for; matrix products, arithmetic and copies ran while one was open for 7% of the time, Pallas kernels for 1%

profile of v24, /device:TPU:1, one launch (start us, length us, event | category | flops | bytes accessed | tf_op | source)
XLA Modules:
  0.0 117.0 jit_solution(7099425230061436203)
XLA Ops:
  6.5 1.7 %pad_maximum_fusion = bf16[96,1152]{1,0:T(8,128)(2,1)} fusion(bf16[96,384]{1,0:T(8,128)(2,1)} %param.9, bf16[96,384]{1,0:T(8,128)(2,1)} %param.11, bf16[96,384]{1,0:T(8,128)(2,1)} %param.10), kind=kLoop, calls=%fused_computation.6 | loop fusion | flops 663552 | bytes 442368 | tf_op jit(solution)/shard_map/concatenate | solution.py:151
  8.2 1.6 %copy.13 = bf16[128,384]{0,1:T(8,128)(2,1)} copy(bf16[128,384]{1,0:T(8,128)(2,1)} %param.8) | data formatting | bytes 196608 | tf_op args[0]
  9.9 4.8 %all-to-all-start = ((bf16[4,128,96]{1,2,0:T(8,128)(2,1)}), bf16[4,128,96]{1,2,0:T(8,128)(2,1)S(1)}, u32[]{:S(2)}, u32[]{:S(2)}) async-start(bf16[4,128,96]{1,2,0:T(8,128)(2,1)} %bitcast.1), calls=%async_computation | async-start | bytes 196608 | tf_op jit(solution)/shard_map/all_to_all | solution.py:160
  14.7 11.5 %collective-permute-start = (bf16[96,384]{1,0:T(8,128)(2,1)}, bf16[96,384]{1,0:T(8,128)(2,1)S(1)}, u32[]{:S(2)}, u32[]{:S(2)}) collective-permute-start(bf16[96,384]{1,0:T(8,128)(2,1)} %bitcast.32), channel_id=1, source_target_pairs={{0,0},{2,256},{4,64},{6,320},{8,128},{10,384},{12,192},{14,448},{6... | collective-permute-start | bytes 221192 | tf_op jit(solution)/shard_map/ppermute | solution.py:157
  26.3 16.0 %all_gather.16 = bf16[8,512,96]{1,2,0:T(8,128)(2,1)S(1)} all-gather(bf16[1,512,96]{1,2,0:T(8,128)(2,1)S(1)} %all_gather_reshape.3), channel_id=1, replica_groups=mesh['z'=8,'x'=4,'y'=4,'core'=2,'cfg'=2] {'y','core'}, dimensions={0}, use_global_device_ids=true | all-gather | bytes 884736 | tf_op jit(solution)/shard_map/all_gather | solution.py:161
  42.3 11.0 %all_to_all.25 = bf16[4,96,384]{2,1,0:T(8,128)(2,1)S(1)} all-to-all(bf16[4,96,384]{2,1,0:T(8,128)(2,1)S(1)} %broadcast_in_dim.4), channel_id=1, replica_groups=mesh['z'=8,'x'=4,'y'=4,'core'=2,'cfg'=2] {'x'}, dimensions={0} | all-to-all | bytes 589824 | tf_op jit(solution)/shard_map/all_to_all | solution.py:166
  53.3 0.9 shard_map.82
  54.2 2.0 %all-gather.4.cloned.1.call-done = bf16[768,1152]{1,0:T(8,128)(2,1)} async-done(((bf16[96,1152]{1,0:T(8,128)(2,1)}), bf16[768,1152]{1,0:T(8,128)(2,1)}) %all-gather.4.cloned.1.call-update) | async-done | bytes 1769488 | tf_op jit(solution)/shard_map/all_gather | solution.py:152
  56.1 3.0 %convolution_convert_fusion = bf16[512,768]{1,0:T(8,128)(2,1)} fusion(bf16[512,768]{0,1:T(8,128)(2,1)S(1)} %bitcast.30, bf16[768,1152]{1,0:T(8,128)(2,1)} %all-gather.4.cloned.1.call-done), kind=kOutput, calls=%fused_computation | convolution fusion | flops 604372992 | bytes 2752512 | tf_op jit(solution)/shard_map/dot_general | solution.py:172
  59.1 3.6 %all-to-all-start.2 = ((bf16[4,128,768]{2,1,0:T(8,128)(2,1)}), bf16[4,128,768]{2,1,0:T(8,128)(2,1)S(1)}, u32[]{:S(2)}, u32[]{:S(2)}) async-start(bf16[4,128,768]{2,1,0:T(8,128)(2,1)} %bitcast.7), calls=%async_computation.2 | async-start | bytes 1572864 | tf_op jit(solution)/shard_map/all_to_all | solution.py:176
  62.8 2.5 %convolution_convert_fusion.1 = bf16[512,384]{1,0:T(8,128)(2,1)} fusion(bf16[512,768]{0,1:T(8,128)(2,1)S(1)} %bitcast.31, bf16[768,1152]{1,0:T(8,128)(2,1)} %all-gather.4.cloned.1.call-done), kind=kOutput, calls=%fused_computation.1 | convolution fusion | flops 302186496 | bytes 1769472 | tf_op jit(solution)/shard_map/dot_general | solution.py:172
  65.3 5.7 %all-to-all-done.2.share_ref = bf16[4,128,768]{2,1,0:T(8,128)(2,1)S(1)} async-done(((bf16[4,128,768]{2,1,0:T(8,128)(2,1)}), bf16[4,128,768]{2,1,0:T(8,128)(2,1)S(1)}, u32[]{:S(2)}, u32[]{:S(2)}) %all-to-all-start.2) | async-done | bytes 786464 | tf_op jit(solution)/shard_map/all_to_all | solution.py:176
  71.0 0.2 shard_map.83.source_ref.own_ref
  71.2 0.7 collective-permute-start.1
  71.9 5.0 %all-to-all-start.3 = ((bf16[4,128,384]{2,1,0:T(8,128)(2,1)}), bf16[4,128,384]{2,1,0:T(8,128)(2,1)S(1)}, u32[]{:S(2)}, u32[]{:S(2)}) async-start(bf16[4,128,384]{2,1,0:T(8,128)(2,1)} %bitcast.6), calls=%async_computation.3 | async-start | bytes 786432 | tf_op jit(solution)/shard_map/all_to_all | solution.py:180
  77.0 3.4 %collective-permute-start.2 = (bf16[128,768]{1,0:T(8,128)(2,1)S(1)}, bf16[128,768]{1,0:T(8,128)(2,1)S(1)}, u32[]{:S(2)}, u32[]{:S(2)}) collective-permute-start(bf16[128,768]{1,0:T(8,128)(2,1)S(1)} %shard_map.85), channel_id=1, source_target_pairs={{0,16},{16,0},{32,48},{48,32},{64,80},{80,64},{96,112},{112,96},{1... | collective-permute-start | bytes 589832 | tf_op jit(solution)/shard_map/ppermute | solution.py:187
  80.5 0.1 compare_reduce_fusion
  80.8 2.4 %all-to-all-done.3.share_ref = bf16[4,128,384]{2,1,0:T(8,128)(2,1)S(1)} async-done(((bf16[4,128,384]{2,1,0:T(8,128)(2,1)}), bf16[4,128,384]{2,1,0:T(8,128)(2,1)S(1)}, u32[]{:S(2)}, u32[]{:S(2)}) %all-to-all-start.3) | async-done | bytes 393248 | tf_op jit(solution)/shard_map/all_to_all | solution.py:180
  83.2 0.1 shard_map.84.query_ref
  83.4 0.8 collective-permute-done.2.even_ref
  84.2 0.5 shard_map.86
  84.7 11.8 %all_to_all.26 = bf16[4,128,384]{2,1,0:T(8,128)(2,1)S(1)} all-to-all(bf16[4,128,384]{2,1,0:T(8,128)(2,1)S(1)} %shard_map.86), channel_id=1, replica_groups=mesh['z'=8,'x'=4,'y'=4,'core'=2,'cfg'=2] {'y'}, dimensions={0} | all-to-all | bytes 786432 | tf_op jit(solution)/shard_map/all_to_all | solution.py:190
  96.5 10.8 %all_gather.17 = bf16[8,128,384]{2,1,0:T(8,128)(2,1)S(1)} all-gather(bf16[4,128,384]{2,1,0:T(8,128)(2,1)S(1)} %all_to_all.26), channel_id=1, replica_groups=mesh['z'=8,'x'=4,'y'=4,'core'=2,'cfg'=2] {'core'}, dimensions={0}, use_global_device_ids=true | all-gather | bytes 1179648 | tf_op jit(solution)/shard_map/all_gather | solution.py:191
  107.3 2.9 %fusion.1 = bf16[128,384]{1,0:T(8,128)(2,1)} fusion(bf16[8,128,384]{2,1,0:T(8,128)(2,1)S(1)} %all_gather.17, bf16[8,384,384]{2,1,0:T(8,128)(2,1)} %bitcast.29), kind=kOutput, calls=%fused_computation.4 | convolution fusion | flops 302039040 | bytes 3244032 | tf_op jit(solution)/shard_map/hrd,hdn->rn/dot_general | solution.py:192
  (25 shorter events, 0.6 us)
Async XLA Ops:
  6.5 49.6 %all-gather.4.cloned.1.call-start = ((), (), s32[]{:S(2)}) async-start(), calls=%async_computation.5 | async-start | bytes 1990656 | tf_op jit(solution)/shard_map/all_gather | solution.py:152
  9.9 16.3 %all-to-all-start = ((bf16[4,128,96]{1,2,0:T(8,128)(2,1)}), bf16[4,128,96]{1,2,0:T(8,128)(2,1)S(1)}, u32[]{:S(2)}, u32[]{:S(2)}) async-start(bf16[4,128,96]{1,2,0:T(8,128)(2,1)} %bitcast.1), calls=%async_computation | async-start | bytes 196608 | tf_op jit(solution)/shard_map/all_to_all | solution.py:160
  14.7 92.6 %all-gather.6.cloned.1.call-start = ((), (), s32[]{:S(2)}) async-start(), calls=%async_computation.6 | async-start | bytes 2654208 | tf_op jit(solution)/shard_map/all_gather | solution.py:168
  14.7 27.6 %collective-permute-start = (bf16[96,384]{1,0:T(8,128)(2,1)}, bf16[96,384]{1,0:T(8,128)(2,1)S(1)}, u32[]{:S(2)}, u32[]{:S(2)}) collective-permute-start(bf16[96,384]{1,0:T(8,128)(2,1)} %bitcast.32), channel_id=1, source_target_pairs={{0,0},{2,256},{4,64},{6,320},{8,128},{10,384},{12,192},{14,448},{6... | collective-permute-start | bytes 221192 | tf_op jit(solution)/shard_map/ppermute | solution.py:157
  59.1 11.9 %copy-start = (f32[128]{0:T(128)S(1)}, f32[128]{0:T(128)}, u32[]{:S(2)}) copy-start(f32[128]{0:T(128)} %param.14) | copy-start | bytes 1540
  59.1 11.9 %all-to-all-start.2 = ((bf16[4,128,768]{2,1,0:T(8,128)(2,1)}), bf16[4,128,768]{2,1,0:T(8,128)(2,1)S(1)}, u32[]{:S(2)}, u32[]{:S(2)}) async-start(bf16[4,128,768]{2,1,0:T(8,128)(2,1)} %bitcast.7), calls=%async_computation.2 | async-start | bytes 1572864 | tf_op jit(solution)/shard_map/all_to_all | solution.py:176
  62.8 17.6 %copy-start.2 = (s32[3,2,6]{2,1,0:T(2,128)S(1)}, s32[3,2,6]{2,1,0:T(2,128)}, u32[]{:S(2)}) copy-start(s32[3,2,6]{2,1,0:T(2,128)} %param.15) | copy-start | bytes 436
  62.8 20.4 %copy-start.1 = (f32[128]{0:T(128)S(1)}, f32[128]{0:T(128)}, u32[]{:S(2)}) copy-start(f32[128]{0:T(128)} %param.13) | copy-start | bytes 1540
  71.2 12.1 %collective-permute-start.1 = (bf16[128,768]{1,0:T(8,128)(2,1)S(1)}, bf16[128,768]{1,0:T(8,128)(2,1)S(1)}, u32[]{:S(2)}, u32[]{:S(2)}) collective-permute-start(bf16[128,768]{1,0:T(8,128)(2,1)S(1)} %shard_map.83.source_ref.own_ref), channel_id=1, source_target_pairs={{16,32},{32,16},{48,64},{64,48},{80,96},{96,80},{112,128},{128,112... | collective-permute-start | bytes 589832 | tf_op jit(solution)/shard_map/ppermute | solution.py:186
  71.9 11.3 %all-to-all-start.3 = ((bf16[4,128,384]{2,1,0:T(8,128)(2,1)}), bf16[4,128,384]{2,1,0:T(8,128)(2,1)S(1)}, u32[]{:S(2)}, u32[]{:S(2)}) async-start(bf16[4,128,384]{2,1,0:T(8,128)(2,1)} %bitcast.6), calls=%async_computation.3 | async-start | bytes 786432 | tf_op jit(solution)/shard_map/all_to_all | solution.py:180
  77.0 7.2 %collective-permute-start.2 = (bf16[128,768]{1,0:T(8,128)(2,1)S(1)}, bf16[128,768]{1,0:T(8,128)(2,1)S(1)}, u32[]{:S(2)}, u32[]{:S(2)}) collective-permute-start(bf16[128,768]{1,0:T(8,128)(2,1)S(1)} %shard_map.85), channel_id=1, source_target_pairs={{0,16},{16,0},{32,48},{48,32},{64,80},{80,64},{96,112},{112,96},{1... | collective-permute-start | bytes 589832 | tf_op jit(solution)/shard_map/ppermute | solution.py:187
Sparse Core Ops, SparseCore 0:
  9.4 46.6 all-gather.3
  58.2 45.2 all-gather.5

commit v25 on v23

--- a/solution.py
+++ b/solution.py
@@ -152,8 +152,14 @@
     weights = lax.all_gather(stacked, "z", axis=0, tiled=True)
 
     n_core = lax.axis_size("core")
-    rank = [h % n_core * (n_head // n_core) + h // n_core for h in range(n_head)]
-    turned = [(z * n_head + h, rank[h] * n_z + z) for z in range(n_z) for h in range(n_head)]
+    n_y = n_head // n_core
+
+    def place_of(head, column):
+        return head % n_core * n_y + (head // n_core ^ column // n_core)
+
+    turned = [
+        (z * n_head + h, place_of(h, z) * n_z + z) for z in range(n_z) for h in range(n_head)
+    ]
     columns = lax.ppermute(out_weight.T, ("z",) + HEAD, turned)
 
     pieces = tokens.reshape(rows, n_x, part).transpose(1, 0, 2)
@@ -184,8 +190,11 @@
     odd = lax.ppermute(packed, SLAB, swaps[0])
     even = lax.ppermute(copied(packed), SLAB, swaps[1])
     live = live_rows(key_tiles, rows // TILE)
-    attended = attention(n_head // n_core, normed_query(query, q_gain), live, odd, packed, even)
-    everyone = lax.all_to_all(attended, "y", split_axis=0, concat_axis=0, tiled=True)
+    attended = attention(1, normed_query(query, q_gain), live, odd, packed, even)
+    line = [
+        lax.ppermute(attended, "y", [(i, i ^ step) for i in range(n_y)]) for step in range(1, n_y)
+    ]
+    everyone = jnp.concatenate([attended, *line], axis=0)
     everyone = lax.all_gather(everyone, "core", axis=0, tiled=True)
     total = jnp.einsum("hrd,hdn->rn", everyone, projection, preferred_element_type=jnp.float32)
     return total.astype(jnp.bfloat16)

time: 118 us -> 118 us (level)
  blocking collectives: 50 us -> 37.9 us
  starting transfers between devices: 29 us -> 38.3 us
  waiting for transfers between devices: 10.6 us -> 14 us
    all_to_all x1 -> x0, blocking collectives: 11.8 us -> none  [on_device(): lax.all_to_all(attended, 'y', split_axis=0, concat_axis=0, tiled=True)]
    ppermute x0 -> x3, starting transfers between devices: none -> 9.27 us  [on_device(): lax.ppermute(attended, 'y', [(i, i ^ step) for i in range(n_y)])]
    ppermute x0 -> x3, waiting for transfers between devices: none -> 3.31 us  [on_device(): lax.ppermute(attended, 'y', [(i, i ^ step) for i in range(n_y)])]
  transfers between devices with their start and end apart: 8 -> 11, of which waited for: 4 -> 6; matrix products, arithmetic and copies ran while one was open for 7% -> 7% of each run, Pallas kernels for 1% -> 1%
where the time goes in v25:
time: 118 us
  starting transfers between devices  38.3 us (32%)
  blocking collectives  37.9 us (32%)
  waiting for transfers between devices  14 us (12%)
  between operations  13.6 us (12%)
  matrix products  8.33 us (7%)
  local copies, waits for them, and re-layouts  1.99 us (2%)
  other arithmetic  1.98 us (2%)
  Pallas kernels  1.67 us (1%)
    all_gather x1, blocking collectives, on_device(): lax.all_gather(pieces.reshape(n_x * rows, part), HEAD, axis=0, tiled=False)  16 us
    ppermute x1, starting transfers between devices, on_device(): columns = lax.ppermute(out_weight.T, ('z',) + HEAD, turned)  11.5 us
    all_gather x1, blocking collectives, on_device(): columns = turned_over(lax.all_gather(columns, 'x', axis=0, tiled=True))  11.4 us
    all_gather x1, blocking collectives, on_device(): everyone = lax.all_gather(everyone, 'core', axis=0, tiled=True)  10.6 us
    ppermute x3, starting transfers between devices, on_device(): lax.ppermute(attended, 'y', [(i, i ^ step) for i in range(n_y)])  9.27 us
    all_to_all x1, waiting for transfers between devices, on_device(): lax.all_to_all(key_value, 'x', split_axis=0, concat_axis=0, tiled=True)  5.75 us
    dot_general x2, matrix products, shares(): jnp.dot(group, piece, preferred_element_type=jnp.float32)  5.43 us
    all_to_all x1, starting transfers between devices, on_device(): query = lax.all_to_all(query, 'x', split_axis=0, concat_axis=0, tiled=True)  5.01 us
  transfers between devices with their start and end apart: 11, of which 6 were waited for; matrix products, arithmetic and copies ran while one was open for 7% of the time, Pallas kernels for 1%

profile of v25, /device:TPU:1, one launch (start us, length us, event | category | flops | bytes accessed | tf_op | source)
XLA Modules:
  0.0 117.7 jit_solution(17616074407725044638)
XLA Ops:
  6.5 1.7 %pad_maximum_fusion.1 = bf16[96,1152]{1,0:T(8,128)(2,1)} fusion(bf16[96,384]{1,0:T(8,128)(2,1)} %param.9, bf16[96,384]{1,0:T(8,128)(2,1)} %param.11, bf16[96,384]{1,0:T(8,128)(2,1)} %param.10), kind=kLoop, calls=%fused_computation.7 | loop fusion | flops 663552 | bytes 442368 | tf_op jit(solution)/shard_map/concatenate | solution.py:151
  8.2 1.6 %copy.13 = bf16[128,384]{0,1:T(8,128)(2,1)} copy(bf16[128,384]{1,0:T(8,128)(2,1)} %param.8) | data formatting | bytes 196608 | tf_op args[0]
  9.9 4.8 %all-to-all-start = ((bf16[4,128,96]{1,2,0:T(8,128)(2,1)}), bf16[4,128,96]{1,2,0:T(8,128)(2,1)S(1)}, u32[]{:S(2)}, u32[]{:S(2)}) async-start(bf16[4,128,96]{1,2,0:T(8,128)(2,1)} %bitcast.1), calls=%async_computation | async-start | bytes 196608 | tf_op jit(solution)/shard_map/all_to_all | solution.py:166
  14.7 11.5 %collective-permute-start = (bf16[96,384]{1,0:T(8,128)(2,1)}, bf16[96,384]{1,0:T(8,128)(2,1)S(1)}, u32[]{:S(2)}, u32[]{:S(2)}) collective-permute-start(bf16[96,384]{1,0:T(8,128)(2,1)} %bitcast.30), channel_id=1, source_target_pairs={{0,0},{2,256},{4,64},{6,320},{8,128},{10,384},{12,192},{14,448},{6... | collective-permute-start | bytes 221192 | tf_op jit(solution)/shard_map/ppermute | solution.py:163
  26.3 16.0 %all_gather.19 = bf16[8,512,96]{1,2,0:T(8,128)(2,1)S(1)} all-gather(bf16[1,512,96]{1,2,0:T(8,128)(2,1)S(1)} %all_gather_reshape.3), channel_id=1, replica_groups=mesh['z'=8,'x'=4,'y'=4,'core'=2,'cfg'=2] {'y','core'}, dimensions={0}, use_global_device_ids=true | all-gather | bytes 884736 | tf_op jit(solution)/shard_map/all_gather | solution.py:167
  42.3 11.4 %all_gather.20.source_ref = bf16[384,384]{1,0:T(8,128)(2,1)S(1)} all-gather(bf16[96,384]{1,0:T(8,128)(2,1)S(1)} %collective-permute-done), channel_id=1, replica_groups=mesh['z'=8,'x'=4,'y'=4,'core'=2,'cfg'=2] {'x'}, dimensions={0}, use_global_device_ids=true | all-gather | bytes 368640 | tf_op jit(solution)/shard_map/all_gather | solution.py:171
  53.7 0.9 shard_map.82
  54.6 1.6 %all-gather.4.cloned.1.call-done = bf16[768,1152]{1,0:T(8,128)(2,1)} async-done(((bf16[96,1152]{1,0:T(8,128)(2,1)}), bf16[768,1152]{1,0:T(8,128)(2,1)}) %all-gather.4.cloned.1.call-update) | async-done | bytes 1769488 | tf_op jit(solution)/shard_map/all_gather | solution.py:152
  56.2 3.0 %convolution_convert_fusion = bf16[512,768]{1,0:T(8,128)(2,1)} fusion(bf16[512,768]{0,1:T(8,128)(2,1)S(1)} %bitcast.28, bf16[768,1152]{1,0:T(8,128)(2,1)} %all-gather.4.cloned.1.call-done), kind=kOutput, calls=%fused_computation | convolution fusion | flops 604372992 | bytes 2752512 | tf_op jit(solution)/shard_map/dot_general | solution.py:176
  59.1 3.6 %all-to-all-start.1 = ((bf16[4,128,768]{2,1,0:T(8,128)(2,1)}), bf16[4,128,768]{2,1,0:T(8,128)(2,1)S(1)}, u32[]{:S(2)}, u32[]{:S(2)}) async-start(bf16[4,128,768]{2,1,0:T(8,128)(2,1)} %bitcast.6), calls=%async_computation.1 | async-start | bytes 1572864 | tf_op jit(solution)/shard_map/all_to_all | solution.py:180
  62.9 2.4 %convolution_convert_fusion.1 = bf16[512,384]{1,0:T(8,128)(2,1)} fusion(bf16[512,768]{0,1:T(8,128)(2,1)S(1)} %bitcast.29, bf16[768,1152]{1,0:T(8,128)(2,1)} %all-gather.4.cloned.1.call-done), kind=kOutput, calls=%fused_computation.1 | convolution fusion | flops 302186496 | bytes 1769472 | tf_op jit(solution)/shard_map/dot_general | solution.py:176
  65.3 5.8 %all-to-all-done.1.share_ref = bf16[4,128,768]{2,1,0:T(8,128)(2,1)S(1)} async-done(((bf16[4,128,768]{2,1,0:T(8,128)(2,1)}), bf16[4,128,768]{2,1,0:T(8,128)(2,1)S(1)}, u32[]{:S(2)}, u32[]{:S(2)}) %all-to-all-start.1) | async-done | bytes 786464 | tf_op jit(solution)/shard_map/all_to_all | solution.py:180
  71.3 0.7 collective-permute-start.1
  72.0 5.0 %all-to-all-start.2 = ((bf16[4,128,384]{2,1,0:T(8,128)(2,1)}), bf16[4,128,384]{2,1,0:T(8,128)(2,1)S(1)}, u32[]{:S(2)}, u32[]{:S(2)}) async-start(bf16[4,128,384]{2,1,0:T(8,128)(2,1)} %bitcast.5), calls=%async_computation.2 | async-start | bytes 786432 | tf_op jit(solution)/shard_map/all_to_all | solution.py:184
  77.0 3.4 %collective-permute-start.2 = (bf16[128,768]{1,0:T(8,128)(2,1)S(1)}, bf16[128,768]{1,0:T(8,128)(2,1)S(1)}, u32[]{:S(2)}, u32[]{:S(2)}) collective-permute-start(bf16[128,768]{1,0:T(8,128)(2,1)S(1)} %shard_map.85), channel_id=1, source_target_pairs={{0,16},{16,0},{32,48},{48,32},{64,80},{80,64},{96,112},{112,96},{1... | collective-permute-start | bytes 589832 | tf_op jit(solution)/shard_map/ppermute | solution.py:191
  80.8 2.5 %all-to-all-done.2.share_ref = bf16[4,128,384]{2,1,0:T(8,128)(2,1)S(1)} async-done(((bf16[4,128,384]{2,1,0:T(8,128)(2,1)}), bf16[4,128,384]{2,1,0:T(8,128)(2,1)S(1)}, u32[]{:S(2)}, u32[]{:S(2)}) %all-to-all-start.2) | async-done | bytes 393248 | tf_op jit(solution)/shard_map/all_to_all | solution.py:184
  83.4 0.8 collective-permute-done.2.even_ref
  84.7 4.9 %collective-permute-start.5 = (bf16[1,128,384]{2,1,0:T(8,128)(2,1)S(1)}, bf16[1,128,384]{2,1,0:T(8,128)(2,1)S(1)}, u32[]{:S(2)}, u32[]{:S(2)}) collective-permute-start(bf16[1,128,384]{2,1,0:T(8,128)(2,1)S(1)} %shard_map.86), channel_id=1, source_target_pairs={{0,12},{4,8},{8,4},{12,0},{1,13},{5,9},{9,5},{13,1},{2,14},{6,10},... | collective-permute-start | bytes 294920 | tf_op jit(solution)/shard_map/ppermute | solution.py:195
  89.6 1.9 %collective-permute-start.4 = (bf16[1,128,384]{2,1,0:T(8,128)(2,1)S(1)}, bf16[1,128,384]{2,1,0:T(8,128)(2,1)S(1)}, u32[]{:S(2)}, u32[]{:S(2)}) collective-permute-start(bf16[1,128,384]{2,1,0:T(8,128)(2,1)S(1)} %shard_map.86), channel_id=1, source_target_pairs={{0,8},{4,12},{8,0},{12,4},{1,9},{5,13},{9,1},{13,5},{2,10},{6,14},... | collective-permute-start | bytes 294920 | tf_op jit(solution)/shard_map/ppermute | solution.py:195
  91.5 2.5 %collective-permute-start.3 = (bf16[1,128,384]{2,1,0:T(8,128)(2,1)S(1)}, bf16[1,128,384]{2,1,0:T(8,128)(2,1)S(1)}, u32[]{:S(2)}, u32[]{:S(2)}) collective-permute-start(bf16[1,128,384]{2,1,0:T(8,128)(2,1)S(1)} %shard_map.86), channel_id=1, source_target_pairs={{0,4},{4,0},{8,12},{12,8},{1,5},{5,1},{9,13},{13,9},{2,6},{6,2},{1... | collective-permute-start | bytes 294920 | tf_op jit(solution)/shard_map/ppermute | solution.py:195
  94.0 2.1 %collective-permute-done.4 = bf16[1,128,384]{2,1,0:T(8,128)(2,1)S(1)} collective-permute-done((bf16[1,128,384]{2,1,0:T(8,128)(2,1)S(1)}, bf16[1,128,384]{2,1,0:T(8,128)(2,1)S(1)}, u32[]{:S(2)}, u32[]{:S(2)}) %collective-permute-start.4) | collective-permute-done | bytes 98336 | tf_op jit(solution)/shard_map/ppermute | solution.py:195
  96.1 1.2 %collective-permute-done.3 = bf16[1,128,384]{2,1,0:T(8,128)(2,1)S(1)} collective-permute-done((bf16[1,128,384]{2,1,0:T(8,128)(2,1)S(1)}, bf16[1,128,384]{2,1,0:T(8,128)(2,1)S(1)}, u32[]{:S(2)}, u32[]{:S(2)}) %collective-permute-start.3) | collective-permute-done | bytes 98336 | tf_op jit(solution)/shard_map/ppermute | solution.py:195
  97.4 10.6 %all_gather.21 = bf16[8,128,384]{2,1,0:T(8,128)(2,1)S(1)} all-gather(bf16[4,128,384]{2,1,0:T(8,128)(2,1)S(1)} %pad_maximum_fusion), channel_id=1, replica_groups=mesh['z'=8,'x'=4,'y'=4,'core'=2,'cfg'=2] {'core'}, dimensions={0}, use_global_device_ids=true | all-gather | bytes 1179648 | tf_op jit(solution)/shard_map/all_gather | solution.py:198
  107.9 2.9 %fusion.1 = bf16[128,384]{1,0:T(8,128)(2,1)} fusion(bf16[8,128,384]{2,1,0:T(8,128)(2,1)S(1)} %all_gather.21, bf16[8,384,384]{2,1,0:T(8,128)(2,1)} %bitcast.27), kind=kOutput, calls=%fused_computation.4 | convolution fusion | flops 302039040 | bytes 3244032 | tf_op jit(solution)/shard_map/hrd,hdn->rn/dot_general | solution.py:199
  (30 shorter events, 1.5 us)
Async XLA Ops:
  6.5 49.6 %all-gather.4.cloned.1.call-start = ((), (), s32[]{:S(2)}) async-start(), calls=%async_computation.3 | async-start | bytes 1990656 | tf_op jit(solution)/shard_map/all_gather | solution.py:152
  9.9 16.3 %all-to-all-start = ((bf16[4,128,96]{1,2,0:T(8,128)(2,1)}), bf16[4,128,96]{1,2,0:T(8,128)(2,1)S(1)}, u32[]{:S(2)}, u32[]{:S(2)}) async-start(bf16[4,128,96]{1,2,0:T(8,128)(2,1)} %bitcast.1), calls=%async_computation | async-start | bytes 196608 | tf_op jit(solution)/shard_map/all_to_all | solution.py:166
  14.7 93.2 %all-gather.6.cloned.1.call-start = ((), (), s32[]{:S(2)}) async-start(), calls=%async_computation.4 | async-start | bytes 2654208 | tf_op jit(solution)/shard_map/all_gather | solution.py:172
  14.7 27.6 %collective-permute-start = (bf16[96,384]{1,0:T(8,128)(2,1)}, bf16[96,384]{1,0:T(8,128)(2,1)S(1)}, u32[]{:S(2)}, u32[]{:S(2)}) collective-permute-start(bf16[96,384]{1,0:T(8,128)(2,1)} %bitcast.30), channel_id=1, source_target_pairs={{0,0},{2,256},{4,64},{6,320},{8,128},{10,384},{12,192},{14,448},{6... | collective-permute-start | bytes 221192 | tf_op jit(solution)/shard_map/ppermute | solution.py:163
  59.1 11.9 %copy-start = (f32[128]{0:T(128)S(1)}, f32[128]{0:T(128)}, u32[]{:S(2)}) copy-start(f32[128]{0:T(128)} %param.14) | copy-start | bytes 1540
  59.1 11.9 %all-to-all-start.1 = ((bf16[4,128,768]{2,1,0:T(8,128)(2,1)}), bf16[4,128,768]{2,1,0:T(8,128)(2,1)S(1)}, u32[]{:S(2)}, u32[]{:S(2)}) async-start(bf16[4,128,768]{2,1,0:T(8,128)(2,1)} %bitcast.6), calls=%async_computation.1 | async-start | bytes 1572864 | tf_op jit(solution)/shard_map/all_to_all | solution.py:180
  62.9 17.6 %copy-start.2 = (s32[3,2,6]{2,1,0:T(2,128)S(1)}, s32[3,2,6]{2,1,0:T(2,128)}, u32[]{:S(2)}) copy-start(s32[3,2,6]{2,1,0:T(2,128)} %param.15) | copy-start | bytes 436
  62.9 20.4 %copy-start.1 = (f32[128]{0:T(128)S(1)}, f32[128]{0:T(128)}, u32[]{:S(2)}) copy-start(f32[128]{0:T(128)} %param.13) | copy-start | bytes 1540
  71.3 12.1 %collective-permute-start.1 = (bf16[128,768]{1,0:T(8,128)(2,1)S(1)}, bf16[128,768]{1,0:T(8,128)(2,1)S(1)}, u32[]{:S(2)}, u32[]{:S(2)}) collective-permute-start(bf16[128,768]{1,0:T(8,128)(2,1)S(1)} %shard_map.83.source_ref.own_ref), channel_id=1, source_target_pairs={{16,32},{32,16},{48,64},{64,48},{80,96},{96,80},{112,128},{128,112... | collective-permute-start | bytes 589832 | tf_op jit(solution)/shard_map/ppermute | solution.py:190
  72.0 11.3 %all-to-all-start.2 = ((bf16[4,128,384]{2,1,0:T(8,128)(2,1)}), bf16[4,128,384]{2,1,0:T(8,128)(2,1)S(1)}, u32[]{:S(2)}, u32[]{:S(2)}) async-start(bf16[4,128,384]{2,1,0:T(8,128)(2,1)} %bitcast.5), calls=%async_computation.2 | async-start | bytes 786432 | tf_op jit(solution)/shard_map/all_to_all | solution.py:184
  77.0 7.2 %collective-permute-start.2 = (bf16[128,768]{1,0:T(8,128)(2,1)S(1)}, bf16[128,768]{1,0:T(8,128)(2,1)S(1)}, u32[]{:S(2)}, u32[]{:S(2)}) collective-permute-start(bf16[128,768]{1,0:T(8,128)(2,1)S(1)} %shard_map.85), channel_id=1, source_target_pairs={{0,16},{16,0},{32,48},{48,32},{64,80},{80,64},{96,112},{112,96},{1... | collective-permute-start | bytes 589832 | tf_op jit(solution)/shard_map/ppermute | solution.py:191
  84.7 9.3 %collective-permute-start.5 = (bf16[1,128,384]{2,1,0:T(8,128)(2,1)S(1)}, bf16[1,128,384]{2,1,0:T(8,128)(2,1)S(1)}, u32[]{:S(2)}, u32[]{:S(2)}) collective-permute-start(bf16[1,128,384]{2,1,0:T(8,128)(2,1)S(1)} %shard_map.86), channel_id=1, source_target_pairs={{0,12},{4,8},{8,4},{12,0},{1,13},{5,9},{9,5},{13,1},{2,14},{6,10},... | collective-permute-start | bytes 294920 | tf_op jit(solution)/shard_map/ppermute | solution.py:195
  89.6 6.5 %collective-permute-start.4 = (bf16[1,128,384]{2,1,0:T(8,128)(2,1)S(1)}, bf16[1,128,384]{2,1,0:T(8,128)(2,1)S(1)}, u32[]{:S(2)}, u32[]{:S(2)}) collective-permute-start(bf16[1,128,384]{2,1,0:T(8,128)(2,1)S(1)} %shard_map.86), channel_id=1, source_target_pairs={{0,8},{4,12},{8,0},{12,4},{1,9},{5,13},{9,1},{13,5},{2,10},{6,14},... | collective-permute-start | bytes 294920 | tf_op jit(solution)/shard_map/ppermute | solution.py:195
  91.5 5.8 %collective-permute-start.3 = (bf16[1,128,384]{2,1,0:T(8,128)(2,1)S(1)}, bf16[1,128,384]{2,1,0:T(8,128)(2,1)S(1)}, u32[]{:S(2)}, u32[]{:S(2)}) collective-permute-start(bf16[1,128,384]{2,1,0:T(8,128)(2,1)S(1)} %shard_map.86), channel_id=1, source_target_pairs={{0,4},{4,0},{8,12},{12,8},{1,5},{5,1},{9,13},{13,9},{2,6},{6,2},{1... | collective-permute-start | bytes 294920 | tf_op jit(solution)/shard_map/ppermute | solution.py:195
Sparse Core Ops, SparseCore 0:
  9.4 46.6 all-gather.3
  58.2 45.3 all-gather.5

commit v26 on v24

--- a/solution.py
+++ b/solution.py
@@ -160,7 +160,7 @@
     pieces = lax.all_to_all(pieces, "x", split_axis=0, concat_axis=0, tiled=True)
     pieces = lax.all_gather(pieces.reshape(n_x * rows, part), HEAD, axis=0, tiled=False)
     pieces, columns = lax.optimization_barrier((pieces, columns))
-    group = pieces.transpose(1, 0, 2).reshape(n_x * rows, n_head * part)
+    group = copied(pieces.transpose(1, 0, 2).reshape(n_x * rows, n_head * part))
 
     columns = jnp.broadcast_to(columns[None], (n_x,) + columns.shape)
     columns = lax.all_to_all(columns, "x", split_axis=0, concat_axis=0, tiled=True)

time: 118 us -> 118 us (level)
  no operation moved by 1% of the time
where the time goes in v26:
time: 118 us; the launch traced here: 117 us
  blocking collectives  49.6 us (42%)
  starting transfers between devices  29 us (25%)
  between operations  13.5 us (11%)
  waiting for transfers between devices  10.7 us (9%)
  matrix products  8.24 us (7%)
  local copies, waits for them, and re-layouts  2.29 us (2%)
  other arithmetic  1.91 us (2%)
  Pallas kernels  1.74 us (1%)
    all_gather x1, blocking collectives, on_device(): lax.all_gather(pieces.reshape(n_x * rows, part), HEAD, axis=0, tiled=False)  16 us
    all_to_all x1, blocking collectives, on_device(): lax.all_to_all(attended, 'y', split_axis=0, concat_axis=0, tiled=True)  11.8 us
    ppermute x1, starting transfers between devices, on_device(): columns = lax.ppermute(out_weight.T, ('z',) + HEAD, turned)  11.5 us
    all_to_all x1, blocking collectives, on_device(): lax.all_to_all(columns, 'x', split_axis=0, concat_axis=0, tiled=True)  11 us
    all_gather x1, blocking collectives, on_device(): everyone = lax.all_gather(everyone, 'core', axis=0, tiled=True)  10.8 us
    all_to_all x1, waiting for transfers between devices, on_device(): lax.all_to_all(key_value, 'x', split_axis=0, concat_axis=0, tiled=True)  5.78 us
    dot_general x2, matrix products, shares(): jnp.dot(group, piece, preferred_element_type=jnp.float32)  5.35 us
    all_to_all x1, starting transfers between devices, on_device(): query = lax.all_to_all(query, 'x', split_axis=0, concat_axis=0, tiled=True)  5.02 us
  transfers between devices with their start and end apart: 8, of which 4 were waited for; matrix products, arithmetic and copies ran while one was open for 7% of the time, Pallas kernels for 1%

profile of v26, /device:TPU:1, one launch (start us, length us, event | category | flops | bytes accessed | tf_op | source)
XLA Modules:
  0.0 117.0 jit_solution(15752221516991599477)
XLA Ops:
  6.5 1.7 %pad_maximum_fusion = bf16[96,1152]{1,0:T(8,128)(2,1)} fusion(bf16[96,384]{1,0:T(8,128)(2,1)} %param.9, bf16[96,384]{1,0:T(8,128)(2,1)} %param.11, bf16[96,384]{1,0:T(8,128)(2,1)} %param.10), kind=kLoop, calls=%fused_computation.6 | loop fusion | flops 663552 | bytes 442368 | tf_op jit(solution)/shard_map/concatenate | solution.py:151
  8.2 1.6 %copy.16 = bf16[128,384]{0,1:T(8,128)(2,1)} copy(bf16[128,384]{1,0:T(8,128)(2,1)} %param.8) | data formatting | bytes 196608 | tf_op args[0]
  9.9 4.8 %all-to-all-start = ((bf16[4,128,96]{1,2,0:T(8,128)(2,1)}), bf16[4,128,96]{1,2,0:T(8,128)(2,1)S(1)}, u32[]{:S(2)}, u32[]{:S(2)}) async-start(bf16[4,128,96]{1,2,0:T(8,128)(2,1)} %bitcast.1), calls=%async_computation | async-start | bytes 196608 | tf_op jit(solution)/shard_map/all_to_all | solution.py:160
  14.7 11.5 %collective-permute-start = (bf16[96,384]{1,0:T(8,128)(2,1)}, bf16[96,384]{1,0:T(8,128)(2,1)S(1)}, u32[]{:S(2)}, u32[]{:S(2)}) collective-permute-start(bf16[96,384]{1,0:T(8,128)(2,1)} %bitcast.31), channel_id=1, source_target_pairs={{0,0},{2,256},{4,64},{6,320},{8,128},{10,384},{12,192},{14,448},{6... | collective-permute-start | bytes 221192 | tf_op jit(solution)/shard_map/ppermute | solution.py:157
  26.3 16.0 %all_gather.16 = bf16[8,512,96]{1,2,0:T(8,128)(2,1)S(1)} all-gather(bf16[1,512,96]{1,2,0:T(8,128)(2,1)S(1)} %all_gather_reshape.3), channel_id=1, replica_groups=mesh['z'=8,'x'=4,'y'=4,'core'=2,'cfg'=2] {'y','core'}, dimensions={0}, use_global_device_ids=true | all-gather | bytes 884736 | tf_op jit(solution)/shard_map/all_gather | solution.py:161
  42.3 11.0 %all_to_all.25 = bf16[4,96,384]{2,1,0:T(8,128)(2,1)S(1)} all-to-all(bf16[4,96,384]{2,1,0:T(8,128)(2,1)S(1)} %broadcast_in_dim.4), channel_id=1, replica_groups=mesh['z'=8,'x'=4,'y'=4,'core'=2,'cfg'=2] {'x'}, dimensions={0} | all-to-all | bytes 589824 | tf_op jit(solution)/shard_map/all_to_all | solution.py:166
  53.3 0.9 shard_map.83
  54.2 0.3 copy.18.source_ref
  54.5 1.6 %all-gather.4.cloned.1.call-done = bf16[768,1152]{1,0:T(8,128)(2,1)} async-done(((bf16[96,1152]{1,0:T(8,128)(2,1)}), bf16[768,1152]{1,0:T(8,128)(2,1)}) %all-gather.4.cloned.1.call-update) | async-done | bytes 1769488 | tf_op jit(solution)/shard_map/all_gather | solution.py:152
  56.1 2.9 %convolution_convert_fusion = bf16[512,768]{1,0:T(8,128)(2,1)} fusion(bf16[512,768]{1,0:T(8,128)(2,1)S(1)} %shard_map.82, bf16[768,1152]{1,0:T(8,128)(2,1)} %all-gather.4.cloned.1.call-done), kind=kOutput, calls=%fused_computation | convolution fusion | flops 604372992 | bytes 2752512 | tf_op jit(solution)/shard_map/dot_general | solution.py:172
  59.1 3.6 %all-to-all-start.2 = ((bf16[4,128,768]{2,1,0:T(8,128)(2,1)}), bf16[4,128,768]{2,1,0:T(8,128)(2,1)S(1)}, u32[]{:S(2)}, u32[]{:S(2)}) async-start(bf16[4,128,768]{2,1,0:T(8,128)(2,1)} %bitcast.7), calls=%async_computation.2 | async-start | bytes 1572864 | tf_op jit(solution)/shard_map/all_to_all | solution.py:176
  62.8 2.4 %convolution_convert_fusion.1 = bf16[512,384]{1,0:T(8,128)(2,1)} fusion(bf16[512,768]{1,0:T(8,128)(2,1)S(1)} %shard_map.82, bf16[768,1152]{1,0:T(8,128)(2,1)} %all-gather.4.cloned.1.call-done), kind=kOutput, calls=%fused_computation.1 | convolution fusion | flops 302186496 | bytes 1769472 | tf_op jit(solution)/shard_map/dot_general | solution.py:172
  65.2 5.8 %all-to-all-done.2.share_ref = bf16[4,128,768]{2,1,0:T(8,128)(2,1)S(1)} async-done(((bf16[4,128,768]{2,1,0:T(8,128)(2,1)}), bf16[4,128,768]{2,1,0:T(8,128)(2,1)S(1)}, u32[]{:S(2)}, u32[]{:S(2)}) %all-to-all-start.2) | async-done | bytes 786464 | tf_op jit(solution)/shard_map/all_to_all | solution.py:176
  71.0 0.2 shard_map.84.source_ref.own_ref
  71.2 0.7 collective-permute-start.1
  71.9 5.0 %all-to-all-start.3 = ((bf16[4,128,384]{2,1,0:T(8,128)(2,1)}), bf16[4,128,384]{2,1,0:T(8,128)(2,1)S(1)}, u32[]{:S(2)}, u32[]{:S(2)}) async-start(bf16[4,128,384]{2,1,0:T(8,128)(2,1)} %bitcast.6), calls=%async_computation.3 | async-start | bytes 786432 | tf_op jit(solution)/shard_map/all_to_all | solution.py:180
  76.9 3.4 %collective-permute-start.2 = (bf16[128,768]{1,0:T(8,128)(2,1)S(1)}, bf16[128,768]{1,0:T(8,128)(2,1)S(1)}, u32[]{:S(2)}, u32[]{:S(2)}) collective-permute-start(bf16[128,768]{1,0:T(8,128)(2,1)S(1)} %shard_map.86), channel_id=1, source_target_pairs={{0,16},{16,0},{32,48},{48,32},{64,80},{80,64},{96,112},{112,96},{1... | collective-permute-start | bytes 589832 | tf_op jit(solution)/shard_map/ppermute | solution.py:187
  80.7 2.4 %all-to-all-done.3.share_ref = bf16[4,128,384]{2,1,0:T(8,128)(2,1)S(1)} async-done(((bf16[4,128,384]{2,1,0:T(8,128)(2,1)}), bf16[4,128,384]{2,1,0:T(8,128)(2,1)S(1)}, u32[]{:S(2)}, u32[]{:S(2)}) %all-to-all-start.3) | async-done | bytes 393248 | tf_op jit(solution)/shard_map/all_to_all | solution.py:180
  83.2 0.1 shard_map.85.query_ref
  83.3 0.8 collective-permute-done.2.even_ref
  84.2 0.5 shard_map.87
  84.7 11.8 %all_to_all.26 = bf16[4,128,384]{2,1,0:T(8,128)(2,1)S(1)} all-to-all(bf16[4,128,384]{2,1,0:T(8,128)(2,1)S(1)} %shard_map.87), channel_id=1, replica_groups=mesh['z'=8,'x'=4,'y'=4,'core'=2,'cfg'=2] {'y'}, dimensions={0} | all-to-all | bytes 786432 | tf_op jit(solution)/shard_map/all_to_all | solution.py:190
  96.4 10.8 %all_gather.17 = bf16[8,128,384]{2,1,0:T(8,128)(2,1)S(1)} all-gather(bf16[4,128,384]{2,1,0:T(8,128)(2,1)S(1)} %all_to_all.26), channel_id=1, replica_groups=mesh['z'=8,'x'=4,'y'=4,'core'=2,'cfg'=2] {'core'}, dimensions={0}, use_global_device_ids=true | all-gather | bytes 1179648 | tf_op jit(solution)/shard_map/all_gather | solution.py:191
  107.3 2.9 %fusion.1 = bf16[128,384]{1,0:T(8,128)(2,1)} fusion(bf16[8,128,384]{2,1,0:T(8,128)(2,1)S(1)} %all_gather.17, bf16[8,384,384]{2,1,0:T(8,128)(2,1)} %bitcast.30), kind=kOutput, calls=%fused_computation.4 | convolution fusion | flops 302039040 | bytes 3244032 | tf_op jit(solution)/shard_map/hrd,hdn->rn/dot_general | solution.py:192
  (27 shorter events, 0.7 us)
Async XLA Ops:
  6.5 49.6 %all-gather.4.cloned.1.call-start = ((), (), s32[]{:S(2)}) async-start(), calls=%async_computation.5 | async-start | bytes 1990656 | tf_op jit(solution)/shard_map/all_gather | solution.py:152
  9.9 16.3 %all-to-all-start = ((bf16[4,128,96]{1,2,0:T(8,128)(2,1)}), bf16[4,128,96]{1,2,0:T(8,128)(2,1)S(1)}, u32[]{:S(2)}, u32[]{:S(2)}) async-start(bf16[4,128,96]{1,2,0:T(8,128)(2,1)} %bitcast.1), calls=%async_computation | async-start | bytes 196608 | tf_op jit(solution)/shard_map/all_to_all | solution.py:160
  14.7 92.5 %all-gather.6.cloned.1.call-start = ((), (), s32[]{:S(2)}) async-start(), calls=%async_computation.6 | async-start | bytes 2654208 | tf_op jit(solution)/shard_map/all_gather | solution.py:168
  14.7 27.6 %collective-permute-start = (bf16[96,384]{1,0:T(8,128)(2,1)}, bf16[96,384]{1,0:T(8,128)(2,1)S(1)}, u32[]{:S(2)}, u32[]{:S(2)}) collective-permute-start(bf16[96,384]{1,0:T(8,128)(2,1)} %bitcast.31), channel_id=1, source_target_pairs={{0,0},{2,256},{4,64},{6,320},{8,128},{10,384},{12,192},{14,448},{6... | collective-permute-start | bytes 221192 | tf_op jit(solution)/shard_map/ppermute | solution.py:157
  59.1 11.9 %copy-start = (f32[128]{0:T(128)S(1)}, f32[128]{0:T(128)}, u32[]{:S(2)}) copy-start(f32[128]{0:T(128)} %param.14) | copy-start | bytes 1540
  59.1 11.9 %all-to-all-start.2 = ((bf16[4,128,768]{2,1,0:T(8,128)(2,1)}), bf16[4,128,768]{2,1,0:T(8,128)(2,1)S(1)}, u32[]{:S(2)}, u32[]{:S(2)}) async-start(bf16[4,128,768]{2,1,0:T(8,128)(2,1)} %bitcast.7), calls=%async_computation.2 | async-start | bytes 1572864 | tf_op jit(solution)/shard_map/all_to_all | solution.py:176
  62.8 17.7 %copy-start.2 = (s32[3,2,6]{2,1,0:T(2,128)S(1)}, s32[3,2,6]{2,1,0:T(2,128)}, u32[]{:S(2)}) copy-start(s32[3,2,6]{2,1,0:T(2,128)} %param.15) | copy-start | bytes 436
  62.8 20.4 %copy-start.1 = (f32[128]{0:T(128)S(1)}, f32[128]{0:T(128)}, u32[]{:S(2)}) copy-start(f32[128]{0:T(128)} %param.13) | copy-start | bytes 1540
  71.2 12.1 %collective-permute-start.1 = (bf16[128,768]{1,0:T(8,128)(2,1)S(1)}, bf16[128,768]{1,0:T(8,128)(2,1)S(1)}, u32[]{:S(2)}, u32[]{:S(2)}) collective-permute-start(bf16[128,768]{1,0:T(8,128)(2,1)S(1)} %shard_map.84.source_ref.own_ref), channel_id=1, source_target_pairs={{16,32},{32,16},{48,64},{64,48},{80,96},{96,80},{112,128},{128,112... | collective-permute-start | bytes 589832 | tf_op jit(solution)/shard_map/ppermute | solution.py:186
  71.9 11.3 %all-to-all-start.3 = ((bf16[4,128,384]{2,1,0:T(8,128)(2,1)}), bf16[4,128,384]{2,1,0:T(8,128)(2,1)S(1)}, u32[]{:S(2)}, u32[]{:S(2)}) async-start(bf16[4,128,384]{2,1,0:T(8,128)(2,1)} %bitcast.6), calls=%async_computation.3 | async-start | bytes 786432 | tf_op jit(solution)/shard_map/all_to_all | solution.py:180
  76.9 7.2 %collective-permute-start.2 = (bf16[128,768]{1,0:T(8,128)(2,1)S(1)}, bf16[128,768]{1,0:T(8,128)(2,1)S(1)}, u32[]{:S(2)}, u32[]{:S(2)}) collective-permute-start(bf16[128,768]{1,0:T(8,128)(2,1)S(1)} %shard_map.86), channel_id=1, source_target_pairs={{0,16},{16,0},{32,48},{48,32},{64,80},{80,64},{96,112},{112,96},{1... | collective-permute-start | bytes 589832 | tf_op jit(solution)/shard_map/ppermute | solution.py:187
Sparse Core Ops, SparseCore 0:
  9.4 46.6 all-gather.3
  58.2 45.1 all-gather.5

commit v27 on v26

--- a/solution.py
+++ b/solution.py
@@ -152,8 +152,14 @@
     weights = lax.all_gather(stacked, "z", axis=0, tiled=True)
 
     n_core = lax.axis_size("core")
-    rank = [h % n_core * (n_head // n_core) + h // n_core for h in range(n_head)]
-    turned = [(z * n_head + h, rank[h] * n_z + z) for z in range(n_z) for h in range(n_head)]
+    n_y = n_head // n_core
+
+    def place_of(head, column):
+        return (head + column) % n_core * n_y + head // n_core
+
+    turned = [
+        (z * n_head + h, place_of(h, z) * n_z + z) for z in range(n_z) for h in range(n_head)
+    ]
     columns = lax.ppermute(out_weight.T, ("z",) + HEAD, turned)
 
     pieces = tokens.reshape(rows, n_x, part).transpose(1, 0, 2)
@@ -188,7 +194,8 @@
     live = live_rows(key_tiles, rows // TILE)
     attended = attention(n_head // n_core, normed_query(query, q_gain), live, odd, packed, even)
     everyone = lax.all_to_all(attended, "y", split_axis=0, concat_axis=0, tiled=True)
-    everyone = lax.all_gather(everyone, "core", axis=0, tiled=True)
+    other = lax.ppermute(everyone, "core", [(i, (i + 1) % n_core) for i in range(n_core)])
+    everyone = jnp.concatenate([everyone, other], axis=0)
     total = jnp.einsum("hrd,hdn->rn", everyone, projection, preferred_element_type=jnp.float32)
     return total.astype(jnp.bfloat16)
 

time: 118 us -> 122 us (1.034)
  blocking collectives: 49.6 us -> 38.3 us
  starting transfers between devices: 29 us -> 39.9 us
  waiting for transfers between devices: 10.7 us -> 15.3 us
    ppermute x0 -> x1, starting transfers between devices: none -> 11.3 us  [on_device(): lax.ppermute(everyone, 'core', [(i, (i + 1) % n_core) for i in range(n_co...]
    all_gather x1 -> x0, blocking collectives: 10.8 us -> none  [on_device(): everyone = lax.all_gather(everyone, 'core', axis=0, tiled=True)]
    all_to_all x1, waiting for transfers between devices: 2.44 us -> 5.81 us  [on_device(): query = lax.all_to_all(query, 'x', split_axis=0, concat_axis=0, tiled=True)]
    all_to_all x1, starting transfers between devices: 5.02 us -> 3.47 us  [on_device(): query = lax.all_to_all(query, 'x', split_axis=0, concat_axis=0, tiled=True)]
    ppermute x0 -> x1, waiting for transfers between devices: none -> 1.3 us  [on_device(): lax.ppermute(everyone, 'core', [(i, (i + 1) % n_core) for i in range(n_co...]
  transfers between devices with their start and end apart: 8 -> 9, of which waited for: 4 -> 4; matrix products, arithmetic and copies ran while one was open for 7% -> 7% of each run, Pallas kernels for 1% -> 1%
where the time goes in v27:
time: 122 us; the launch traced here: 121 us
  starting transfers between devices  39.9 us (33%)
  blocking collectives  38.3 us (31%)
  waiting for transfers between devices  15.3 us (13%)
  between operations  13.5 us (11%)
  matrix products  8.25 us (7%)
  local copies, waits for them, and re-layouts  2.29 us (2%)
  other arithmetic  1.91 us (2%)
  Pallas kernels  1.73 us (1%)
    all_gather x1, blocking collectives, on_device(): lax.all_gather(pieces.reshape(n_x * rows, part), HEAD, axis=0, tiled=False)  15.8 us
    ppermute x1, starting transfers between devices, on_device(): columns = lax.ppermute(out_weight.T, ('z',) + HEAD, turned)  11.5 us
    all_to_all x1, blocking collectives, on_device(): lax.all_to_all(attended, 'y', split_axis=0, concat_axis=0, tiled=True)  11.3 us
    ppermute x1, starting transfers between devices, on_device(): lax.ppermute(everyone, 'core', [(i, (i + 1) % n_core) for i in range(n_co...  11.3 us
    all_to_all x1, blocking collectives, on_device(): lax.all_to_all(columns, 'x', split_axis=0, concat_axis=0, tiled=True)  11.2 us
    all_to_all x1, waiting for transfers between devices, on_device(): lax.all_to_all(key_value, 'x', split_axis=0, concat_axis=0, tiled=True)  6.44 us
    all_to_all x1, waiting for transfers between devices, on_device(): query = lax.all_to_all(query, 'x', split_axis=0, concat_axis=0, tiled=True)  5.81 us
    dot_general x2, matrix products, shares(): jnp.dot(group, piece, preferred_element_type=jnp.float32)  5.36 us
  transfers between devices with their start and end apart: 9, of which 4 were waited for; matrix products, arithmetic and copies ran while one was open for 7% of the time, Pallas kernels for 1%

profile of v27, /device:TPU:1, one launch (start us, length us, event | category | flops | bytes accessed | tf_op | source)
XLA Modules:
  0.0 121.2 jit_solution(6103710755790352694)
XLA Ops:
  6.5 1.7 %pad_maximum_fusion = bf16[96,1152]{1,0:T(8,128)(2,1)} fusion(bf16[96,384]{1,0:T(8,128)(2,1)} %param.9, bf16[96,384]{1,0:T(8,128)(2,1)} %param.11, bf16[96,384]{1,0:T(8,128)(2,1)} %param.10), kind=kLoop, calls=%fused_computation.9 | loop fusion | flops 663552 | bytes 442368 | tf_op jit(solution)/shard_map/concatenate | solution.py:151
  8.2 1.6 %copy.16 = bf16[128,384]{0,1:T(8,128)(2,1)} copy(bf16[128,384]{1,0:T(8,128)(2,1)} %param.8) | data formatting | bytes 196608 | tf_op args[0]
  9.9 4.8 %all-to-all-start = ((bf16[4,128,96]{1,2,0:T(8,128)(2,1)}), bf16[4,128,96]{1,2,0:T(8,128)(2,1)S(1)}, u32[]{:S(2)}, u32[]{:S(2)}) async-start(bf16[4,128,96]{1,2,0:T(8,128)(2,1)} %bitcast.1), calls=%async_computation | async-start | bytes 196608 | tf_op jit(solution)/shard_map/all_to_all | solution.py:166
  14.7 11.5 %collective-permute-start = (bf16[96,384]{1,0:T(8,128)(2,1)}, bf16[96,384]{1,0:T(8,128)(2,1)S(1)}, u32[]{:S(2)}, u32[]{:S(2)}) collective-permute-start(bf16[96,384]{1,0:T(8,128)(2,1)} %bitcast.30), channel_id=1, source_target_pairs={{0,0},{2,256},{4,64},{6,320},{8,128},{10,384},{12,192},{14,448},{6... | collective-permute-start | bytes 221192 | tf_op jit(solution)/shard_map/ppermute | solution.py:163
  26.3 15.8 %all_gather.13 = bf16[8,512,96]{1,2,0:T(8,128)(2,1)S(1)} all-gather(bf16[1,512,96]{1,2,0:T(8,128)(2,1)S(1)} %all_gather_reshape.3), channel_id=1, replica_groups=mesh['z'=8,'x'=4,'y'=4,'core'=2,'cfg'=2] {'y','core'}, dimensions={0}, use_global_device_ids=true | all-gather | bytes 884736 | tf_op jit(solution)/shard_map/all_gather | solution.py:167
  42.1 11.2 %all_to_all.25 = bf16[4,96,384]{2,1,0:T(8,128)(2,1)S(1)} all-to-all(bf16[4,96,384]{2,1,0:T(8,128)(2,1)S(1)} %broadcast_in_dim.4), channel_id=1, replica_groups=mesh['z'=8,'x'=4,'y'=4,'core'=2,'cfg'=2] {'x'}, dimensions={0} | all-to-all | bytes 589824 | tf_op jit(solution)/shard_map/all_to_all | solution.py:172
  53.3 0.9 shard_map.83
  54.2 0.3 copy.18.source_ref
  54.5 1.7 %all-gather.4.cloned.1.call-done = bf16[768,1152]{1,0:T(8,128)(2,1)} async-done(((bf16[96,1152]{1,0:T(8,128)(2,1)}), bf16[768,1152]{1,0:T(8,128)(2,1)}) %all-gather.4.cloned.1.call-update) | async-done | bytes 1769488 | tf_op jit(solution)/shard_map/all_gather | solution.py:152
  56.2 2.9 %convolution_convert_fusion = bf16[512,768]{1,0:T(8,128)(2,1)} fusion(bf16[512,768]{1,0:T(8,128)(2,1)S(1)} %shard_map.82, bf16[768,1152]{1,0:T(8,128)(2,1)} %all-gather.4.cloned.1.call-done), kind=kOutput, calls=%fused_computation | convolution fusion | flops 604372992 | bytes 2752512 | tf_op jit(solution)/shard_map/dot_general | solution.py:178
  59.2 4.7 %all-to-all-start.2 = ((bf16[4,128,768]{2,1,0:T(8,128)(2,1)}), bf16[4,128,768]{2,1,0:T(8,128)(2,1)S(1)}, u32[]{:S(2)}, u32[]{:S(2)}) async-start(bf16[4,128,768]{2,1,0:T(8,128)(2,1)} %bitcast.7), calls=%async_computation.2 | async-start | bytes 1572864 | tf_op jit(solution)/shard_map/all_to_all | solution.py:182
  63.9 2.4 %convolution_convert_fusion.1 = bf16[512,384]{1,0:T(8,128)(2,1)} fusion(bf16[512,768]{1,0:T(8,128)(2,1)S(1)} %shard_map.82, bf16[768,1152]{1,0:T(8,128)(2,1)} %all-gather.4.cloned.1.call-done), kind=kOutput, calls=%fused_computation.1 | convolution fusion | flops 302186496 | bytes 1769472 | tf_op jit(solution)/shard_map/dot_general | solution.py:178
  66.3 6.4 %all-to-all-done.2.share_ref = bf16[4,128,768]{2,1,0:T(8,128)(2,1)S(1)} async-done(((bf16[4,128,768]{2,1,0:T(8,128)(2,1)}), bf16[4,128,768]{2,1,0:T(8,128)(2,1)S(1)}, u32[]{:S(2)}, u32[]{:S(2)}) %all-to-all-start.2) | async-done | bytes 786464 | tf_op jit(solution)/shard_map/all_to_all | solution.py:182
  72.8 0.2 shard_map.84.source_ref.own_ref
  73.0 0.7 collective-permute-start.1
  73.7 3.4 %collective-permute-start.2 = (bf16[128,768]{1,0:T(8,128)(2,1)S(1)}, bf16[128,768]{1,0:T(8,128)(2,1)S(1)}, u32[]{:S(2)}, u32[]{:S(2)}) collective-permute-start(bf16[128,768]{1,0:T(8,128)(2,1)S(1)} %shard_map.86), channel_id=1, source_target_pairs={{0,16},{16,0},{32,48},{48,32},{64,80},{80,64},{96,112},{112,96},{1... | collective-permute-start | bytes 589832 | tf_op jit(solution)/shard_map/ppermute | solution.py:193
  77.1 3.5 %all-to-all-start.3 = ((bf16[4,128,384]{2,1,0:T(8,128)(2,1)}), bf16[4,128,384]{2,1,0:T(8,128)(2,1)S(1)}, u32[]{:S(2)}, u32[]{:S(2)}) async-start(bf16[4,128,384]{2,1,0:T(8,128)(2,1)} %bitcast.6), calls=%async_computation.3 | async-start | bytes 786432 | tf_op jit(solution)/shard_map/all_to_all | solution.py:186
  81.0 5.8 %all-to-all-done.3.share_ref = bf16[4,128,384]{2,1,0:T(8,128)(2,1)S(1)} async-done(((bf16[4,128,384]{2,1,0:T(8,128)(2,1)}), bf16[4,128,384]{2,1,0:T(8,128)(2,1)S(1)}, u32[]{:S(2)}, u32[]{:S(2)}) %all-to-all-start.3) | async-done | bytes 393248 | tf_op jit(solution)/shard_map/all_to_all | solution.py:186
  86.9 0.1 shard_map.85.query_ref
  87.0 0.5 shard_map.87
  87.5 11.3 %all_to_all.26 = bf16[4,128,384]{2,1,0:T(8,128)(2,1)S(1)} all-to-all(bf16[4,128,384]{2,1,0:T(8,128)(2,1)S(1)} %shard_map.87), channel_id=1, replica_groups=mesh['z'=8,'x'=4,'y'=4,'core'=2,'cfg'=2] {'y'}, dimensions={0} | all-to-all | bytes 786432 | tf_op jit(solution)/shard_map/all_to_all | solution.py:196
  98.9 11.3 %collective-permute-start.3 = (bf16[4,128,384]{2,1,0:T(8,128)(2,1)S(1)}, bf16[4,128,384]{2,1,0:T(8,128)(2,1)S(1)}, u32[]{:S(2)}, u32[]{:S(2)}) collective-permute-start(bf16[4,128,384]{2,1,0:T(8,128)(2,1)S(1)} %all_to_all.26), channel_id=1, source_target_pairs={{0,2},{2,0},{1,3},{3,1},{4,6},{6,4},{5,7},{7,5},{8,10},{10,8},{9,1... | collective-permute-start | bytes 1179656 | tf_op jit(solution)/shard_map/ppermute | solution.py:197
  110.2 1.3 %collective-permute-done.3 = bf16[4,128,384]{2,1,0:T(8,128)(2,1)S(1)} collective-permute-done((bf16[4,128,384]{2,1,0:T(8,128)(2,1)S(1)}, bf16[4,128,384]{2,1,0:T(8,128)(2,1)S(1)}, u32[]{:S(2)}, u32[]{:S(2)}) %collective-permute-start.3) | collective-permute-done | bytes 393248 | tf_op jit(solution)/shard_map/ppermute | solution.py:197
  111.5 2.9 %fusion.1 = bf16[128,384]{1,0:T(8,128)(2,1)} fusion(bf16[8,384,384]{2,1,0:T(8,128)(2,1)} %bitcast.29, bf16[4,128,384]{2,1,0:T(8,128)(2,1)S(1)} %collective-permute-done.3, bf16[4,128,384]{2,1,0:T(8,128)(2,1)S(1)} %all_to_all.26), kind=kOutput, calls=%fused_computation.4 | convolution fusion | flops 302432256 | bytes 3244032 | tf_op jit(solution)/shard_map/hrd,hdn->rn/dot_general | solution.py:199
  (28 shorter events, 0.8 us)
Async XLA Ops:
  6.5 49.7 %all-gather.4.cloned.1.call-start = ((), (), s32[]{:S(2)}) async-start(), calls=%async_computation.5 | async-start | bytes 1990656 | tf_op jit(solution)/shard_map/all_gather | solution.py:152
  9.9 16.3 %all-to-all-start = ((bf16[4,128,96]{1,2,0:T(8,128)(2,1)}), bf16[4,128,96]{1,2,0:T(8,128)(2,1)S(1)}, u32[]{:S(2)}, u32[]{:S(2)}) async-start(bf16[4,128,96]{1,2,0:T(8,128)(2,1)} %bitcast.1), calls=%async_computation | async-start | bytes 196608 | tf_op jit(solution)/shard_map/all_to_all | solution.py:166
  14.7 95.5 %all-gather.6.cloned.1.call-start = ((), (), s32[]{:S(2)}) async-start(), calls=%async_computation.6 | async-start | bytes 2654208 | tf_op jit(solution)/shard_map/all_gather | solution.py:174
  14.7 27.4 %collective-permute-start = (bf16[96,384]{1,0:T(8,128)(2,1)}, bf16[96,384]{1,0:T(8,128)(2,1)S(1)}, u32[]{:S(2)}, u32[]{:S(2)}) collective-permute-start(bf16[96,384]{1,0:T(8,128)(2,1)} %bitcast.30), channel_id=1, source_target_pairs={{0,0},{2,256},{4,64},{6,320},{8,128},{10,384},{12,192},{14,448},{6... | collective-permute-start | bytes 221192 | tf_op jit(solution)/shard_map/ppermute | solution.py:163
  59.2 13.6 %copy-start = (f32[128]{0:T(128)S(1)}, f32[128]{0:T(128)}, u32[]{:S(2)}) copy-start(f32[128]{0:T(128)} %param.14) | copy-start | bytes 1540
  59.2 13.6 %all-to-all-start.2 = ((bf16[4,128,768]{2,1,0:T(8,128)(2,1)}), bf16[4,128,768]{2,1,0:T(8,128)(2,1)S(1)}, u32[]{:S(2)}, u32[]{:S(2)}) async-start(bf16[4,128,768]{2,1,0:T(8,128)(2,1)} %bitcast.7), calls=%async_computation.2 | async-start | bytes 1572864 | tf_op jit(solution)/shard_map/all_to_all | solution.py:182
  63.9 16.8 %copy-start.2 = (s32[3,2,6]{2,1,0:T(2,128)S(1)}, s32[3,2,6]{2,1,0:T(2,128)}, u32[]{:S(2)}) copy-start(s32[3,2,6]{2,1,0:T(2,128)} %param.15) | copy-start | bytes 436
  63.9 22.9 %copy-start.1 = (f32[128]{0:T(128)S(1)}, f32[128]{0:T(128)}, u32[]{:S(2)}) copy-start(f32[128]{0:T(128)} %param.13) | copy-start | bytes 1540
  73.0 14.0 %collective-permute-start.1 = (bf16[128,768]{1,0:T(8,128)(2,1)S(1)}, bf16[128,768]{1,0:T(8,128)(2,1)S(1)}, u32[]{:S(2)}, u32[]{:S(2)}) collective-permute-start(bf16[128,768]{1,0:T(8,128)(2,1)S(1)} %shard_map.84.source_ref.own_ref), channel_id=1, source_target_pairs={{16,32},{32,16},{48,64},{64,48},{80,96},{96,80},{112,128},{128,112... | collective-permute-start | bytes 589832 | tf_op jit(solution)/shard_map/ppermute | solution.py:192
  73.7 13.3 %collective-permute-start.2 = (bf16[128,768]{1,0:T(8,128)(2,1)S(1)}, bf16[128,768]{1,0:T(8,128)(2,1)S(1)}, u32[]{:S(2)}, u32[]{:S(2)}) collective-permute-start(bf16[128,768]{1,0:T(8,128)(2,1)S(1)} %shard_map.86), channel_id=1, source_target_pairs={{0,16},{16,0},{32,48},{48,32},{64,80},{80,64},{96,112},{112,96},{1... | collective-permute-start | bytes 589832 | tf_op jit(solution)/shard_map/ppermute | solution.py:193
  77.1 9.7 %all-to-all-start.3 = ((bf16[4,128,384]{2,1,0:T(8,128)(2,1)}), bf16[4,128,384]{2,1,0:T(8,128)(2,1)S(1)}, u32[]{:S(2)}, u32[]{:S(2)}) async-start(bf16[4,128,384]{2,1,0:T(8,128)(2,1)} %bitcast.6), calls=%async_computation.3 | async-start | bytes 786432 | tf_op jit(solution)/shard_map/all_to_all | solution.py:186
  98.9 12.6 %collective-permute-start.3 = (bf16[4,128,384]{2,1,0:T(8,128)(2,1)S(1)}, bf16[4,128,384]{2,1,0:T(8,128)(2,1)S(1)}, u32[]{:S(2)}, u32[]{:S(2)}) collective-permute-start(bf16[4,128,384]{2,1,0:T(8,128)(2,1)S(1)} %all_to_all.26), channel_id=1, source_target_pairs={{0,2},{2,0},{1,3},{3,1},{4,6},{6,4},{5,7},{7,5},{8,10},{10,8},{9,1... | collective-permute-start | bytes 1179656 | tf_op jit(solution)/shard_map/ppermute | solution.py:197
Sparse Core Ops, SparseCore 0:
  9.4 46.7 all-gather.3
  58.3 45.7 all-gather.5

commit v28 on v26

--- a/solution.py
+++ b/solution.py
@@ -159,7 +159,6 @@
     pieces = tokens.reshape(rows, n_x, part).transpose(1, 0, 2)
     pieces = lax.all_to_all(pieces, "x", split_axis=0, concat_axis=0, tiled=True)
     pieces = lax.all_gather(pieces.reshape(n_x * rows, part), HEAD, axis=0, tiled=False)
-    pieces, columns = lax.optimization_barrier((pieces, columns))
     group = copied(pieces.transpose(1, 0, 2).reshape(n_x * rows, n_head * part))
 
     columns = jnp.broadcast_to(columns[None], (n_x,) + columns.shape)

time: 118 us -> 127 us (1.076)
  waiting for transfers between devices: 10.7 us -> 17.6 us
  blocking collectives: 49.6 us -> 55.4 us
  starting transfers between devices: 29 us -> 27 us
  local copies, waits for them, and re-layouts: 2.29 us -> 0.77 us
    all_to_all x0 -> x1, blocking collectives: none -> 7.03 us  [on_device(): lax.all_to_all(pieces, 'x', split_axis=0, concat_axis=0, tiled=True)]
    all_gather x1, blocking collectives: 10.8 us -> 5.15 us  [on_device(): everyone = lax.all_gather(everyone, 'core', axis=0, tiled=True)]
    all_to_all x1 -> x0, starting transfers between devices: 4.84 us -> none  [on_device(): lax.all_to_all(pieces, 'x', split_axis=0, concat_axis=0, tiled=True)]
    all_gather x1, blocking collectives: 16 us -> 20.2 us  [on_device(): lax.all_gather(pieces.reshape(n_x * rows, part), HEAD, axis=0, tiled=False)]
    all_to_all x1, waiting for transfers between devices: 5.78 us -> 9.72 us  [on_device(): lax.all_to_all(key_value, 'x', split_axis=0, concat_axis=0, tiled=True)]
    ppermute x1, waiting for transfers between devices: 0.01 us -> 2.41 us  [on_device(): columns = lax.ppermute(out_weight.T, ('z',) + HEAD, turned)]
    all_to_all x1, starting transfers between devices: 5.02 us -> 7.29 us  [on_device(): query = lax.all_to_all(query, 'x', split_axis=0, concat_axis=0, tiled=True)]
    ppermute x1, waiting for transfers between devices: 0.84 us -> 2.9 us  [on_device(): even = lax.ppermute(copied(packed), SLAB, swaps[1])]
  transfers between devices with their start and end apart: 8 -> 7, of which waited for: 4 -> 4; matrix products, arithmetic and copies ran while one was open for 7% -> 5% of each run, Pallas kernels for 1% -> 1%
where the time goes in v28:
time: 127 us; the launch traced here: 126 us
  blocking collectives  55.4 us (44%)
  starting transfers between devices  27 us (21%)
  waiting for transfers between devices  17.6 us (14%)
  between operations  13.5 us (11%)
  matrix products  8.25 us (6%)
  other arithmetic  1.94 us (2%)
  Pallas kernels  1.75 us (1%)
    all_gather x1, blocking collectives, on_device(): lax.all_gather(pieces.reshape(n_x * rows, part), HEAD, axis=0, tiled=False)  20.2 us
    all_to_all x1, blocking collectives, on_device(): lax.all_to_all(attended, 'y', split_axis=0, concat_axis=0, tiled=True)  13.5 us
    ppermute x1, starting transfers between devices, on_device(): columns = lax.ppermute(out_weight.T, ('z',) + HEAD, turned)  12 us
    all_to_all x1, waiting for transfers between devices, on_device(): lax.all_to_all(key_value, 'x', split_axis=0, concat_axis=0, tiled=True)  9.72 us
    all_to_all x1, blocking collectives, on_device(): lax.all_to_all(columns, 'x', split_axis=0, concat_axis=0, tiled=True)  9.52 us
    all_to_all x1, starting transfers between devices, on_device(): query = lax.all_to_all(query, 'x', split_axis=0, concat_axis=0, tiled=True)  7.29 us
    all_to_all x1, blocking collectives, on_device(): lax.all_to_all(pieces, 'x', split_axis=0, concat_axis=0, tiled=True)  7.03 us
    dot_general x2, matrix products, shares(): jnp.dot(group, piece, preferred_element_type=jnp.float32)  5.35 us
  transfers between devices with their start and end apart: 7, of which 4 were waited for; matrix products, arithmetic and copies ran while one was open for 5% of the time, Pallas kernels for 1%

profile of v28, /device:TPU:1, one launch (start us, length us, event | category | flops | bytes accessed | tf_op | source)
XLA Modules:
  0.0 126.2 jit_solution(14921075609057942907)
XLA Ops:
  6.5 1.7 %pad_maximum_fusion = bf16[96,1152]{1,0:T(8,128)(2,1)} fusion(bf16[96,384]{1,0:T(8,128)(2,1)} %param.9, bf16[96,384]{1,0:T(8,128)(2,1)} %param.11, bf16[96,384]{1,0:T(8,128)(2,1)} %param.10), kind=kLoop, calls=%fused_computation.6 | loop fusion | flops 663552 | bytes 442368 | tf_op jit(solution)/shard_map/concatenate | solution.py:151
  8.3 12.0 %collective-permute-start = (bf16[96,384]{1,0:T(8,128)(2,1)}, bf16[96,384]{1,0:T(8,128)(2,1)S(1)}, u32[]{:S(2)}, u32[]{:S(2)}) collective-permute-start(bf16[96,384]{1,0:T(8,128)(2,1)} %bitcast.32), channel_id=1, source_target_pairs={{0,0},{2,256},{4,64},{6,320},{8,128},{10,384},{12,192},{14,448},{6... | collective-permute-start | bytes 221192 | tf_op jit(solution)/shard_map/ppermute | solution.py:157
  20.3 2.4 %collective-permute-done = bf16[96,384]{1,0:T(8,128)(2,1)S(1)} collective-permute-done((bf16[96,384]{1,0:T(8,128)(2,1)}, bf16[96,384]{1,0:T(8,128)(2,1)S(1)}, u32[]{:S(2)}, u32[]{:S(2)}) %collective-permute-start) | collective-permute-done | bytes 73760 | tf_op jit(solution)/shard_map/ppermute | solution.py:157
  22.8 9.5 %all_to_all.25 = bf16[4,96,384]{2,1,0:T(8,128)(2,1)S(1)} all-to-all(bf16[4,96,384]{2,1,0:T(8,128)(2,1)S(1)} %broadcast_in_dim.4), channel_id=1, replica_groups=mesh['z'=8,'x'=4,'y'=4,'core'=2,'cfg'=2] {'x'}, dimensions={0} | all-to-all | bytes 589824 | tf_op jit(solution)/shard_map/all_to_all | solution.py:165
  32.3 0.9 shard_map.83
  33.2 0.1 copy.16
  33.3 7.0 %all_to_all.26 = bf16[4,128,96]{1,2,0:T(8,128)(2,1)S(1)} all-to-all(bf16[4,128,96]{1,2,0:T(8,128)(2,1)S(1)} %bitcast.31), channel_id=1, replica_groups=mesh['z'=8,'x'=4,'y'=4,'core'=2,'cfg'=2] {'x'}, dimensions={0} | all-to-all | bytes 196608 | tf_op jit(solution)/shard_map/all_to_all | solution.py:160
  40.5 20.2 %all_gather.16 = bf16[8,512,96]{1,2,0:T(8,128)(2,1)S(1)} all-gather(bf16[1,512,96]{1,2,0:T(8,128)(2,1)S(1)} %all_gather_reshape.3), channel_id=1, replica_groups=mesh['z'=8,'x'=4,'y'=4,'core'=2,'cfg'=2] {'y','core'}, dimensions={0}, use_global_device_ids=true | all-gather | bytes 884736 | tf_op jit(solution)/shard_map/all_gather | solution.py:161
  60.6 0.3 copy.18.source_ref
  61.0 2.9 %convolution_convert_fusion = bf16[512,768]{1,0:T(8,128)(2,1)} fusion(bf16[512,768]{1,0:T(8,128)(2,1)S(1)} %shard_map.82, bf16[768,1152]{1,0:T(8,128)(2,1)} %all-gather.4.cloned.1.call-done), kind=kOutput, calls=%fused_computation | convolution fusion | flops 604372992 | bytes 2752512 | tf_op jit(solution)/shard_map/dot_general | solution.py:171
  63.9 3.6 %all-to-all-start.2 = ((bf16[4,128,768]{2,1,0:T(8,128)(2,1)}), bf16[4,128,768]{2,1,0:T(8,128)(2,1)S(1)}, u32[]{:S(2)}, u32[]{:S(2)}) async-start(bf16[4,128,768]{2,1,0:T(8,128)(2,1)} %bitcast.7), calls=%async_computation.2 | async-start | bytes 1572864 | tf_op jit(solution)/shard_map/all_to_all | solution.py:175
  67.7 2.4 %convolution_convert_fusion.1 = bf16[512,384]{1,0:T(8,128)(2,1)} fusion(bf16[512,768]{1,0:T(8,128)(2,1)S(1)} %shard_map.82, bf16[768,1152]{1,0:T(8,128)(2,1)} %all-gather.4.cloned.1.call-done), kind=kOutput, calls=%fused_computation.1 | convolution fusion | flops 302186496 | bytes 1769472 | tf_op jit(solution)/shard_map/dot_general | solution.py:171
  70.1 9.7 %all-to-all-done.2.share_ref = bf16[4,128,768]{2,1,0:T(8,128)(2,1)S(1)} async-done(((bf16[4,128,768]{2,1,0:T(8,128)(2,1)}), bf16[4,128,768]{2,1,0:T(8,128)(2,1)S(1)}, u32[]{:S(2)}, u32[]{:S(2)}) %all-to-all-start.2) | async-done | bytes 786464 | tf_op jit(solution)/shard_map/all_to_all | solution.py:175
  79.8 0.2 shard_map.84.source_ref.own_ref
  80.0 0.7 collective-permute-start.1
  80.7 7.3 %all-to-all-start.3 = ((bf16[4,128,384]{2,1,0:T(8,128)(2,1)}), bf16[4,128,384]{2,1,0:T(8,128)(2,1)S(1)}, u32[]{:S(2)}, u32[]{:S(2)}) async-start(bf16[4,128,384]{2,1,0:T(8,128)(2,1)} %bitcast.6), calls=%async_computation.3 | async-start | bytes 786432 | tf_op jit(solution)/shard_map/all_to_all | solution.py:179
  88.0 3.4 %collective-permute-start.2 = (bf16[128,768]{1,0:T(8,128)(2,1)S(1)}, bf16[128,768]{1,0:T(8,128)(2,1)S(1)}, u32[]{:S(2)}, u32[]{:S(2)}) collective-permute-start(bf16[128,768]{1,0:T(8,128)(2,1)S(1)} %shard_map.86), channel_id=1, source_target_pairs={{0,16},{16,0},{32,48},{48,32},{64,80},{80,64},{96,112},{112,96},{1... | collective-permute-start | bytes 589832 | tf_op jit(solution)/shard_map/ppermute | solution.py:186
  91.8 2.5 %all-to-all-done.3.share_ref = bf16[4,128,384]{2,1,0:T(8,128)(2,1)S(1)} async-done(((bf16[4,128,384]{2,1,0:T(8,128)(2,1)}), bf16[4,128,384]{2,1,0:T(8,128)(2,1)S(1)}, u32[]{:S(2)}, u32[]{:S(2)}) %all-to-all-start.3) | async-done | bytes 393248 | tf_op jit(solution)/shard_map/all_to_all | solution.py:179
  94.3 0.1 shard_map.85.query_ref
  94.4 2.9 %collective-permute-done.2.even_ref = bf16[128,768]{1,0:T(8,128)(2,1)S(1)} collective-permute-done((bf16[128,768]{1,0:T(8,128)(2,1)S(1)}, bf16[128,768]{1,0:T(8,128)(2,1)S(1)}, u32[]{:S(2)}, u32[]{:S(2)}) %collective-permute-start.2) | collective-permute-done | bytes 196640 | tf_op jit(solution)/shard_map/ppermute | solution.py:186
  97.3 0.5 shard_map.87
  97.8 13.5 %all_to_all.27 = bf16[4,128,384]{2,1,0:T(8,128)(2,1)S(1)} all-to-all(bf16[4,128,384]{2,1,0:T(8,128)(2,1)S(1)} %shard_map.87), channel_id=1, replica_groups=mesh['z'=8,'x'=4,'y'=4,'core'=2,'cfg'=2] {'y'}, dimensions={0} | all-to-all | bytes 786432 | tf_op jit(solution)/shard_map/all_to_all | solution.py:189
  111.4 5.1 %all_gather.17 = bf16[8,128,384]{2,1,0:T(8,128)(2,1)S(1)} all-gather(bf16[4,128,384]{2,1,0:T(8,128)(2,1)S(1)} %all_to_all.27), channel_id=1, replica_groups=mesh['z'=8,'x'=4,'y'=4,'core'=2,'cfg'=2] {'core'}, dimensions={0}, use_global_device_ids=true | all-gather | bytes 1179648 | tf_op jit(solution)/shard_map/all_gather | solution.py:190
  116.5 2.9 %fusion.1 = bf16[128,384]{1,0:T(8,128)(2,1)} fusion(bf16[8,128,384]{2,1,0:T(8,128)(2,1)S(1)} %all_gather.17, bf16[8,384,384]{2,1,0:T(8,128)(2,1)} %bitcast.30), kind=kOutput, calls=%fused_computation.4 | convolution fusion | flops 302039040 | bytes 3244032 | tf_op jit(solution)/shard_map/hrd,hdn->rn/dot_general | solution.py:191
  (28 shorter events, 0.8 us)
Async XLA Ops:
  6.5 26.7 %copy-start.2 = (bf16[128,384]{1,0:T(8,128)(2,1)S(1)}, bf16[128,384]{1,0:T(8,128)(2,1)}, u32[]{:S(2)}) copy-start(bf16[128,384]{1,0:T(8,128)(2,1)} %param.8) | copy-start | bytes 294916
  6.5 54.4 %all-gather.4.cloned.1.call-start = ((), (), s32[]{:S(2)}) async-start(), calls=%async_computation.5 | async-start | bytes 1990656 | tf_op jit(solution)/shard_map/all_gather | solution.py:152
  8.2 108.3 %all-gather.6.cloned.1.call-start = ((), (), s32[]{:S(2)}) async-start(), calls=%async_computation.6 | async-start | bytes 2654208 | tf_op jit(solution)/shard_map/all_gather | solution.py:167
  8.3 14.5 %collective-permute-start = (bf16[96,384]{1,0:T(8,128)(2,1)}, bf16[96,384]{1,0:T(8,128)(2,1)S(1)}, u32[]{:S(2)}, u32[]{:S(2)}) collective-permute-start(bf16[96,384]{1,0:T(8,128)(2,1)} %bitcast.32), channel_id=1, source_target_pairs={{0,0},{2,256},{4,64},{6,320},{8,128},{10,384},{12,192},{14,448},{6... | collective-permute-start | bytes 221192 | tf_op jit(solution)/shard_map/ppermute | solution.py:157
  63.9 15.9 %copy-start = (f32[128]{0:T(128)S(1)}, f32[128]{0:T(128)}, u32[]{:S(2)}) copy-start(f32[128]{0:T(128)} %param.14) | copy-start | bytes 1540
  63.9 15.9 %all-to-all-start.2 = ((bf16[4,128,768]{2,1,0:T(8,128)(2,1)}), bf16[4,128,768]{2,1,0:T(8,128)(2,1)S(1)}, u32[]{:S(2)}, u32[]{:S(2)}) async-start(bf16[4,128,768]{2,1,0:T(8,128)(2,1)} %bitcast.7), calls=%async_computation.2 | async-start | bytes 1572864 | tf_op jit(solution)/shard_map/all_to_all | solution.py:175
  67.7 23.9 %copy-start.3 = (s32[3,2,6]{2,1,0:T(2,128)S(1)}, s32[3,2,6]{2,1,0:T(2,128)}, u32[]{:S(2)}) copy-start(s32[3,2,6]{2,1,0:T(2,128)} %param.15) | copy-start | bytes 436
  67.7 26.6 %copy-start.1 = (f32[128]{0:T(128)S(1)}, f32[128]{0:T(128)}, u32[]{:S(2)}) copy-start(f32[128]{0:T(128)} %param.13) | copy-start | bytes 1540
  80.0 14.4 %collective-permute-start.1 = (bf16[128,768]{1,0:T(8,128)(2,1)S(1)}, bf16[128,768]{1,0:T(8,128)(2,1)S(1)}, u32[]{:S(2)}, u32[]{:S(2)}) collective-permute-start(bf16[128,768]{1,0:T(8,128)(2,1)S(1)} %shard_map.84.source_ref.own_ref), channel_id=1, source_target_pairs={{16,32},{32,16},{48,64},{64,48},{80,96},{96,80},{112,128},{128,112... | collective-permute-start | bytes 589832 | tf_op jit(solution)/shard_map/ppermute | solution.py:185
  80.7 13.6 %all-to-all-start.3 = ((bf16[4,128,384]{2,1,0:T(8,128)(2,1)}), bf16[4,128,384]{2,1,0:T(8,128)(2,1)S(1)}, u32[]{:S(2)}, u32[]{:S(2)}) async-start(bf16[4,128,384]{2,1,0:T(8,128)(2,1)} %bitcast.6), calls=%async_computation.3 | async-start | bytes 786432 | tf_op jit(solution)/shard_map/all_to_all | solution.py:179
  88.0 9.4 %collective-permute-start.2 = (bf16[128,768]{1,0:T(8,128)(2,1)S(1)}, bf16[128,768]{1,0:T(8,128)(2,1)S(1)}, u32[]{:S(2)}, u32[]{:S(2)}) collective-permute-start(bf16[128,768]{1,0:T(8,128)(2,1)S(1)} %shard_map.86), channel_id=1, source_target_pairs={{0,16},{16,0},{32,48},{48,32},{64,80},{80,64},{96,112},{112,96},{1... | collective-permute-start | bytes 589832 | tf_op jit(solution)/shard_map/ppermute | solution.py:186
Sparse Core Ops, SparseCore 0:
  9.4 45.5 all-gather.3
  57.1 47.4 all-gather.5
